TPU v7x, 32 devices: a whole 2x2x4 slice. The times are simulated.
32 devices in a mesh: chan: 4 (over x, core), vox: 8 (over z, y).
Axes of the slice: x: 2, y: 2, z: 4, core: 2. Of those that a mesh axis runs over, the one named last changes fastest.
Arguments:
- features: bfloat16 [256, 5632], P('chan'), may hold values from -6 to 6
- hrf_filters: float32 [3, 5632, 16], P(None, 'chan'), may hold values from -1.5 to 1.5
- weights: bfloat16 [3, 5632, 40960], P(None, 'chan', 'vox'), may hold values from -0.046875 to 0.046875
- voxel_parcel: int32 [40960], P('vox'), may hold values from 0 to 799, as said below
- parcel_owner: int32 [800], replicated, may hold values from 0 to 7, as said below
Outputs:
- owned: bfloat16 [64, 1280, 256], P('vox', None, 'chan')
Inputs may be any that keep to these rules, and one draw needn't show every extreme that they name: `voxel_parcel`: among the 5120 voxels of one index of vox, at most 1280 belong to parcels of one owner, and some owner gets exactly 1280; one owner gets exactly 1280 from every index of vox. `parcel_owner`: every owner holds exactly 100 parcels.
All inputs are finite; a program needn't handle non-finite values.
Results may differ from a plain program's by a relative error of at most 0.01.
Values may be sent and summed in bfloat16 or wider, within the bound.
No kernel may reach another device: no remote copies, remote signals or barrier semaphores. Data moves between devices by JAX's collectives and lax.ppermute only.
A program may use at most 128 MiB of HBM per device.

v0:
```python
import jax
import jax.numpy as jnp
from jax import lax
from jax.sharding import PartitionSpec as P

FILTER_TAPS = 16
TAP_SPACING = 2


def shards(features, hrf_filters, weights, voxel_parcel, parcel_owner):
    by_channel = lax.all_to_all(features, "chan", split_axis=1, concat_axis=0, tiled=True)
    series = by_channel.astype(jnp.float32).T
    time_len = series.shape[1]
    chan_width = series.shape[0]
    largest_delay = TAP_SPACING * (FILTER_TAPS - 1)
    padded = jnp.pad(series, ((0, 0), (largest_delay, 0)))
    filtered = jnp.zeros((hrf_filters.shape[0], chan_width, time_len), jnp.float32)
    for delay_index in range(FILTER_TAPS):
        window_start = largest_delay - TAP_SPACING * delay_index
        lagged = padded[:, window_start : window_start + time_len]
        filtered = filtered + hrf_filters[:, :, delay_index][:, :, None] * lagged[None]
    design = filtered.astype(jnp.bfloat16).reshape(-1, time_len)
    weight_panel = weights.reshape(-1, weights.shape[2])
    partial_value = lax.dot_general(
        weight_panel, design, (((0,), (0,)), ((), ())), preferred_element_type=jnp.float32
    )
    owner_count = lax.axis_size("vox")
    chan_count = lax.axis_size("chan")
    block_len = time_len // chan_count
    send_cap = 2 * voxel_parcel.shape[0] // owner_count
    owners_here = jnp.take(parcel_owner, voxel_parcel)
    onehot = (owners_here[:, None] == jnp.arange(owner_count, dtype=jnp.int32)[None, :]).astype(
        jnp.int32
    )
    before = jnp.cumsum(onehot, axis=0) - onehot
    slot_index = jnp.sum(before * onehot, axis=1)
    target_row = owners_here * send_cap + slot_index
    rounded = partial_value.astype(jnp.bfloat16)
    packed = jnp.zeros((owner_count * send_cap, time_len), jnp.bfloat16).at[target_row].set(rounded)
    packed = packed.reshape(owner_count, send_cap, time_len)
    received = lax.all_to_all(
        lax.all_to_all(packed, "chan", split_axis=2, concat_axis=2, tiled=True),
        "vox",
        split_axis=0,
        concat_axis=0,
        tiled=True,
    )
    summed = (
        received.astype(jnp.float32)
        .reshape(owner_count, send_cap, chan_count, block_len)
        .sum(axis=2)
    )
    return summed.astype(jnp.bfloat16)


def solution(mesh):
    return jax.shard_map(
        shards,
        mesh=mesh,
        in_specs=(P("chan", None), P(None, "chan", None), P(None, "chan", "vox"), P("vox"), P()),
        out_specs=P("vox", None, "chan"),
        check_vma=False,
    )
```

profile of v0, /device:TPU:0, one launch (start us, length us, event | category | flops | bytes accessed | tf_op | source)
XLA Modules:
  0.0 292.0 jit_solution(2070411900357518932)
XLA Ops:
  0.0 0.0 copy-start
  0.0 0.0 copy-start.2
  0.0 0.0 copy-start.3
  0.0 2.1 copy.52
  2.1 4.2 %all-to-all-start = ((bf16[64,4,1408]{2,0,1:T(8,128)(2,1)}), bf16[64,4,1408]{2,0,1:T(8,128)(2,1)S(1)}, u32[]{:S(2)}, u32[]{:S(2)}) async-start(bf16[64,4,1408]{2,0,1:T(8,128)(2,1)} %bitcast.70), calls=%async_computation | async-start | bytes 1441792 | tf_op jit(solution)/shard_map/all_to_all | solution.py:11
  6.3 0.0 copy-done.2
  6.3 0.2 fusion.41
  6.5 0.0 copy-done.3
  6.5 0.0 copy-done
  6.5 20.7 %gather_fusion = s32[5120]{0:T(1024)S(1)} fusion(s32[800]{0:T(1024)S(1)} %copy-done, s32[5120]{0:T(1024)S(1)} %fusion.40), kind=kCustom, calls=%fused_computation | custom fusion | bytes 61440 | tf_op jit(solution)/shard_map/jit(_take)/gather | solution.py:31
  27.3 2.3 reduce-window.6
  29.6 0.3 slice_reduce_fusion
  30.0 0.2 reduce-window.9
  30.1 0.1 add_bitcast_fusion
  30.3 0.1 fusion.38
  30.5 0.0 all-to-all-done
  30.6 0.1 transpose.61
  30.7 5.0 %pad_slice_fusion.14 = (f32[1408,256]{0,1:T(8,128)S(1)}, f32[1408,256]{0,1:T(8,128)S(1)}, f32[1408,256]{0,1:T(8,128)S(1)}, f32[1408,256]{0,1:T(8,128)S(1)}, f32[...) fusion(f32[1408,256]{0,1:T(8,128)S(1)} %bitcast.72), kind=kLoop, calls=%fused_computation.54 | loop fusion | bytes 23068672 | tf_op jit(solution)/shard_map/slice | solution.py:20
  35.6 28.1 %fusion.1 = bf16[5120,256]{0,1:T(8,128)(2,1)} fusion(bf16[3,1408,5120]{2,1,0:T(8,128)(2,1)} %param.7, f32[1408,256]{0,1:T(8,128)} %get-tuple-element.19, f32[3,1408]{1,0:T(4,128)S(1)} %get-tuple-element.36, f32[1408,256]{0,1:T(8,128)} %get-tuple-element.18, f32[3,1408]{1,0:T(4,128)S(1)} %get-tuple-element.37, f32[1408,256]{0,1:T(8,128)} %get-tuple-element.17, ...), kind=kOutput, calls=%fused_computation.4 | convolution fusion | flops 11108876288 | bytes 69214208 | tf_op jit(solution)/shard_map/dot_general | solution.py:24
  63.7 3.0 %copy.13 = bf16[5120,256]{1,0:T(8,128)(2,1)S(1)} copy(bf16[5120,256]{0,1:T(8,128)(2,1)} %fusion.1) | data formatting | bytes 5242880 | tf_op jit(solution)/shard_map/convert_element_type | solution.py:38
  66.7 25.4 %scatter_custom_fusion = bf16[10240,256]{1,0:T(8,128)(2,1)} fusion(s32[5120]{0:T(1024)S(1)} %compare_select_fusion, bf16[5120,256]{1,0:T(8,128)(2,1)S(1)} %copy.13, bf16[]{:T(256)} %constant.10.clone.1), kind=kCustom, calls=%fused_computation.6 | custom fusion | bytes 5242882 | tf_op jit(solution)/shard_map/scatter | solution.py:39
  92.2 8.7 %copy.14 = bf16[8,1280,256]{1,0,2:T(8,128)(2,1)} copy(bf16[8,1280,256]{2,1,0:T(8,128)(2,1)} %bitcast.74) | data formatting | bytes 10485760 | tf_op jit(solution)/shard_map/reshape | solution.py:40
  100.8 63.5 %all_to_all.23 = bf16[8,1280,256]{1,0,2:T(8,128)(2,1)S(1)} all-to-all(bf16[8,1280,256]{1,0,2:T(8,128)(2,1)} %copy.14), channel_id=1, replica_groups=mesh['chan'=4,'vox'=8] {'chan'}, dimensions={2} | all-to-all | bytes 10485760 | tf_op jit(solution)/shard_map/all_to_all | solution.py:42
  164.3 1.0 copy.15
  165.3 122.0 %all_to_all.24 = bf16[8,1280,256]{1,2,0:T(8,128)(2,1)} all-to-all(bf16[8,1280,256]{1,2,0:T(8,128)(2,1)S(1)} %copy.15), channel_id=1, replica_groups=mesh['chan'=4,'vox'=8] {'vox'}, dimensions={0} | all-to-all | bytes 10485760 | tf_op jit(solution)/shard_map/all_to_all | solution.py:41
  287.3 0.0 copy-start.1
  287.3 4.7 %reduce = bf16[8,1280,64]{1,2,0:T(8,128)(2,1)} reduce(bf16[8,1280,4,64]{1,3,2,0:T(8,128)(2,1)} %bitcast.75, bf16[]{:T(256)} %constant.10.clone.1), dimensions={2}, to_apply=%region_4.5.clone | reduce | flops 1966080 | bytes 6553602 | tf_op jit(solution)/shard_map/reduce_sum | solution.py:51
  292.0 0.0 copy-done.1
  (12 shorter events, 0.2 us)
Async XLA Ops:
  0.0 6.5 %copy-start = (s32[800]{0:T(1024)S(1)}, s32[800]{0:T(1024)}, u32[]{:S(2)}) copy-start(s32[800]{0:T(1024)} %param.9) | copy-start | bytes 9604
  0.0 6.3 %copy-start.2 = (f32[3,1408,16]{1,2,0:T(8,128)S(1)}, f32[3,1408,16]{1,2,0:T(8,128)}, u32[]{:S(2)}) copy-start(f32[3,1408,16]{1,2,0:T(8,128)} %param.6) | copy-start | bytes 811012
  0.0 6.5 %copy-start.3 = (s32[5120]{0:T(1024)S(1)}, s32[5120]{0:T(1024)}, u32[]{:S(2)}) copy-start(s32[5120]{0:T(1024)} %param.8) | copy-start | bytes 61444
  2.1 28.5 %all-to-all-start = ((bf16[64,4,1408]{2,0,1:T(8,128)(2,1)}), bf16[64,4,1408]{2,0,1:T(8,128)(2,1)S(1)}, u32[]{:S(2)}, u32[]{:S(2)}) async-start(bf16[64,4,1408]{2,0,1:T(8,128)(2,1)} %bitcast.70), calls=%async_computation | async-start | bytes 1441792 | tf_op jit(solution)/shard_map/all_to_all | solution.py:11
  287.3 4.7 %copy-start.1 = (s32[800]{0:T(1024)S(1)}, s32[800]{0:T(1024)}, u32[]{:S(2)}) copy-start(s32[800]{0:T(1024)} %param.9) | copy-start | bytes 9604
where the time goes:
time: 293 us; the launch traced here: 292 us
  blocking collectives  185 us (63%)
  local copies, waits for them, and re-layouts  66.5 us (23%)
  matrix products  28.1 us (10%)
  other arithmetic  7.55 us (3%)
  starting transfers between devices  4.21 us (1%)
    all_to_all x1, blocking collectives, shards(): lax.all_to_all(lax.all_to_all(packed, 'chan', split_axis=2, concat_axis=2...  122 us
    all_to_all x1, blocking collectives, shards(): lax.all_to_all(packed, 'chan', split_axis=2, concat_axis=2, tiled=True)  63.5 us
    dot_general x1, matrix products, shards(): lax.dot_general(weight_panel, design, (((0,), (0,)), ((), ())), preferred...  28.1 us
    scatter x1, local copies, waits for them, and re-layouts, shards(): jnp.zeros((owner_count * send_cap, time_len), jnp.bfloat16).at[target_row]  25.4 us
    gather x1, local copies, waits for them, and re-layouts, shards(): owners_here = jnp.take(parcel_owner, voxel_parcel)  20.7 us
    reshape x1, local copies, waits for them, and re-layouts, shards(): packed = packed.reshape(owner_count, send_cap, time_len)  8.67 us
  transfers between devices with their start and end apart: 1, of which 0 were waited for; matrix products, arithmetic and copies ran while one was open for 8% of the time, Pallas kernels for 0%

commit v1 on v0

v1 whole, which is shorter than its diff:
```python
import functools

import jax
import jax.numpy as jnp
from jax import lax
from jax.experimental import pallas as pl
from jax.experimental.pallas import tpu as pltpu
from jax.sharding import PartitionSpec as P

FILTER_TAPS = 16
TAP_SPACING = 2
LANES = 128
SLOT_TILE = 128
VOX_BLOCK = 256
GROUP = 8
CHUNKS = 5
MIB = 1 << 20

VMEM = functools.partial(pl.BlockSpec, memory_space=pltpu.VMEM)
SMEM = functools.partial(pl.BlockSpec, memory_space=pltpu.SMEM)


def places_kernel(send_cap, owners, parcel_ref, table_ref, key_ref, start_ref):
    rows = parcel_ref.shape[0]
    parcel = parcel_ref[...]
    high, low = parcel >> 7, parcel & 127
    owner = jnp.zeros_like(parcel)
    for entry in range(table_ref.shape[0]):
        line = jnp.broadcast_to(table_ref[entry : entry + 1, :], parcel.shape)
        found = jnp.take_along_axis(line, low, axis=1, mode="promise_in_bounds")
        owner = jnp.where(high == entry, found, owner)
    above = lax.broadcasted_iota(jnp.int32, (LANES, LANES), 0) < lax.broadcasted_iota(jnp.int32, (LANES, LANES), 1)
    above = above.astype(jnp.float32).astype(jnp.bfloat16)
    ones = jnp.ones((LANES, LANES), jnp.bfloat16)
    ahead = lax.broadcasted_iota(jnp.int32, (rows, rows), 1) < lax.broadcasted_iota(jnp.int32, (rows, rows), 0)
    ahead = ahead.astype(jnp.float32).astype(jnp.bfloat16)
    step = VOX_BLOCK // LANES
    marks = start_ref.shape[0]
    block_ahead = lax.broadcasted_iota(jnp.int32, (marks, rows), 1) < step * lax.broadcasted_iota(jnp.int32, (marks, rows), 0)
    block_ahead = block_ahead.astype(jnp.float32).astype(jnp.bfloat16)
    lane = lax.broadcasted_iota(jnp.int32, (marks, LANES), 1)
    dot = functools.partial(jnp.dot, preferred_element_type=jnp.float32)
    key = jnp.zeros(parcel.shape, jnp.float32)
    starts = jnp.zeros((marks, LANES), jnp.float32)
    for o in range(owners):
        mine = owner == o
        hot = mine.astype(jnp.float32).astype(jnp.bfloat16)
        totals = dot(hot, ones).astype(jnp.bfloat16)
        slot = dot(hot, above) + dot(ahead, totals)
        key = jnp.where(mine, slot + float(o * send_cap), key)
        starts = jnp.where(lane == o, dot(block_ahead, totals), starts)
    key_ref[...] = key.astype(jnp.int32)
    start_ref[...] = starts.astype(jnp.int32)


def pairs_kernel(blocks, owners, start_ref, list_ref, count_ref):
    def at(index, count):
        block, owner = index // owners, lax.rem(index, owners)
        first, last = start_ref[block, owner], start_ref[block + 1, owner]
        low, high = first >> 7, (last - 1) >> 7
        word = (block << 16) | (owner << 8) | low
        for extra in range(VOX_BLOCK // SLOT_TILE + 1):
            list_ref[count + extra] = word + extra
        return count + jnp.where(last > first, high - low + 1, 0)

    count = lax.fori_loop(0, blocks * owners, at, jnp.int32(0))
    for extra in range(GROUP):
        list_ref[count + extra] = -1
    count_ref[0] = (count + GROUP - 1) // GROUP


def design_kernel(place_ref, series_ref, filter_ref, design_ref, shifted):
    time_len, width = series_ref.shape
    bases = filter_ref.shape[0]
    parts = place_ref.shape[0]
    block = time_len // parts
    rows = 32
    lead = TAP_SPACING * FILTER_TAPS
    for s in range(shifted.shape[0]):
        shifted[s, : lead + 8, :] = jnp.zeros((lead + 8, LANES), jnp.float32)

    def columns(tile, carry):
        at = pl.ds(pl.multiple_of(tile * LANES, LANES), LANES)
        series = series_ref[:, at].astype(jnp.float32)
        for s in range(shifted.shape[0]):
            shifted[s, lead + s * TAP_SPACING : lead + s * TAP_SPACING + time_len, :] = series
        for group in range(time_len // rows):
            sums = [jnp.zeros((rows, LANES), jnp.float32) for _ in range(bases)]
            for tap in range(FILTER_TAPS):
                delay = tap * TAP_SPACING
                start = lead + group * rows - 8 * (delay // 8)
                lagged = shifted[(delay % 8) // TAP_SPACING, start : start + rows, :]
                for b in range(bases):
                    sums[b] = sums[b] + filter_ref[b, tap : tap + 1, at] * lagged
            part, inner = (group * rows) // block, (group * rows) % block
            row = pl.ds(pl.multiple_of(place_ref[part] * block + inner, rows), rows)
            for b in range(bases):
                lanes = pl.ds(pl.multiple_of(b * width + tile * LANES, LANES), LANES)
                design_ref[row, lanes] = sums[b].astype(jnp.bfloat16)
        return carry

    lax.fori_loop(0, width // LANES, columns, 0)


def product_kernel(design_ref, weight_ref, keep_ref, send_ref):
    half = keep_ref.shape[0]
    weight = weight_ref[...]
    weight = weight.reshape(-1, weight.shape[2])
    total = jnp.dot(design_ref[...], weight, preferred_element_type=jnp.float32).astype(jnp.bfloat16)
    keep_ref[...] = total[:half]
    send_ref[...] = total[half:]


def product(design, weights, first, width):
    bases, depth, _ = weights.shape
    time_len = design.shape[0]
    out = jax.ShapeDtypeStruct((time_len // 2, width), jnp.bfloat16)
    offset = first // VOX_BLOCK
    return pl.pallas_call(
        product_kernel,
        grid=(width // VOX_BLOCK,),
        in_specs=[
            pl.BlockSpec(design.shape, lambda i: (0, 0)),
            pl.BlockSpec((bases, depth, VOX_BLOCK), lambda i: (0, 0, i + offset)),
        ],
        out_specs=[pl.BlockSpec((time_len // 2, VOX_BLOCK), lambda i: (0, i))] * 2,
        out_shape=[out, out],
        compiler_params=pltpu.CompilerParams(vmem_limit_bytes=24 * MIB),
        cost_estimate=pl.CostEstimate(
            flops=2 * time_len * bases * depth * width,
            bytes_accessed=2 * bases * depth * width + 2 * time_len * width,
            transcendentals=0,
        ),
        name="product",
    )(design, weights)


def pack_kernel(send_cap, chunks, list_ref, count_ref, key_ref, *refs):
    mine, theirs, packed_ref, summed = refs[:chunks], refs[chunks : 2 * chunks], refs[-2], refs[-1]
    width = mine[0].shape[1]
    for c in range(chunks):
        total = mine[c][...] + theirs[c][...].astype(jnp.float32)
        summed[:, c * width : (c + 1) * width] = total.astype(jnp.bfloat16)
    packed_ref[...] = jnp.zeros_like(packed_ref)
    slots = lax.broadcasted_iota(jnp.int32, (SLOT_TILE, VOX_BLOCK), 0)

    def group(g, carry):
        for i in range(GROUP):
            word = list_ref[g * GROUP + i]
            real = word >= 0
            word = jnp.where(real, word, 0)
            block, owner, tile = word >> 16, (word >> 8) & 255, word & 255
            base = jnp.where(real, owner * send_cap + tile * SLOT_TILE, -(1 << 20))
            hit = (key_ref[block] - base) == slots
            hit = jnp.where(hit, 1.0, 0.0).astype(jnp.bfloat16)
            values = summed[:, pl.ds(pl.multiple_of(block * VOX_BLOCK, VOX_BLOCK), VOX_BLOCK)]
            moved = lax.dot_general(values, hit, (((1,), (1,)), ((), ())), preferred_element_type=jnp.float32)
            at = pl.ds(pl.multiple_of(tile * SLOT_TILE, SLOT_TILE), SLOT_TILE)
            packed_ref[owner, :, at] = packed_ref[owner, :, at] + moved.astype(jnp.bfloat16)
        return carry

    lax.fori_loop(0, count_ref[0], group, 0)


def shards(features, hrf_filters, weights, voxel_parcel, parcel_owner):
    owners, parts = lax.axis_size("vox"), lax.axis_size("chan")
    me = lax.axis_index("chan")
    voxels = voxel_parcel.shape[0]
    send_cap = 2 * voxels // owners
    bases, depth, _ = weights.shape
    blocks = voxels // VOX_BLOCK
    time_block = features.shape[0]
    time_len = time_block * parts

    by_channel = lax.all_to_all(features, "chan", split_axis=1, concat_axis=0, tiled=True)

    table_rows = -(-parcel_owner.shape[0] // LANES)
    table = jnp.pad(parcel_owner, (0, table_rows * LANES - parcel_owner.shape[0])).reshape(table_rows, LANES)
    marks = -(-(blocks + 1) // 8) * 8
    key, starts = pl.pallas_call(
        functools.partial(places_kernel, send_cap, owners),
        in_specs=[VMEM(), VMEM()],
        out_specs=[VMEM(), VMEM()],
        out_shape=[
            jax.ShapeDtypeStruct((voxels // LANES, LANES), jnp.int32),
            jax.ShapeDtypeStruct((marks, LANES), jnp.int32),
        ],
        name="places",
    )(voxel_parcel.reshape(-1, LANES), table)
    pairs = blocks * owners + voxels // SLOT_TILE + owners + 2 * GROUP
    pair_list, pair_groups = pl.pallas_call(
        functools.partial(pairs_kernel, blocks, owners),
        in_specs=[SMEM()],
        out_specs=[SMEM(), SMEM()],
        out_shape=[jax.ShapeDtypeStruct((pairs,), jnp.int32), jax.ShapeDtypeStruct((1,), jnp.int32)],
        name="pairs",
    )(starts)
    key = key.reshape(blocks, 1, VOX_BLOCK)

    bits = parts.bit_length() - 1
    order = jnp.arange(parts, dtype=jnp.int32) ^ me
    place = sum(((order >> bit) & 1) << (bits - 1 - bit) for bit in range(bits)).astype(jnp.int32)
    design = pl.pallas_call(
        design_kernel,
        in_specs=[SMEM(), VMEM(), VMEM()],
        out_specs=VMEM(),
        out_shape=jax.ShapeDtypeStruct((time_len, bases * depth), jnp.bfloat16),
        scratch_shapes=[pltpu.VMEM((8 // TAP_SPACING, time_len + TAP_SPACING * FILTER_TAPS + 8, LANES), jnp.float32)],
        compiler_params=pltpu.CompilerParams(vmem_limit_bytes=24 * MIB),
        name="design",
    )(place, by_channel, jnp.transpose(hrf_filters, (0, 2, 1)))

    width = voxels // CHUNKS
    mine, theirs = [], []
    for c in range(CHUNKS):
        keep, send = product(design, weights, c * width, width)
        keep = keep.astype(jnp.float32)
        for bit in range(bits):
            got = lax.ppermute(send, "chan", [(i, i ^ (1 << bit)) for i in range(parts)])
            if bit == bits - 1:
                mine.append(keep)
                theirs.append(got)
            else:
                total = keep + got.astype(jnp.float32)
                rows = total.shape[0] // 2
                keep, send = total[:rows], total[rows:].astype(jnp.bfloat16)

    packed = pl.pallas_call(
        functools.partial(pack_kernel, send_cap, CHUNKS),
        in_specs=[SMEM(), SMEM()] + [VMEM()] * (1 + 2 * CHUNKS),
        out_specs=VMEM(),
        out_shape=jax.ShapeDtypeStruct((owners, time_block, send_cap), jnp.bfloat16),
        scratch_shapes=[pltpu.VMEM((time_block, voxels), jnp.bfloat16)],
        compiler_params=pltpu.CompilerParams(vmem_limit_bytes=24 * MIB),
        name="pack",
    )(pair_list, pair_groups, key, *mine, *theirs)
    received = lax.all_to_all(packed, "vox", split_axis=0, concat_axis=0, tiled=True)
    return jnp.transpose(received, (0, 2, 1))


def solution(mesh):
    return jax.shard_map(
        shards,
        mesh=mesh,
        in_specs=(P("chan", None), P(None, "chan", None), P(None, "chan", "vox"), P("vox"), P()),
        out_specs=P("vox", None, "chan"),
        check_vma=False,
    )
```

time: 293 us -> 118 us (0.40)
  blocking collectives: 185 us -> 37.6 us
  local copies, waits for them, and re-layouts: 66.5 us -> 5.85 us
  Pallas kernels: 0 us -> 50.6 us
  matrix products: 28.1 us -> 0 us
  waiting for transfers between devices: 0.01 us -> 13.3 us
  other arithmetic: 7.55 us -> 0.31 us
  starting transfers between devices: 4.21 us -> 10 us
    all_to_all x2 -> x1, blocking collectives: 185 us -> 37.6 us  [shards(): lax.all_to_all(packed, 'vox', split_axis=0, concat_axis=0, tiled=True)]
    pallas_call x0 -> x9, Pallas kernels: none -> 50.6 us  [the longest x5 28.5 us: product(): pl.pallas_call(product_kernel, grid=(width // VOX_BLOCK,), in_specs=[pl.B...]
    dot_general x1 -> x0, matrix products: 28.1 us -> none  [shards(): lax.dot_general(weight_panel, design, (((0,), (0,)), ((), ())), preferred...]
    scatter x1 -> x0, local copies, waits for them, and re-layouts: 25.4 us -> none  [shards(): jnp.zeros((owner_count * send_cap, time_len), jnp.bfloat16).at[target_row]]
    gather x1 -> x0, local copies, waits for them, and re-layouts: 20.7 us -> none  [shards(): owners_here = jnp.take(parcel_owner, voxel_parcel)]
    all_to_all x1, waiting for transfers between devices: 0.01 us -> 10.9 us  [shards(): lax.all_to_all(features, 'chan', split_axis=1, concat_axis=0, tiled=True)]
    reshape x1, local copies, waits for them, and re-layouts: 8.67 us -> 0.58 us  [shards(): jnp.pad(parcel_owner, (0, table_rows * LANES - parcel_owner.shape[0]))]
    ppermute x0 -> x10, starting transfers between devices: none -> 5.82 us  [shards(): got = lax.ppermute(send, 'chan', [(i, i ^ 1 << bit) for i in range(parts)])]
  transfers between devices with their start and end apart: 1 -> 11, of which waited for: 0 -> 2; matrix products, arithmetic and copies ran while one was open for 8% -> 3% of each run, Pallas kernels for 0% -> 16%
where the time goes in v1:
time: 118 us
  Pallas kernels  50.6 us (43%)
  blocking collectives  37.6 us (32%)
  waiting for transfers between devices  13.3 us (11%)
  starting transfers between devices  10 us (8%)
  local copies, waits for them, and re-layouts  5.85 us (5%)
    all_to_all x1, blocking collectives, shards(): lax.all_to_all(packed, 'vox', split_axis=0, concat_axis=0, tiled=True)  37.6 us
    pallas_call x5, Pallas kernels, product(): pl.pallas_call(product_kernel, grid=(width // VOX_BLOCK,), in_specs=[pl.B...  28.5 us
    all_to_all x1, waiting for transfers between devices, shards(): lax.all_to_all(features, 'chan', split_axis=1, concat_axis=0, tiled=True)  10.9 us
    pallas_call x1, Pallas kernels, shards(): pl.pallas_call(functools.partial(pack_kernel, send_cap, CHUNKS), in_specs...  9.33 us
    ppermute x10, starting transfers between devices, shards(): got = lax.ppermute(send, 'chan', [(i, i ^ 1 << bit) for i in range(parts)])  5.82 us
    pallas_call x1, Pallas kernels, shards(): pl.pallas_call(design_kernel, in_specs=[SMEM(), VMEM(), VMEM()], out_spec...  5.59 us
    pallas_call x1, Pallas kernels, shards(): pl.pallas_call(functools.partial(pairs_kernel, blocks, owners), in_specs=...  4.29 us
    all_to_all x1, starting transfers between devices, shards(): lax.all_to_all(features, 'chan', split_axis=1, concat_axis=0, tiled=True)  4.21 us
  transfers between devices with their start and end apart: 11, of which 2 were waited for; matrix products, arithmetic and copies ran while one was open for 3% of the time, Pallas kernels for 16%

profile of v1, /device:TPU:0, one launch (start us, length us, event | category | flops | bytes accessed | tf_op | source)
XLA Modules:
  0.0 117.9 jit_solution(16439619262360470157)
XLA Ops:
  0.0 2.1 %copy.9 = bf16[8,4,8,1408]{3,2,0,1:T(8,128)(2,1)} copy(bf16[8,4,8,1408]{3,2,1,0:T(8,128)(2,1)} %bitcast.17) | data formatting | bytes 1441792 | tf_op jit(solution)/shard_map/all_to_all | solution.py:175
  2.1 4.2 %all-to-all-start = ((bf16[64,4,1408]{2,0,1:T(8,128)(2,1)}), bf16[64,4,1408]{2,0,1:T(8,128)(2,1)S(1)}, u32[]{:S(2)}, u32[]{:S(2)}) async-start(bf16[64,4,1408]{2,0,1:T(8,128)(2,1)} %bitcast.12), calls=%async_computation | async-start | bytes 1441792 | tf_op jit(solution)/shard_map/all_to_all | solution.py:175
  6.3 10.9 %all-to-all-done = bf16[64,4,1408]{2,0,1:T(8,128)(2,1)S(1)} async-done(((bf16[64,4,1408]{2,0,1:T(8,128)(2,1)}), bf16[64,4,1408]{2,0,1:T(8,128)(2,1)S(1)}, u32[]{:S(2)}, u32[]{:S(2)}) %all-to-all-start) | async-done | bytes 720928 | tf_op jit(solution)/shard_map/all_to_all | solution.py:175
  17.2 5.6 %design.1.design_ref = bf16[256,4224]{1,0:T(8,128)(2,1)S(1)} custom-call(s32[4]{0:T(128)S(1)} %shift-left_add_fusion.place_ref, bf16[256,1408]{1,0:T(8,128)(2,1)S(1)} %bitcast.13, f32[3,16,1408]{2,1,0:T(8,128)S(1)} %bitcast.14), custom_call_target="tpu_custom_call" | custom-call | tf_op jit(solution)/shard_map/design/pallas_call | solution.py:203
  22.8 5.7 %product.8 = (bf16[128,1024]{1,0:T(8,128)(2,1)S(1)}, bf16[128,1024]{1,0:T(8,128)(2,1)S(1)}) custom-call(bf16[256,4224]{1,0:T(8,128)(2,1)S(1)} %design.1.design_ref, bf16[3,1408,5120]{2,1,0:T(8,128)(2,1)} %weight_ref.9), custom_call_target="tpu_custom_call" | custom-call | flops 2214592512 | bytes 9175040 | tf_op jit(solution)/shard_map/product/pallas_call | solution.py:119
  28.6 5.7 %product.9 = (bf16[128,1024]{1,0:T(8,128)(2,1)S(1)}, bf16[128,1024]{1,0:T(8,128)(2,1)S(1)}) custom-call(bf16[256,4224]{1,0:T(8,128)(2,1)S(1)} %design.1.design_ref, bf16[3,1408,5120]{2,1,0:T(8,128)(2,1)} %weight_ref.9), custom_call_target="tpu_custom_call" | custom-call | flops 2214592512 | bytes 9175040 | tf_op jit(solution)/shard_map/product/pallas_call | solution.py:119
  34.3 5.7 %product.7 = (bf16[128,1024]{1,0:T(8,128)(2,1)S(1)}, bf16[128,1024]{1,0:T(8,128)(2,1)S(1)}) custom-call(bf16[256,4224]{1,0:T(8,128)(2,1)S(1)} %design.1.design_ref, bf16[3,1408,5120]{2,1,0:T(8,128)(2,1)} %weight_ref.9), custom_call_target="tpu_custom_call" | custom-call | flops 2214592512 | bytes 9175040 | tf_op jit(solution)/shard_map/product/pallas_call | solution.py:119
  40.0 0.1 collective-permute-start.3
  40.1 5.7 %product.6 = (bf16[128,1024]{1,0:T(8,128)(2,1)S(1)}, bf16[128,1024]{1,0:T(8,128)(2,1)S(1)}) custom-call(bf16[256,4224]{1,0:T(8,128)(2,1)S(1)} %design.1.design_ref, bf16[3,1408,5120]{2,1,0:T(8,128)(2,1)} %weight_ref.9), custom_call_target="tpu_custom_call" | custom-call | flops 2214592512 | bytes 9175040 | tf_op jit(solution)/shard_map/product/pallas_call | solution.py:119
  45.8 0.5 collective-permute-start.4
  46.3 5.7 %product.5 = (bf16[128,1024]{1,0:T(8,128)(2,1)S(1)}, bf16[128,1024]{1,0:T(8,128)(2,1)S(1)}) custom-call(bf16[256,4224]{1,0:T(8,128)(2,1)S(1)} %design.1.design_ref, bf16[3,1408,5120]{2,1,0:T(8,128)(2,1)} %weight_ref.9), custom_call_target="tpu_custom_call" | custom-call | flops 2214592512 | bytes 9175040 | tf_op jit(solution)/shard_map/product/pallas_call | solution.py:119
  52.0 0.1 collective-permute-start.2
  52.1 0.5 collective-permute-start.1
  52.6 0.1 collective-permute-start
  52.7 0.1 convert_add_fusion.1
  52.8 0.4 collective-permute-start.8
  53.3 1.7 %collective-permute-start.9 = (bf16[64,1024]{1,0:T(8,128)(2,1)S(1)}, bf16[64,1024]{1,0:T(8,128)(2,1)S(1)}, u32[]{:S(2)}, u32[]{:S(2)}) collective-permute-start(bf16[64,1024]{1,0:T(8,128)(2,1)S(1)} %slice.60), channel_id=1, source_target_pairs={{0,16},{8,24},{16,0},{24,8},{1,17},{9,25},{17,1},{25,9},{2,18},{10... | collective-permute-start | bytes 393224 | tf_op jit(solution)/shard_map/ppermute | solution.py:219
  55.0 0.1 convert_add_fusion.2
  55.1 0.7 slice.62
  55.8 0.4 collective-permute-start.7
  56.2 0.7 slice.63
  56.9 1.7 %collective-permute-start.6 = (bf16[64,1024]{1,0:T(8,128)(2,1)}, bf16[64,1024]{1,0:T(8,128)(2,1)S(1)}, u32[]{:S(2)}, u32[]{:S(2)}) collective-permute-start(bf16[64,1024]{1,0:T(8,128)(2,1)} %slice.63), channel_id=1, source_target_pairs={{0,16},{8,24},{16,0},{24,8},{1,17},{9,25},{17,1},{25,9},{2,18},{10... | collective-permute-start | bytes 393224 | tf_op jit(solution)/shard_map/ppermute | solution.py:219
  58.5 0.1 convert_add_fusion.4
  58.6 0.7 slice.64
  59.3 0.4 collective-permute-start.5
  59.6 0.6 pad_bitcast_fusion.table_ref
  60.2 2.9 %places.1 = (s32[40,128]{1,0:T(8,128)}, s32[24,128]{1,0:T(8,128)}) custom-call(s32[40,128]{1,0:T(8,128)} %bitcast.18, s32[7,128]{1,0:T(8,128)} %pad_bitcast_fusion.table_ref), custom_call_target="tpu_custom_call" | custom-call | tf_op jit(solution)/shard_map/places/pallas_call | solution.py:180
  63.1 4.3 %pairs.1 = (s32[224]{0:T(256)}, s32[1]{0:T(128)}) custom-call(s32[24,128]{1,0:T(8,128)} %get-tuple-element.19.start_ref), custom_call_target="tpu_custom_call" | custom-call | tf_op jit(solution)/shard_map/pairs/pallas_call | solution.py:191
  67.6 2.3 %collective-permute-done.5.refs_5_ = bf16[64,1024]{1,0:T(8,128)(2,1)S(1)} collective-permute-done((bf16[64,1024]{1,0:T(8,128)(2,1)}, bf16[64,1024]{1,0:T(8,128)(2,1)S(1)}, u32[]{:S(2)}, u32[]{:S(2)}) %collective-permute-start.5) | collective-permute-done | bytes 131104 | tf_op jit(solution)/shard_map/ppermute | solution.py:219
  69.9 9.3 %pack.1 = bf16[8,64,1280]{2,1,0:T(8,128)(2,1)S(1)} custom-call(s32[224]{0:T(256)S(1)} %copy-done.2, s32[1]{0:T(128)} %get-tuple-element.21.count_ref, s32[20,1,256]{2,1,0:T(1,128)S(1)} %bitcast.15, f32[64,1024]{1,0:T(8,128)S(1)} %slice.45.refs_0_, f32[64,1024]{1,0:T(8,128)S(1)} %slice.46.refs_1_, f32[64,1024]{1,0:T(8,128)S(1)} %slice.47.refs_2_, ...), custom_call_target="tpu_custom_call" | custom-call | tf_op jit(solution)/shard_map/pack/pallas_call | solution.py:228
  79.3 37.6 %all_to_all.24 = bf16[8,64,1280]{2,1,0:T(8,128)(2,1)S(1)} all-to-all(bf16[8,64,1280]{2,1,0:T(8,128)(2,1)S(1)} %pack.1), channel_id=1, replica_groups=mesh['chan'=4,'vox'=8] {'vox'}, dimensions={0} | all-to-all | bytes 2621440 | tf_op jit(solution)/shard_map/all_to_all | solution.py:237
  116.8 1.1 copy.11
  (27 shorter events, 0.3 us)
Async XLA Ops:
  0.0 17.2 %copy-start = (f32[3,1408,16]{1,2,0:T(8,128)S(1)}, f32[3,1408,16]{1,2,0:T(8,128)}, u32[]{:S(2)}) copy-start(f32[3,1408,16]{1,2,0:T(8,128)} %param.6) | copy-start | bytes 811012
  2.1 15.2 %all-to-all-start = ((bf16[64,4,1408]{2,0,1:T(8,128)(2,1)}), bf16[64,4,1408]{2,0,1:T(8,128)(2,1)S(1)}, u32[]{:S(2)}, u32[]{:S(2)}) async-start(bf16[64,4,1408]{2,0,1:T(8,128)(2,1)} %bitcast.12), calls=%async_computation | async-start | bytes 1441792 | tf_op jit(solution)/shard_map/all_to_all | solution.py:175
  40.0 12.7 %collective-permute-start.3 = (bf16[128,1024]{1,0:T(8,128)(2,1)S(1)}, bf16[128,1024]{1,0:T(8,128)(2,1)S(1)}, u32[]{:S(2)}, u32[]{:S(2)}) collective-permute-start(bf16[128,1024]{1,0:T(8,128)(2,1)S(1)} %get-tuple-element.30), channel_id=1, source_target_pairs={{0,8},{8,0},{16,24},{24,16},{1,9},{9,1},{17,25},{25,17},{2,10},{10... | collective-permute-start | bytes 786440 | tf_op jit(solution)/shard_map/ppermute | solution.py:219
  45.8 7.4 %collective-permute-start.4 = (bf16[128,1024]{1,0:T(8,128)(2,1)S(1)}, bf16[128,1024]{1,0:T(8,128)(2,1)S(1)}, u32[]{:S(2)}, u32[]{:S(2)}) collective-permute-start(bf16[128,1024]{1,0:T(8,128)(2,1)S(1)} %get-tuple-element.32), channel_id=1, source_target_pairs={{0,8},{8,0},{16,24},{24,16},{1,9},{9,1},{17,25},{25,17},{2,10},{10... | collective-permute-start | bytes 786440 | tf_op jit(solution)/shard_map/ppermute | solution.py:219
  52.0 3.0 %collective-permute-start.2 = (bf16[128,1024]{1,0:T(8,128)(2,1)S(1)}, bf16[128,1024]{1,0:T(8,128)(2,1)S(1)}, u32[]{:S(2)}, u32[]{:S(2)}) collective-permute-start(bf16[128,1024]{1,0:T(8,128)(2,1)S(1)} %get-tuple-element.28), channel_id=1, source_target_pairs={{0,8},{8,0},{16,24},{24,16},{1,9},{9,1},{17,25},{25,17},{2,10},{10... | collective-permute-start | bytes 786440 | tf_op jit(solution)/shard_map/ppermute | solution.py:219
  52.1 4.0 %collective-permute-start.1 = (bf16[128,1024]{1,0:T(8,128)(2,1)S(1)}, bf16[128,1024]{1,0:T(8,128)(2,1)S(1)}, u32[]{:S(2)}, u32[]{:S(2)}) collective-permute-start(bf16[128,1024]{1,0:T(8,128)(2,1)S(1)} %get-tuple-element.26), channel_id=1, source_target_pairs={{0,8},{8,0},{16,24},{24,16},{1,9},{9,1},{17,25},{25,17},{2,10},{10... | collective-permute-start | bytes 786440 | tf_op jit(solution)/shard_map/ppermute | solution.py:219
  52.6 5.9 %collective-permute-start = (bf16[128,1024]{1,0:T(8,128)(2,1)S(1)}, bf16[128,1024]{1,0:T(8,128)(2,1)S(1)}, u32[]{:S(2)}, u32[]{:S(2)}) collective-permute-start(bf16[128,1024]{1,0:T(8,128)(2,1)S(1)} %get-tuple-element.24), channel_id=1, source_target_pairs={{0,8},{8,0},{16,24},{24,16},{1,9},{9,1},{17,25},{25,17},{2,10},{10... | collective-permute-start | bytes 786440 | tf_op jit(solution)/shard_map/ppermute | solution.py:219
  52.8 14.8 %collective-permute-start.8 = (bf16[64,1024]{1,0:T(8,128)(2,1)S(1)}, bf16[64,1024]{1,0:T(8,128)(2,1)S(1)}, u32[]{:S(2)}, u32[]{:S(2)}) collective-permute-start(bf16[64,1024]{1,0:T(8,128)(2,1)S(1)} %slice.61), channel_id=1, source_target_pairs={{0,16},{8,24},{16,0},{24,8},{1,17},{9,25},{17,1},{25,9},{2,18},{10... | collective-permute-start | bytes 393224 | tf_op jit(solution)/shard_map/ppermute | solution.py:219
  53.3 14.3 %collective-permute-start.9 = (bf16[64,1024]{1,0:T(8,128)(2,1)S(1)}, bf16[64,1024]{1,0:T(8,128)(2,1)S(1)}, u32[]{:S(2)}, u32[]{:S(2)}) collective-permute-start(bf16[64,1024]{1,0:T(8,128)(2,1)S(1)} %slice.60), channel_id=1, source_target_pairs={{0,16},{8,24},{16,0},{24,8},{1,17},{9,25},{17,1},{25,9},{2,18},{10... | collective-permute-start | bytes 393224 | tf_op jit(solution)/shard_map/ppermute | solution.py:219
  55.8 11.8 %collective-permute-start.7 = (bf16[64,1024]{1,0:T(8,128)(2,1)}, bf16[64,1024]{1,0:T(8,128)(2,1)S(1)}, u32[]{:S(2)}, u32[]{:S(2)}) collective-permute-start(bf16[64,1024]{1,0:T(8,128)(2,1)} %slice.62), channel_id=1, source_target_pairs={{0,16},{8,24},{16,0},{24,8},{1,17},{9,25},{17,1},{25,9},{2,18},{10... | collective-permute-start | bytes 393224 | tf_op jit(solution)/shard_map/ppermute | solution.py:219
  56.1 3.5 %copy-start.3 = (s32[800]{0:T(1024)S(1)}, s32[800]{0:T(1024)}, u32[]{:S(2)}) copy-start(s32[800]{0:T(1024)} %param.9) | copy-start | bytes 9604
  56.9 10.7 %collective-permute-start.6 = (bf16[64,1024]{1,0:T(8,128)(2,1)}, bf16[64,1024]{1,0:T(8,128)(2,1)S(1)}, u32[]{:S(2)}, u32[]{:S(2)}) collective-permute-start(bf16[64,1024]{1,0:T(8,128)(2,1)} %slice.63), channel_id=1, source_target_pairs={{0,16},{8,24},{16,0},{24,8},{1,17},{9,25},{17,1},{25,9},{2,18},{10... | collective-permute-start | bytes 393224 | tf_op jit(solution)/shard_map/ppermute | solution.py:219
  59.3 10.7 %collective-permute-start.5 = (bf16[64,1024]{1,0:T(8,128)(2,1)}, bf16[64,1024]{1,0:T(8,128)(2,1)S(1)}, u32[]{:S(2)}, u32[]{:S(2)}) collective-permute-start(bf16[64,1024]{1,0:T(8,128)(2,1)} %slice.64), channel_id=1, source_target_pairs={{0,16},{8,24},{16,0},{24,8},{1,17},{9,25},{17,1},{25,9},{2,18},{10... | collective-permute-start | bytes 393224 | tf_op jit(solution)/shard_map/ppermute | solution.py:219
  67.4 2.5 %copy-start.1 = (s32[40,128]{1,0:T(8,128)S(1)}, s32[40,128]{1,0:T(8,128)}, u32[]{:S(2)}) copy-start(s32[40,128]{1,0:T(8,128)} %get-tuple-element.22) | copy-start | bytes 61444
  67.4 2.5 %copy-start.2 = (s32[224]{0:T(256)S(1)}, s32[224]{0:T(256)}, u32[]{:S(2)}) copy-start(s32[224]{0:T(256)} %get-tuple-element.20.list_ref) | copy-start | bytes 2692

commit v2 on v1

--- a/solution.py
+++ b/solution.py
@@ -12,12 +12,14 @@
 LANES = 128
 SLOT_TILE = 128
 VOX_BLOCK = 256
+PRODUCT_BLOCK = 512
 GROUP = 8
 CHUNKS = 5
 MIB = 1 << 20
 
 VMEM = functools.partial(pl.BlockSpec, memory_space=pltpu.VMEM)
 SMEM = functools.partial(pl.BlockSpec, memory_space=pltpu.SMEM)
+ANY = functools.partial(pl.BlockSpec, memory_space=pl.ANY)
 
 
 def places_kernel(send_cap, owners, parcel_ref, table_ref, key_ref, start_ref):
@@ -49,7 +51,10 @@
         slot = dot(hot, above) + dot(ahead, totals)
         key = jnp.where(mine, slot + float(o * send_cap), key)
         starts = jnp.where(lane == o, dot(block_ahead, totals), starts)
-    key_ref[...] = key.astype(jnp.int32)
+    key = key.astype(jnp.int32)
+    for row in range(rows):
+        line = jnp.broadcast_to(key[row : row + 1, :], (LANES, LANES))
+        key_ref[row * LANES : (row + 1) * LANES, :] = line.T
     start_ref[...] = starts.astype(jnp.int32)
 
 
@@ -69,11 +74,11 @@
     count_ref[0] = (count + GROUP - 1) // GROUP
 
 
-def design_kernel(place_ref, series_ref, filter_ref, design_ref, shifted):
-    time_len, width = series_ref.shape
+def design_kernel(parts, block_ref, place_ref, *refs):
+    series_refs, (filter_ref, _, design_ref, plain, shifted) = refs[:parts], refs[parts:]
+    block, width = series_refs[0].shape
     bases = filter_ref.shape[0]
-    parts = place_ref.shape[0]
-    block = time_len // parts
+    time_len = parts * block
     rows = 32
     lead = TAP_SPACING * FILTER_TAPS
     for s in range(shifted.shape[0]):
@@ -81,7 +86,10 @@
 
     def columns(tile, carry):
         at = pl.ds(pl.multiple_of(tile * LANES, LANES), LANES)
-        series = series_ref[:, at].astype(jnp.float32)
+        for d in range(parts):
+            row = pl.ds(pl.multiple_of(block_ref[d] * block, block), block)
+            plain[row, :] = series_refs[d][:, at].astype(jnp.float32)
+        series = plain[...]
         for s in range(shifted.shape[0]):
             shifted[s, lead + s * TAP_SPACING : lead + s * TAP_SPACING + time_len, :] = series
         for group in range(time_len // rows):
@@ -102,7 +110,8 @@
     lax.fori_loop(0, width // LANES, columns, 0)
 
 
-def product_kernel(design_ref, weight_ref, keep_ref, send_ref):
+def product_kernel(design_ref, weight_ref, *refs):
+    keep_ref, send_ref = refs[-2:]
     half = keep_ref.shape[0]
     weight = weight_ref[...]
     weight = weight.reshape(-1, weight.shape[2])
@@ -111,38 +120,40 @@
     send_ref[...] = total[half:]
 
 
-def product(design, weights, first, width):
+def product(design, weights, first, width, after):
     bases, depth, _ = weights.shape
     time_len = design.shape[0]
     out = jax.ShapeDtypeStruct((time_len // 2, width), jnp.bfloat16)
-    offset = first // VOX_BLOCK
+    offset = first // PRODUCT_BLOCK
     return pl.pallas_call(
         product_kernel,
-        grid=(width // VOX_BLOCK,),
+        grid=(width // PRODUCT_BLOCK,),
         in_specs=[
             pl.BlockSpec(design.shape, lambda i: (0, 0)),
-            pl.BlockSpec((bases, depth, VOX_BLOCK), lambda i: (0, 0, i + offset)),
-        ],
-        out_specs=[pl.BlockSpec((time_len // 2, VOX_BLOCK), lambda i: (0, i))] * 2,
+            pl.BlockSpec((bases, depth, PRODUCT_BLOCK), lambda i: (0, 0, i + offset)),
+        ]
+        + [ANY()] * len(after),
+        out_specs=[pl.BlockSpec((time_len // 2, PRODUCT_BLOCK), lambda i: (0, i))] * 2,
         out_shape=[out, out],
-        compiler_params=pltpu.CompilerParams(vmem_limit_bytes=24 * MIB),
+        compiler_params=pltpu.CompilerParams(vmem_limit_bytes=32 * MIB),
         cost_estimate=pl.CostEstimate(
             flops=2 * time_len * bases * depth * width,
             bytes_accessed=2 * bases * depth * width + 2 * time_len * width,
             transcendentals=0,
         ),
         name="product",
-    )(design, weights)
+    )(design, weights, *after)
 
 
 def pack_kernel(send_cap, chunks, list_ref, count_ref, key_ref, *refs):
-    mine, theirs, packed_ref, summed = refs[:chunks], refs[chunks : 2 * chunks], refs[-2], refs[-1]
-    width = mine[0].shape[1]
+    terms, packed_ref, summed = refs[:-2], refs[-2], refs[-1]
+    each = len(terms) // chunks
+    width = terms[0].shape[1]
     for c in range(chunks):
-        total = mine[c][...] + theirs[c][...].astype(jnp.float32)
+        total = sum(term[: summed.shape[0], :].astype(jnp.float32) for term in terms[c * each : (c + 1) * each])
         summed[:, c * width : (c + 1) * width] = total.astype(jnp.bfloat16)
     packed_ref[...] = jnp.zeros_like(packed_ref)
-    slots = lax.broadcasted_iota(jnp.int32, (SLOT_TILE, VOX_BLOCK), 0)
+    slots = lax.broadcasted_iota(jnp.int32, (VOX_BLOCK, SLOT_TILE), 1)
 
     def group(g, carry):
         for i in range(GROUP):
@@ -151,10 +162,10 @@
             word = jnp.where(real, word, 0)
             block, owner, tile = word >> 16, (word >> 8) & 255, word & 255
             base = jnp.where(real, owner * send_cap + tile * SLOT_TILE, -(1 << 20))
-            hit = (key_ref[block] - base) == slots
+            voxel = pl.ds(pl.multiple_of(block * VOX_BLOCK, VOX_BLOCK), VOX_BLOCK)
+            hit = key_ref[voxel, :] == slots + base
             hit = jnp.where(hit, 1.0, 0.0).astype(jnp.bfloat16)
-            values = summed[:, pl.ds(pl.multiple_of(block * VOX_BLOCK, VOX_BLOCK), VOX_BLOCK)]
-            moved = lax.dot_general(values, hit, (((1,), (1,)), ((), ())), preferred_element_type=jnp.float32)
+            moved = jnp.dot(summed[:, voxel], hit, preferred_element_type=jnp.float32)
             at = pl.ds(pl.multiple_of(tile * SLOT_TILE, SLOT_TILE), SLOT_TILE)
             packed_ref[owner, :, at] = packed_ref[owner, :, at] + moved.astype(jnp.bfloat16)
         return carry
@@ -172,7 +183,9 @@
     time_block = features.shape[0]
     time_len = time_block * parts
 
-    by_channel = lax.all_to_all(features, "chan", split_axis=1, concat_axis=0, tiled=True)
+    series = [lax.dynamic_slice_in_dim(features, (me ^ d) * depth, depth, 1) for d in range(parts)]
+    for d in range(1, parts):
+        series[d] = lax.ppermute(series[d], "chan", [(i, i ^ d) for i in range(parts)])
 
     table_rows = -(-parcel_owner.shape[0] // LANES)
     table = jnp.pad(parcel_owner, (0, table_rows * LANES - parcel_owner.shape[0])).reshape(table_rows, LANES)
@@ -182,7 +195,7 @@
         in_specs=[VMEM(), VMEM()],
         out_specs=[VMEM(), VMEM()],
         out_shape=[
-            jax.ShapeDtypeStruct((voxels // LANES, LANES), jnp.int32),
+            jax.ShapeDtypeStruct((voxels, LANES), jnp.int32),
             jax.ShapeDtypeStruct((marks, LANES), jnp.int32),
         ],
         name="places",
@@ -195,45 +208,47 @@
         out_shape=[jax.ShapeDtypeStruct((pairs,), jnp.int32), jax.ShapeDtypeStruct((1,), jnp.int32)],
         name="pairs",
     )(starts)
-    key = key.reshape(blocks, 1, VOX_BLOCK)
 
     bits = parts.bit_length() - 1
     order = jnp.arange(parts, dtype=jnp.int32) ^ me
     place = sum(((order >> bit) & 1) << (bits - 1 - bit) for bit in range(bits)).astype(jnp.int32)
     design = pl.pallas_call(
-        design_kernel,
-        in_specs=[SMEM(), VMEM(), VMEM()],
+        functools.partial(design_kernel, parts),
+        in_specs=[SMEM(), SMEM()] + [VMEM()] * (parts + 1) + [ANY()],
         out_specs=VMEM(),
         out_shape=jax.ShapeDtypeStruct((time_len, bases * depth), jnp.bfloat16),
-        scratch_shapes=[pltpu.VMEM((8 // TAP_SPACING, time_len + TAP_SPACING * FILTER_TAPS + 8, LANES), jnp.float32)],
-        compiler_params=pltpu.CompilerParams(vmem_limit_bytes=24 * MIB),
+        scratch_shapes=[
+            pltpu.VMEM((time_len, LANES), jnp.float32),
+            pltpu.VMEM((8 // TAP_SPACING, time_len + TAP_SPACING * FILTER_TAPS + 8, LANES), jnp.float32),
+        ],
+        compiler_params=pltpu.CompilerParams(vmem_limit_bytes=32 * MIB),
         name="design",
-    )(place, by_channel, jnp.transpose(hrf_filters, (0, 2, 1)))
+    )(order, place, *series, jnp.transpose(hrf_filters, (0, 2, 1)), pair_list)
 
     width = voxels // CHUNKS
-    mine, theirs = [], []
+    terms, sent, got = [], [], []
     for c in range(CHUNKS):
-        keep, send = product(design, weights, c * width, width)
-        keep = keep.astype(jnp.float32)
+        keep, send = product(design, weights, c * width, width, sent[max(c - 2, 0) : max(c - 1, 0)] + got[max(c - 3, 0) : max(c - 2, 0)])
+        own = [keep]
         for bit in range(bits):
-            got = lax.ppermute(send, "chan", [(i, i ^ (1 << bit)) for i in range(parts)])
-            if bit == bits - 1:
-                mine.append(keep)
-                theirs.append(got)
-            else:
-                total = keep + got.astype(jnp.float32)
-                rows = total.shape[0] // 2
-                keep, send = total[:rows], total[rows:].astype(jnp.bfloat16)
+            if bit > 0:
+                rows = own[-1].shape[0] // 2
+                send = sum(term[rows : 2 * rows].astype(jnp.float32) for term in own).astype(jnp.bfloat16)
+                if bit == 1:
+                    sent.append(send)
+            own.append(lax.ppermute(send, "chan", [(i, i ^ (1 << bit)) for i in range(parts)]))
+        terms.extend(own)
+        got.append(own[-1])
 
     packed = pl.pallas_call(
         functools.partial(pack_kernel, send_cap, CHUNKS),
-        in_specs=[SMEM(), SMEM()] + [VMEM()] * (1 + 2 * CHUNKS),
+        in_specs=[SMEM(), SMEM()] + [VMEM()] * (1 + len(terms)),
         out_specs=VMEM(),
         out_shape=jax.ShapeDtypeStruct((owners, time_block, send_cap), jnp.bfloat16),
         scratch_shapes=[pltpu.VMEM((time_block, voxels), jnp.bfloat16)],
-        compiler_params=pltpu.CompilerParams(vmem_limit_bytes=24 * MIB),
+        compiler_params=pltpu.CompilerParams(vmem_limit_bytes=32 * MIB),
         name="pack",
-    )(pair_list, pair_groups, key, *mine, *theirs)
+    )(pair_list, pair_groups, key, *terms)
     received = lax.all_to_all(packed, "vox", split_axis=0, concat_axis=0, tiled=True)
     return jnp.transpose(received, (0, 2, 1))
 

time: 118 us -> 108 us (0.915)
  waiting for transfers between devices: 13.3 us -> 7.82 us
  Pallas kernels: 50.6 us -> 46.9 us
    all_to_all x1 -> x0, waiting for transfers between devices: 10.9 us -> none  [shards(): lax.all_to_all(features, 'chan', split_axis=1, concat_axis=0, tiled=True)]
    ppermute x10 -> x13, waiting for transfers between devices: 2.35 us -> 7.82 us  [the longest x10 7.81 us: shards(): lax.ppermute(send, 'chan', [(i, i ^ 1 << bit) for i in range(parts)])]
    ppermute x10 -> x13, starting transfers between devices: 5.82 us -> 10.6 us  [the longest x10 7.4 us: shards(): lax.ppermute(send, 'chan', [(i, i ^ 1 << bit) for i in range(parts)])]
    all_to_all x1 -> x0, starting transfers between devices: 4.21 us -> none  [shards(): lax.all_to_all(features, 'chan', split_axis=1, concat_axis=0, tiled=True)]
    pallas_call x6, Pallas kernels: 34.1 us -> 30.7 us  [the longest x5 24.9 us: product(): pl.pallas_call(product_kernel, grid=(width // PRODUCT_BLOCK,), in_specs=[...]
    slice x10 -> x0, local copies, waits for them, and re-layouts: 2.13 us -> none  [shards(): keep, send = (total[:rows], total[rows:].astype(jnp.bfloat16))]
    all_to_all x1 -> x0, local copies, waits for them, and re-layouts: 2.07 us -> none  [shards(): lax.all_to_all(features, 'chan', split_axis=1, concat_axis=0, tiled=True)]
    pallas_call x1, Pallas kernels: 9.33 us -> 7.36 us  [shards(): pl.pallas_call(functools.partial(pack_kernel, send_cap, CHUNKS), in_specs...]
  transfers between devices with their start and end apart: 11 -> 13, of which waited for: 2 -> 4; matrix products, arithmetic and copies ran while one was open for 3% -> 1% of each run, Pallas kernels for 16% -> 27%
where the time goes in v2:
time: 108 us
  Pallas kernels  46.9 us (43%)
  blocking collectives  36.9 us (34%)
  starting transfers between devices  10.6 us (10%)
  waiting for transfers between devices  7.82 us (7%)
  local copies, waits for them, and re-layouts  5.2 us (5%)
    all_to_all x1, blocking collectives, shards(): lax.all_to_all(packed, 'vox', split_axis=0, concat_axis=0, tiled=True)  36.9 us
    pallas_call x5, Pallas kernels, product(): pl.pallas_call(product_kernel, grid=(width // PRODUCT_BLOCK,), in_specs=[...  24.9 us
    ppermute x10, waiting for transfers between devices, shards(): lax.ppermute(send, 'chan', [(i, i ^ 1 << bit) for i in range(parts)])  7.81 us
    ppermute x10, starting transfers between devices, shards(): lax.ppermute(send, 'chan', [(i, i ^ 1 << bit) for i in range(parts)])  7.4 us
    pallas_call x1, Pallas kernels, shards(): pl.pallas_call(functools.partial(pack_kernel, send_cap, CHUNKS), in_specs...  7.36 us
    pallas_call x1, Pallas kernels, shards(): pl.pallas_call(functools.partial(design_kernel, parts), in_specs=[SMEM(),...  5.84 us
    pallas_call x1, Pallas kernels, shards(): pl.pallas_call(functools.partial(places_kernel, send_cap, owners), in_spe...  4.52 us
    pallas_call x1, Pallas kernels, shards(): pl.pallas_call(functools.partial(pairs_kernel, blocks, owners), in_specs=...  4.29 us
  transfers between devices with their start and end apart: 13, of which 4 were waited for; matrix products, arithmetic and copies ran while one was open for 1% of the time, Pallas kernels for 27%

profile of v2, /device:TPU:0, one launch (start us, length us, event | category | flops | bytes accessed | tf_op | source)
XLA Modules:
  0.0 107.7 jit_solution(9110641492947400889)
XLA Ops:
  0.0 1.2 %constant_dynamic-slice_fusion = (bf16[64,1408]{1,0:T(8,128)(2,1)S(1)}, bf16[64,1408]{1,0:T(8,128)(2,1)S(1)}, bf16[64,1408]{1,0:T(8,128)(2,1)S(1)}, bf16[64,1408]{1,0:T(8,128)(2,1)S(1)}) fusion(bf16[64,5632]{1,0:T(8,128)(2,1)} %param.5, s32[]{:T(128)S(6)} %select_n.15, s32[]{:T(128)S(6)} %select_n.13, s32[]{:T(128)S(6)} %select_n.12, s32[]{:T(128)S(6)} %select_n.14), kind=kLoop, calls=%fused_computation.6 | loop fusion | bytes 1441808 | tf_op jit(solution)/shard_map/dynamic_slice | solution.py:186
  1.2 2.4 %collective-permute-start.2 = (bf16[64,1408]{1,0:T(8,128)(2,1)S(1)}, bf16[64,1408]{1,0:T(8,128)(2,1)S(1)}, u32[]{:S(2)}, u32[]{:S(2)}) collective-permute-start(bf16[64,1408]{1,0:T(8,128)(2,1)S(1)} %get-tuple-element.33), channel_id=1, source_target_pairs={{0,24},{8,16},{16,8},{24,0},{1,25},{9,17},{17,9},{25,1},{2,26},{10... | collective-permute-start | bytes 540680 | tf_op jit(solution)/shard_map/ppermute | solution.py:188
  3.7 0.7 collective-permute-start
  4.4 0.0 collective-permute-start.1
  4.4 1.3 %pad_bitcast_fusion.table_ref = s32[7,128]{1,0:T(8,128)} fusion(s32[800]{0:T(1024)} %param.9), kind=kLoop, calls=%fused_computation.5 | loop fusion | bytes 6784 | tf_op jit(solution)/shard_map/reshape | solution.py:191
  5.7 4.5 %places.1 = (s32[5120,128]{1,0:T(8,128)}, s32[24,128]{1,0:T(8,128)}) custom-call(s32[40,128]{1,0:T(8,128)} %bitcast.7, s32[7,128]{1,0:T(8,128)} %pad_bitcast_fusion.table_ref), custom_call_target="tpu_custom_call" | custom-call | tf_op jit(solution)/shard_map/places/pallas_call | solution.py:193
  10.2 4.3 %pairs.1 = (s32[224]{0:T(256)}, s32[1]{0:T(128)}) custom-call(s32[24,128]{1,0:T(8,128)} %get-tuple-element.19.start_ref), custom_call_target="tpu_custom_call" | custom-call | tf_op jit(solution)/shard_map/pairs/pallas_call | solution.py:204
  14.6 0.9 copy-done.1
  15.5 0.7 copy-done.2
  16.2 5.8 %design.1.design_ref = bf16[256,4224]{1,0:T(8,128)(2,1)S(1)} custom-call(s32[4]{0:T(128)S(1)} %get-tuple-element.38.block_ref, s32[4]{0:T(128)S(1)} %get-tuple-element.37.place_ref, bf16[64,1408]{1,0:T(8,128)(2,1)S(1)} %get-tuple-element.35.refs_0_, bf16[64,1408]{1,0:T(8,128)(2,1)S(1)} %collective-permute-done.refs_1_, ...), custom_call_target="tpu_custom_call" | custom-call | tf_op jit(solution)/shard_map/design/pallas_call | solution.py:215
  22.0 4.9 %product.5 = (bf16[128,1024]{1,0:T(8,128)(2,1)S(1)}, bf16[128,1024]{1,0:T(8,128)(2,1)S(1)}) custom-call(bf16[256,4224]{1,0:T(8,128)(2,1)S(1)} %design.1.design_ref, bf16[3,1408,5120]{2,1,0:T(8,128)(2,1)} %weight_ref.9), custom_call_target="tpu_custom_call" | custom-call | flops 2214592512 | bytes 9175040 | tf_op jit(solution)/shard_map/product/pallas_call | solution.py:128
  26.9 0.2 collective-permute-start.3
  27.2 5.0 %product.6 = (bf16[128,1024]{1,0:T(8,128)(2,1)S(1)}, bf16[128,1024]{1,0:T(8,128)(2,1)S(1)}) custom-call(bf16[256,4224]{1,0:T(8,128)(2,1)S(1)} %design.1.design_ref, bf16[3,1408,5120]{2,1,0:T(8,128)(2,1)} %weight_ref.9), custom_call_target="tpu_custom_call" | custom-call | flops 2214592512 | bytes 9175040 | tf_op jit(solution)/shard_map/product/pallas_call | solution.py:128
  32.2 0.4 collective-permute-start.5
  32.7 2.0 %collective-permute-start.4 = (bf16[64,1024]{1,0:T(8,128)(2,1)S(1)}, bf16[64,1024]{1,0:T(8,128)(2,1)S(1)}, u32[]{:S(2)}, u32[]{:S(2)}) collective-permute-start(bf16[64,1024]{1,0:T(8,128)(2,1)S(1)} %add_convert_fusion.4.refs_0_), channel_id=1, source_target_pairs={{0,16},{8,24},{16,0},{24,8},{1,17},{9,25},{17,1},{25,9},{2,18},{10... | collective-permute-start | bytes 393224 | tf_op jit(solution)/shard_map/ppermute | solution.py:239
  34.7 4.9 %product.7 = (bf16[128,1024]{1,0:T(8,128)(2,1)S(1)}, bf16[128,1024]{1,0:T(8,128)(2,1)S(1)}) custom-call(bf16[256,4224]{1,0:T(8,128)(2,1)S(1)} %design.1.design_ref, bf16[3,1408,5120]{2,1,0:T(8,128)(2,1)} %weight_ref.9, bf16[64,1024]{1,0:T(8,128)(2,1)S(1)} %add_convert_fusion.4.refs_0_), custom_call_target="tpu_custom_call" | custom-call | flops 2214592512 | bytes 9175040 | tf_op jit(solution)/shard_map/product/pallas_call | solution.py:128
  39.6 0.1 collective-permute-start.7
  39.8 0.1 collective-permute-start.6
  39.9 5.0 %product.8 = (bf16[128,1024]{1,0:T(8,128)(2,1)S(1)}, bf16[128,1024]{1,0:T(8,128)(2,1)S(1)}) custom-call(bf16[256,4224]{1,0:T(8,128)(2,1)S(1)} %design.1.design_ref, bf16[3,1408,5120]{2,1,0:T(8,128)(2,1)} %weight_ref.9, bf16[64,1024]{1,0:T(8,128)(2,1)S(1)} %add_convert_fusion.3.refs_0_, bf16[64,1024]{1,0:T(8,128)(2,1)S(1)} %collective-permute-done.4.refs_1_.refs_2_), custom_call_target="tpu_custom_call" | custom-call | flops 2214592512 | bytes 9175040 | tf_op jit(solution)/shard_map/product/pallas_call | solution.py:128
  44.9 0.5 collective-permute-start.9
  45.4 0.3 collective-permute-done.6.refs_1_.refs_5_
  45.7 5.1 %product.9 = (bf16[128,1024]{1,0:T(8,128)(2,1)S(1)}, bf16[128,1024]{1,0:T(8,128)(2,1)S(1)}) custom-call(bf16[256,4224]{1,0:T(8,128)(2,1)S(1)} %design.1.design_ref, bf16[3,1408,5120]{2,1,0:T(8,128)(2,1)} %weight_ref.9, bf16[64,1024]{1,0:T(8,128)(2,1)S(1)} %add_convert_fusion.2.refs_0_, bf16[64,1024]{1,0:T(8,128)(2,1)S(1)} %collective-permute-done.6.refs_1_.refs_5_), custom_call_target="tpu_custom_call" | custom-call | flops 2214592512 | bytes 9175040 | tf_op jit(solution)/shard_map/product/pallas_call | solution.py:128
  50.8 0.1 collective-permute-start.11
  50.9 1.8 %collective-permute-start.8 = (bf16[64,1024]{1,0:T(8,128)(2,1)S(1)}, bf16[64,1024]{1,0:T(8,128)(2,1)S(1)}, u32[]{:S(2)}, u32[]{:S(2)}) collective-permute-start(bf16[64,1024]{1,0:T(8,128)(2,1)S(1)} %add_convert_fusion.2.refs_0_), channel_id=1, source_target_pairs={{0,16},{8,24},{16,0},{24,8},{1,17},{9,25},{17,1},{25,9},{2,18},{10... | collective-permute-start | bytes 393224 | tf_op jit(solution)/shard_map/ppermute | solution.py:239
  52.7 0.4 collective-permute-start.10
  53.1 1.8 %collective-permute-start.12 = (bf16[64,1024]{1,0:T(8,128)(2,1)S(1)}, bf16[64,1024]{1,0:T(8,128)(2,1)S(1)}, u32[]{:S(2)}, u32[]{:S(2)}) collective-permute-start(bf16[64,1024]{1,0:T(8,128)(2,1)S(1)} %add_convert_fusion), channel_id=1, source_target_pairs={{0,16},{8,24},{16,0},{24,8},{1,17},{9,25},{17,1},{25,9},{2,18},{10... | collective-permute-start | bytes 393224 | tf_op jit(solution)/shard_map/ppermute | solution.py:239
  54.9 2.4 %collective-permute-done.8.refs_8_ = bf16[64,1024]{1,0:T(8,128)(2,1)S(1)} collective-permute-done((bf16[64,1024]{1,0:T(8,128)(2,1)S(1)}, bf16[64,1024]{1,0:T(8,128)(2,1)S(1)}, u32[]{:S(2)}, u32[]{:S(2)}) %collective-permute-start.8) | collective-permute-done | bytes 131104 | tf_op jit(solution)/shard_map/ppermute | solution.py:239
  57.2 2.8 %collective-permute-done.10.refs_11_ = bf16[64,1024]{1,0:T(8,128)(2,1)S(1)} collective-permute-done((bf16[64,1024]{1,0:T(8,128)(2,1)S(1)}, bf16[64,1024]{1,0:T(8,128)(2,1)S(1)}, u32[]{:S(2)}, u32[]{:S(2)}) %collective-permute-start.10) | collective-permute-done | bytes 131104 | tf_op jit(solution)/shard_map/ppermute | solution.py:239
  60.0 2.4 %collective-permute-done.12.refs_14_ = bf16[64,1024]{1,0:T(8,128)(2,1)S(1)} collective-permute-done((bf16[64,1024]{1,0:T(8,128)(2,1)S(1)}, bf16[64,1024]{1,0:T(8,128)(2,1)S(1)}, u32[]{:S(2)}, u32[]{:S(2)}) %collective-permute-start.12) | collective-permute-done | bytes 131104 | tf_op jit(solution)/shard_map/ppermute | solution.py:239
  62.4 7.4 %pack.1 = bf16[8,64,1280]{2,1,0:T(8,128)(2,1)S(1)} custom-call(s32[224]{0:T(256)S(1)} %copy-done.3, s32[1]{0:T(128)} %get-tuple-element.21.count_ref, s32[5120,128]{1,0:T(8,128)S(1)} %copy-done, bf16[128,1024]{1,0:T(8,128)(2,1)S(1)} %get-tuple-element.23.refs_0_, bf16[128,1024]{1,0:T(8,128)(2,1)S(1)} %collective-permute-done.3.refs_1_, ...), custom_call_target="tpu_custom_call" | custom-call | tf_op jit(solution)/shard_map/pack/pallas_call | solution.py:243
  69.8 36.9 %all_to_all.5 = bf16[8,64,1280]{2,1,0:T(8,128)(2,1)S(1)} all-to-all(bf16[8,64,1280]{2,1,0:T(8,128)(2,1)S(1)} %pack.1), channel_id=1, replica_groups=mesh['chan'=4,'vox'=8] {'vox'}, dimensions={0} | all-to-all | bytes 2621440 | tf_op jit(solution)/shard_map/all_to_all | solution.py:252
  106.6 1.1 copy.7
  (21 shorter events, 0.2 us)
Async XLA Ops:
  1.2 13.3 %collective-permute-start.2 = (bf16[64,1408]{1,0:T(8,128)(2,1)S(1)}, bf16[64,1408]{1,0:T(8,128)(2,1)S(1)}, u32[]{:S(2)}, u32[]{:S(2)}) collective-permute-start(bf16[64,1408]{1,0:T(8,128)(2,1)S(1)} %get-tuple-element.33), channel_id=1, source_target_pairs={{0,24},{8,16},{16,8},{24,0},{1,25},{9,17},{17,9},{25,1},{2,26},{10... | collective-permute-start | bytes 540680 | tf_op jit(solution)/shard_map/ppermute | solution.py:188
  3.7 10.8 %collective-permute-start = (bf16[64,1408]{1,0:T(8,128)(2,1)S(1)}, bf16[64,1408]{1,0:T(8,128)(2,1)S(1)}, u32[]{:S(2)}, u32[]{:S(2)}) collective-permute-start(bf16[64,1408]{1,0:T(8,128)(2,1)S(1)} %get-tuple-element.34), channel_id=1, source_target_pairs={{0,8},{8,0},{16,24},{24,16},{1,9},{9,1},{17,25},{25,17},{2,10},{10... | collective-permute-start | bytes 540680 | tf_op jit(solution)/shard_map/ppermute | solution.py:188
  4.4 10.2 %collective-permute-start.1 = (bf16[64,1408]{1,0:T(8,128)(2,1)S(1)}, bf16[64,1408]{1,0:T(8,128)(2,1)S(1)}, u32[]{:S(2)}, u32[]{:S(2)}) collective-permute-start(bf16[64,1408]{1,0:T(8,128)(2,1)S(1)} %get-tuple-element.36), channel_id=1, source_target_pairs={{0,16},{8,24},{16,0},{24,8},{1,17},{9,25},{17,1},{25,9},{2,18},{10... | collective-permute-start | bytes 540680 | tf_op jit(solution)/shard_map/ppermute | solution.py:188
  14.6 1.0 copy-start.1
  15.5 0.7 copy-start.2
  26.9 5.7 %collective-permute-start.3 = (bf16[128,1024]{1,0:T(8,128)(2,1)S(1)}, bf16[128,1024]{1,0:T(8,128)(2,1)S(1)}, u32[]{:S(2)}, u32[]{:S(2)}) collective-permute-start(bf16[128,1024]{1,0:T(8,128)(2,1)S(1)} %get-tuple-element.24), channel_id=1, source_target_pairs={{0,8},{8,0},{16,24},{24,16},{1,9},{9,1},{17,25},{25,17},{2,10},{10... | collective-permute-start | bytes 786440 | tf_op jit(solution)/shard_map/ppermute | solution.py:239
  32.2 7.5 %collective-permute-start.5 = (bf16[128,1024]{1,0:T(8,128)(2,1)S(1)}, bf16[128,1024]{1,0:T(8,128)(2,1)S(1)}, u32[]{:S(2)}, u32[]{:S(2)}) collective-permute-start(bf16[128,1024]{1,0:T(8,128)(2,1)S(1)} %get-tuple-element.26), channel_id=1, source_target_pairs={{0,8},{8,0},{16,24},{24,16},{1,9},{9,1},{17,25},{25,17},{2,10},{10... | collective-permute-start | bytes 786440 | tf_op jit(solution)/shard_map/ppermute | solution.py:239
  32.7 7.2 %collective-permute-start.4 = (bf16[64,1024]{1,0:T(8,128)(2,1)S(1)}, bf16[64,1024]{1,0:T(8,128)(2,1)S(1)}, u32[]{:S(2)}, u32[]{:S(2)}) collective-permute-start(bf16[64,1024]{1,0:T(8,128)(2,1)S(1)} %add_convert_fusion.4.refs_0_), channel_id=1, source_target_pairs={{0,16},{8,24},{16,0},{24,8},{1,17},{9,25},{17,1},{25,9},{2,18},{10... | collective-permute-start | bytes 393224 | tf_op jit(solution)/shard_map/ppermute | solution.py:239
  39.6 5.8 %collective-permute-start.7 = (bf16[128,1024]{1,0:T(8,128)(2,1)S(1)}, bf16[128,1024]{1,0:T(8,128)(2,1)S(1)}, u32[]{:S(2)}, u32[]{:S(2)}) collective-permute-start(bf16[128,1024]{1,0:T(8,128)(2,1)S(1)} %get-tuple-element.28), channel_id=1, source_target_pairs={{0,8},{8,0},{16,24},{24,16},{1,9},{9,1},{17,25},{25,17},{2,10},{10... | collective-permute-start | bytes 786440 | tf_op jit(solution)/shard_map/ppermute | solution.py:239
  39.8 6.0 %collective-permute-start.6 = (bf16[64,1024]{1,0:T(8,128)(2,1)S(1)}, bf16[64,1024]{1,0:T(8,128)(2,1)S(1)}, u32[]{:S(2)}, u32[]{:S(2)}) collective-permute-start(bf16[64,1024]{1,0:T(8,128)(2,1)S(1)} %add_convert_fusion.3.refs_0_), channel_id=1, source_target_pairs={{0,16},{8,24},{16,0},{24,8},{1,17},{9,25},{17,1},{25,9},{2,18},{10... | collective-permute-start | bytes 393224 | tf_op jit(solution)/shard_map/ppermute | solution.py:239
  44.9 7.8 %collective-permute-start.9 = (bf16[128,1024]{1,0:T(8,128)(2,1)S(1)}, bf16[128,1024]{1,0:T(8,128)(2,1)S(1)}, u32[]{:S(2)}, u32[]{:S(2)}) collective-permute-start(bf16[128,1024]{1,0:T(8,128)(2,1)S(1)} %get-tuple-element.30), channel_id=1, source_target_pairs={{0,8},{8,0},{16,24},{24,16},{1,9},{9,1},{17,25},{25,17},{2,10},{10... | collective-permute-start | bytes 786440 | tf_op jit(solution)/shard_map/ppermute | solution.py:239
  45.4 17.0 %copy-start.3 = (s32[224]{0:T(256)S(1)}, s32[224]{0:T(256)}, u32[]{:S(2)}) copy-start(s32[224]{0:T(256)} %get-tuple-element.20.refs_5_.list_ref) | copy-start | bytes 2692
  45.7 16.7 %copy-start = (s32[5120,128]{1,0:T(8,128)S(1)}, s32[5120,128]{1,0:T(8,128)}, u32[]{:S(2)}) copy-start(s32[5120,128]{1,0:T(8,128)} %get-tuple-element.22.key_ref) | copy-start | bytes 7864324
  50.8 2.3 %collective-permute-start.11 = (bf16[128,1024]{1,0:T(8,128)(2,1)S(1)}, bf16[128,1024]{1,0:T(8,128)(2,1)S(1)}, u32[]{:S(2)}, u32[]{:S(2)}) collective-permute-start(bf16[128,1024]{1,0:T(8,128)(2,1)S(1)} %get-tuple-element.32), channel_id=1, source_target_pairs={{0,8},{8,0},{16,24},{24,16},{1,9},{9,1},{17,25},{25,17},{2,10},{10... | collective-permute-start | bytes 786440 | tf_op jit(solution)/shard_map/ppermute | solution.py:239
  50.9 6.4 %collective-permute-start.8 = (bf16[64,1024]{1,0:T(8,128)(2,1)S(1)}, bf16[64,1024]{1,0:T(8,128)(2,1)S(1)}, u32[]{:S(2)}, u32[]{:S(2)}) collective-permute-start(bf16[64,1024]{1,0:T(8,128)(2,1)S(1)} %add_convert_fusion.2.refs_0_), channel_id=1, source_target_pairs={{0,16},{8,24},{16,0},{24,8},{1,17},{9,25},{17,1},{25,9},{2,18},{10... | collective-permute-start | bytes 393224 | tf_op jit(solution)/shard_map/ppermute | solution.py:239
  52.7 7.4 %collective-permute-start.10 = (bf16[64,1024]{1,0:T(8,128)(2,1)S(1)}, bf16[64,1024]{1,0:T(8,128)(2,1)S(1)}, u32[]{:S(2)}, u32[]{:S(2)}) collective-permute-start(bf16[64,1024]{1,0:T(8,128)(2,1)S(1)} %add_convert_fusion.1), channel_id=1, source_target_pairs={{0,16},{8,24},{16,0},{24,8},{1,17},{9,25},{17,1},{25,9},{2,18},{10... | collective-permute-start | bytes 393224 | tf_op jit(solution)/shard_map/ppermute | solution.py:239
  53.1 9.3 %collective-permute-start.12 = (bf16[64,1024]{1,0:T(8,128)(2,1)S(1)}, bf16[64,1024]{1,0:T(8,128)(2,1)S(1)}, u32[]{:S(2)}, u32[]{:S(2)}) collective-permute-start(bf16[64,1024]{1,0:T(8,128)(2,1)S(1)} %add_convert_fusion), channel_id=1, source_target_pairs={{0,16},{8,24},{16,0},{24,8},{1,17},{9,25},{17,1},{25,9},{2,18},{10... | collective-permute-start | bytes 393224 | tf_op jit(solution)/shard_map/ppermute | solution.py:239

commit v3 on v0

v3 whole, which is shorter than its diff:
```python
import functools

import jax
import jax.numpy as jnp
from jax import lax
from jax.experimental import pallas as pl
from jax.experimental.pallas import tpu as pltpu
from jax.sharding import PartitionSpec as P

FILTER_TAPS = 16
TAP_SPACING = 2
LANES = 128
SLOT_TILE = 128
VOX_BLOCK = 256
CHAN_SLICE = 512
CHUNK_UNITS = (2, 2, 2, 2, 1, 1)
PACK_FIRST = 4
MIB = 1 << 20

VMEM = functools.partial(pl.BlockSpec, memory_space=pltpu.VMEM)
SMEM = functools.partial(pl.BlockSpec, memory_space=pltpu.SMEM)
ANY = functools.partial(pl.BlockSpec, memory_space=pl.ANY)


def slices_of(depth):
    out = []
    for first in range(0, depth, CHAN_SLICE):
        size = min(CHAN_SLICE, depth - first)
        out.append((first, size, -(-size // LANES) * LANES))
    return out


def places_kernel(owners, spread, parcel_ref, table_ref, onehot_ref, tile_ref, start_ref):
    rows = parcel_ref.shape[0]
    parcel = parcel_ref[...]
    high, low = parcel >> 7, parcel & 127
    owner = jnp.zeros_like(parcel)
    for entry in range(table_ref.shape[0]):
        line = jnp.broadcast_to(table_ref[entry : entry + 1, :], parcel.shape)
        found = jnp.take_along_axis(line, low, axis=1, mode="promise_in_bounds")
        owner = jnp.where(high == entry, found, owner)

    def below(shape, scale=1):
        less = lax.broadcasted_iota(jnp.int32, shape, 1) < scale * lax.broadcasted_iota(jnp.int32, shape, 0)
        return less.astype(jnp.float32).astype(jnp.bfloat16)

    lane = lax.broadcasted_iota(jnp.int32, (LANES, LANES), 1)
    above = (lax.broadcasted_iota(jnp.int32, (LANES, LANES), 0) < lane).astype(jnp.float32).astype(jnp.bfloat16)
    ones = jnp.ones((LANES, LANES), jnp.bfloat16)
    marks = start_ref.shape[0]
    ahead, block_ahead = below((rows, rows)), below((marks, rows), VOX_BLOCK // LANES)
    mark_lane = lax.broadcasted_iota(jnp.int32, (marks, LANES), 1)
    dot = functools.partial(jnp.dot, preferred_element_type=jnp.float32)
    slots = jnp.zeros(parcel.shape, jnp.float32)
    starts = jnp.zeros((marks, LANES), jnp.float32)
    for o in range(owners):
        mine = owner == o
        hot = mine.astype(jnp.float32).astype(jnp.bfloat16)
        totals = dot(hot, ones).astype(jnp.bfloat16)
        slots = jnp.where(mine, dot(hot, above) + dot(ahead, totals), slots)
        starts = jnp.where(mark_lane == o, dot(block_ahead, totals), starts)
    slots = slots.astype(jnp.int32)
    start_ref[...] = starts.astype(jnp.int32)
    tile_ref[...] = owner * spread + (slots >> 7)
    inner = slots & 127
    for row in range(rows):
        line = jnp.broadcast_to(inner[row : row + 1, :], (LANES, LANES))
        hit = jnp.where(line.T == lane, 1.0, 0.0)
        onehot_ref[row * LANES : (row + 1) * LANES, :] = hit.astype(jnp.bfloat16)


def filter_tile(block_ref, place_ref, series_refs, filter_ref, design_ref, plain, shifted, at, lanes):
    parts, block = len(series_refs), series_refs[0].shape[0]
    time_len = parts * block
    rows = 32
    lead = TAP_SPACING * FILTER_TAPS
    column = slice(at, at + LANES)
    for d in range(parts):
        row = pl.ds(pl.multiple_of(block_ref[d] * block, block), block)
        plain[row, :] = series_refs[d][:, column].astype(jnp.float32)
    series = plain[...]
    for s in range(shifted.shape[0]):
        shifted[s, lead + s * TAP_SPACING : lead + s * TAP_SPACING + time_len, :] = series
    for group in range(time_len // rows):
        sums = [jnp.zeros((rows, LANES), jnp.float32) for _ in lanes]
        for tap in range(FILTER_TAPS):
            delay = tap * TAP_SPACING
            start = lead + group * rows - 8 * (delay // 8)
            lagged = shifted[(delay % 8) // TAP_SPACING, start : start + rows, :]
            for b in range(len(lanes)):
                sums[b] = sums[b] + filter_ref[b, tap : tap + 1, column] * lagged
        part, inner = (group * rows) // block, (group * rows) % block
        row = pl.ds(pl.multiple_of(place_ref[part] * block + inner, rows), rows)
        for b, lane in enumerate(lanes):
            design_ref[row, lane : lane + LANES] = sums[b].astype(jnp.bfloat16)


def weight_copies(weight_ref, buffers, sems, first, width):
    copies, depth = [], weight_ref.shape[1]
    for i, (start, size, padded) in enumerate(slices_of(depth)):
        if size < padded:
            buffers[i][:, size:, :] = jnp.zeros_like(buffers[i][:, size:, :])
        copies.append(
            pltpu.make_async_copy(
                weight_ref.at[:, pl.ds(start, size), pl.ds(first, width)],
                buffers[i].at[:, pl.ds(0, size), :],
                sems.at[i],
            )
        )
    for copy in copies:
        copy.start()
    return copies


def add_slice(design_ref, buffer, lane, total):
    weight = buffer[...]
    weight = weight.reshape(-1, weight.shape[2])
    total[...] += jnp.dot(
        design_ref[:, lane : lane + weight.shape[0]], weight, preferred_element_type=jnp.float32
    )


def hand_out(total, keep_ref, send_ref):
    half = keep_ref.shape[0]
    keep_ref[...] = total[:half, :].astype(jnp.bfloat16)
    send_ref[...] = total[half:, :].astype(jnp.bfloat16)


def product_kernel(first, extra, design_ref, weight_ref, *refs):
    keep_ref, send_ref, total, sems, *buffers = refs[extra:]
    copies = weight_copies(weight_ref, buffers, sems, first, keep_ref.shape[1])
    total[...] = jnp.zeros_like(total)
    lane = 0
    for copy, buffer in zip(copies, buffers):
        copy.wait()
        add_slice(design_ref, buffer, lane, total)
        lane += buffer.shape[0] * buffer.shape[1]
    hand_out(total, keep_ref, send_ref)


def first_kernel(parts, extra, block_ref, place_ref, *refs):
    series_refs, (filter_ref, weight_ref), refs = refs[:parts], refs[parts : parts + 2], refs[parts + 2 + extra :]
    design_ref, keep_ref, send_ref, plain, shifted, total, sems, *buffers = refs
    copies = weight_copies(weight_ref, buffers, sems, 0, keep_ref.shape[1])
    total[...] = jnp.zeros_like(total)
    bases = weight_ref.shape[0]
    lead = TAP_SPACING * FILTER_TAPS
    for s in range(shifted.shape[0]):
        shifted[s, : lead + 8, :] = jnp.zeros((lead + 8, LANES), jnp.float32)
    slices = slices_of(weight_ref.shape[1])

    def filters(i):
        start, _, padded = slices[i]
        for at in range(0, padded, LANES):
            lanes = [bases * start + b * padded + at for b in range(bases)]
            filter_tile(
                block_ref, place_ref, series_refs, filter_ref, design_ref, plain, shifted, start + at, lanes
            )

    filters(0)
    for i, (copy, buffer) in enumerate(zip(copies, buffers)):
        copy.wait()
        add_slice(design_ref, buffer, bases * slices[i][0], total)
        if i + 1 < len(copies):
            filters(i + 1)
    hand_out(total, keep_ref, send_ref)


def product(weights, time_len, first, width, after, design=None, sources=()):
    bases, depth, _ = weights.shape
    slices = slices_of(depth)
    half = jax.ShapeDtypeStruct((time_len // 2, width), jnp.bfloat16)
    lanes = bases * sum(padded for _, _, padded in slices)
    scratch = [pltpu.VMEM((time_len, width), jnp.float32), pltpu.SemaphoreType.DMA((len(slices),))]
    scratch += [pltpu.VMEM((bases, padded, width), jnp.bfloat16) for _, _, padded in slices]
    flops = 2 * time_len * bases * depth * width
    common = dict(
        compiler_params=pltpu.CompilerParams(vmem_limit_bytes=40 * MIB),
        cost_estimate=pl.CostEstimate(
            flops=flops, bytes_accessed=2 * bases * depth * width + 2 * time_len * width, transcendentals=0
        ),
    )
    if design is not None:
        return pl.pallas_call(
            functools.partial(product_kernel, first, len(after)),
            in_specs=[VMEM(), ANY()] + [ANY()] * len(after),
            out_specs=[VMEM(), VMEM()],
            out_shape=[half, half],
            scratch_shapes=scratch,
            name="product",
            **common,
        )(design, weights, *after)
    order, place, series, filters = sources
    parts = len(series)
    return pl.pallas_call(
        functools.partial(first_kernel, parts, len(after)),
        in_specs=[SMEM(), SMEM()] + [VMEM()] * (parts + 1) + [ANY()] + [ANY()] * len(after),
        out_specs=[VMEM(), VMEM(), VMEM()],
        out_shape=[jax.ShapeDtypeStruct((time_len, lanes), jnp.bfloat16), half, half],
        scratch_shapes=[
            pltpu.VMEM((time_len, LANES), jnp.float32),
            pltpu.VMEM((8 // TAP_SPACING, time_len + TAP_SPACING * FILTER_TAPS + 8, LANES), jnp.float32),
        ]
        + scratch,
        name="first_product",
        **common,
    )(order, place, *series, filters, weights, *after)


def pack_kernel(spread, widths, first, more, start_ref, onehot_ref, tile_ref, *refs):
    *terms, packed_ref, summed = refs
    if more:
        packed_ref[...] = terms.pop(0)[...]
    else:
        packed_ref[...] = jnp.zeros_like(packed_ref)
    owners, time_block, send_cap = packed_ref.shape
    each, at = len(terms) // len(widths), 0
    for c, width in enumerate(widths):
        total = sum(term[:time_block, :].astype(jnp.float32) for term in terms[c * each : (c + 1) * each])
        summed[:, at : at + width] = total.astype(jnp.bfloat16)
        at += width
    last_tile = send_cap // SLOT_TILE - 1
    step = VOX_BLOCK // LANES

    def block_step(index, carry):
        block = first + index
        values = summed[:, pl.ds(pl.multiple_of(index * VOX_BLOCK, VOX_BLOCK), VOX_BLOCK)]
        onehot = onehot_ref[pl.ds(pl.multiple_of(block * VOX_BLOCK, VOX_BLOCK), VOX_BLOCK), :]
        tiles = jnp.concatenate([tile_ref[pl.ds(block * step + i, 1), :] for i in range(step)], axis=1)

        def move(owner, tile):
            chosen = jnp.where(tiles == owner * spread + tile, 1.0, 0.0).astype(jnp.bfloat16)
            return jnp.dot(values * chosen, onehot, preferred_element_type=jnp.float32).astype(jnp.bfloat16)

        def put(owner, tile, moved):
            tile = jnp.minimum(tile, last_tile)
            at = pl.ds(pl.multiple_of(tile * SLOT_TILE, SLOT_TILE), SLOT_TILE)
            packed_ref[owner, :, at] = packed_ref[owner, :, at] + moved

        low = [start_ref[block, o] >> 7 for o in range(owners)]
        moved = [move(o, low[o] + extra) for o in range(owners) for extra in range(2)]
        for o in range(owners):
            for extra in range(2):
                put(o, low[o] + extra, moved[2 * o + extra])
        for o in range(owners):

            @pl.when((start_ref[block + 1, o] - 1) >> 7 > low[o] + 1)
            def _():
                put(o, low[o] + 2, move(o, low[o] + 2))

        return carry

    lax.fori_loop(0, sum(widths) // VOX_BLOCK, block_step, 0)


def shards(features, hrf_filters, weights, voxel_parcel, parcel_owner):
    owners, parts = lax.axis_size("vox"), lax.axis_size("chan")
    me = lax.axis_index("chan")
    voxels = voxel_parcel.shape[0]
    send_cap = 2 * voxels // owners
    bases, depth, _ = weights.shape
    blocks = voxels // VOX_BLOCK
    time_block = features.shape[0]
    time_len = time_block * parts

    series = [lax.dynamic_slice_in_dim(features, (me ^ d) * depth, depth, 1) for d in range(parts)]
    for d in range(1, parts):
        series[d] = lax.ppermute(series[d], "chan", [(i, i ^ d) for i in range(parts)])
    filters = jnp.transpose(hrf_filters, (0, 2, 1))
    spare = -depth % LANES
    if spare:
        series = [jnp.pad(part, ((0, 0), (0, spare))) for part in series]
        filters = jnp.pad(filters, ((0, 0), (0, 0), (0, spare)))

    table_rows = -(-parcel_owner.shape[0] // LANES)
    table = jnp.pad(parcel_owner, (0, table_rows * LANES - parcel_owner.shape[0])).reshape(table_rows, LANES)
    marks = -(-(blocks + 1) // 8) * 8
    spread = send_cap // SLOT_TILE + 3
    onehot, tiles, starts = pl.pallas_call(
        functools.partial(places_kernel, owners, spread),
        in_specs=[VMEM(), VMEM()],
        out_specs=[VMEM(), VMEM(), VMEM()],
        out_shape=[
            jax.ShapeDtypeStruct((voxels, LANES), jnp.bfloat16),
            jax.ShapeDtypeStruct((voxels // LANES, LANES), jnp.int32),
            jax.ShapeDtypeStruct((marks, LANES), jnp.int32),
        ],
        name="places",
    )(voxel_parcel.reshape(-1, LANES), table)

    bits = parts.bit_length() - 1
    order = jnp.arange(parts, dtype=jnp.int32) ^ me
    place = sum(((order >> bit) & 1) << (bits - 1 - bit) for bit in range(bits)).astype(jnp.int32)

    unit = voxels // sum(CHUNK_UNITS)
    widths = [unit * units for units in CHUNK_UNITS]
    terms, sent, got = [], [], []
    design, first = None, 0
    for c, width in enumerate(widths):
        if c == 0:
            design, keep, send = product(
                weights, time_len, first, width, [starts], sources=(order, place, series, filters)
            )
        else:
            after = sent[max(c - 2, 0) : max(c - 1, 0)] + got[max(c - 3, 0) : max(c - 2, 0)]
            keep, send = product(weights, time_len, first, width, after, design)
        first += width
        own = [keep]
        for bit in range(bits):
            if bit > 0:
                rows = own[-1].shape[0] // 2
                send = sum(term[rows : 2 * rows].astype(jnp.float32) for term in own).astype(jnp.bfloat16)
                if bit == 1:
                    sent.append(send)
            own.append(lax.ppermute(send, "chan", [(i, i ^ (1 << bit)) for i in range(parts)]))
        terms.append(own)
        got.append(own[-1])

    packed = []
    for low, high in ((0, PACK_FIRST), (PACK_FIRST, len(widths))):
        args = packed + [term for own in terms[low:high] for term in own]
        here = widths[low:high]
        packed = [
            pl.pallas_call(
                functools.partial(pack_kernel, spread, here, sum(widths[:low]) // VOX_BLOCK, len(packed)),
                in_specs=[SMEM(), VMEM(), VMEM()] + [VMEM()] * len(args),
                out_specs=VMEM(),
                out_shape=jax.ShapeDtypeStruct((owners, time_block, send_cap), jnp.bfloat16),
                scratch_shapes=[pltpu.VMEM((time_block, sum(here)), jnp.bfloat16)],
                compiler_params=pltpu.CompilerParams(vmem_limit_bytes=32 * MIB),
                name="pack",
            )(starts, onehot, tiles, *args)
        ]
    received = lax.all_to_all(packed[0], "vox", split_axis=0, concat_axis=0, tiled=True)
    return jnp.transpose(received, (0, 2, 1))


def solution(mesh):
    return jax.shard_map(
        shards,
        mesh=mesh,
        in_specs=(P("chan", None), P(None, "chan", None), P(None, "chan", "vox"), P("vox"), P()),
        out_specs=P("vox", None, "chan"),
        check_vma=False,
    )
```

time: 293 us -> 99.2 us (0.34)
  blocking collectives: 185 us -> 37.1 us
  local copies, waits for them, and re-layouts: 66.5 us -> 3.65 us
  Pallas kernels: 0 us -> 41.3 us
  matrix products: 28.1 us -> 0 us
  starting transfers between devices: 4.21 us -> 12.3 us
  other arithmetic: 7.55 us -> 0.37 us
  waiting for transfers between devices: 0.01 us -> 4.11 us
    all_to_all x2 -> x1, blocking collectives: 185 us -> 37.1 us  [shards(): lax.all_to_all(packed[0], 'vox', split_axis=0, concat_axis=0, tiled=True)]
    pallas_call x0 -> x9, Pallas kernels: none -> 41.3 us  [the longest x5 19.8 us: product(): pl.pallas_call(functools.partial(product_kernel, first, len(after)), in_s...]
    dot_general x1 -> x0, matrix products: 28.1 us -> none  [shards(): lax.dot_general(weight_panel, design, (((0,), (0,)), ((), ())), preferred...]
    scatter x1 -> x0, local copies, waits for them, and re-layouts: 25.4 us -> none  [shards(): jnp.zeros((owner_count * send_cap, time_len), jnp.bfloat16).at[target_row]]
    gather x1 -> x0, local copies, waits for them, and re-layouts: 20.7 us -> none  [shards(): owners_here = jnp.take(parcel_owner, voxel_parcel)]
    ppermute x0 -> x15, starting transfers between devices: none -> 12.3 us  [the longest x12 9.12 us: shards(): lax.ppermute(send, 'chan', [(i, i ^ 1 << bit) for i in range(parts)])]
    reshape x1, local copies, waits for them, and re-layouts: 8.67 us -> 0.58 us  [shards(): jnp.pad(parcel_owner, (0, table_rows * LANES - parcel_owner.shape[0]))]
    slice x3 -> x0, local copies, waits for them, and re-layouts: 5.44 us -> none  [the longest x1 4.96 us: shards(): lagged = padded[:, window_start:window_start + time_len]]
  transfers between devices with their start and end apart: 1 -> 15, of which waited for: 0 -> 2; matrix products, arithmetic and copies ran while one was open for 8% -> 1% of each run, Pallas kernels for 0% -> 31%
where the time goes in v3:
time: 99.2 us; the launch traced here: 98.9 us
  Pallas kernels  41.3 us (42%)
  blocking collectives  37.1 us (37%)
  starting transfers between devices  12.3 us (12%)
  waiting for transfers between devices  4.11 us (4%)
  local copies, waits for them, and re-layouts  3.65 us (4%)
    all_to_all x1, blocking collectives, shards(): lax.all_to_all(packed[0], 'vox', split_axis=0, concat_axis=0, tiled=True)  37.1 us
    pallas_call x5, Pallas kernels, product(): pl.pallas_call(functools.partial(product_kernel, first, len(after)), in_s...  19.8 us
    pallas_call x2, Pallas kernels, shards(): pl.pallas_call(functools.partial(pack_kernel, spread, here, sum(widths[:l...  9.28 us
    ppermute x12, starting transfers between devices, shards(): lax.ppermute(send, 'chan', [(i, i ^ 1 << bit) for i in range(parts)])  9.12 us
    pallas_call x1, Pallas kernels, product(): pl.pallas_call(functools.partial(first_kernel, parts, len(after)), in_spe...  8.14 us
    pallas_call x1, Pallas kernels, shards(): pl.pallas_call(functools.partial(places_kernel, owners, spread), in_specs...  4.07 us
    ppermute x3, waiting for transfers between devices, shards(): lax.ppermute(series[d], 'chan', [(i, i ^ d) for i in range(parts)])  3.58 us
    ppermute x3, starting transfers between devices, shards(): lax.ppermute(series[d], 'chan', [(i, i ^ d) for i in range(parts)])  3.16 us
  transfers between devices with their start and end apart: 15, of which 2 were waited for; matrix products, arithmetic and copies ran while one was open for 1% of the time, Pallas kernels for 31%

profile of v3, /device:TPU:0, one launch (start us, length us, event | category | flops | bytes accessed | tf_op | source)
XLA Modules:
  0.0 98.9 jit_solution(13986711024158963296)
XLA Ops:
  0.0 1.3 %constant_dynamic-slice_fusion = (bf16[64,1408]{1,0:T(8,128)(2,1)S(1)}, bf16[64,1408]{1,0:T(8,128)(2,1)S(1)}, bf16[64,1408]{1,0:T(8,128)(2,1)S(1)}, bf16[64,1408]{1,0:T(8,128)(2,1)S(1)}) fusion(bf16[64,5632]{1,0:T(8,128)(2,1)} %param.5, s32[]{:T(128)S(6)} %select_n.15, s32[]{:T(128)S(6)} %select_n.13, s32[]{:T(128)S(6)} %select_n.12, s32[]{:T(128)S(6)} %select_n.14), kind=kLoop, calls=%fused_computation.7 | loop fusion | bytes 1441808 | tf_op jit(solution)/shard_map/dynamic_slice | solution.py:266
  1.3 2.4 %collective-permute-start.2 = (bf16[64,1408]{1,0:T(8,128)(2,1)S(1)}, bf16[64,1408]{1,0:T(8,128)(2,1)S(1)}, u32[]{:S(2)}, u32[]{:S(2)}) collective-permute-start(bf16[64,1408]{1,0:T(8,128)(2,1)S(1)} %get-tuple-element.37), channel_id=1, source_target_pairs={{0,24},{8,16},{16,8},{24,0},{1,25},{9,17},{17,9},{25,1},{2,26},{10... | collective-permute-start | bytes 540680 | tf_op jit(solution)/shard_map/ppermute | solution.py:268
  3.7 0.7 collective-permute-start
  4.4 0.0 collective-permute-start.1
  4.5 0.6 pad_bitcast_fusion.table_ref
  5.0 4.1 %places.1 = (bf16[5120,128]{1,0:T(8,128)(2,1)}, s32[40,128]{1,0:T(8,128)}, s32[24,128]{1,0:T(8,128)}) custom-call(s32[40,128]{1,0:T(8,128)} %bitcast.7, s32[7,128]{1,0:T(8,128)} %pad_bitcast_fusion.table_ref), custom_call_target="tpu_custom_call" | custom-call | tf_op jit(solution)/shard_map/places/pallas_call | solution.py:279
  9.1 3.6 %collective-permute-done.1.refs_2_ = bf16[64,1408]{1,0:T(8,128)(2,1)S(1)} collective-permute-done((bf16[64,1408]{1,0:T(8,128)(2,1)S(1)}, bf16[64,1408]{1,0:T(8,128)(2,1)S(1)}, u32[]{:S(2)}, u32[]{:S(2)}) %collective-permute-start.1) | collective-permute-done | bytes 180256 | tf_op jit(solution)/shard_map/ppermute | solution.py:268
  12.7 0.7 copy-done.2
  13.4 8.1 %first_product.1 = (bf16[256,4224]{1,0:T(8,128)(2,1)S(1)}, bf16[128,1024]{1,0:T(8,128)(2,1)S(1)}, bf16[128,1024]{1,0:T(8,128)(2,1)S(1)}) custom-call(s32[4]{0:T(128)S(1)} %get-tuple-element.42.block_ref, s32[4]{0:T(128)S(1)} %get-tuple-element.41.place_ref, bf16[64,1408]{1,0:T(8,128)(2,1)S(1)} %get-tuple-element.39.refs_0_, ...), custom_call_target="tpu_custom_call" | custom-call | flops 2214592512 | bytes 9175040 | tf_op jit(solution)/shard_map/first_product/pallas_call | solution.py:195
  21.6 0.1 collective-permute-start.3
  21.6 4.7 %product.5 = (bf16[128,1024]{1,0:T(8,128)(2,1)S(1)}, bf16[128,1024]{1,0:T(8,128)(2,1)S(1)}) custom-call(bf16[256,4224]{1,0:T(8,128)(2,1)S(1)} %get-tuple-element.26.design_ref, bf16[3,1408,5120]{2,1,0:T(8,128)(2,1)} %weight_ref.9), custom_call_target="tpu_custom_call" | custom-call | flops 2214592512 | bytes 9175040 | tf_op jit(solution)/shard_map/product/pallas_call | solution.py:184
  26.3 0.6 collective-permute-start.5
  26.9 2.4 %collective-permute-start.4 = (bf16[64,1024]{1,0:T(8,128)(2,1)S(1)}, bf16[64,1024]{1,0:T(8,128)(2,1)S(1)}, u32[]{:S(2)}, u32[]{:S(2)}) collective-permute-start(bf16[64,1024]{1,0:T(8,128)(2,1)S(1)} %add_convert_fusion.3.refs_0_), channel_id=1, source_target_pairs={{0,16},{8,24},{16,0},{24,8},{1,17},{9,25},{17,1},{25,9},{2,18},{10... | collective-permute-start | bytes 393224 | tf_op jit(solution)/shard_map/ppermute | solution.py:315
  29.3 4.6 %product.6 = (bf16[128,1024]{1,0:T(8,128)(2,1)S(1)}, bf16[128,1024]{1,0:T(8,128)(2,1)S(1)}) custom-call(bf16[256,4224]{1,0:T(8,128)(2,1)S(1)} %get-tuple-element.26.design_ref, bf16[3,1408,5120]{2,1,0:T(8,128)(2,1)} %weight_ref.9, bf16[64,1024]{1,0:T(8,128)(2,1)S(1)} %add_convert_fusion.3.refs_0_), custom_call_target="tpu_custom_call" | custom-call | flops 2214592512 | bytes 9175040 | tf_op jit(solution)/shard_map/product/pallas_call | solution.py:184
  33.9 0.1 collective-permute-start.7
  34.0 0.2 add_convert_fusion.2.refs_0_
  34.2 0.2 collective-permute-start.6
  34.4 4.6 %product.7 = (bf16[128,1024]{1,0:T(8,128)(2,1)S(1)}, bf16[128,1024]{1,0:T(8,128)(2,1)S(1)}) custom-call(bf16[256,4224]{1,0:T(8,128)(2,1)S(1)} %get-tuple-element.26.design_ref, bf16[3,1408,5120]{2,1,0:T(8,128)(2,1)} %weight_ref.9, bf16[64,1024]{1,0:T(8,128)(2,1)S(1)} %add_convert_fusion.2.refs_0_, bf16[64,1024]{1,0:T(8,128)(2,1)S(1)} %collective-permute-done.4.refs_1_.refs_2_), custom_call_target="tpu_custom_call" | custom-call | flops 2214592512 | bytes 9175040 | tf_op jit(solution)/shard_map/product/pallas_call | solution.py:184
  39.1 0.5 collective-permute-start.9
  39.6 1.8 %collective-permute-start.8 = (bf16[64,1024]{1,0:T(8,128)(2,1)S(1)}, bf16[64,1024]{1,0:T(8,128)(2,1)S(1)}, u32[]{:S(2)}, u32[]{:S(2)}) collective-permute-start(bf16[64,1024]{1,0:T(8,128)(2,1)S(1)} %add_convert_fusion.1.refs_0_), channel_id=1, source_target_pairs={{0,16},{8,24},{16,0},{24,8},{1,17},{9,25},{17,1},{25,9},{2,18},{10... | collective-permute-start | bytes 393224 | tf_op jit(solution)/shard_map/ppermute | solution.py:315
  41.4 2.9 %product.8 = (bf16[128,512]{1,0:T(8,128)(2,1)S(1)}, bf16[128,512]{1,0:T(8,128)(2,1)S(1)}) custom-call(bf16[256,4224]{1,0:T(8,128)(2,1)S(1)} %get-tuple-element.26.design_ref, bf16[3,1408,5120]{2,1,0:T(8,128)(2,1)} %weight_ref.9, bf16[64,1024]{1,0:T(8,128)(2,1)S(1)} %add_convert_fusion.1.refs_0_, bf16[64,1024]{1,0:T(8,128)(2,1)S(1)} %collective-permute-done.6.refs_5_.refs_1_), custom_call_target="tpu_custom_call" | custom-call | flops 1107296256 | bytes 4587520 | tf_op jit(solution)/shard_map/product/pallas_call | solution.py:184
  44.3 0.1 collective-permute-start.11
  44.5 0.4 collective-permute-start.10
  44.8 0.5 collective-permute-done.8.refs_8_.refs_1_
  45.3 2.9 %product.9 = (bf16[128,512]{1,0:T(8,128)(2,1)S(1)}, bf16[128,512]{1,0:T(8,128)(2,1)S(1)}) custom-call(bf16[256,4224]{1,0:T(8,128)(2,1)S(1)} %get-tuple-element.26.design_ref, bf16[3,1408,5120]{2,1,0:T(8,128)(2,1)} %weight_ref.9, bf16[64,1024]{1,0:T(8,128)(2,1)S(1)} %add_convert_fusion.refs_0_, bf16[64,1024]{1,0:T(8,128)(2,1)S(1)} %collective-permute-done.8.refs_8_.refs_1_), custom_call_target="tpu_custom_call" | custom-call | flops 1107296256 | bytes 4587520 | tf_op jit(solution)/shard_map/product/pallas_call | solution.py:184
  48.2 0.1 collective-permute-start.13
  48.4 1.8 %collective-permute-start.12 = (bf16[64,512]{1,0:T(8,128)(2,1)S(1)}, bf16[64,512]{1,0:T(8,128)(2,1)S(1)}, u32[]{:S(2)}, u32[]{:S(2)}) collective-permute-start(bf16[64,512]{1,0:T(8,128)(2,1)S(1)} %add_convert_fusion.5), channel_id=1, source_target_pairs={{0,16},{8,24},{16,0},{24,8},{1,17},{9,25},{17,1},{25,9},{2,18},{10... | collective-permute-start | bytes 196616 | tf_op jit(solution)/shard_map/ppermute | solution.py:315
  50.2 1.3 %collective-permute-start.14 = (bf16[64,512]{1,0:T(8,128)(2,1)S(1)}, bf16[64,512]{1,0:T(8,128)(2,1)S(1)}, u32[]{:S(2)}, u32[]{:S(2)}) collective-permute-start(bf16[64,512]{1,0:T(8,128)(2,1)S(1)} %add_convert_fusion.4), channel_id=1, source_target_pairs={{0,16},{8,24},{16,0},{24,8},{1,17},{9,25},{17,1},{25,9},{2,18},{10... | collective-permute-start | bytes 196616 | tf_op jit(solution)/shard_map/ppermute | solution.py:315
  51.5 6.9 %pack.2.refs_0_ = bf16[8,64,1280]{2,1,0:T(8,128)(2,1)S(1)} custom-call(s32[24,128]{1,0:T(8,128)S(1)} %copy-done.3, bf16[5120,128]{1,0:T(8,128)(2,1)S(1)} %copy-done, s32[40,128]{1,0:T(8,128)S(1)} %copy-done.4, bf16[128,1024]{1,0:T(8,128)(2,1)S(1)} %get-tuple-element.24.refs_0_, bf16[128,1024]{1,0:T(8,128)(2,1)S(1)} %collective-permute-done.3.refs_1_, ...), custom_call_target="tpu_custom_call" | custom-call | tf_op jit(solution)/shard_map/pack/pallas_call | solution.py:324
  58.5 2.4 %pack.3 = bf16[8,64,1280]{2,1,0:T(8,128)(2,1)S(1)} custom-call(s32[24,128]{1,0:T(8,128)S(1)} %copy-done.3, bf16[5120,128]{1,0:T(8,128)(2,1)S(1)} %copy-done, s32[40,128]{1,0:T(8,128)S(1)} %copy-done.4, bf16[8,64,1280]{2,1,0:T(8,128)(2,1)S(1)} %pack.2.refs_0_, bf16[128,512]{1,0:T(8,128)(2,1)S(1)} %get-tuple-element.33.refs_1_, ...), custom_call_target="tpu_custom_call" | custom-call | tf_op jit(solution)/shard_map/pack/pallas_call | solution.py:324
  60.8 37.1 %all_to_all.5 = bf16[8,64,1280]{2,1,0:T(8,128)(2,1)S(1)} all-to-all(bf16[8,64,1280]{2,1,0:T(8,128)(2,1)S(1)} %pack.3), channel_id=1, replica_groups=mesh['chan'=4,'vox'=8] {'vox'}, dimensions={0} | all-to-all | bytes 2621440 | tf_op jit(solution)/shard_map/all_to_all | solution.py:334
  97.9 1.1 %copy.7 = bf16[8,1280,64]{1,2,0:T(8,128)(2,1)} copy(bf16[8,1280,64]{1,2,0:T(8,128)(2,1)S(1)} %bitcast.6) | data formatting | bytes 2621440
  (30 shorter events, 0.2 us)
Async XLA Ops:
  0.0 4.5 %copy-start.5 = (s32[800]{0:T(1024)S(1)}, s32[800]{0:T(1024)}, u32[]{:S(2)}) copy-start(s32[800]{0:T(1024)} %param.9) | copy-start | bytes 9604
  0.0 12.7 %copy-start.1 = (f32[3,1408,16]{1,2,0:T(8,128)S(1)}, f32[3,1408,16]{1,2,0:T(8,128)}, u32[]{:S(2)}) copy-start(f32[3,1408,16]{1,2,0:T(8,128)} %param.6) | copy-start | bytes 811012
  1.3 7.8 %collective-permute-start.2 = (bf16[64,1408]{1,0:T(8,128)(2,1)S(1)}, bf16[64,1408]{1,0:T(8,128)(2,1)S(1)}, u32[]{:S(2)}, u32[]{:S(2)}) collective-permute-start(bf16[64,1408]{1,0:T(8,128)(2,1)S(1)} %get-tuple-element.37), channel_id=1, source_target_pairs={{0,24},{8,16},{16,8},{24,0},{1,25},{9,17},{17,9},{25,1},{2,26},{10... | collective-permute-start | bytes 540680 | tf_op jit(solution)/shard_map/ppermute | solution.py:268
  3.7 5.4 %collective-permute-start = (bf16[64,1408]{1,0:T(8,128)(2,1)S(1)}, bf16[64,1408]{1,0:T(8,128)(2,1)S(1)}, u32[]{:S(2)}, u32[]{:S(2)}) collective-permute-start(bf16[64,1408]{1,0:T(8,128)(2,1)S(1)} %get-tuple-element.38), channel_id=1, source_target_pairs={{0,8},{8,0},{16,24},{24,16},{1,9},{9,1},{17,25},{25,17},{2,10},{10... | collective-permute-start | bytes 540680 | tf_op jit(solution)/shard_map/ppermute | solution.py:268
  4.4 8.3 %collective-permute-start.1 = (bf16[64,1408]{1,0:T(8,128)(2,1)S(1)}, bf16[64,1408]{1,0:T(8,128)(2,1)S(1)}, u32[]{:S(2)}, u32[]{:S(2)}) collective-permute-start(bf16[64,1408]{1,0:T(8,128)(2,1)S(1)} %get-tuple-element.40), channel_id=1, source_target_pairs={{0,16},{8,24},{16,0},{24,8},{1,17},{9,25},{17,1},{25,9},{2,18},{10... | collective-permute-start | bytes 540680 | tf_op jit(solution)/shard_map/ppermute | solution.py:268
  12.7 0.7 copy-start.2
  21.6 5.3 %collective-permute-start.3 = (bf16[128,1024]{1,0:T(8,128)(2,1)S(1)}, bf16[128,1024]{1,0:T(8,128)(2,1)S(1)}, u32[]{:S(2)}, u32[]{:S(2)}) collective-permute-start(bf16[128,1024]{1,0:T(8,128)(2,1)S(1)} %get-tuple-element.25), channel_id=1, source_target_pairs={{0,8},{8,0},{16,24},{24,16},{1,9},{9,1},{17,25},{25,17},{2,10},{10... | collective-permute-start | bytes 786440 | tf_op jit(solution)/shard_map/ppermute | solution.py:315
  26.3 7.7 %collective-permute-start.5 = (bf16[128,1024]{1,0:T(8,128)(2,1)S(1)}, bf16[128,1024]{1,0:T(8,128)(2,1)S(1)}, u32[]{:S(2)}, u32[]{:S(2)}) collective-permute-start(bf16[128,1024]{1,0:T(8,128)(2,1)S(1)} %get-tuple-element.28), channel_id=1, source_target_pairs={{0,8},{8,0},{16,24},{24,16},{1,9},{9,1},{17,25},{25,17},{2,10},{10... | collective-permute-start | bytes 786440 | tf_op jit(solution)/shard_map/ppermute | solution.py:315
  26.9 7.5 %collective-permute-start.4 = (bf16[64,1024]{1,0:T(8,128)(2,1)S(1)}, bf16[64,1024]{1,0:T(8,128)(2,1)S(1)}, u32[]{:S(2)}, u32[]{:S(2)}) collective-permute-start(bf16[64,1024]{1,0:T(8,128)(2,1)S(1)} %add_convert_fusion.3.refs_0_), channel_id=1, source_target_pairs={{0,16},{8,24},{16,0},{24,8},{1,17},{9,25},{17,1},{25,9},{2,18},{10... | collective-permute-start | bytes 393224 | tf_op jit(solution)/shard_map/ppermute | solution.py:315
  33.9 5.6 %collective-permute-start.7 = (bf16[128,1024]{1,0:T(8,128)(2,1)S(1)}, bf16[128,1024]{1,0:T(8,128)(2,1)S(1)}, u32[]{:S(2)}, u32[]{:S(2)}) collective-permute-start(bf16[128,1024]{1,0:T(8,128)(2,1)S(1)} %get-tuple-element.30), channel_id=1, source_target_pairs={{0,8},{8,0},{16,24},{24,16},{1,9},{9,1},{17,25},{25,17},{2,10},{10... | collective-permute-start | bytes 786440 | tf_op jit(solution)/shard_map/ppermute | solution.py:315
  34.2 7.1 %collective-permute-start.6 = (bf16[64,1024]{1,0:T(8,128)(2,1)S(1)}, bf16[64,1024]{1,0:T(8,128)(2,1)S(1)}, u32[]{:S(2)}, u32[]{:S(2)}) collective-permute-start(bf16[64,1024]{1,0:T(8,128)(2,1)S(1)} %add_convert_fusion.2.refs_0_), channel_id=1, source_target_pairs={{0,16},{8,24},{16,0},{24,8},{1,17},{9,25},{17,1},{25,9},{2,18},{10... | collective-permute-start | bytes 393224 | tf_op jit(solution)/shard_map/ppermute | solution.py:315
  39.1 5.3 %collective-permute-start.9 = (bf16[128,1024]{1,0:T(8,128)(2,1)S(1)}, bf16[128,1024]{1,0:T(8,128)(2,1)S(1)}, u32[]{:S(2)}, u32[]{:S(2)}) collective-permute-start(bf16[128,1024]{1,0:T(8,128)(2,1)S(1)} %get-tuple-element.32), channel_id=1, source_target_pairs={{0,8},{8,0},{16,24},{24,16},{1,9},{9,1},{17,25},{25,17},{2,10},{10... | collective-permute-start | bytes 786440 | tf_op jit(solution)/shard_map/ppermute | solution.py:315
  39.6 5.7 %collective-permute-start.8 = (bf16[64,1024]{1,0:T(8,128)(2,1)S(1)}, bf16[64,1024]{1,0:T(8,128)(2,1)S(1)}, u32[]{:S(2)}, u32[]{:S(2)}) collective-permute-start(bf16[64,1024]{1,0:T(8,128)(2,1)S(1)} %add_convert_fusion.1.refs_0_), channel_id=1, source_target_pairs={{0,16},{8,24},{16,0},{24,8},{1,17},{9,25},{17,1},{25,9},{2,18},{10... | collective-permute-start | bytes 393224 | tf_op jit(solution)/shard_map/ppermute | solution.py:315
  44.3 4.0 %collective-permute-start.11 = (bf16[128,512]{1,0:T(8,128)(2,1)S(1)}, bf16[128,512]{1,0:T(8,128)(2,1)S(1)}, u32[]{:S(2)}, u32[]{:S(2)}) collective-permute-start(bf16[128,512]{1,0:T(8,128)(2,1)S(1)} %get-tuple-element.34), channel_id=1, source_target_pairs={{0,8},{8,0},{16,24},{24,16},{1,9},{9,1},{17,25},{25,17},{2,10},{10... | collective-permute-start | bytes 393224 | tf_op jit(solution)/shard_map/ppermute | solution.py:315
  44.4 7.1 %copy-start = (bf16[5120,128]{1,0:T(8,128)(2,1)S(1)}, bf16[5120,128]{1,0:T(8,128)(2,1)}, u32[]{:S(2)}) copy-start(bf16[5120,128]{1,0:T(8,128)(2,1)} %get-tuple-element.22.onehot_ref) | copy-start | bytes 3932164
  44.4 7.1 %copy-start.3 = (s32[24,128]{1,0:T(8,128)S(1)}, s32[24,128]{1,0:T(8,128)}, u32[]{:S(2)}) copy-start(s32[24,128]{1,0:T(8,128)} %get-tuple-element.21.refs_6_.start_ref) | copy-start | bytes 36868
  44.4 7.1 %copy-start.4 = (s32[40,128]{1,0:T(8,128)S(1)}, s32[40,128]{1,0:T(8,128)}, u32[]{:S(2)}) copy-start(s32[40,128]{1,0:T(8,128)} %get-tuple-element.23.tile_ref) | copy-start | bytes 61444
  44.5 7.0 %collective-permute-start.10 = (bf16[64,1024]{1,0:T(8,128)(2,1)S(1)}, bf16[64,1024]{1,0:T(8,128)(2,1)S(1)}, u32[]{:S(2)}, u32[]{:S(2)}) collective-permute-start(bf16[64,1024]{1,0:T(8,128)(2,1)S(1)} %add_convert_fusion.refs_0_), channel_id=1, source_target_pairs={{0,16},{8,24},{16,0},{24,8},{1,17},{9,25},{17,1},{25,9},{2,18},{10... | collective-permute-start | bytes 393224 | tf_op jit(solution)/shard_map/ppermute | solution.py:315
  48.2 1.9 %collective-permute-start.13 = (bf16[128,512]{1,0:T(8,128)(2,1)S(1)}, bf16[128,512]{1,0:T(8,128)(2,1)S(1)}, u32[]{:S(2)}, u32[]{:S(2)}) collective-permute-start(bf16[128,512]{1,0:T(8,128)(2,1)S(1)} %get-tuple-element.36), channel_id=1, source_target_pairs={{0,8},{8,0},{16,24},{24,16},{1,9},{9,1},{17,25},{25,17},{2,10},{10... | collective-permute-start | bytes 393224 | tf_op jit(solution)/shard_map/ppermute | solution.py:315
  48.4 10.1 %collective-permute-start.12 = (bf16[64,512]{1,0:T(8,128)(2,1)S(1)}, bf16[64,512]{1,0:T(8,128)(2,1)S(1)}, u32[]{:S(2)}, u32[]{:S(2)}) collective-permute-start(bf16[64,512]{1,0:T(8,128)(2,1)S(1)} %add_convert_fusion.5), channel_id=1, source_target_pairs={{0,16},{8,24},{16,0},{24,8},{1,17},{9,25},{17,1},{25,9},{2,18},{10... | collective-permute-start | bytes 196616 | tf_op jit(solution)/shard_map/ppermute | solution.py:315
  50.2 8.3 %collective-permute-start.14 = (bf16[64,512]{1,0:T(8,128)(2,1)S(1)}, bf16[64,512]{1,0:T(8,128)(2,1)S(1)}, u32[]{:S(2)}, u32[]{:S(2)}) collective-permute-start(bf16[64,512]{1,0:T(8,128)(2,1)S(1)} %add_convert_fusion.4), channel_id=1, source_target_pairs={{0,16},{8,24},{16,0},{24,8},{1,17},{9,25},{17,1},{25,9},{2,18},{10... | collective-permute-start | bytes 196616 | tf_op jit(solution)/shard_map/ppermute | solution.py:315

commit v4 on v3

--- a/solution.py
+++ b/solution.py
@@ -13,8 +13,10 @@
 SLOT_TILE = 128
 VOX_BLOCK = 256
 CHAN_SLICE = 512
-CHUNK_UNITS = (2, 2, 2, 2, 1, 1)
-PACK_FIRST = 4
+COLUMNS = 512
+CHUNK_UNITS = (5, 5, 4, 4, 2)
+EARLY = 2
+PACK_FIRST = 3
 MIB = 1 << 20
 
 VMEM = functools.partial(pl.BlockSpec, memory_space=pltpu.VMEM)
@@ -22,15 +24,23 @@
 ANY = functools.partial(pl.BlockSpec, memory_space=pl.ANY)
 
 
-def slices_of(depth):
-    out = []
-    for first in range(0, depth, CHAN_SLICE):
-        size = min(CHAN_SLICE, depth - first)
-        out.append((first, size, -(-size // LANES) * LANES))
-    return out
-
-
-def places_kernel(owners, spread, parcel_ref, table_ref, onehot_ref, tile_ref, start_ref):
+def copy_weights(weight_ref, held, sems, first):
+    copies, depth = [], weight_ref.shape[1]
+    for i, ref in enumerate(held):
+        if ref.shape[1] > depth:
+            ref[:, depth:, :] = jnp.zeros_like(ref[:, depth:, :])
+        copies.append(
+            pltpu.make_async_copy(
+                weight_ref.at[:, :, pl.ds(first, ref.shape[2])], ref.at[:, pl.ds(0, depth), :], sems.at[i]
+            )
+        )
+        copies[-1].start()
+        first += ref.shape[2]
+    return copies
+
+
+def places_kernel(owners, spread, parcel_ref, table_ref, weight_ref, onehot_ref, tile_ref, start_ref, *refs):
+    copies = copy_weights(weight_ref, refs[:-1], refs[-1], 0)
     rows = parcel_ref.shape[0]
     parcel = parcel_ref[...]
     high, low = parcel >> 7, parcel & 127
@@ -67,6 +77,8 @@
         line = jnp.broadcast_to(inner[row : row + 1, :], (LANES, LANES))
         hit = jnp.where(line.T == lane, 1.0, 0.0)
         onehot_ref[row * LANES : (row + 1) * LANES, :] = hit.astype(jnp.bfloat16)
+    for copy in copies:
+        copy.wait()
 
 
 def filter_tile(block_ref, place_ref, series_refs, filter_ref, design_ref, plain, shifted, at, lanes):
@@ -95,116 +107,94 @@
             design_ref[row, lane : lane + LANES] = sums[b].astype(jnp.bfloat16)
 
 
-def weight_copies(weight_ref, buffers, sems, first, width):
-    copies, depth = [], weight_ref.shape[1]
-    for i, (start, size, padded) in enumerate(slices_of(depth)):
-        if size < padded:
-            buffers[i][:, size:, :] = jnp.zeros_like(buffers[i][:, size:, :])
-        copies.append(
-            pltpu.make_async_copy(
-                weight_ref.at[:, pl.ds(start, size), pl.ds(first, width)],
-                buffers[i].at[:, pl.ds(0, size), :],
-                sems.at[i],
-            )
-        )
-    for copy in copies:
-        copy.start()
-    return copies
-
-
-def add_slice(design_ref, buffer, lane, total):
-    weight = buffer[...]
-    weight = weight.reshape(-1, weight.shape[2])
-    total[...] += jnp.dot(
-        design_ref[:, lane : lane + weight.shape[0]], weight, preferred_element_type=jnp.float32
-    )
-
-
-def hand_out(total, keep_ref, send_ref):
+def hand_out(total, keep_ref, send_ref, columns):
     half = keep_ref.shape[0]
-    keep_ref[...] = total[:half, :].astype(jnp.bfloat16)
-    send_ref[...] = total[half:, :].astype(jnp.bfloat16)
-
-
-def product_kernel(first, extra, design_ref, weight_ref, *refs):
-    keep_ref, send_ref, total, sems, *buffers = refs[extra:]
-    copies = weight_copies(weight_ref, buffers, sems, first, keep_ref.shape[1])
+    keep_ref[:, columns] = total[:half].astype(jnp.bfloat16)
+    send_ref[:, columns] = total[half:].astype(jnp.bfloat16)
+
+
+def product_kernel(extra, design_ref, weight_ref, *refs):
+    keep_ref, send_ref = refs[extra:]
+    width = keep_ref.shape[1]
+    for at in range(0, width, COLUMNS):
+        columns = slice(at, min(at + COLUMNS, width))
+        weight = weight_ref[:, :, columns]
+        weight = weight.reshape(-1, weight.shape[2])
+        total = jnp.dot(design_ref[...], weight, preferred_element_type=jnp.float32)
+        hand_out(total, keep_ref, send_ref, columns)
+
+
+def first_kernel(parts, extra, ahead, block_ref, place_ref, *refs):
+    series_refs, (filter_ref, weight_ref, rest_ref), refs = refs[:parts], refs[parts : parts + 3], refs[parts + 3 + extra :]
+    design_ref, keep_ref, send_ref, *held, plain, shifted, total, sems = refs
+    copies = copy_weights(rest_ref, held, sems, ahead)
     total[...] = jnp.zeros_like(total)
-    lane = 0
-    for copy, buffer in zip(copies, buffers):
-        copy.wait()
-        add_slice(design_ref, buffer, lane, total)
-        lane += buffer.shape[0] * buffer.shape[1]
-    hand_out(total, keep_ref, send_ref)
-
-
-def first_kernel(parts, extra, block_ref, place_ref, *refs):
-    series_refs, (filter_ref, weight_ref), refs = refs[:parts], refs[parts : parts + 2], refs[parts + 2 + extra :]
-    design_ref, keep_ref, send_ref, plain, shifted, total, sems, *buffers = refs
-    copies = weight_copies(weight_ref, buffers, sems, 0, keep_ref.shape[1])
-    total[...] = jnp.zeros_like(total)
-    bases = weight_ref.shape[0]
+    bases, depth, width = weight_ref.shape
     lead = TAP_SPACING * FILTER_TAPS
     for s in range(shifted.shape[0]):
         shifted[s, : lead + 8, :] = jnp.zeros((lead + 8, LANES), jnp.float32)
-    slices = slices_of(weight_ref.shape[1])
-
-    def filters(i):
-        start, _, padded = slices[i]
-        for at in range(0, padded, LANES):
-            lanes = [bases * start + b * padded + at for b in range(bases)]
-            filter_tile(
-                block_ref, place_ref, series_refs, filter_ref, design_ref, plain, shifted, start + at, lanes
-            )
+
+    def filters(start):
+        for at in range(start, min(start + CHAN_SLICE, depth), LANES):
+            lanes = [b * depth + at for b in range(bases)]
+            filter_tile(block_ref, place_ref, series_refs, filter_ref, design_ref, plain, shifted, at, lanes)
 
     filters(0)
-    for i, (copy, buffer) in enumerate(zip(copies, buffers)):
+    for start in range(0, depth, CHAN_SLICE):
+        end = min(start + CHAN_SLICE, depth)
+        for b in range(bases):
+            part = design_ref[:, b * depth + start : b * depth + end]
+            total[...] += jnp.dot(part, weight_ref[b, start:end, :], preferred_element_type=jnp.float32)
+        if end < depth:
+            filters(end)
+    hand_out(total[...], keep_ref, send_ref, slice(0, width))
+    for copy in copies:
         copy.wait()
-        add_slice(design_ref, buffer, bases * slices[i][0], total)
-        if i + 1 < len(copies):
-            filters(i + 1)
-    hand_out(total, keep_ref, send_ref)
-
-
-def product(weights, time_len, first, width, after, design=None, sources=()):
-    bases, depth, _ = weights.shape
-    slices = slices_of(depth)
-    half = jax.ShapeDtypeStruct((time_len // 2, width), jnp.bfloat16)
-    lanes = bases * sum(padded for _, _, padded in slices)
-    scratch = [pltpu.VMEM((time_len, width), jnp.float32), pltpu.SemaphoreType.DMA((len(slices),))]
-    scratch += [pltpu.VMEM((bases, padded, width), jnp.bfloat16) for _, _, padded in slices]
-    flops = 2 * time_len * bases * depth * width
-    common = dict(
-        compiler_params=pltpu.CompilerParams(vmem_limit_bytes=40 * MIB),
-        cost_estimate=pl.CostEstimate(
-            flops=flops, bytes_accessed=2 * bases * depth * width + 2 * time_len * width, transcendentals=0
-        ),
-    )
-    if design is not None:
-        return pl.pallas_call(
-            functools.partial(product_kernel, first, len(after)),
-            in_specs=[VMEM(), ANY()] + [ANY()] * len(after),
-            out_specs=[VMEM(), VMEM()],
-            out_shape=[half, half],
-            scratch_shapes=scratch,
-            name="product",
-            **common,
-        )(design, weights, *after)
-    order, place, series, filters = sources
+
+
+def cost(flops, read):
+    return pl.CostEstimate(flops=flops, bytes_accessed=read, transcendentals=0)
+
+
+def halves(time_len, width):
+    return [jax.ShapeDtypeStruct((time_len // 2, width), jnp.bfloat16)] * 2
+
+
+def first_product(order, place, series, filters, weight, weights, widths, ahead, after):
     parts = len(series)
+    bases, depth, width = weight.shape
+    time_len = parts * series[0].shape[0]
     return pl.pallas_call(
-        functools.partial(first_kernel, parts, len(after)),
-        in_specs=[SMEM(), SMEM()] + [VMEM()] * (parts + 1) + [ANY()] + [ANY()] * len(after),
-        out_specs=[VMEM(), VMEM(), VMEM()],
-        out_shape=[jax.ShapeDtypeStruct((time_len, lanes), jnp.bfloat16), half, half],
+        functools.partial(first_kernel, parts, len(after), ahead),
+        in_specs=[SMEM(), SMEM()] + [VMEM()] * (parts + 2) + [ANY()] * (1 + len(after)),
+        out_specs=[VMEM()] * (3 + len(widths)),
+        out_shape=[jax.ShapeDtypeStruct((time_len, bases * depth), jnp.bfloat16)]
+        + halves(time_len, width)
+        + [pltpu.VMEM((bases, depth, w), jnp.bfloat16) for w in widths],
         scratch_shapes=[
             pltpu.VMEM((time_len, LANES), jnp.float32),
             pltpu.VMEM((8 // TAP_SPACING, time_len + TAP_SPACING * FILTER_TAPS + 8, LANES), jnp.float32),
-        ]
-        + scratch,
+            pltpu.VMEM((time_len, width), jnp.float32),
+            pltpu.SemaphoreType.DMA((len(widths),)),
+        ],
+        compiler_params=pltpu.CompilerParams(vmem_limit_bytes=12 * MIB),
+        cost_estimate=cost(4 * time_len * bases * depth * width, 2 * bases * depth * sum(widths)),
         name="first_product",
-        **common,
-    )(order, place, *series, filters, weights, *after)
+    )(order, place, *series, filters, weight, weights, *after)
+
+
+def product(design, weight, after):
+    time_len, lanes = design.shape
+    width = weight.shape[2]
+    return pl.pallas_call(
+        functools.partial(product_kernel, len(after)),
+        in_specs=[VMEM(), VMEM()] + [ANY()] * len(after),
+        out_specs=[VMEM(), VMEM()],
+        out_shape=halves(time_len, width),
+        compiler_params=pltpu.CompilerParams(vmem_limit_bytes=12 * MIB),
+        cost_estimate=cost(2 * time_len * lanes * width, 2 * lanes * width),
+        name="product",
+    )(design, weight, *after)
 
 
 def pack_kernel(spread, widths, first, more, start_ref, onehot_ref, tile_ref, *refs):
@@ -276,35 +266,38 @@
     table = jnp.pad(parcel_owner, (0, table_rows * LANES - parcel_owner.shape[0])).reshape(table_rows, LANES)
     marks = -(-(blocks + 1) // 8) * 8
     spread = send_cap // SLOT_TILE + 3
-    onehot, tiles, starts = pl.pallas_call(
+    unit = voxels // sum(CHUNK_UNITS)
+    widths = [unit * units for units in CHUNK_UNITS]
+    onehot, tiles, starts, *held = pl.pallas_call(
         functools.partial(places_kernel, owners, spread),
-        in_specs=[VMEM(), VMEM()],
-        out_specs=[VMEM(), VMEM(), VMEM()],
+        in_specs=[VMEM(), VMEM(), ANY()],
+        out_specs=[VMEM()] * (3 + EARLY),
         out_shape=[
             jax.ShapeDtypeStruct((voxels, LANES), jnp.bfloat16),
             jax.ShapeDtypeStruct((voxels // LANES, LANES), jnp.int32),
             jax.ShapeDtypeStruct((marks, LANES), jnp.int32),
-        ],
+        ]
+        + [pltpu.VMEM((bases, depth + spare, width), jnp.bfloat16) for width in widths[:EARLY]],
+        scratch_shapes=[pltpu.SemaphoreType.DMA((EARLY,))],
+        compiler_params=pltpu.CompilerParams(vmem_limit_bytes=8 * MIB),
+        cost_estimate=cost(0, 2 * bases * depth * sum(widths[:EARLY])),
         name="places",
-    )(voxel_parcel.reshape(-1, LANES), table)
+    )(voxel_parcel.reshape(-1, LANES), table, weights)
 
     bits = parts.bit_length() - 1
     order = jnp.arange(parts, dtype=jnp.int32) ^ me
     place = sum(((order >> bit) & 1) << (bits - 1 - bit) for bit in range(bits)).astype(jnp.int32)
 
-    unit = voxels // sum(CHUNK_UNITS)
-    widths = [unit * units for units in CHUNK_UNITS]
     terms, sent, got = [], [], []
-    design, first = None, 0
-    for c, width in enumerate(widths):
+    for c in range(len(widths)):
         if c == 0:
-            design, keep, send = product(
-                weights, time_len, first, width, [starts], sources=(order, place, series, filters)
+            design, keep, send, *rest = first_product(
+                order, place, series, filters, held[0], weights, widths[EARLY:], sum(widths[:EARLY]), [starts]
             )
+            held = held + rest
         else:
             after = sent[max(c - 2, 0) : max(c - 1, 0)] + got[max(c - 3, 0) : max(c - 2, 0)]
-            keep, send = product(weights, time_len, first, width, after, design)
-        first += width
+            keep, send = product(design, held[c], after)
         own = [keep]
         for bit in range(bits):
             if bit > 0:
@@ -327,7 +320,7 @@
                 out_specs=VMEM(),
                 out_shape=jax.ShapeDtypeStruct((owners, time_block, send_cap), jnp.bfloat16),
                 scratch_shapes=[pltpu.VMEM((time_block, sum(here)), jnp.bfloat16)],
-                compiler_params=pltpu.CompilerParams(vmem_limit_bytes=32 * MIB),
+                compiler_params=pltpu.CompilerParams(vmem_limit_bytes=12 * MIB),
                 name="pack",
             )(starts, onehot, tiles, *args)
         ]

time: 99.2 us -> 95.4 us (0.962)
  starting transfers between devices: 12.3 us -> 9.2 us
  waiting for transfers between devices: 4.11 us -> 3.1 us
    pallas_call x1, Pallas kernels: 4.07 us -> 8.79 us  [shards(): pl.pallas_call(functools.partial(places_kernel, owners, spread), in_specs...]
    pallas_call x6 -> x5, Pallas kernels: 27.9 us -> 23.6 us  [the longest x1 14.1 us: first_product(): pl.pallas_call(functools.partial(first_kernel, parts, len(after), ahead),...]
    ppermute x3, waiting for transfers between devices: 3.58 us -> 0.01 us  [shards(): lax.ppermute(series[d], 'chan', [(i, i ^ d) for i in range(parts)])]
    ppermute x12 -> x10, starting transfers between devices: 9.12 us -> 6.04 us  [shards(): lax.ppermute(send, 'chan', [(i, i ^ 1 << bit) for i in range(parts)])]
    ppermute x12 -> x10, waiting for transfers between devices: 0.53 us -> 3.09 us  [shards(): lax.ppermute(send, 'chan', [(i, i ^ 1 << bit) for i in range(parts)])]
  transfers between devices with their start and end apart: 15 -> 13, of which waited for: 2 -> 3; matrix products, arithmetic and copies ran while one was open for 1% -> 1% of each run, Pallas kernels for 31% -> 26%
where the time goes in v4:
time: 95.4 us; the launch traced here: 95.2 us
  Pallas kernels  41.7 us (44%)
  blocking collectives  37.1 us (39%)
  starting transfers between devices  9.2 us (10%)
  local copies, waits for them, and re-layouts  3.72 us (4%)
  waiting for transfers between devices  3.1 us (3%)
    all_to_all x1, blocking collectives, shards(): lax.all_to_all(packed[0], 'vox', split_axis=0, concat_axis=0, tiled=True)  37.1 us
    pallas_call x1, Pallas kernels, first_product(): pl.pallas_call(functools.partial(first_kernel, parts, len(after), ahead),...  14.1 us
    pallas_call x4, Pallas kernels, product(): pl.pallas_call(functools.partial(product_kernel, len(after)), in_specs=[V...  9.46 us
    pallas_call x2, Pallas kernels, shards(): pl.pallas_call(functools.partial(pack_kernel, spread, here, sum(widths[:l...  9.28 us
    pallas_call x1, Pallas kernels, shards(): pl.pallas_call(functools.partial(places_kernel, owners, spread), in_specs...  8.79 us
    ppermute x10, starting transfers between devices, shards(): lax.ppermute(send, 'chan', [(i, i ^ 1 << bit) for i in range(parts)])  6.04 us
    ppermute x3, starting transfers between devices, shards(): lax.ppermute(series[d], 'chan', [(i, i ^ d) for i in range(parts)])  3.16 us
    ppermute x10, waiting for transfers between devices, shards(): lax.ppermute(send, 'chan', [(i, i ^ 1 << bit) for i in range(parts)])  3.09 us
  transfers between devices with their start and end apart: 13, of which 3 were waited for; matrix products, arithmetic and copies ran while one was open for 1% of the time, Pallas kernels for 26%

profile of v4, /device:TPU:0, one launch (start us, length us, event | category | flops | bytes accessed | tf_op | source)
XLA Modules:
  0.0 95.2 jit_solution(16885217787797912740)
XLA Ops:
  0.0 1.2 %constant_dynamic-slice_fusion = (bf16[64,1408]{1,0:T(8,128)(2,1)S(1)}, bf16[64,1408]{1,0:T(8,128)(2,1)S(1)}, bf16[64,1408]{1,0:T(8,128)(2,1)S(1)}, bf16[64,1408]{1,0:T(8,128)(2,1)S(1)}) fusion(bf16[64,5632]{1,0:T(8,128)(2,1)} %param.5, s32[]{:T(128)S(6)} %select_n.15, s32[]{:T(128)S(6)} %select_n.13, s32[]{:T(128)S(6)} %select_n.12, s32[]{:T(128)S(6)} %select_n.14), kind=kLoop, calls=%fused_computation.6 | loop fusion | bytes 1441808 | tf_op jit(solution)/shard_map/dynamic_slice | solution.py:256
  1.2 2.4 %collective-permute-start.2 = (bf16[64,1408]{1,0:T(8,128)(2,1)S(1)}, bf16[64,1408]{1,0:T(8,128)(2,1)S(1)}, u32[]{:S(2)}, u32[]{:S(2)}) collective-permute-start(bf16[64,1408]{1,0:T(8,128)(2,1)S(1)} %get-tuple-element.43), channel_id=1, source_target_pairs={{0,24},{8,16},{16,8},{24,0},{1,25},{9,17},{17,9},{25,1},{2,26},{10... | collective-permute-start | bytes 540680 | tf_op jit(solution)/shard_map/ppermute | solution.py:258
  3.7 0.7 collective-permute-start
  4.4 0.0 collective-permute-start.1
  4.4 0.7 pad_bitcast_fusion.table_ref
  5.1 0.7 copy-done.1
  5.8 8.8 %places.1 = (bf16[5120,128]{1,0:T(8,128)(2,1)S(1)}, s32[40,128]{1,0:T(8,128)S(1)}, s32[24,128]{1,0:T(8,128)S(1)}, bf16[3,1408,1280]{2,1,0:T(8,128)(2,1)S(1)}, bf16[3,1408,1280]{2,1,0:T(8,128)(2,1)S(1)}) custom-call(s32[40,128]{1,0:T(8,128)S(1)} %bitcast.6, s32[7,128]{1,0:T(8,128)S(1)} %pad_bitcast_fusion.table_ref, bf16[3,1408,5120]{2,1,0:T(8,128)(2,1)} %refs_6_.1), custom_call_target="tpu_custom_call" | custom-call | bytes 21626880 | tf_op jit(solution)/shard_map/places/pallas_call | solution.py:271
  14.7 0.0 collective-permute-done.refs_1_
  14.7 0.0 collective-permute-done.1.refs_2_
  14.7 14.1 %first_product.1 = (bf16[256,4224]{1,0:T(8,128)(2,1)S(1)}, bf16[128,1280]{1,0:T(8,128)(2,1)S(1)}, bf16[128,1280]{1,0:T(8,128)(2,1)S(1)}, bf16[3,1408,1024]{2,1,0...) custom-call(s32[4]{0:T(128)S(1)} %get-tuple-element.48.block_ref, ...), custom_call_target="tpu_custom_call" | custom-call | flops 5536481280 | bytes 21626880 | tf_op jit(solution)/shard_map/first_product/pallas_call | solution.py:167
  28.8 0.2 collective-permute-start.3
  29.1 3.0 %product.4 = (bf16[128,1280]{1,0:T(8,128)(2,1)S(1)}, bf16[128,1280]{1,0:T(8,128)(2,1)S(1)}) custom-call(bf16[256,4224]{1,0:T(8,128)(2,1)S(1)} %get-tuple-element.30.design_ref, bf16[3,1408,1280]{2,1,0:T(8,128)(2,1)S(1)} %get-tuple-element.31.weight_ref), custom_call_target="tpu_custom_call" | custom-call | flops 2768240640 | bytes 10813440 | tf_op jit(solution)/shard_map/product/pallas_call | solution.py:189
  32.1 0.4 collective-permute-start.5
  32.6 2.0 %collective-permute-start.4 = (bf16[64,1280]{1,0:T(8,128)(2,1)S(1)}, bf16[64,1280]{1,0:T(8,128)(2,1)S(1)}, u32[]{:S(2)}, u32[]{:S(2)}) collective-permute-start(bf16[64,1280]{1,0:T(8,128)(2,1)S(1)} %add_convert_fusion.1.refs_0_), channel_id=1, source_target_pairs={{0,16},{8,24},{16,0},{24,8},{1,17},{9,25},{17,1},{25,9},{2,18},{10... | collective-permute-start | bytes 491528 | tf_op jit(solution)/shard_map/ppermute | solution.py:308
  34.6 2.7 %product.5 = (bf16[128,1024]{1,0:T(8,128)(2,1)S(1)}, bf16[128,1024]{1,0:T(8,128)(2,1)S(1)}) custom-call(bf16[256,4224]{1,0:T(8,128)(2,1)S(1)} %get-tuple-element.30.design_ref, bf16[3,1408,1024]{2,1,0:T(8,128)(2,1)S(1)} %get-tuple-element.34.weight_ref, bf16[64,1280]{1,0:T(8,128)(2,1)S(1)} %add_convert_fusion.1.refs_0_), custom_call_target="tpu_custom_call" | custom-call | flops 2214592512 | bytes 8650752 | tf_op jit(solution)/shard_map/product/pallas_call | solution.py:189
  37.3 0.1 collective-permute-start.7
  37.4 0.1 collective-permute-start.6
  37.5 1.5 %collective-permute-done.4.refs_2_.refs_1_ = bf16[64,1280]{1,0:T(8,128)(2,1)S(1)} collective-permute-done((bf16[64,1280]{1,0:T(8,128)(2,1)S(1)}, bf16[64,1280]{1,0:T(8,128)(2,1)S(1)}, u32[]{:S(2)}, u32[]{:S(2)}) %collective-permute-start.4) | collective-permute-done | bytes 163872 | tf_op jit(solution)/shard_map/ppermute | solution.py:308
  39.0 2.5 %product.6 = (bf16[128,1024]{1,0:T(8,128)(2,1)S(1)}, bf16[128,1024]{1,0:T(8,128)(2,1)S(1)}) custom-call(bf16[256,4224]{1,0:T(8,128)(2,1)S(1)} %get-tuple-element.30.design_ref, bf16[3,1408,1024]{2,1,0:T(8,128)(2,1)S(1)} %get-tuple-element.37.weight_ref, bf16[64,1280]{1,0:T(8,128)(2,1)S(1)} %add_convert_fusion.refs_0_, ...), custom_call_target="tpu_custom_call" | custom-call | flops 2214592512 | bytes 8650752 | tf_op jit(solution)/shard_map/product/pallas_call | solution.py:189
  41.5 0.1 collective-permute-start.9
  41.5 0.0 collective-permute-done.7.refs_7_
  41.6 1.8 %collective-permute-start.8 = (bf16[64,1024]{1,0:T(8,128)(2,1)S(1)}, bf16[64,1024]{1,0:T(8,128)(2,1)S(1)}, u32[]{:S(2)}, u32[]{:S(2)}) collective-permute-start(bf16[64,1024]{1,0:T(8,128)(2,1)S(1)} %add_convert_fusion.3.refs_0_), channel_id=1, source_target_pairs={{0,16},{8,24},{16,0},{24,8},{1,17},{9,25},{17,1},{25,9},{2,18},{10... | collective-permute-start | bytes 393224 | tf_op jit(solution)/shard_map/ppermute | solution.py:308
  43.4 0.7 collective-permute-done.6.refs_5_.refs_1_
  44.1 1.3 %product.7 = (bf16[128,512]{1,0:T(8,128)(2,1)S(1)}, bf16[128,512]{1,0:T(8,128)(2,1)S(1)}) custom-call(bf16[256,4224]{1,0:T(8,128)(2,1)S(1)} %get-tuple-element.30.design_ref, bf16[3,1408,512]{2,1,0:T(8,128)(2,1)S(1)} %get-tuple-element.40.weight_ref, bf16[64,1024]{1,0:T(8,128)(2,1)S(1)} %add_convert_fusion.3.refs_0_, ...), custom_call_target="tpu_custom_call" | custom-call | flops 1107296256 | bytes 4325376 | tf_op jit(solution)/shard_map/product/pallas_call | solution.py:189
  45.4 0.1 collective-permute-start.11
  45.5 0.4 collective-permute-start.10
  45.9 0.9 collective-permute-done.11.refs_5_
  46.8 0.9 collective-permute-start.12
  47.7 6.2 %pack.2.refs_0_ = bf16[8,64,1280]{2,1,0:T(8,128)(2,1)S(1)} custom-call(s32[24,128]{1,0:T(8,128)S(1)} %get-tuple-element.24.refs_7_.start_ref, bf16[5120,128]{1,0:T(8,128)(2,1)S(1)} %get-tuple-element.25.onehot_ref, s32[40,128]{1,0:T(8,128)S(1)} %get-tuple-element.26.tile_ref, bf16[128,1280]{1,0:T(8,128)(2,1)S(1)} %get-tuple-element.28.refs_0_, ...), custom_call_target="tpu_custom_call" | custom-call | tf_op jit(solution)/shard_map/pack/pallas_call | solution.py:317
  53.9 3.1 %pack.3 = bf16[8,64,1280]{2,1,0:T(8,128)(2,1)S(1)} custom-call(s32[24,128]{1,0:T(8,128)S(1)} %get-tuple-element.24.refs_7_.start_ref, bf16[5120,128]{1,0:T(8,128)(2,1)S(1)} %get-tuple-element.25.onehot_ref, s32[40,128]{1,0:T(8,128)S(1)} %get-tuple-element.26.tile_ref, bf16[8,64,1280]{2,1,0:T(8,128)(2,1)S(1)} %pack.2.refs_0_, ...), custom_call_target="tpu_custom_call" | custom-call | tf_op jit(solution)/shard_map/pack/pallas_call | solution.py:317
  57.0 37.1 %all_to_all.5 = bf16[8,64,1280]{2,1,0:T(8,128)(2,1)S(1)} all-to-all(bf16[8,64,1280]{2,1,0:T(8,128)(2,1)S(1)} %pack.3), channel_id=1, replica_groups=mesh['chan'=4,'vox'=8] {'vox'}, dimensions={0} | all-to-all | bytes 2621440 | tf_op jit(solution)/shard_map/all_to_all | solution.py:327
  94.1 1.1 %copy.7 = bf16[8,1280,64]{1,2,0:T(8,128)(2,1)} copy(bf16[8,1280,64]{1,2,0:T(8,128)(2,1)S(1)} %bitcast.7) | data formatting | bytes 2621440
  (16 shorter events, 0.2 us)
Async XLA Ops:
  1.2 13.4 %collective-permute-start.2 = (bf16[64,1408]{1,0:T(8,128)(2,1)S(1)}, bf16[64,1408]{1,0:T(8,128)(2,1)S(1)}, u32[]{:S(2)}, u32[]{:S(2)}) collective-permute-start(bf16[64,1408]{1,0:T(8,128)(2,1)S(1)} %get-tuple-element.43), channel_id=1, source_target_pairs={{0,24},{8,16},{16,8},{24,0},{1,25},{9,17},{17,9},{25,1},{2,26},{10... | collective-permute-start | bytes 540680 | tf_op jit(solution)/shard_map/ppermute | solution.py:258
  3.7 11.0 %collective-permute-start = (bf16[64,1408]{1,0:T(8,128)(2,1)S(1)}, bf16[64,1408]{1,0:T(8,128)(2,1)S(1)}, u32[]{:S(2)}, u32[]{:S(2)}) collective-permute-start(bf16[64,1408]{1,0:T(8,128)(2,1)S(1)} %get-tuple-element.44), channel_id=1, source_target_pairs={{0,8},{8,0},{16,24},{24,16},{1,9},{9,1},{17,25},{25,17},{2,10},{10... | collective-permute-start | bytes 540680 | tf_op jit(solution)/shard_map/ppermute | solution.py:258
  4.4 10.3 %collective-permute-start.1 = (bf16[64,1408]{1,0:T(8,128)(2,1)S(1)}, bf16[64,1408]{1,0:T(8,128)(2,1)S(1)}, u32[]{:S(2)}, u32[]{:S(2)}) collective-permute-start(bf16[64,1408]{1,0:T(8,128)(2,1)S(1)} %get-tuple-element.46), channel_id=1, source_target_pairs={{0,16},{8,24},{16,0},{24,8},{1,17},{9,25},{17,1},{25,9},{2,18},{10... | collective-permute-start | bytes 540680 | tf_op jit(solution)/shard_map/ppermute | solution.py:258
  5.1 0.7 copy-start.1
  5.8 8.9 %copy-start = (f32[3,1408,16]{1,2,0:T(8,128)S(1)}, f32[3,1408,16]{1,2,0:T(8,128)}, u32[]{:S(2)}) copy-start(f32[3,1408,16]{1,2,0:T(8,128)} %param.6) | copy-start | bytes 811012
  28.8 3.7 %collective-permute-start.3 = (bf16[128,1280]{1,0:T(8,128)(2,1)S(1)}, bf16[128,1280]{1,0:T(8,128)(2,1)S(1)}, u32[]{:S(2)}, u32[]{:S(2)}) collective-permute-start(bf16[128,1280]{1,0:T(8,128)(2,1)S(1)} %get-tuple-element.29), channel_id=1, source_target_pairs={{0,8},{8,0},{16,24},{24,16},{1,9},{9,1},{17,25},{25,17},{2,10},{10... | collective-permute-start | bytes 983048 | tf_op jit(solution)/shard_map/ppermute | solution.py:308
  32.1 5.2 %collective-permute-start.5 = (bf16[128,1280]{1,0:T(8,128)(2,1)S(1)}, bf16[128,1280]{1,0:T(8,128)(2,1)S(1)}, u32[]{:S(2)}, u32[]{:S(2)}) collective-permute-start(bf16[128,1280]{1,0:T(8,128)(2,1)S(1)} %get-tuple-element.33), channel_id=1, source_target_pairs={{0,8},{8,0},{16,24},{24,16},{1,9},{9,1},{17,25},{25,17},{2,10},{10... | collective-permute-start | bytes 983048 | tf_op jit(solution)/shard_map/ppermute | solution.py:308
  32.6 6.4 %collective-permute-start.4 = (bf16[64,1280]{1,0:T(8,128)(2,1)S(1)}, bf16[64,1280]{1,0:T(8,128)(2,1)S(1)}, u32[]{:S(2)}, u32[]{:S(2)}) collective-permute-start(bf16[64,1280]{1,0:T(8,128)(2,1)S(1)} %add_convert_fusion.1.refs_0_), channel_id=1, source_target_pairs={{0,16},{8,24},{16,0},{24,8},{1,17},{9,25},{17,1},{25,9},{2,18},{10... | collective-permute-start | bytes 491528 | tf_op jit(solution)/shard_map/ppermute | solution.py:308
  37.3 4.3 %collective-permute-start.7 = (bf16[128,1024]{1,0:T(8,128)(2,1)S(1)}, bf16[128,1024]{1,0:T(8,128)(2,1)S(1)}, u32[]{:S(2)}, u32[]{:S(2)}) collective-permute-start(bf16[128,1024]{1,0:T(8,128)(2,1)S(1)} %get-tuple-element.36), channel_id=1, source_target_pairs={{0,8},{8,0},{16,24},{24,16},{1,9},{9,1},{17,25},{25,17},{2,10},{10... | collective-permute-start | bytes 786440 | tf_op jit(solution)/shard_map/ppermute | solution.py:308
  37.4 6.7 %collective-permute-start.6 = (bf16[64,1280]{1,0:T(8,128)(2,1)S(1)}, bf16[64,1280]{1,0:T(8,128)(2,1)S(1)}, u32[]{:S(2)}, u32[]{:S(2)}) collective-permute-start(bf16[64,1280]{1,0:T(8,128)(2,1)S(1)} %add_convert_fusion.refs_0_), channel_id=1, source_target_pairs={{0,16},{8,24},{16,0},{24,8},{1,17},{9,25},{17,1},{25,9},{2,18},{10... | collective-permute-start | bytes 491528 | tf_op jit(solution)/shard_map/ppermute | solution.py:308
  41.5 4.0 %collective-permute-start.9 = (bf16[128,1024]{1,0:T(8,128)(2,1)S(1)}, bf16[128,1024]{1,0:T(8,128)(2,1)S(1)}, u32[]{:S(2)}, u32[]{:S(2)}) collective-permute-start(bf16[128,1024]{1,0:T(8,128)(2,1)S(1)} %get-tuple-element.39), channel_id=1, source_target_pairs={{0,8},{8,0},{16,24},{24,16},{1,9},{9,1},{17,25},{25,17},{2,10},{10... | collective-permute-start | bytes 786440 | tf_op jit(solution)/shard_map/ppermute | solution.py:308
  41.6 6.1 %collective-permute-start.8 = (bf16[64,1024]{1,0:T(8,128)(2,1)S(1)}, bf16[64,1024]{1,0:T(8,128)(2,1)S(1)}, u32[]{:S(2)}, u32[]{:S(2)}) collective-permute-start(bf16[64,1024]{1,0:T(8,128)(2,1)S(1)} %add_convert_fusion.3.refs_0_), channel_id=1, source_target_pairs={{0,16},{8,24},{16,0},{24,8},{1,17},{9,25},{17,1},{25,9},{2,18},{10... | collective-permute-start | bytes 393224 | tf_op jit(solution)/shard_map/ppermute | solution.py:308
  45.4 1.4 %collective-permute-start.11 = (bf16[128,512]{1,0:T(8,128)(2,1)S(1)}, bf16[128,512]{1,0:T(8,128)(2,1)S(1)}, u32[]{:S(2)}, u32[]{:S(2)}) collective-permute-start(bf16[128,512]{1,0:T(8,128)(2,1)S(1)} %get-tuple-element.42), channel_id=1, source_target_pairs={{0,8},{8,0},{16,24},{24,16},{1,9},{9,1},{17,25},{25,17},{2,10},{10... | collective-permute-start | bytes 393224 | tf_op jit(solution)/shard_map/ppermute | solution.py:308
  45.5 8.4 %collective-permute-start.10 = (bf16[64,1024]{1,0:T(8,128)(2,1)S(1)}, bf16[64,1024]{1,0:T(8,128)(2,1)S(1)}, u32[]{:S(2)}, u32[]{:S(2)}) collective-permute-start(bf16[64,1024]{1,0:T(8,128)(2,1)S(1)} %add_convert_fusion.2), channel_id=1, source_target_pairs={{0,16},{8,24},{16,0},{24,8},{1,17},{9,25},{17,1},{25,9},{2,18},{10... | collective-permute-start | bytes 393224 | tf_op jit(solution)/shard_map/ppermute | solution.py:308
  46.8 7.1 %collective-permute-start.12 = (bf16[64,512]{1,0:T(8,128)(2,1)S(1)}, bf16[64,512]{1,0:T(8,128)(2,1)S(1)}, u32[]{:S(2)}, u32[]{:S(2)}) collective-permute-start(bf16[64,512]{1,0:T(8,128)(2,1)S(1)} %add_convert_fusion.4), channel_id=1, source_target_pairs={{0,16},{8,24},{16,0},{24,8},{1,17},{9,25},{17,1},{25,9},{2,18},{10... | collective-permute-start | bytes 196616 | tf_op jit(solution)/shard_map/ppermute | solution.py:308

commit v5 on v4

v5 whole, which is shorter than its diff:
```python
import functools

import jax
import jax.numpy as jnp
from jax import lax
from jax.experimental import pallas as pl
from jax.experimental.pallas import tpu as pltpu
from jax.sharding import PartitionSpec as P

FILTER_TAPS = 16
TAP_SPACING = 2
LANES = 128
SLOT_TILE = 128
VOX_BLOCK = 256
COLUMNS = 512
ROWS = 32
PIECE_UNITS = (9, 4, 1, 3, 3)
CHUNK_PARTS = (
    ((0, 0, 2),),
    ((0, 2, 6),),
    ((0, 6, 9), (1, 0, 2)),
    ((1, 2, 4), (2, 0, 1), (3, 0, 2)),
    ((3, 2, 3), (4, 0, 3)),
)
PACK_FIRST = 3
MIB = 1 << 20

VMEM = functools.partial(pl.BlockSpec, memory_space=pltpu.VMEM)
SMEM = functools.partial(pl.BlockSpec, memory_space=pltpu.SMEM)
ANY = functools.partial(pl.BlockSpec, memory_space=pl.ANY)


def copy_piece(weight_ref, piece_ref, sem, first):
    depth = weight_ref.shape[1]
    if piece_ref.shape[1] > depth:
        piece_ref[:, depth:, :] = jnp.zeros_like(piece_ref[:, depth:, :])
    copy = pltpu.make_async_copy(
        weight_ref.at[:, :, pl.ds(first, piece_ref.shape[2])], piece_ref.at[:, pl.ds(0, depth), :], sem
    )
    copy.start()
    return copy


def cost(flops, read):
    return pl.CostEstimate(flops=flops, bytes_accessed=read, transcendentals=0)


def places(owners, spread, parcel_ref, table_ref, onehot_ref, tile_ref, start_ref):
    rows = parcel_ref.shape[0]
    parcel = parcel_ref[...]
    high, low = parcel >> 7, parcel & 127
    owner = jnp.zeros_like(parcel)
    for entry in range(table_ref.shape[0]):
        line = jnp.broadcast_to(table_ref[entry : entry + 1, :], parcel.shape)
        found = jnp.take_along_axis(line, low, axis=1, mode="promise_in_bounds")
        owner = jnp.where(high == entry, found, owner)

    def below(shape, scale=1):
        less = lax.broadcasted_iota(jnp.int32, shape, 1) < scale * lax.broadcasted_iota(jnp.int32, shape, 0)
        return less.astype(jnp.float32).astype(jnp.bfloat16)

    lane = lax.broadcasted_iota(jnp.int32, (LANES, LANES), 1)
    above = (lax.broadcasted_iota(jnp.int32, (LANES, LANES), 0) < lane).astype(jnp.float32).astype(jnp.bfloat16)
    ones = jnp.ones((LANES, LANES), jnp.bfloat16)
    marks = start_ref.shape[0]
    ahead, block_ahead = below((rows, rows)), below((marks, rows), VOX_BLOCK // LANES)
    mark_lane = lax.broadcasted_iota(jnp.int32, (marks, LANES), 1)
    dot = functools.partial(jnp.dot, preferred_element_type=jnp.float32)
    slots = jnp.zeros(parcel.shape, jnp.float32)
    starts = jnp.zeros((marks, LANES), jnp.float32)
    for o in range(owners):
        mine = owner == o
        hot = mine.astype(jnp.float32).astype(jnp.bfloat16)
        totals = dot(hot, ones).astype(jnp.bfloat16)
        slots = jnp.where(mine, dot(hot, above) + dot(ahead, totals), slots)
        starts = jnp.where(mark_lane == o, dot(block_ahead, totals), starts)
    slots = slots.astype(jnp.int32)
    start_ref[...] = starts.astype(jnp.int32)
    tile_ref[...] = owner * spread + (slots >> 7)
    inner = slots & 127
    for row in range(rows):
        line = jnp.broadcast_to(inner[row : row + 1, :], (LANES, LANES))
        hit = jnp.where(line.T == lane, 1.0, 0.0)
        onehot_ref[row * LANES : (row + 1) * LANES, :] = hit.astype(jnp.bfloat16)


def clear_lead(shifted):
    lead = TAP_SPACING * FILTER_TAPS
    for s in range(shifted.shape[0]):
        shifted[s, : lead + 8, :] = jnp.zeros((lead + 8, LANES), jnp.float32)


def shift(plain, shifted):
    lead, time_len = TAP_SPACING * FILTER_TAPS, plain.shape[0]
    series = plain[...]
    for s in range(shifted.shape[0]):
        shifted[s, lead + s * TAP_SPACING : lead + s * TAP_SPACING + time_len, :] = series


def filter_rows(shifted, filter_ref, column, first):
    lead = TAP_SPACING * FILTER_TAPS
    sums = [jnp.zeros((ROWS, LANES), jnp.float32) for _ in range(filter_ref.shape[0])]
    for tap in range(FILTER_TAPS):
        delay = tap * TAP_SPACING
        start = lead + first - 8 * (delay // 8)
        if not isinstance(start, int):
            start = pl.multiple_of(start, 8)
        lagged = shifted[(delay % 8) // TAP_SPACING, pl.ds(start, ROWS), :]
        for b in range(len(sums)):
            sums[b] = sums[b] + filter_ref[b, tap : tap + 1, column] * lagged
    return sums


def lane_tile(tile):
    return pl.ds(pl.multiple_of(tile * LANES, LANES), LANES)


def early_kernel(owners, spread, order_ref, own_ref, pair_ref, parcel_ref, table_ref, filter_ref, weight_ref, *refs):
    onehot_ref, tile_ref, start_ref, design_ref, piece_ref, plain, shifted, sems = refs
    copy = copy_piece(weight_ref, piece_ref, sems.at[0], 0)
    block, width = own_ref.shape
    core = lax.rem(order_ref[0], 2)
    own = pl.ds(pl.multiple_of(core * block, block), block)
    pair = pl.ds(pl.multiple_of((1 - core) * block, block), block)
    clear_lead(shifted)

    def columns(tile, carry):
        column = lane_tile(tile)
        plain[own, :] = own_ref[:, column].astype(jnp.float32)
        plain[pair, :] = pair_ref[:, column].astype(jnp.float32)
        shift(plain, shifted)
        for first in range(ROWS, 2 * block, ROWS):
            for b, rows in enumerate(filter_rows(shifted, filter_ref, column, first)):
                lanes = pl.ds(pl.multiple_of(b * width + tile * LANES, LANES), LANES)
                design_ref[first - ROWS : first, lanes] = rows.astype(jnp.bfloat16)
        return carry

    lax.fori_loop(0, width // LANES, columns, 0)
    places(owners, spread, parcel_ref, table_ref, onehot_ref, tile_ref, start_ref)
    copy.wait()


def design_kernel(parts, first, order_ref, place_ref, early_ref, filter_ref, weight_ref, *refs):
    series_refs, (design_ref, piece_ref, plain, shifted, sems) = refs[:parts], refs[parts:]
    copy = copy_piece(weight_ref, piece_ref, sems.at[0], first)
    block, width = series_refs[0].shape
    chip = order_ref[0] >> 1
    clear_lead(shifted)

    def place(part, inner):
        return pl.ds(pl.multiple_of(place_ref[part] * block + inner, ROWS), ROWS)

    for first in range(ROWS, 2 * block, ROWS):
        row = place(2 * chip + first // block, first % block)
        design_ref[row, :] = early_ref[first - ROWS : first, :]

    def columns(tile, carry):
        column = lane_tile(tile)
        for d in range(parts):
            row = pl.ds(pl.multiple_of(order_ref[d] * block, block), block)
            plain[row, :] = series_refs[d][:, column].astype(jnp.float32)
        shift(plain, shifted)
        for other in range(parts // 2):
            for inner in range(0, 2 * block if other else ROWS, ROWS):
                part = 2 * (chip ^ other) + inner // block
                start = part * block + inner % block
                row = place(part, inner % block)
                for b, rows in enumerate(filter_rows(shifted, filter_ref, column, start)):
                    lanes = pl.ds(pl.multiple_of(b * width + tile * LANES, LANES), LANES)
                    design_ref[row, lanes] = rows.astype(jnp.bfloat16)
        return carry

    lax.fori_loop(0, width // LANES, columns, 0)
    copy.wait()


def filter_scratch(time_len):
    return [
        pltpu.VMEM((time_len, LANES), jnp.float32),
        pltpu.VMEM((8 // TAP_SPACING, time_len + TAP_SPACING * FILTER_TAPS + 8, LANES), jnp.float32),
    ]


def product_kernel(extra, bounds, first, design_ref, *refs):
    weight_refs, refs = refs[: len(bounds)], refs[len(bounds) + extra :]
    copy = None
    if first is not None:
        weight_ref, keep_ref, send_ref, piece_ref, sems = refs
        copy = copy_piece(weight_ref, piece_ref, sems.at[0], first)
    else:
        keep_ref, send_ref = refs
    half, at = keep_ref.shape[0], 0
    for ref, (low, high) in zip(weight_refs, bounds):
        for start in range(low, high, COLUMNS):
            weight = ref[:, :, start : min(start + COLUMNS, high)]
            weight = weight.reshape(-1, weight.shape[2])
            total = jnp.dot(design_ref[...], weight, preferred_element_type=jnp.float32)
            columns = slice(at, at + weight.shape[1])
            keep_ref[:, columns] = total[:half].astype(jnp.bfloat16)
            send_ref[:, columns] = total[half:].astype(jnp.bfloat16)
            at += weight.shape[1]
    if copy is not None:
        copy.wait()


def product(design, parts, after, weights, ahead):
    time_len, lanes = design.shape
    bounds = tuple((low, high) for _, low, high in parts)
    width = sum(high - low for low, high in bounds)
    half = jax.ShapeDtypeStruct((time_len // 2, width), jnp.bfloat16)
    held = parts[0][0].shape
    more = [ahead] if ahead else []
    return pl.pallas_call(
        functools.partial(product_kernel, len(after), bounds, ahead[0] if ahead else None),
        in_specs=[VMEM()] * (1 + len(parts)) + [ANY()] * (len(after) + len(more)),
        out_specs=[VMEM()] * (2 + len(more)),
        out_shape=[half, half] + [pltpu.VMEM((*held[:2], size), jnp.bfloat16) for _, size in more],
        scratch_shapes=[pltpu.SemaphoreType.DMA((1,)) for _ in more],
        compiler_params=pltpu.CompilerParams(vmem_limit_bytes=10 * MIB),
        cost_estimate=cost(2 * time_len * lanes * width, 2 * lanes * width),
        name="product",
    )(design, *(piece for piece, _, _ in parts), *after, *([weights] if ahead else []))


def pack_kernel(spread, widths, first, more, start_ref, onehot_ref, tile_ref, *refs):
    *terms, packed_ref, summed = refs
    if more:
        packed_ref[...] = terms.pop(0)[...]
    else:
        packed_ref[...] = jnp.zeros_like(packed_ref)
    owners, time_block, send_cap = packed_ref.shape
    each, at = len(terms) // len(widths), 0
    for c, width in enumerate(widths):
        total = sum(term[:time_block, :].astype(jnp.float32) for term in terms[c * each : (c + 1) * each])
        summed[:, at : at + width] = total.astype(jnp.bfloat16)
        at += width
    last_tile = send_cap // SLOT_TILE - 1
    step = VOX_BLOCK // LANES

    def block_step(index, carry):
        block = first + index
        values = summed[:, pl.ds(pl.multiple_of(index * VOX_BLOCK, VOX_BLOCK), VOX_BLOCK)]
        onehot = onehot_ref[pl.ds(pl.multiple_of(block * VOX_BLOCK, VOX_BLOCK), VOX_BLOCK), :]
        tiles = jnp.concatenate([tile_ref[pl.ds(block * step + i, 1), :] for i in range(step)], axis=1)

        def chosen(owner, tile):
            hit = jnp.where(tiles == owner * spread + tile, 1.0, 0.0)
            return values * hit.astype(jnp.bfloat16)

        def put(owner, tile, moved):
            tile = jnp.minimum(tile, last_tile)
            at = pl.ds(pl.multiple_of(tile * SLOT_TILE, SLOT_TILE), SLOT_TILE)
            packed_ref[owner, :, at] = packed_ref[owner, :, at] + moved

        def move(targets):
            rows = jnp.concatenate([chosen(owner, tile) for owner, tile in targets], axis=0)
            moved = jnp.dot(rows, onehot, preferred_element_type=jnp.float32).astype(jnp.bfloat16)
            for i, (owner, tile) in enumerate(targets):
                put(owner, tile, moved[i * time_block : (i + 1) * time_block])

        low = [start_ref[block, o] >> 7 for o in range(owners)]
        high = [(start_ref[block + 1, o] - 1) >> 7 for o in range(owners)]
        move([(o, low[o] + extra) for extra in range(2) for o in range(owners)])
        longest = functools.reduce(jnp.maximum, [high[o] - low[o] for o in range(owners)])

        @pl.when(longest > 1)
        def _():
            move([(o, low[o] + 2) for o in range(owners)])

        return carry

    lax.fori_loop(0, sum(widths) // VOX_BLOCK, block_step, 0)


def shards(features, hrf_filters, weights, voxel_parcel, parcel_owner):
    owners, parts = lax.axis_size("vox"), lax.axis_size("chan")
    me = lax.axis_index("chan")
    voxels = voxel_parcel.shape[0]
    send_cap = 2 * voxels // owners
    bases, depth, _ = weights.shape
    blocks = voxels // VOX_BLOCK
    time_block = features.shape[0]
    time_len = time_block * parts

    series = [lax.dynamic_slice_in_dim(features, (me ^ d) * depth, depth, 1) for d in range(parts)]
    for d in range(1, parts):
        series[d] = lax.ppermute(series[d], "chan", [(i, i ^ d) for i in range(parts)])
    filters = jnp.transpose(hrf_filters, (0, 2, 1))
    unit = voxels // sum(PIECE_UNITS)
    pieces = [unit * units for units in PIECE_UNITS]
    firsts = [sum(pieces[:i]) for i in range(len(pieces))]
    spare = -depth % LANES
    held = lambda i: pltpu.VMEM((bases, depth + spare, pieces[i]), jnp.bfloat16)
    lanes = bases * (depth + spare)
    if spare:
        series = [jnp.pad(part, ((0, 0), (0, spare))) for part in series]
        filters = jnp.pad(filters, ((0, 0), (0, 0), (0, spare)))

    table_rows = -(-parcel_owner.shape[0] // LANES)
    table = jnp.pad(parcel_owner, (0, table_rows * LANES - parcel_owner.shape[0])).reshape(table_rows, LANES)
    marks = -(-(blocks + 1) // 8) * 8
    spread = send_cap // SLOT_TILE + 3
    bits = parts.bit_length() - 1
    order = jnp.arange(parts, dtype=jnp.int32) ^ me
    place = sum(((order >> bit) & 1) << (bits - 1 - bit) for bit in range(bits)).astype(jnp.int32)

    early_rows = 2 * time_block - ROWS
    onehot, tiles, starts, early, piece = pl.pallas_call(
        functools.partial(early_kernel, owners, spread),
        in_specs=[SMEM()] + [VMEM()] * 5 + [ANY()],
        out_specs=[VMEM()] * 5,
        out_shape=[
            jax.ShapeDtypeStruct((voxels, LANES), jnp.bfloat16),
            jax.ShapeDtypeStruct((voxels // LANES, LANES), jnp.int32),
            jax.ShapeDtypeStruct((marks, LANES), jnp.int32),
            jax.ShapeDtypeStruct((early_rows, lanes), jnp.bfloat16),
            held(0),
        ],
        scratch_shapes=filter_scratch(2 * time_block) + [pltpu.SemaphoreType.DMA((1,))],
        compiler_params=pltpu.CompilerParams(vmem_limit_bytes=10 * MIB),
        cost_estimate=cost(0, 2 * bases * depth * pieces[0]),
        name="early",
    )(order, series[0], series[1], voxel_parcel.reshape(-1, LANES), table, filters, weights)
    copied = [piece]
    design, piece = pl.pallas_call(
        functools.partial(design_kernel, parts, firsts[1]),
        in_specs=[SMEM(), SMEM(), VMEM(), VMEM(), ANY()] + [VMEM()] * parts,
        out_specs=[VMEM(), VMEM()],
        out_shape=[jax.ShapeDtypeStruct((time_len, lanes), jnp.bfloat16), held(1)],
        scratch_shapes=filter_scratch(time_len) + [pltpu.SemaphoreType.DMA((1,))],
        compiler_params=pltpu.CompilerParams(vmem_limit_bytes=10 * MIB),
        cost_estimate=cost(0, 2 * bases * depth * pieces[1]),
        name="design",
    )(order, place, early, filters, weights, *series)
    copied.append(piece)

    widths, terms, sent, got = [], [], [], []
    for c, chunk in enumerate(CHUNK_PARTS):
        takes = [(copied[i], unit * low, unit * high) for i, low, high in chunk]
        widths.append(sum(high - low for _, low, high in takes))
        after = sent[max(c - 2, 0) : max(c - 1, 0)] + got[max(c - 3, 0) : max(c - 2, 0)]
        more = len(copied) < len(pieces)
        ahead = (firsts[len(copied)], pieces[len(copied)]) if more else None
        keep, send, *piece = product(design, takes, after, weights, ahead)
        copied.extend(piece)
        own = [keep]
        for bit in range(bits):
            if bit > 0:
                rows = own[-1].shape[0] // 2
                send = sum(term[rows : 2 * rows].astype(jnp.float32) for term in own).astype(jnp.bfloat16)
                if bit == 1:
                    sent.append(send)
            own.append(lax.ppermute(send, "chan", [(i, i ^ (1 << bit)) for i in range(parts)]))
        terms.append(own)
        got.append(own[-1])

    packed = []
    for low, high in ((0, PACK_FIRST), (PACK_FIRST, len(widths))):
        args = packed + [term for own in terms[low:high] for term in own]
        here = widths[low:high]
        packed = [
            pl.pallas_call(
                functools.partial(pack_kernel, spread, here, sum(widths[:low]) // VOX_BLOCK, len(packed)),
                in_specs=[SMEM(), VMEM(), VMEM()] + [VMEM()] * len(args),
                out_specs=VMEM(),
                out_shape=jax.ShapeDtypeStruct((owners, time_block, send_cap), jnp.bfloat16),
                scratch_shapes=[pltpu.VMEM((time_block, sum(here)), jnp.bfloat16)],
                compiler_params=pltpu.CompilerParams(vmem_limit_bytes=12 * MIB),
                name="pack",
            )(starts, onehot, tiles, *args)
        ]
    received = lax.all_to_all(packed[0], "vox", split_axis=0, concat_axis=0, tiled=True)
    return jnp.transpose(received, (0, 2, 1))


def solution(mesh):
    return jax.shard_map(
        shards,
        mesh=mesh,
        in_specs=(P("chan", None), P(None, "chan", None), P(None, "chan", "vox"), P("vox"), P()),
        out_specs=P("vox", None, "chan"),
        check_vma=False,
    )
```

time: 95.4 us -> 110 us (1.15)
  local copies, waits for them, and re-layouts: 3.72 us -> 14.7 us
  Pallas kernels: 41.7 us -> 44.5 us
    unnamed x5 -> x15, local copies, waits for them, and re-layouts: 1.79 us -> 12.8 us
    pallas_call x6 -> x7, Pallas kernels: 32.4 us -> 35.5 us  [the longest x5 18.1 us: product(): pl.pallas_call(functools.partial(product_kernel, len(after), bounds, ahea...]
  transfers between devices with their start and end apart: 13 -> 13, of which waited for: 3 -> 4; matrix products, arithmetic and copies ran while one was open for 1% -> 1% of each run, Pallas kernels for 26% -> 23%
where the time goes in v5:
time: 110 us
  Pallas kernels  44.5 us (40%)
  blocking collectives  36.9 us (34%)
  local copies, waits for them, and re-layouts  14.7 us (13%)
  starting transfers between devices  9.24 us (8%)
  waiting for transfers between devices  4.13 us (4%)
    all_to_all x1, blocking collectives, shards(): lax.all_to_all(packed[0], 'vox', split_axis=0, concat_axis=0, tiled=True)  36.9 us
    pallas_call x5, Pallas kernels, product(): pl.pallas_call(functools.partial(product_kernel, len(after), bounds, ahea...  18.1 us
    unnamed x15, local copies, waits for them, and re-layouts  12.8 us
    pallas_call x1, Pallas kernels, shards(): pl.pallas_call(functools.partial(design_kernel, parts, firsts[1]), in_spe...  10.3 us
    pallas_call x2, Pallas kernels, shards(): pl.pallas_call(functools.partial(pack_kernel, spread, here, sum(widths[:l...  9.06 us
    pallas_call x1, Pallas kernels, shards(): pl.pallas_call(functools.partial(early_kernel, owners, spread), in_specs=...  7.11 us
    ppermute x10, starting transfers between devices, shards(): lax.ppermute(send, 'chan', [(i, i ^ 1 << bit) for i in range(parts)])  6.08 us
    ppermute x10, waiting for transfers between devices, shards(): lax.ppermute(send, 'chan', [(i, i ^ 1 << bit) for i in range(parts)])  3.81 us
  transfers between devices with their start and end apart: 13, of which 4 were waited for; matrix products, arithmetic and copies ran while one was open for 1% of the time, Pallas kernels for 23%

profile of v5, /device:TPU:0, one launch (start us, length us, event | category | flops | bytes accessed | tf_op | source)
XLA Modules:
  0.0 109.9 jit_solution(7526953567574053297)
XLA Ops:
  0.0 1.2 %constant_dynamic-slice_fusion = (bf16[64,1408]{1,0:T(8,128)(2,1)S(1)}, bf16[64,1408]{1,0:T(8,128)(2,1)S(1)}, bf16[64,1408]{1,0:T(8,128)(2,1)S(1)}, bf16[64,1408]{1,0:T(8,128)(2,1)S(1)}) fusion(bf16[64,5632]{1,0:T(8,128)(2,1)} %param.5, s32[]{:T(128)S(6)} %select_n.15, s32[]{:T(128)S(6)} %select_n.13, s32[]{:T(128)S(6)} %select_n.12, s32[]{:T(128)S(6)} %select_n.14), kind=kLoop, calls=%fused_computation.6 | loop fusion | bytes 1441808 | tf_op jit(solution)/shard_map/dynamic_slice | solution.py:285
  1.2 2.4 %collective-permute-start.2 = (bf16[64,1408]{1,0:T(8,128)(2,1)S(1)}, bf16[64,1408]{1,0:T(8,128)(2,1)S(1)}, u32[]{:S(2)}, u32[]{:S(2)}) collective-permute-start(bf16[64,1408]{1,0:T(8,128)(2,1)S(1)} %get-tuple-element.45), channel_id=1, source_target_pairs={{0,24},{8,16},{16,8},{24,0},{1,25},{9,17},{17,9},{25,1},{2,26},{10... | collective-permute-start | bytes 540680 | tf_op jit(solution)/shard_map/ppermute | solution.py:287
  3.7 0.7 collective-permute-start
  4.4 0.7 pad_bitcast_fusion.table_ref
  5.1 0.3 collective-permute-done.pair_ref.refs_1_
  5.4 1.0 copy-done.4
  6.4 0.7 copy-done.6
  7.1 7.1 %early.1 = (bf16[5120,128]{1,0:T(8,128)(2,1)S(1)}, s32[40,128]{1,0:T(8,128)S(1)}, s32[24,128]{1,0:T(8,128)S(1)}, bf16[96,4224]{1,0:T(8,128)(2,1)S(1)}, bf16[3,1408,2304]{2,1,0:T(8,128)(2,1)S(1)}) custom-call(s32[4]{0:T(128)S(1)} %get-tuple-element.50.order_ref, bf16[64,1408]{1,0:T(8,128)(2,1)S(1)} %get-tuple-element.47.own_ref.refs_0_, ...), custom_call_target="tpu_custom_call" | custom-call | bytes 19464192 | tf_op jit(solution)/shard_map/early/pallas_call | solution.py:308
  14.3 10.3 %design.1 = (bf16[256,4224]{1,0:T(8,128)(2,1)S(1)}, bf16[3,1408,1024]{2,1,0:T(8,128)(2,1)S(1)}) custom-call(s32[4]{0:T(128)S(1)} %get-tuple-element.50.order_ref, s32[4]{0:T(128)S(1)} %get-tuple-element.49.place_ref, bf16[96,4224]{1,0:T(8,128)(2,1)S(1)} %get-tuple-element.28.early_ref, f32[3,16,1408]{2,1,0:T(8,128)S(1)} %bitcast.6, ...), custom_call_target="tpu_custom_call" | custom-call | bytes 8650752 | tf_op jit(solution)/shard_map/design/pallas_call | solution.py:325
  24.5 4.3 %product.5 = (bf16[128,512]{1,0:T(8,128)(2,1)S(1)}, bf16[128,512]{1,0:T(8,128)(2,1)S(1)}, bf16[3,1408,256]{2,1,0:T(8,128)(2,1)S(1)}) custom-call(bf16[256,4224]{1,0:T(8,128)(2,1)S(1)} %get-tuple-element.29.design_ref, bf16[3,1408,2304]{2,1,0:T(8,128)(2,1)S(1)} %get-tuple-element.30.refs_0_, bf16[3,1408,5120]{2,1,0:T(8,128)(2,1)} %refs_3_.1), custom_call_target="tpu_custom_call" | custom-call | flops 1107296256 | bytes 4325376 | tf_op jit(solution)/shard_map/product/pallas_call | solution.py:213
  28.9 0.4 collective-permute-start.3
  29.3 5.2 %product.6 = (bf16[128,1024]{1,0:T(8,128)(2,1)S(1)}, bf16[128,1024]{1,0:T(8,128)(2,1)S(1)}, bf16[3,1408,768]{2,1,0:T(8,128)(2,1)S(1)}) custom-call(bf16[256,4224]{1,0:T(8,128)(2,1)S(1)} %get-tuple-element.29.design_ref, bf16[3,1408,2304]{2,1,0:T(8,128)(2,1)S(1)} %get-tuple-element.30.refs_0_, bf16[3,1408,5120]{2,1,0:T(8,128)(2,1)} %refs_3_.1), custom_call_target="tpu_custom_call" | custom-call | flops 2214592512 | bytes 8650752 | tf_op jit(solution)/shard_map/product/pallas_call | solution.py:213
  34.6 0.2 collective-permute-start.5
  34.8 1.7 %collective-permute-start.4 = (bf16[64,512]{1,0:T(8,128)(2,1)S(1)}, bf16[64,512]{1,0:T(8,128)(2,1)S(1)}, u32[]{:S(2)}, u32[]{:S(2)}) collective-permute-start(bf16[64,512]{1,0:T(8,128)(2,1)S(1)} %add_convert_fusion.4.refs_2_), channel_id=1, source_target_pairs={{0,16},{8,24},{16,0},{24,8},{1,17},{9,25},{17,1},{25,9},{2,18},{10... | collective-permute-start | bytes 196616 | tf_op jit(solution)/shard_map/ppermute | solution.py:353
  36.5 6.5 %copy-done.1 = bf16[3,1408,2304]{2,1,0:T(8,128)(2,1)S(1)} copy-done((bf16[3,1408,2304]{2,1,0:T(8,128)(2,1)S(1)}, bf16[3,1408,2304]{2,1,0:T(8,128)(2,1)}, u32[]{:S(2)}) %copy-start.1) | copy-done | bytes 19464216
  43.1 3.5 %copy-done.3 = bf16[3,1408,1024]{2,1,0:T(8,128)(2,1)S(1)} copy-done((bf16[3,1408,1024]{2,1,0:T(8,128)(2,1)S(1)}, bf16[3,1408,1024]{2,1,0:T(8,128)(2,1)}, u32[]{:S(2)}) %copy-start.3) | copy-done | bytes 8650776
  46.6 3.0 %product.7 = (bf16[128,1280]{1,0:T(8,128)(2,1)S(1)}, bf16[128,1280]{1,0:T(8,128)(2,1)S(1)}, bf16[3,1408,768]{2,1,0:T(8,128)(2,1)S(1)}) custom-call(bf16[256,4224]{1,0:T(8,128)(2,1)S(1)} %get-tuple-element.29.design_ref, bf16[3,1408,2304]{2,1,0:T(8,128)(2,1)S(1)} %copy-done.1, bf16[3,1408,1024]{2,1,0:T(8,128)(2,1)S(1)} %copy-done.3, ...), custom_call_target="tpu_custom_call" | custom-call | flops 2768240640 | bytes 10813440 | tf_op jit(solution)/shard_map/product/pallas_call | solution.py:213
  49.7 0.1 collective-permute-start.7
  49.8 0.5 collective-permute-start.6
  50.3 3.0 %product.8 = (bf16[128,1280]{1,0:T(8,128)(2,1)S(1)}, bf16[128,1280]{1,0:T(8,128)(2,1)S(1)}) custom-call(bf16[256,4224]{1,0:T(8,128)(2,1)S(1)} %get-tuple-element.29.design_ref, bf16[3,1408,1024]{2,1,0:T(8,128)(2,1)S(1)} %copy-done.3, bf16[3,1408,256]{2,1,0:T(8,128)(2,1)S(1)} %get-tuple-element.38.refs_1_, ...), custom_call_target="tpu_custom_call" | custom-call | flops 2768240640 | bytes 10813440 | tf_op jit(solution)/shard_map/product/pallas_call | solution.py:213
  53.3 0.2 collective-permute-start.9
  53.6 1.7 %collective-permute-start.8 = (bf16[64,1280]{1,0:T(8,128)(2,1)S(1)}, bf16[64,1280]{1,0:T(8,128)(2,1)S(1)}, u32[]{:S(2)}, u32[]{:S(2)}) collective-permute-start(bf16[64,1280]{1,0:T(8,128)(2,1)S(1)} %add_convert_fusion.1.refs_2_), channel_id=1, source_target_pairs={{0,16},{8,24},{16,0},{24,8},{1,17},{9,25},{17,1},{25,9},{2,18},{10... | collective-permute-start | bytes 491528 | tf_op jit(solution)/shard_map/ppermute | solution.py:353
  55.3 0.4 collective-permute-done.6.refs_5_.refs_3_
  55.7 2.5 %product.9 = (bf16[128,1024]{1,0:T(8,128)(2,1)S(1)}, bf16[128,1024]{1,0:T(8,128)(2,1)S(1)}) custom-call(bf16[256,4224]{1,0:T(8,128)(2,1)S(1)} %get-tuple-element.29.design_ref, bf16[3,1408,768]{2,1,0:T(8,128)(2,1)S(1)} %get-tuple-element.39.refs_2_.refs_0_, bf16[3,1408,768]{2,1,0:T(8,128)(2,1)S(1)} %get-tuple-element.42.refs_1_, ...), custom_call_target="tpu_custom_call" | custom-call | flops 2214592512 | bytes 8650752 | tf_op jit(solution)/shard_map/product/pallas_call | solution.py:213
  58.3 0.4 collective-permute-start.10
  58.8 1.0 collective-permute-done.11.refs_5_
  59.8 0.7 collective-permute-start.12
  60.5 4.9 %pack.2.refs_0_ = bf16[8,64,1280]{2,1,0:T(8,128)(2,1)S(1)} custom-call(s32[24,128]{1,0:T(8,128)S(1)} %get-tuple-element.25.start_ref, bf16[5120,128]{1,0:T(8,128)(2,1)S(1)} %get-tuple-element.26.onehot_ref, s32[40,128]{1,0:T(8,128)S(1)} %get-tuple-element.27.tile_ref, bf16[128,512]{1,0:T(8,128)(2,1)S(1)} %get-tuple-element.31.refs_0_, ...), custom_call_target="tpu_custom_call" | custom-call | tf_op jit(solution)/shard_map/pack/pallas_call | solution.py:362
  65.5 2.3 %collective-permute-done.12.refs_6_ = bf16[64,1024]{1,0:T(8,128)(2,1)S(1)} collective-permute-done((bf16[64,1024]{1,0:T(8,128)(2,1)S(1)}, bf16[64,1024]{1,0:T(8,128)(2,1)S(1)}, u32[]{:S(2)}, u32[]{:S(2)}) %collective-permute-start.12) | collective-permute-done | bytes 131104 | tf_op jit(solution)/shard_map/ppermute | solution.py:353
  67.8 4.2 %pack.3 = bf16[8,64,1280]{2,1,0:T(8,128)(2,1)S(1)} custom-call(s32[24,128]{1,0:T(8,128)S(1)} %get-tuple-element.25.start_ref, bf16[5120,128]{1,0:T(8,128)(2,1)S(1)} %get-tuple-element.26.onehot_ref, s32[40,128]{1,0:T(8,128)S(1)} %get-tuple-element.27.tile_ref, bf16[8,64,1280]{2,1,0:T(8,128)(2,1)S(1)} %pack.2.refs_0_, ...), custom_call_target="tpu_custom_call" | custom-call | tf_op jit(solution)/shard_map/pack/pallas_call | solution.py:362
  72.0 36.9 %all_to_all.5 = bf16[8,64,1280]{2,1,0:T(8,128)(2,1)S(1)} all-to-all(bf16[8,64,1280]{2,1,0:T(8,128)(2,1)S(1)} %pack.3), channel_id=1, replica_groups=mesh['chan'=4,'vox'=8] {'vox'}, dimensions={0} | all-to-all | bytes 2621440 | tf_op jit(solution)/shard_map/all_to_all | solution.py:372
  108.9 1.1 copy.7
  (27 shorter events, 0.3 us)
Async XLA Ops:
  1.2 13.0 %collective-permute-start.2 = (bf16[64,1408]{1,0:T(8,128)(2,1)S(1)}, bf16[64,1408]{1,0:T(8,128)(2,1)S(1)}, u32[]{:S(2)}, u32[]{:S(2)}) collective-permute-start(bf16[64,1408]{1,0:T(8,128)(2,1)S(1)} %get-tuple-element.45), channel_id=1, source_target_pairs={{0,24},{8,16},{16,8},{24,0},{1,25},{9,17},{17,9},{25,1},{2,26},{10... | collective-permute-start | bytes 540680 | tf_op jit(solution)/shard_map/ppermute | solution.py:287
  3.7 1.7 %collective-permute-start = (bf16[64,1408]{1,0:T(8,128)(2,1)S(1)}, bf16[64,1408]{1,0:T(8,128)(2,1)S(1)}, u32[]{:S(2)}, u32[]{:S(2)}) collective-permute-start(bf16[64,1408]{1,0:T(8,128)(2,1)S(1)} %get-tuple-element.46), channel_id=1, source_target_pairs={{0,8},{8,0},{16,24},{24,16},{1,9},{9,1},{17,25},{25,17},{2,10},{10... | collective-permute-start | bytes 540680 | tf_op jit(solution)/shard_map/ppermute | solution.py:287
  4.4 9.9 %collective-permute-start.1 = (bf16[64,1408]{1,0:T(8,128)(2,1)S(1)}, bf16[64,1408]{1,0:T(8,128)(2,1)S(1)}, u32[]{:S(2)}, u32[]{:S(2)}) collective-permute-start(bf16[64,1408]{1,0:T(8,128)(2,1)S(1)} %get-tuple-element.48), channel_id=1, source_target_pairs={{0,16},{8,24},{16,0},{24,8},{1,17},{9,25},{17,1},{25,9},{2,18},{10... | collective-permute-start | bytes 540680 | tf_op jit(solution)/shard_map/ppermute | solution.py:287
  5.4 1.0 copy-start.4
  6.4 0.7 copy-start.6
  7.1 7.2 %copy-start.5 = (f32[3,1408,16]{1,2,0:T(8,128)S(1)}, f32[3,1408,16]{1,2,0:T(8,128)}, u32[]{:S(2)}) copy-start(f32[3,1408,16]{1,2,0:T(8,128)} %param.6) | copy-start | bytes 811012
  14.2 15.1 %copy-start = (bf16[3,1408,2304]{2,1,0:T(8,128)(2,1)}, bf16[3,1408,2304]{2,1,0:T(8,128)(2,1)S(1)}, u32[]{:S(2)}) copy-start(bf16[3,1408,2304]{2,1,0:T(8,128)(2,1)S(1)} %get-tuple-element.30.refs_0_) | copy-start | bytes 58392580
  24.5 4.3 %copy-start.2 = (bf16[3,1408,1024]{2,1,0:T(8,128)(2,1)}, bf16[3,1408,1024]{2,1,0:T(8,128)(2,1)S(1)}, u32[]{:S(2)}) copy-start(bf16[3,1408,1024]{2,1,0:T(8,128)(2,1)S(1)} %get-tuple-element.35.refs_1_.refs_0_) | copy-start | bytes 25952260
  28.9 5.9 %collective-permute-start.3 = (bf16[128,512]{1,0:T(8,128)(2,1)S(1)}, bf16[128,512]{1,0:T(8,128)(2,1)S(1)}, u32[]{:S(2)}, u32[]{:S(2)}) collective-permute-start(bf16[128,512]{1,0:T(8,128)(2,1)S(1)} %get-tuple-element.32), channel_id=1, source_target_pairs={{0,8},{8,0},{16,24},{24,16},{1,9},{9,1},{17,25},{25,17},{2,10},{10... | collective-permute-start | bytes 393224 | tf_op jit(solution)/shard_map/ppermute | solution.py:353
  34.6 15.2 %collective-permute-start.5 = (bf16[128,1024]{1,0:T(8,128)(2,1)S(1)}, bf16[128,1024]{1,0:T(8,128)(2,1)S(1)}, u32[]{:S(2)}, u32[]{:S(2)}) collective-permute-start(bf16[128,1024]{1,0:T(8,128)(2,1)S(1)} %get-tuple-element.34), channel_id=1, source_target_pairs={{0,8},{8,0},{16,24},{24,16},{1,9},{9,1},{17,25},{25,17},{2,10},{10... | collective-permute-start | bytes 786440 | tf_op jit(solution)/shard_map/ppermute | solution.py:353
  34.8 15.5 %collective-permute-start.4 = (bf16[64,512]{1,0:T(8,128)(2,1)S(1)}, bf16[64,512]{1,0:T(8,128)(2,1)S(1)}, u32[]{:S(2)}, u32[]{:S(2)}) collective-permute-start(bf16[64,512]{1,0:T(8,128)(2,1)S(1)} %add_convert_fusion.4.refs_2_), channel_id=1, source_target_pairs={{0,16},{8,24},{16,0},{24,8},{1,17},{9,25},{17,1},{25,9},{2,18},{10... | collective-permute-start | bytes 196616 | tf_op jit(solution)/shard_map/ppermute | solution.py:353
  36.5 6.5 %copy-start.1 = (bf16[3,1408,2304]{2,1,0:T(8,128)(2,1)S(1)}, bf16[3,1408,2304]{2,1,0:T(8,128)(2,1)}, u32[]{:S(2)}) copy-start(bf16[3,1408,2304]{2,1,0:T(8,128)(2,1)} %copy-done) | copy-start | bytes 58392580
  43.1 3.5 %copy-start.3 = (bf16[3,1408,1024]{2,1,0:T(8,128)(2,1)S(1)}, bf16[3,1408,1024]{2,1,0:T(8,128)(2,1)}, u32[]{:S(2)}) copy-start(bf16[3,1408,1024]{2,1,0:T(8,128)(2,1)} %copy-done.2) | copy-start | bytes 25952260
  49.7 3.9 %collective-permute-start.7 = (bf16[128,1280]{1,0:T(8,128)(2,1)S(1)}, bf16[128,1280]{1,0:T(8,128)(2,1)S(1)}, u32[]{:S(2)}, u32[]{:S(2)}) collective-permute-start(bf16[128,1280]{1,0:T(8,128)(2,1)S(1)} %get-tuple-element.37), channel_id=1, source_target_pairs={{0,8},{8,0},{16,24},{24,16},{1,9},{9,1},{17,25},{25,17},{2,10},{10... | collective-permute-start | bytes 983048 | tf_op jit(solution)/shard_map/ppermute | solution.py:353
  49.8 6.0 %collective-permute-start.6 = (bf16[64,1024]{1,0:T(8,128)(2,1)S(1)}, bf16[64,1024]{1,0:T(8,128)(2,1)S(1)}, u32[]{:S(2)}, u32[]{:S(2)}) collective-permute-start(bf16[64,1024]{1,0:T(8,128)(2,1)S(1)} %add_convert_fusion.3.refs_3_), channel_id=1, source_target_pairs={{0,16},{8,24},{16,0},{24,8},{1,17},{9,25},{17,1},{25,9},{2,18},{10... | collective-permute-start | bytes 393224 | tf_op jit(solution)/shard_map/ppermute | solution.py:353
  53.3 5.0 %collective-permute-start.9 = (bf16[128,1280]{1,0:T(8,128)(2,1)S(1)}, bf16[128,1280]{1,0:T(8,128)(2,1)S(1)}, u32[]{:S(2)}, u32[]{:S(2)}) collective-permute-start(bf16[128,1280]{1,0:T(8,128)(2,1)S(1)} %get-tuple-element.41), channel_id=1, source_target_pairs={{0,8},{8,0},{16,24},{24,16},{1,9},{9,1},{17,25},{25,17},{2,10},{10... | collective-permute-start | bytes 983048 | tf_op jit(solution)/shard_map/ppermute | solution.py:353
  53.6 6.9 %collective-permute-start.8 = (bf16[64,1280]{1,0:T(8,128)(2,1)S(1)}, bf16[64,1280]{1,0:T(8,128)(2,1)S(1)}, u32[]{:S(2)}, u32[]{:S(2)}) collective-permute-start(bf16[64,1280]{1,0:T(8,128)(2,1)S(1)} %add_convert_fusion.1.refs_2_), channel_id=1, source_target_pairs={{0,16},{8,24},{16,0},{24,8},{1,17},{9,25},{17,1},{25,9},{2,18},{10... | collective-permute-start | bytes 491528 | tf_op jit(solution)/shard_map/ppermute | solution.py:353
  58.2 1.6 %collective-permute-start.11 = (bf16[128,1024]{1,0:T(8,128)(2,1)S(1)}, bf16[128,1024]{1,0:T(8,128)(2,1)S(1)}, u32[]{:S(2)}, u32[]{:S(2)}) collective-permute-start(bf16[128,1024]{1,0:T(8,128)(2,1)S(1)} %get-tuple-element.44), channel_id=1, source_target_pairs={{0,8},{8,0},{16,24},{24,16},{1,9},{9,1},{17,25},{25,17},{2,10},{10... | collective-permute-start | bytes 786440 | tf_op jit(solution)/shard_map/ppermute | solution.py:353
  58.3 7.1 %collective-permute-start.10 = (bf16[64,1280]{1,0:T(8,128)(2,1)S(1)}, bf16[64,1280]{1,0:T(8,128)(2,1)S(1)}, u32[]{:S(2)}, u32[]{:S(2)}) collective-permute-start(bf16[64,1280]{1,0:T(8,128)(2,1)S(1)} %add_convert_fusion), channel_id=1, source_target_pairs={{0,16},{8,24},{16,0},{24,8},{1,17},{9,25},{17,1},{25,9},{2,18},{10... | collective-permute-start | bytes 491528 | tf_op jit(solution)/shard_map/ppermute | solution.py:353
  59.8 8.0 %collective-permute-start.12 = (bf16[64,1024]{1,0:T(8,128)(2,1)S(1)}, bf16[64,1024]{1,0:T(8,128)(2,1)S(1)}, u32[]{:S(2)}, u32[]{:S(2)}) collective-permute-start(bf16[64,1024]{1,0:T(8,128)(2,1)S(1)} %add_convert_fusion.2), channel_id=1, source_target_pairs={{0,16},{8,24},{16,0},{24,8},{1,17},{9,25},{17,1},{25,9},{2,18},{10... | collective-permute-start | bytes 393224 | tf_op jit(solution)/shard_map/ppermute | solution.py:353

commit v6 on v5

--- a/solution.py
+++ b/solution.py
@@ -14,31 +14,34 @@
 VOX_BLOCK = 256
 COLUMNS = 512
 ROWS = 32
-PIECE_UNITS = (9, 4, 1, 3, 3)
-CHUNK_PARTS = (
-    ((0, 0, 2),),
-    ((0, 2, 6),),
-    ((0, 6, 9), (1, 0, 2)),
-    ((1, 2, 4), (2, 0, 1), (3, 0, 2)),
-    ((3, 2, 3), (4, 0, 3)),
-)
-PACK_FIRST = 3
+CHUNKS = 5
+COPIES = (((0, 2), (1, 4), (2, 3)), ((2, 2), (3, 2)), ((3, 1),), ((3, 2), (4, 1)), ((4, 3),))
+PACK_FIRST = 4
 MIB = 1 << 20
 
 VMEM = functools.partial(pl.BlockSpec, memory_space=pltpu.VMEM)
 SMEM = functools.partial(pl.BlockSpec, memory_space=pltpu.SMEM)
 ANY = functools.partial(pl.BlockSpec, memory_space=pl.ANY)
-
-
-def copy_piece(weight_ref, piece_ref, sem, first):
-    depth = weight_ref.shape[1]
-    if piece_ref.shape[1] > depth:
-        piece_ref[:, depth:, :] = jnp.zeros_like(piece_ref[:, depth:, :])
-    copy = pltpu.make_async_copy(
-        weight_ref.at[:, :, pl.ds(first, piece_ref.shape[2])], piece_ref.at[:, pl.ds(0, depth), :], sem
-    )
-    copy.start()
-    return copy
+HBM = functools.partial(pl.BlockSpec, memory_space=pltpu.HBM)
+
+
+def copy_pieces(weight_ref, piece_refs, sems, first):
+    depth, copies = weight_ref.shape[1], []
+    for i, ref in enumerate(piece_refs):
+        if ref.shape[1] > depth:
+            ref[:, depth:, :] = jnp.zeros_like(ref[:, depth:, :])
+        copy = pltpu.make_async_copy(
+            weight_ref.at[:, :, pl.ds(first, ref.shape[2])], ref.at[:, pl.ds(0, depth), :], sems.at[i]
+        )
+        copy.start()
+        copies.append(copy)
+        first += ref.shape[2]
+    return copies
+
+
+def wait_all(copies):
+    for copy in copies:
+        copy.wait()
 
 
 def cost(flops, read):
@@ -115,14 +118,20 @@
     return pl.ds(pl.multiple_of(tile * LANES, LANES), LANES)
 
 
-def early_kernel(owners, spread, order_ref, own_ref, pair_ref, parcel_ref, table_ref, filter_ref, weight_ref, *refs):
-    onehot_ref, tile_ref, start_ref, design_ref, piece_ref, plain, shifted, sems = refs
-    copy = copy_piece(weight_ref, piece_ref, sems.at[0], 0)
+def early_kernel(owners, spread, order_ref, own_ref, pair_ref, parcel_hbm, table_ref, filter_hbm, weight_ref, *refs):
+    onehot_ref, tile_ref, start_ref, design_ref, *piece_refs, plain, shifted, filter_ref, parcel_ref, sems = refs
+    count = len(piece_refs)
+    load_filter = pltpu.make_async_copy(filter_hbm, filter_ref, sems.at[count])
+    load_parcel = pltpu.make_async_copy(parcel_hbm, parcel_ref, sems.at[count + 1])
+    load_filter.start()
+    load_parcel.start()
+    copies = copy_pieces(weight_ref, piece_refs, sems, 0)
     block, width = own_ref.shape
     core = lax.rem(order_ref[0], 2)
     own = pl.ds(pl.multiple_of(core * block, block), block)
     pair = pl.ds(pl.multiple_of((1 - core) * block, block), block)
     clear_lead(shifted)
+    load_filter.wait()
 
     def columns(tile, carry):
         column = lane_tile(tile)
@@ -136,13 +145,14 @@
         return carry
 
     lax.fori_loop(0, width // LANES, columns, 0)
+    load_parcel.wait()
     places(owners, spread, parcel_ref, table_ref, onehot_ref, tile_ref, start_ref)
-    copy.wait()
+    wait_all(copies)
 
 
 def design_kernel(parts, first, order_ref, place_ref, early_ref, filter_ref, weight_ref, *refs):
-    series_refs, (design_ref, piece_ref, plain, shifted, sems) = refs[:parts], refs[parts:]
-    copy = copy_piece(weight_ref, piece_ref, sems.at[0], first)
+    series_refs, (design_ref, *piece_refs, plain, shifted, sems) = refs[:parts], refs[parts:]
+    copies = copy_pieces(weight_ref, piece_refs, sems, first)
     block, width = series_refs[0].shape
     chip = order_ref[0] >> 1
     clear_lead(shifted)
@@ -171,7 +181,7 @@
         return carry
 
     lax.fori_loop(0, width // LANES, columns, 0)
-    copy.wait()
+    wait_all(copies)
 
 
 def filter_scratch(time_len):
@@ -181,95 +191,102 @@
     ]
 
 
-def product_kernel(extra, bounds, first, design_ref, *refs):
-    weight_refs, refs = refs[: len(bounds)], refs[len(bounds) + extra :]
-    copy = None
+def product_kernel(taken, extra, first, design_ref, *refs):
+    weight_refs, refs = refs[:taken], refs[taken + extra :]
+    copies = []
     if first is not None:
-        weight_ref, keep_ref, send_ref, piece_ref, sems = refs
-        copy = copy_piece(weight_ref, piece_ref, sems.at[0], first)
+        weight_ref, keep_ref, send_ref, *piece_refs, sems = refs
+        copies = copy_pieces(weight_ref, piece_refs, sems, first)
     else:
         keep_ref, send_ref = refs
     half, at = keep_ref.shape[0], 0
-    for ref, (low, high) in zip(weight_refs, bounds):
-        for start in range(low, high, COLUMNS):
-            weight = ref[:, :, start : min(start + COLUMNS, high)]
+    for ref in weight_refs:
+        for start in range(0, ref.shape[2], COLUMNS):
+            weight = ref[:, :, start : min(start + COLUMNS, ref.shape[2])]
             weight = weight.reshape(-1, weight.shape[2])
             total = jnp.dot(design_ref[...], weight, preferred_element_type=jnp.float32)
             columns = slice(at, at + weight.shape[1])
             keep_ref[:, columns] = total[:half].astype(jnp.bfloat16)
             send_ref[:, columns] = total[half:].astype(jnp.bfloat16)
             at += weight.shape[1]
-    if copy is not None:
-        copy.wait()
-
-
-def product(design, parts, after, weights, ahead):
+    wait_all(copies)
+
+
+def product(design, taken, after, weights, first, ahead):
     time_len, lanes = design.shape
-    bounds = tuple((low, high) for _, low, high in parts)
-    width = sum(high - low for low, high in bounds)
+    width = sum(piece.shape[2] for piece in taken)
     half = jax.ShapeDtypeStruct((time_len // 2, width), jnp.bfloat16)
-    held = parts[0][0].shape
-    more = [ahead] if ahead else []
     return pl.pallas_call(
-        functools.partial(product_kernel, len(after), bounds, ahead[0] if ahead else None),
-        in_specs=[VMEM()] * (1 + len(parts)) + [ANY()] * (len(after) + len(more)),
-        out_specs=[VMEM()] * (2 + len(more)),
-        out_shape=[half, half] + [pltpu.VMEM((*held[:2], size), jnp.bfloat16) for _, size in more],
-        scratch_shapes=[pltpu.SemaphoreType.DMA((1,)) for _ in more],
+        functools.partial(product_kernel, len(taken), len(after), first if ahead else None),
+        in_specs=[VMEM()] * (1 + len(taken)) + [ANY()] * (len(after) + bool(ahead)),
+        out_specs=[VMEM()] * (2 + len(ahead)),
+        out_shape=[half, half] + ahead,
+        scratch_shapes=[pltpu.SemaphoreType.DMA((len(ahead),))] if ahead else [],
         compiler_params=pltpu.CompilerParams(vmem_limit_bytes=10 * MIB),
         cost_estimate=cost(2 * time_len * lanes * width, 2 * lanes * width),
         name="product",
-    )(design, *(piece for piece, _, _ in parts), *after, *([weights] if ahead else []))
-
-
-def pack_kernel(spread, widths, first, more, start_ref, onehot_ref, tile_ref, *refs):
-    *terms, packed_ref, summed = refs
-    if more:
-        packed_ref[...] = terms.pop(0)[...]
+    )(design, *taken, *after, *([weights] if ahead else []))
+
+
+def pack_kernel(spread, widths, first, start_ref, onehot_ref, tile_ref, *refs):
+    *terms, out_ref, summed, packed = refs
+    owners, time_block = packed.shape[:2]
+    if first:
+        packed[...] = terms.pop(0)[...]
     else:
-        packed_ref[...] = jnp.zeros_like(packed_ref)
-    owners, time_block, send_cap = packed_ref.shape
+        packed[...] = jnp.zeros_like(packed)
     each, at = len(terms) // len(widths), 0
     for c, width in enumerate(widths):
         total = sum(term[:time_block, :].astype(jnp.float32) for term in terms[c * each : (c + 1) * each])
         summed[:, at : at + width] = total.astype(jnp.bfloat16)
         at += width
-    last_tile = send_cap // SLOT_TILE - 1
     step = VOX_BLOCK // LANES
 
-    def block_step(index, carry):
+    def moves(index, extras):
         block = first + index
         values = summed[:, pl.ds(pl.multiple_of(index * VOX_BLOCK, VOX_BLOCK), VOX_BLOCK)]
         onehot = onehot_ref[pl.ds(pl.multiple_of(block * VOX_BLOCK, VOX_BLOCK), VOX_BLOCK), :]
         tiles = jnp.concatenate([tile_ref[pl.ds(block * step + i, 1), :] for i in range(step)], axis=1)
-
-        def chosen(owner, tile):
+        low = [start_ref[block, o] >> 7 for o in range(owners)]
+        targets = [(o, low[o] + extra) for extra in extras for o in range(owners)]
+        rows = []
+        for owner, tile in targets:
             hit = jnp.where(tiles == owner * spread + tile, 1.0, 0.0)
-            return values * hit.astype(jnp.bfloat16)
-
-        def put(owner, tile, moved):
-            tile = jnp.minimum(tile, last_tile)
-            at = pl.ds(pl.multiple_of(tile * SLOT_TILE, SLOT_TILE), SLOT_TILE)
-            packed_ref[owner, :, at] = packed_ref[owner, :, at] + moved
-
-        def move(targets):
-            rows = jnp.concatenate([chosen(owner, tile) for owner, tile in targets], axis=0)
-            moved = jnp.dot(rows, onehot, preferred_element_type=jnp.float32).astype(jnp.bfloat16)
-            for i, (owner, tile) in enumerate(targets):
-                put(owner, tile, moved[i * time_block : (i + 1) * time_block])
-
-        low = [start_ref[block, o] >> 7 for o in range(owners)]
+            rows.append(values * hit.astype(jnp.bfloat16))
+        moved = jnp.dot(jnp.concatenate(rows, axis=0), onehot, preferred_element_type=jnp.float32)
+        moved = moved.astype(jnp.bfloat16)
+        out = []
+        for i, (owner, tile) in enumerate(targets):
+            lanes = pl.ds(pl.multiple_of(tile * SLOT_TILE, SLOT_TILE), SLOT_TILE)
+            out.append((owner, lanes, moved[i * time_block : (i + 1) * time_block]))
         high = [(start_ref[block + 1, o] - 1) >> 7 for o in range(owners)]
-        move([(o, low[o] + extra) for extra in range(2) for o in range(owners)])
-        longest = functools.reduce(jnp.maximum, [high[o] - low[o] for o in range(owners)])
-
-        @pl.when(longest > 1)
-        def _():
-            move([(o, low[o] + 2) for o in range(owners)])
-
+        return out, functools.reduce(jnp.maximum, [high[o] - low[o] for o in range(owners)])
+
+    def add(targets):
+        sums = [packed[owner, :, lanes] + moved for owner, lanes, moved in targets]
+        for (owner, lanes, _), total in zip(targets, sums):
+            packed[owner, :, lanes] = total
+
+    def blocks(indices):
+        found = [moves(index, range(2)) for index in indices]
+        for targets, _ in found:
+            add(targets)
+        for index, (_, longest) in zip(indices, found):
+
+            @pl.when(longest > 1)
+            def _():
+                add(moves(index, (2,))[0])
+
+    count = sum(widths) // VOX_BLOCK
+
+    def two(i, carry):
+        blocks([2 * i, 2 * i + 1])
         return carry
 
-    lax.fori_loop(0, sum(widths) // VOX_BLOCK, block_step, 0)
+    lax.fori_loop(0, count // 2, two, 0)
+    if count % 2:
+        blocks([count - 1])
+    out_ref[...] = packed[:, :, : out_ref.shape[2]]
 
 
 def shards(features, hrf_filters, weights, voxel_parcel, parcel_owner):
@@ -286,12 +303,22 @@
     for d in range(1, parts):
         series[d] = lax.ppermute(series[d], "chan", [(i, i ^ d) for i in range(parts)])
     filters = jnp.transpose(hrf_filters, (0, 2, 1))
-    unit = voxels // sum(PIECE_UNITS)
-    pieces = [unit * units for units in PIECE_UNITS]
-    firsts = [sum(pieces[:i]) for i in range(len(pieces))]
     spare = -depth % LANES
-    held = lambda i: pltpu.VMEM((bases, depth + spare, pieces[i]), jnp.bfloat16)
     lanes = bases * (depth + spare)
+    unit = voxels // sum(units for pieces in COPIES for _, units in pieces)
+    copied = [unit * sum(units for _, units in pieces) for pieces in COPIES]
+    firsts = [sum(copied[:i]) for i in range(len(copied))]
+    held = [[] for _ in range(CHUNKS)]
+
+    def room(i):
+        if i >= len(COPIES):
+            return []
+        return [pltpu.VMEM((bases, depth + spare, unit * units), jnp.bfloat16) for _, units in COPIES[i]]
+
+    def keep_pieces(i, pieces):
+        for (chunk, _), piece in zip(COPIES[i] if i < len(COPIES) else (), pieces):
+            held[chunk].append(piece)
+
     if spare:
         series = [jnp.pad(part, ((0, 0), (0, spare))) for part in series]
         filters = jnp.pad(filters, ((0, 0), (0, 0), (0, spare)))
@@ -305,44 +332,55 @@
     place = sum(((order >> bit) & 1) << (bits - 1 - bit) for bit in range(bits)).astype(jnp.int32)
 
     early_rows = 2 * time_block - ROWS
-    onehot, tiles, starts, early, piece = pl.pallas_call(
+    onehot, tiles, starts, early, *pieces = pl.pallas_call(
         functools.partial(early_kernel, owners, spread),
-        in_specs=[SMEM()] + [VMEM()] * 5 + [ANY()],
-        out_specs=[VMEM()] * 5,
+        in_specs=[SMEM(), VMEM(), VMEM(), HBM(), VMEM(), HBM(), ANY()],
+        out_specs=[VMEM()] * (4 + len(COPIES[0])),
         out_shape=[
             jax.ShapeDtypeStruct((voxels, LANES), jnp.bfloat16),
             jax.ShapeDtypeStruct((voxels // LANES, LANES), jnp.int32),
             jax.ShapeDtypeStruct((marks, LANES), jnp.int32),
             jax.ShapeDtypeStruct((early_rows, lanes), jnp.bfloat16),
-            held(0),
+        ]
+        + room(0),
+        scratch_shapes=filter_scratch(2 * time_block)
+        + [
+            pltpu.VMEM(filters.shape, jnp.float32),
+            pltpu.VMEM((voxels // LANES, LANES), jnp.int32),
+            pltpu.SemaphoreType.DMA((len(COPIES[0]) + 2,)),
         ],
-        scratch_shapes=filter_scratch(2 * time_block) + [pltpu.SemaphoreType.DMA((1,))],
         compiler_params=pltpu.CompilerParams(vmem_limit_bytes=10 * MIB),
-        cost_estimate=cost(0, 2 * bases * depth * pieces[0]),
+        cost_estimate=cost(0, 2 * bases * depth * copied[0]),
         name="early",
-    )(order, series[0], series[1], voxel_parcel.reshape(-1, LANES), table, filters, weights)
-    copied = [piece]
-    design, piece = pl.pallas_call(
+    )(
+        order,
+        series[0],
+        series[1],
+        pltpu.with_memory_space_constraint(voxel_parcel.reshape(-1, LANES), pltpu.HBM),
+        table,
+        pltpu.with_memory_space_constraint(filters, pltpu.HBM),
+        weights,
+    )
+    keep_pieces(0, pieces)
+    design, *pieces = pl.pallas_call(
         functools.partial(design_kernel, parts, firsts[1]),
         in_specs=[SMEM(), SMEM(), VMEM(), VMEM(), ANY()] + [VMEM()] * parts,
-        out_specs=[VMEM(), VMEM()],
-        out_shape=[jax.ShapeDtypeStruct((time_len, lanes), jnp.bfloat16), held(1)],
-        scratch_shapes=filter_scratch(time_len) + [pltpu.SemaphoreType.DMA((1,))],
+        out_specs=[VMEM()] * (1 + len(COPIES[1])),
+        out_shape=[jax.ShapeDtypeStruct((time_len, lanes), jnp.bfloat16)] + room(1),
+        scratch_shapes=filter_scratch(time_len) + [pltpu.SemaphoreType.DMA((len(COPIES[1]),))],
         compiler_params=pltpu.CompilerParams(vmem_limit_bytes=10 * MIB),
-        cost_estimate=cost(0, 2 * bases * depth * pieces[1]),
+        cost_estimate=cost(0, 2 * bases * depth * copied[1]),
         name="design",
     )(order, place, early, filters, weights, *series)
-    copied.append(piece)
+    keep_pieces(1, pieces)
 
     widths, terms, sent, got = [], [], [], []
-    for c, chunk in enumerate(CHUNK_PARTS):
-        takes = [(copied[i], unit * low, unit * high) for i, low, high in chunk]
-        widths.append(sum(high - low for _, low, high in takes))
+    for c in range(CHUNKS):
         after = sent[max(c - 2, 0) : max(c - 1, 0)] + got[max(c - 3, 0) : max(c - 2, 0)]
-        more = len(copied) < len(pieces)
-        ahead = (firsts[len(copied)], pieces[len(copied)]) if more else None
-        keep, send, *piece = product(design, takes, after, weights, ahead)
-        copied.extend(piece)
+        ahead = room(c + 2)
+        keep, send, *pieces = product(design, held[c], after, weights, firsts[c + 2] if ahead else 0, ahead)
+        keep_pieces(c + 2, pieces)
+        widths.append(keep.shape[1])
         own = [keep]
         for bit in range(bits):
             if bit > 0:
@@ -355,17 +393,21 @@
         got.append(own[-1])
 
     packed = []
-    for low, high in ((0, PACK_FIRST), (PACK_FIRST, len(widths))):
+    for low, high in ((0, PACK_FIRST), (PACK_FIRST, CHUNKS)):
         args = packed + [term for own in terms[low:high] for term in own]
         here = widths[low:high]
+        room_here = send_cap if high == CHUNKS else spread * SLOT_TILE
         packed = [
             pl.pallas_call(
-                functools.partial(pack_kernel, spread, here, sum(widths[:low]) // VOX_BLOCK, len(packed)),
+                functools.partial(pack_kernel, spread, here, sum(widths[:low]) // VOX_BLOCK),
                 in_specs=[SMEM(), VMEM(), VMEM()] + [VMEM()] * len(args),
                 out_specs=VMEM(),
-                out_shape=jax.ShapeDtypeStruct((owners, time_block, send_cap), jnp.bfloat16),
-                scratch_shapes=[pltpu.VMEM((time_block, sum(here)), jnp.bfloat16)],
-                compiler_params=pltpu.CompilerParams(vmem_limit_bytes=12 * MIB),
+                out_shape=jax.ShapeDtypeStruct((owners, time_block, room_here), jnp.bfloat16),
+                scratch_shapes=[
+                    pltpu.VMEM((time_block, sum(here)), jnp.bfloat16),
+                    pltpu.VMEM((owners, time_block, spread * SLOT_TILE), jnp.bfloat16),
+                ],
+                compiler_params=pltpu.CompilerParams(vmem_limit_bytes=14 * MIB),
                 name="pack",
             )(starts, onehot, tiles, *args)
         ]

time: 110 us -> 92.5 us (0.84)
  local copies, waits for them, and re-layouts: 14.7 us -> 2.99 us
  Pallas kernels: 44.5 us -> 36 us
  waiting for transfers between devices: 4.13 us -> 6.72 us
    unnamed x15 -> x3, local copies, waits for them, and re-layouts: 12.8 us -> 1.06 us
    pallas_call x1, Pallas kernels: 10.3 us -> 4.15 us  [shards(): pl.pallas_call(functools.partial(design_kernel, parts, firsts[1]), in_spe...]
    ppermute x10, waiting for transfers between devices: 3.81 us -> 6.41 us  [shards(): lax.ppermute(send, 'chan', [(i, i ^ 1 << bit) for i in range(parts)])]
    pallas_call x2, Pallas kernels: 9.06 us -> 7.63 us  [shards(): pl.pallas_call(functools.partial(pack_kernel, spread, here, sum(widths[:l...]
    pallas_call x5, Pallas kernels: 18.1 us -> 16.9 us  [product(): pl.pallas_call(functools.partial(product_kernel, len(taken), len(after),...]
  transfers between devices with their start and end apart: 13 -> 13, of which waited for: 4 -> 4; matrix products, arithmetic and copies ran while one was open for 1% -> 1% of each run, Pallas kernels for 23% -> 29%
where the time goes in v6:
time: 92.5 us; the launch traced here: 92.2 us
  blocking collectives  36.5 us (39%)
  Pallas kernels  36 us (39%)
  starting transfers between devices  9.65 us (10%)
  waiting for transfers between devices  6.72 us (7%)
  local copies, waits for them, and re-layouts  2.99 us (3%)
    all_to_all x1, blocking collectives, shards(): lax.all_to_all(packed[0], 'vox', split_axis=0, concat_axis=0, tiled=True)  36.5 us
    pallas_call x5, Pallas kernels, product(): pl.pallas_call(functools.partial(product_kernel, len(taken), len(after),...  16.9 us
    pallas_call x2, Pallas kernels, shards(): pl.pallas_call(functools.partial(pack_kernel, spread, here, sum(widths[:l...  7.63 us
    pallas_call x1, Pallas kernels, shards(): pl.pallas_call(functools.partial(early_kernel, owners, spread), in_specs=...  7.34 us
    ppermute x10, starting transfers between devices, shards(): lax.ppermute(send, 'chan', [(i, i ^ 1 << bit) for i in range(parts)])  6.49 us
    ppermute x10, waiting for transfers between devices, shards(): lax.ppermute(send, 'chan', [(i, i ^ 1 << bit) for i in range(parts)])  6.41 us
    pallas_call x1, Pallas kernels, shards(): pl.pallas_call(functools.partial(design_kernel, parts, firsts[1]), in_spe...  4.15 us
    ppermute x3, starting transfers between devices, shards(): lax.ppermute(series[d], 'chan', [(i, i ^ d) for i in range(parts)])  3.16 us
  transfers between devices with their start and end apart: 13, of which 4 were waited for; matrix products, arithmetic and copies ran while one was open for 1% of the time, Pallas kernels for 29%

profile of v6, /device:TPU:0, one launch (start us, length us, event | category | flops | bytes accessed | tf_op | source)
XLA Modules:
  0.0 92.2 jit_solution(8435438528180779522)
XLA Ops:
  0.0 1.2 %constant_dynamic-slice_fusion = (bf16[64,1408]{1,0:T(8,128)(2,1)S(1)}, bf16[64,1408]{1,0:T(8,128)(2,1)S(1)}, bf16[64,1408]{1,0:T(8,128)(2,1)S(1)}, bf16[64,1408]{1,0:T(8,128)(2,1)S(1)}) fusion(bf16[64,5632]{1,0:T(8,128)(2,1)} %param.5, s32[]{:T(128)S(6)} %select_n.15, s32[]{:T(128)S(6)} %select_n.13, s32[]{:T(128)S(6)} %select_n.12, s32[]{:T(128)S(6)} %select_n.14), kind=kLoop, calls=%fused_computation.6 | loop fusion | bytes 1441808 | tf_op jit(solution)/shard_map/dynamic_slice | solution.py:302
  1.2 2.4 %collective-permute-start.2 = (bf16[64,1408]{1,0:T(8,128)(2,1)S(1)}, bf16[64,1408]{1,0:T(8,128)(2,1)S(1)}, u32[]{:S(2)}, u32[]{:S(2)}) collective-permute-start(bf16[64,1408]{1,0:T(8,128)(2,1)S(1)} %get-tuple-element.53), channel_id=1, source_target_pairs={{0,24},{8,16},{16,8},{24,0},{1,25},{9,17},{17,9},{25,1},{2,26},{10... | collective-permute-start | bytes 540680 | tf_op jit(solution)/shard_map/ppermute | solution.py:304
  3.7 0.7 collective-permute-start
  4.4 0.0 collective-permute-start.1
  4.4 0.7 pad_bitcast_fusion.table_ref
  5.1 0.3 collective-permute-done.pair_ref.refs_1_
  5.4 7.3 %early.1 = (bf16[5120,128]{1,0:T(8,128)(2,1)S(1)}, s32[40,128]{1,0:T(8,128)S(1)}, s32[24,128]{1,0:T(8,128)S(1)}, bf16[96,4224]{1,0:T(8,128)(2,1)S(1)}, bf16[3,14...) custom-call(s32[4]{0:T(128)S(1)} %get-tuple-element.58.order_ref, ...), custom_call_target="tpu_custom_call" | custom-call | bytes 19464192 | tf_op jit(solution)/shard_map/early/pallas_call | solution.py:335
  12.8 0.0 collective-permute-done.1.refs_2_
  12.8 4.2 %design.1 = (bf16[256,4224]{1,0:T(8,128)(2,1)S(1)}, bf16[3,1408,512]{2,1,0:T(8,128)(2,1)S(1)}, bf16[3,1408,512]{2,1,0:T(8,128)(2,1)S(1)}) custom-call(s32[4]{0:T(128)S(1)} %get-tuple-element.58.order_ref, s32[4]{0:T(128)S(1)} %get-tuple-element.57.place_ref, bf16[96,4224]{1,0:T(8,128)(2,1)S(1)} %get-tuple-element.32.early_ref, f32[3,16,1408]{2,1,0:T(8,128)S(1)} %bitcast.6, ...), custom_call_target="tpu_custom_call" | custom-call | bytes 8650752 | tf_op jit(solution)/shard_map/design/pallas_call | solution.py:365
  17.0 2.7 %product.5 = (bf16[128,512]{1,0:T(8,128)(2,1)S(1)}, bf16[128,512]{1,0:T(8,128)(2,1)S(1)}, bf16[3,1408,256]{2,1,0:T(8,128)(2,1)S(1)}) custom-call(bf16[256,4224]{1,0:T(8,128)(2,1)S(1)} %get-tuple-element.33.design_ref, bf16[3,1408,512]{2,1,0:T(8,128)(2,1)S(1)} %get-tuple-element.34.refs_0_, bf16[3,1408,5120]{2,1,0:T(8,128)(2,1)} %refs_3_.1), custom_call_target="tpu_custom_call" | custom-call | flops 1107296256 | bytes 4325376 | tf_op jit(solution)/shard_map/product/pallas_call | solution.py:219
  19.6 0.4 collective-permute-start.3
  20.1 3.1 %product.6 = (bf16[128,1024]{1,0:T(8,128)(2,1)S(1)}, bf16[128,1024]{1,0:T(8,128)(2,1)S(1)}, bf16[3,1408,512]{2,1,0:T(8,128)(2,1)S(1)}, bf16[3,1408,256]{2,1,0:T(8,128)(2,1)S(1)}) custom-call(bf16[256,4224]{1,0:T(8,128)(2,1)S(1)} %get-tuple-element.33.design_ref, bf16[3,1408,1024]{2,1,0:T(8,128)(2,1)S(1)} %get-tuple-element.37.refs_0_, ...), custom_call_target="tpu_custom_call" | custom-call | flops 2214592512 | bytes 8650752 | tf_op jit(solution)/shard_map/product/pallas_call | solution.py:219
  23.2 0.2 collective-permute-start.5
  23.4 0.0 collective-permute-done.3.refs_1_
  23.4 2.2 %collective-permute-start.4 = (bf16[64,512]{1,0:T(8,128)(2,1)S(1)}, bf16[64,512]{1,0:T(8,128)(2,1)S(1)}, u32[]{:S(2)}, u32[]{:S(2)}) collective-permute-start(bf16[64,512]{1,0:T(8,128)(2,1)S(1)} %add_convert_fusion.4.refs_2_), channel_id=1, source_target_pairs={{0,16},{8,24},{16,0},{24,8},{1,17},{9,25},{17,1},{25,9},{2,18},{10... | collective-permute-start | bytes 196616 | tf_op jit(solution)/shard_map/ppermute | solution.py:391
  25.6 5.6 %product.7 = (bf16[128,1280]{1,0:T(8,128)(2,1)S(1)}, bf16[128,1280]{1,0:T(8,128)(2,1)S(1)}, bf16[3,1408,768]{2,1,0:T(8,128)(2,1)S(1)}) custom-call(bf16[256,4224]{1,0:T(8,128)(2,1)S(1)} %get-tuple-element.33.design_ref, bf16[3,1408,768]{2,1,0:T(8,128)(2,1)S(1)} %get-tuple-element.40.refs_0_, bf16[3,1408,512]{2,1,0:T(8,128)(2,1)S(1)} %get-tuple-element.41.refs_1_, ...), custom_call_target="tpu_custom_call" | custom-call | flops 2768240640 | bytes 10813440 | tf_op jit(solution)/shard_map/product/pallas_call | solution.py:219
  31.2 0.1 collective-permute-start.7
  31.4 0.2 collective-permute-start.6
  31.5 3.0 %product.8 = (bf16[128,1280]{1,0:T(8,128)(2,1)S(1)}, bf16[128,1280]{1,0:T(8,128)(2,1)S(1)}) custom-call(bf16[256,4224]{1,0:T(8,128)(2,1)S(1)} %get-tuple-element.33.design_ref, bf16[3,1408,512]{2,1,0:T(8,128)(2,1)S(1)} %get-tuple-element.44.refs_0_, bf16[3,1408,256]{2,1,0:T(8,128)(2,1)S(1)} %get-tuple-element.45.refs_1_, ...), custom_call_target="tpu_custom_call" | custom-call | flops 2768240640 | bytes 10813440 | tf_op jit(solution)/shard_map/product/pallas_call | solution.py:219
  34.6 0.5 collective-permute-start.9
  35.1 1.8 %collective-permute-start.8 = (bf16[64,1280]{1,0:T(8,128)(2,1)S(1)}, bf16[64,1280]{1,0:T(8,128)(2,1)S(1)}, u32[]{:S(2)}, u32[]{:S(2)}) collective-permute-start(bf16[64,1280]{1,0:T(8,128)(2,1)S(1)} %add_convert_fusion.1.refs_2_), channel_id=1, source_target_pairs={{0,16},{8,24},{16,0},{24,8},{1,17},{9,25},{17,1},{25,9},{2,18},{10... | collective-permute-start | bytes 491528 | tf_op jit(solution)/shard_map/ppermute | solution.py:391
  36.9 0.4 collective-permute-done.6.refs_5_.refs_3_
  37.3 2.5 %product.9 = (bf16[128,1024]{1,0:T(8,128)(2,1)S(1)}, bf16[128,1024]{1,0:T(8,128)(2,1)S(1)}) custom-call(bf16[256,4224]{1,0:T(8,128)(2,1)S(1)} %get-tuple-element.33.design_ref, bf16[3,1408,256]{2,1,0:T(8,128)(2,1)S(1)} %get-tuple-element.49.refs_0_, bf16[3,1408,768]{2,1,0:T(8,128)(2,1)S(1)} %get-tuple-element.50.refs_1_, ...), custom_call_target="tpu_custom_call" | custom-call | flops 2214592512 | bytes 8650752 | tf_op jit(solution)/shard_map/product/pallas_call | solution.py:219
  39.8 0.1 collective-permute-start.11
  39.9 0.4 collective-permute-start.10
  40.3 1.1 %collective-permute-done.11.refs_2_ = bf16[128,1024]{1,0:T(8,128)(2,1)S(1)} collective-permute-done((bf16[128,1024]{1,0:T(8,128)(2,1)S(1)}, bf16[128,1024]{1,0:T(8,128)(2,1)S(1)}, u32[]{:S(2)}, u32[]{:S(2)}) %collective-permute-start.11) | collective-permute-done | bytes 262176 | tf_op jit(solution)/shard_map/ppermute | solution.py:391
  41.4 0.7 collective-permute-start.12
  42.1 4.9 %collective-permute-done.10.refs_11_ = bf16[64,1280]{1,0:T(8,128)(2,1)S(1)} collective-permute-done((bf16[64,1280]{1,0:T(8,128)(2,1)S(1)}, bf16[64,1280]{1,0:T(8,128)(2,1)S(1)}, u32[]{:S(2)}, u32[]{:S(2)}) %collective-permute-start.10) | collective-permute-done | bytes 163872 | tf_op jit(solution)/shard_map/ppermute | solution.py:391
  47.0 5.5 %pack.2.refs_0_ = bf16[8,64,1664]{2,1,0:T(8,128)(2,1)S(1)} custom-call(s32[24,128]{1,0:T(8,128)S(1)} %get-tuple-element.29.start_ref, bf16[5120,128]{1,0:T(8,128)(2,1)S(1)} %get-tuple-element.30.onehot_ref, s32[40,128]{1,0:T(8,128)S(1)} %get-tuple-element.31.tile_ref, bf16[128,512]{1,0:T(8,128)(2,1)S(1)} %get-tuple-element.35.refs_0_, ...), custom_call_target="tpu_custom_call" | custom-call | tf_op jit(solution)/shard_map/pack/pallas_call | solution.py:401
  52.5 2.1 %pack.3 = bf16[8,64,1280]{2,1,0:T(8,128)(2,1)S(1)} custom-call(s32[24,128]{1,0:T(8,128)S(1)} %get-tuple-element.29.start_ref, bf16[5120,128]{1,0:T(8,128)(2,1)S(1)} %get-tuple-element.30.onehot_ref, s32[40,128]{1,0:T(8,128)S(1)} %get-tuple-element.31.tile_ref, bf16[8,64,1664]{2,1,0:T(8,128)(2,1)S(1)} %pack.2.refs_0_, ...), custom_call_target="tpu_custom_call" | custom-call | tf_op jit(solution)/shard_map/pack/pallas_call | solution.py:401
  54.7 36.5 %all_to_all.5 = bf16[8,64,1280]{2,1,0:T(8,128)(2,1)S(1)} all-to-all(bf16[8,64,1280]{2,1,0:T(8,128)(2,1)S(1)} %pack.3), channel_id=1, replica_groups=mesh['chan'=4,'vox'=8] {'vox'}, dimensions={0} | all-to-all | bytes 2621440 | tf_op jit(solution)/shard_map/all_to_all | solution.py:414
  91.2 1.1 %copy.7 = bf16[8,1280,64]{1,2,0:T(8,128)(2,1)} copy(bf16[8,1280,64]{1,2,0:T(8,128)(2,1)S(1)} %bitcast.7) | data formatting | bytes 2621440
  (15 shorter events, 0.2 us)
Async XLA Ops:
  1.2 11.5 %collective-permute-start.2 = (bf16[64,1408]{1,0:T(8,128)(2,1)S(1)}, bf16[64,1408]{1,0:T(8,128)(2,1)S(1)}, u32[]{:S(2)}, u32[]{:S(2)}) collective-permute-start(bf16[64,1408]{1,0:T(8,128)(2,1)S(1)} %get-tuple-element.53), channel_id=1, source_target_pairs={{0,24},{8,16},{16,8},{24,0},{1,25},{9,17},{17,9},{25,1},{2,26},{10... | collective-permute-start | bytes 540680 | tf_op jit(solution)/shard_map/ppermute | solution.py:304
  3.7 1.7 %collective-permute-start = (bf16[64,1408]{1,0:T(8,128)(2,1)S(1)}, bf16[64,1408]{1,0:T(8,128)(2,1)S(1)}, u32[]{:S(2)}, u32[]{:S(2)}) collective-permute-start(bf16[64,1408]{1,0:T(8,128)(2,1)S(1)} %get-tuple-element.54), channel_id=1, source_target_pairs={{0,8},{8,0},{16,24},{24,16},{1,9},{9,1},{17,25},{25,17},{2,10},{10... | collective-permute-start | bytes 540680 | tf_op jit(solution)/shard_map/ppermute | solution.py:304
  4.4 8.4 %collective-permute-start.1 = (bf16[64,1408]{1,0:T(8,128)(2,1)S(1)}, bf16[64,1408]{1,0:T(8,128)(2,1)S(1)}, u32[]{:S(2)}, u32[]{:S(2)}) collective-permute-start(bf16[64,1408]{1,0:T(8,128)(2,1)S(1)} %get-tuple-element.56), channel_id=1, source_target_pairs={{0,16},{8,24},{16,0},{24,8},{1,17},{9,25},{17,1},{25,9},{2,18},{10... | collective-permute-start | bytes 540680 | tf_op jit(solution)/shard_map/ppermute | solution.py:304
  5.4 7.4 %copy-start = (f32[3,1408,16]{1,2,0:T(8,128)S(1)}, f32[3,1408,16]{1,2,0:T(8,128)}, u32[]{:S(2)}) copy-start(f32[3,1408,16]{1,2,0:T(8,128)} %param.6) | copy-start | bytes 811012
  19.6 3.7 %collective-permute-start.3 = (bf16[128,512]{1,0:T(8,128)(2,1)S(1)}, bf16[128,512]{1,0:T(8,128)(2,1)S(1)}, u32[]{:S(2)}, u32[]{:S(2)}) collective-permute-start(bf16[128,512]{1,0:T(8,128)(2,1)S(1)} %get-tuple-element.36), channel_id=1, source_target_pairs={{0,8},{8,0},{16,24},{24,16},{1,9},{9,1},{17,25},{25,17},{2,10},{10... | collective-permute-start | bytes 393224 | tf_op jit(solution)/shard_map/ppermute | solution.py:391
  23.2 8.2 %collective-permute-start.5 = (bf16[128,1024]{1,0:T(8,128)(2,1)S(1)}, bf16[128,1024]{1,0:T(8,128)(2,1)S(1)}, u32[]{:S(2)}, u32[]{:S(2)}) collective-permute-start(bf16[128,1024]{1,0:T(8,128)(2,1)S(1)} %get-tuple-element.39), channel_id=1, source_target_pairs={{0,8},{8,0},{16,24},{24,16},{1,9},{9,1},{17,25},{25,17},{2,10},{10... | collective-permute-start | bytes 786440 | tf_op jit(solution)/shard_map/ppermute | solution.py:391
  23.4 8.2 %collective-permute-start.4 = (bf16[64,512]{1,0:T(8,128)(2,1)S(1)}, bf16[64,512]{1,0:T(8,128)(2,1)S(1)}, u32[]{:S(2)}, u32[]{:S(2)}) collective-permute-start(bf16[64,512]{1,0:T(8,128)(2,1)S(1)} %add_convert_fusion.4.refs_2_), channel_id=1, source_target_pairs={{0,16},{8,24},{16,0},{24,8},{1,17},{9,25},{17,1},{25,9},{2,18},{10... | collective-permute-start | bytes 196616 | tf_op jit(solution)/shard_map/ppermute | solution.py:391
  31.2 3.8 %collective-permute-start.7 = (bf16[128,1280]{1,0:T(8,128)(2,1)S(1)}, bf16[128,1280]{1,0:T(8,128)(2,1)S(1)}, u32[]{:S(2)}, u32[]{:S(2)}) collective-permute-start(bf16[128,1280]{1,0:T(8,128)(2,1)S(1)} %get-tuple-element.43), channel_id=1, source_target_pairs={{0,8},{8,0},{16,24},{24,16},{1,9},{9,1},{17,25},{25,17},{2,10},{10... | collective-permute-start | bytes 983048 | tf_op jit(solution)/shard_map/ppermute | solution.py:391
  31.4 6.0 %collective-permute-start.6 = (bf16[64,1024]{1,0:T(8,128)(2,1)S(1)}, bf16[64,1024]{1,0:T(8,128)(2,1)S(1)}, u32[]{:S(2)}, u32[]{:S(2)}) collective-permute-start(bf16[64,1024]{1,0:T(8,128)(2,1)S(1)} %add_convert_fusion.3.refs_3_), channel_id=1, source_target_pairs={{0,16},{8,24},{16,0},{24,8},{1,17},{9,25},{17,1},{25,9},{2,18},{10... | collective-permute-start | bytes 393224 | tf_op jit(solution)/shard_map/ppermute | solution.py:391
  34.6 5.3 %collective-permute-start.9 = (bf16[128,1280]{1,0:T(8,128)(2,1)S(1)}, bf16[128,1280]{1,0:T(8,128)(2,1)S(1)}, u32[]{:S(2)}, u32[]{:S(2)}) collective-permute-start(bf16[128,1280]{1,0:T(8,128)(2,1)S(1)} %get-tuple-element.48), channel_id=1, source_target_pairs={{0,8},{8,0},{16,24},{24,16},{1,9},{9,1},{17,25},{25,17},{2,10},{10... | collective-permute-start | bytes 983048 | tf_op jit(solution)/shard_map/ppermute | solution.py:391
  35.1 7.0 %collective-permute-start.8 = (bf16[64,1280]{1,0:T(8,128)(2,1)S(1)}, bf16[64,1280]{1,0:T(8,128)(2,1)S(1)}, u32[]{:S(2)}, u32[]{:S(2)}) collective-permute-start(bf16[64,1280]{1,0:T(8,128)(2,1)S(1)} %add_convert_fusion.1.refs_2_), channel_id=1, source_target_pairs={{0,16},{8,24},{16,0},{24,8},{1,17},{9,25},{17,1},{25,9},{2,18},{10... | collective-permute-start | bytes 491528 | tf_op jit(solution)/shard_map/ppermute | solution.py:391
  39.8 1.6 %collective-permute-start.11 = (bf16[128,1024]{1,0:T(8,128)(2,1)S(1)}, bf16[128,1024]{1,0:T(8,128)(2,1)S(1)}, u32[]{:S(2)}, u32[]{:S(2)}) collective-permute-start(bf16[128,1024]{1,0:T(8,128)(2,1)S(1)} %get-tuple-element.52), channel_id=1, source_target_pairs={{0,8},{8,0},{16,24},{24,16},{1,9},{9,1},{17,25},{25,17},{2,10},{10... | collective-permute-start | bytes 786440 | tf_op jit(solution)/shard_map/ppermute | solution.py:391
  39.9 7.1 %collective-permute-start.10 = (bf16[64,1280]{1,0:T(8,128)(2,1)S(1)}, bf16[64,1280]{1,0:T(8,128)(2,1)S(1)}, u32[]{:S(2)}, u32[]{:S(2)}) collective-permute-start(bf16[64,1280]{1,0:T(8,128)(2,1)S(1)} %add_convert_fusion), channel_id=1, source_target_pairs={{0,16},{8,24},{16,0},{24,8},{1,17},{9,25},{17,1},{25,9},{2,18},{10... | collective-permute-start | bytes 491528 | tf_op jit(solution)/shard_map/ppermute | solution.py:391
  41.4 11.1 %collective-permute-start.12 = (bf16[64,1024]{1,0:T(8,128)(2,1)S(1)}, bf16[64,1024]{1,0:T(8,128)(2,1)S(1)}, u32[]{:S(2)}, u32[]{:S(2)}) collective-permute-start(bf16[64,1024]{1,0:T(8,128)(2,1)S(1)} %add_convert_fusion.2), channel_id=1, source_target_pairs={{0,16},{8,24},{16,0},{24,8},{1,17},{9,25},{17,1},{25,9},{2,18},{10... | collective-permute-start | bytes 393224 | tf_op jit(solution)/shard_map/ppermute | solution.py:391

commit v7 on v6

--- a/solution.py
+++ b/solution.py
@@ -14,9 +14,9 @@
 VOX_BLOCK = 256
 COLUMNS = 512
 ROWS = 32
-CHUNKS = 5
-COPIES = (((0, 2), (1, 4), (2, 3)), ((2, 2), (3, 2)), ((3, 1),), ((3, 2), (4, 1)), ((4, 3),))
-PACK_FIRST = 4
+CHUNKS = 4
+COPIES = (((0, 5), (1, 4)), ((1, 2), (2, 2)), ((2, 2),), ((2, 2),), ((3, 3),))
+PACK_FIRST = 3
 MIB = 1 << 20
 
 VMEM = functools.partial(pl.BlockSpec, memory_space=pltpu.VMEM)
@@ -30,11 +30,12 @@
     for i, ref in enumerate(piece_refs):
         if ref.shape[1] > depth:
             ref[:, depth:, :] = jnp.zeros_like(ref[:, depth:, :])
-        copy = pltpu.make_async_copy(
-            weight_ref.at[:, :, pl.ds(first, ref.shape[2])], ref.at[:, pl.ds(0, depth), :], sems.at[i]
-        )
-        copy.start()
-        copies.append(copy)
+        for b in range(ref.shape[0]):
+            copy = pltpu.make_async_copy(
+                weight_ref.at[b, :, pl.ds(first, ref.shape[2])], ref.at[b, pl.ds(0, depth), :], sems.at[i, b]
+            )
+            copy.start()
+            copies.append(copy)
         first += ref.shape[2]
     return copies
 
@@ -69,22 +70,29 @@
     ahead, block_ahead = below((rows, rows)), below((marks, rows), VOX_BLOCK // LANES)
     mark_lane = lax.broadcasted_iota(jnp.int32, (marks, LANES), 1)
     dot = functools.partial(jnp.dot, preferred_element_type=jnp.float32)
+    row_block = lax.broadcasted_iota(jnp.int32, (rows, rows), 0) & -(VOX_BLOCK // LANES)
+    before = lax.broadcasted_iota(jnp.int32, (rows, rows), 1) < row_block
+    before = before.astype(jnp.float32).astype(jnp.bfloat16)
     slots = jnp.zeros(parcel.shape, jnp.float32)
+    bases = jnp.zeros(parcel.shape, jnp.float32)
     starts = jnp.zeros((marks, LANES), jnp.float32)
     for o in range(owners):
         mine = owner == o
         hot = mine.astype(jnp.float32).astype(jnp.bfloat16)
         totals = dot(hot, ones).astype(jnp.bfloat16)
         slots = jnp.where(mine, dot(hot, above) + dot(ahead, totals), slots)
+        bases = jnp.where(mine, dot(before, totals), bases)
         starts = jnp.where(mark_lane == o, dot(block_ahead, totals), starts)
     slots = slots.astype(jnp.int32)
     start_ref[...] = starts.astype(jnp.int32)
     tile_ref[...] = owner * spread + (slots >> 7)
-    inner = slots & 127
+    inner = (slots - (bases.astype(jnp.int32) & -SLOT_TILE)) & (2 * SLOT_TILE - 1)
     for row in range(rows):
-        line = jnp.broadcast_to(inner[row : row + 1, :], (LANES, LANES))
-        hit = jnp.where(line.T == lane, 1.0, 0.0)
-        onehot_ref[row * LANES : (row + 1) * LANES, :] = hit.astype(jnp.bfloat16)
+        line = jnp.broadcast_to(inner[row : row + 1, :], (LANES, LANES)).T
+        for side in range(2):
+            hit = jnp.where(line == lane + side * LANES, 1.0, 0.0)
+            at = slice(side * LANES, (side + 1) * LANES)
+            onehot_ref[row * LANES : (row + 1) * LANES, at] = hit.astype(jnp.bfloat16)
 
 
 def clear_lead(shifted):
@@ -119,10 +127,9 @@
 
 
 def early_kernel(owners, spread, order_ref, own_ref, pair_ref, parcel_hbm, table_ref, filter_hbm, weight_ref, *refs):
-    onehot_ref, tile_ref, start_ref, design_ref, *piece_refs, plain, shifted, filter_ref, parcel_ref, sems = refs
-    count = len(piece_refs)
-    load_filter = pltpu.make_async_copy(filter_hbm, filter_ref, sems.at[count])
-    load_parcel = pltpu.make_async_copy(parcel_hbm, parcel_ref, sems.at[count + 1])
+    onehot_ref, tile_ref, start_ref, design_ref, *piece_refs, plain, shifted, filter_ref, parcel_ref, sems, small_sems = refs
+    load_filter = pltpu.make_async_copy(filter_hbm, filter_ref, small_sems.at[0])
+    load_parcel = pltpu.make_async_copy(parcel_hbm, parcel_ref, small_sems.at[1])
     load_filter.start()
     load_parcel.start()
     copies = copy_pieces(weight_ref, piece_refs, sems, 0)
@@ -221,44 +228,58 @@
         in_specs=[VMEM()] * (1 + len(taken)) + [ANY()] * (len(after) + bool(ahead)),
         out_specs=[VMEM()] * (2 + len(ahead)),
         out_shape=[half, half] + ahead,
-        scratch_shapes=[pltpu.SemaphoreType.DMA((len(ahead),))] if ahead else [],
-        compiler_params=pltpu.CompilerParams(vmem_limit_bytes=10 * MIB),
+        scratch_shapes=[pltpu.SemaphoreType.DMA((len(ahead), weights.shape[0]))] if ahead else [],
+        compiler_params=pltpu.CompilerParams(vmem_limit_bytes=8 * MIB),
         cost_estimate=cost(2 * time_len * lanes * width, 2 * lanes * width),
         name="product",
     )(design, *taken, *after, *([weights] if ahead else []))
 
 
-def pack_kernel(spread, widths, first, start_ref, onehot_ref, tile_ref, *refs):
+def late_kernel(each, first, *refs):
+    out_ref, at = refs[-1], 0
+    for c in range(0, len(refs) - 3, each):
+        terms, width = refs[c : c + each], refs[c].shape[1]
+        total = sum(term[first : first + out_ref.shape[0], :].astype(jnp.float32) for term in terms)
+        out_ref[:, at : at + width] = total.astype(jnp.bfloat16)
+        at += width
+
+
+def pack_kernel(spread, widths, places, first, extra, start_ref, onehot_ref, tile_ref, *refs):
     *terms, out_ref, summed, packed = refs
-    owners, time_block = packed.shape[:2]
+    terms = terms[: len(terms) - extra]
+    owners, rows = packed.shape[:2]
     if first:
         packed[...] = terms.pop(0)[...]
     else:
         packed[...] = jnp.zeros_like(packed)
-    each, at = len(terms) // len(widths), 0
-    for c, width in enumerate(widths):
-        total = sum(term[:time_block, :].astype(jnp.float32) for term in terms[c * each : (c + 1) * each])
+    at = 0
+    for width, spots in zip(widths, places):
+        total = 0.0
+        for row, column in spots:
+            total = total + terms.pop(0)[row : row + rows, column : column + width].astype(jnp.float32)
         summed[:, at : at + width] = total.astype(jnp.bfloat16)
         at += width
     step = VOX_BLOCK // LANES
 
-    def moves(index, extras):
+    def moves(index, far):
         block = first + index
         values = summed[:, pl.ds(pl.multiple_of(index * VOX_BLOCK, VOX_BLOCK), VOX_BLOCK)]
         onehot = onehot_ref[pl.ds(pl.multiple_of(block * VOX_BLOCK, VOX_BLOCK), VOX_BLOCK), :]
         tiles = jnp.concatenate([tile_ref[pl.ds(block * step + i, 1), :] for i in range(step)], axis=1)
         low = [start_ref[block, o] >> 7 for o in range(owners)]
-        targets = [(o, low[o] + extra) for extra in extras for o in range(owners)]
-        rows = []
-        for owner, tile in targets:
-            hit = jnp.where(tiles == owner * spread + tile, 1.0, 0.0)
-            rows.append(values * hit.astype(jnp.bfloat16))
-        moved = jnp.dot(jnp.concatenate(rows, axis=0), onehot, preferred_element_type=jnp.float32)
+        chosen = []
+        for o in range(owners):
+            tile = tiles - (o * spread + low[o])
+            hit = jnp.where((tile == 2) if far else ((tile == 0) | (tile == 1)), 1.0, 0.0)
+            chosen.append(values * hit.astype(jnp.bfloat16))
+        moved = jnp.dot(jnp.concatenate(chosen, axis=0), onehot, preferred_element_type=jnp.float32)
         moved = moved.astype(jnp.bfloat16)
         out = []
-        for i, (owner, tile) in enumerate(targets):
-            lanes = pl.ds(pl.multiple_of(tile * SLOT_TILE, SLOT_TILE), SLOT_TILE)
-            out.append((owner, lanes, moved[i * time_block : (i + 1) * time_block]))
+        for o in range(owners):
+            here = moved[o * rows : (o + 1) * rows]
+            tile, here = (low[o] + 2, here[:, :SLOT_TILE]) if far else (low[o], here)
+            lanes = pl.ds(pl.multiple_of(tile * SLOT_TILE, SLOT_TILE), here.shape[1])
+            out.append((o, lanes, here))
         high = [(start_ref[block + 1, o] - 1) >> 7 for o in range(owners)]
         return out, functools.reduce(jnp.maximum, [high[o] - low[o] for o in range(owners)])
 
@@ -268,14 +289,14 @@
             packed[owner, :, lanes] = total
 
     def blocks(indices):
-        found = [moves(index, range(2)) for index in indices]
+        found = [moves(index, False) for index in indices]
         for targets, _ in found:
             add(targets)
         for index, (_, longest) in zip(indices, found):
 
             @pl.when(longest > 1)
             def _():
-                add(moves(index, (2,))[0])
+                add(moves(index, True)[0])
 
     count = sum(widths) // VOX_BLOCK
 
@@ -337,7 +358,7 @@
         in_specs=[SMEM(), VMEM(), VMEM(), HBM(), VMEM(), HBM(), ANY()],
         out_specs=[VMEM()] * (4 + len(COPIES[0])),
         out_shape=[
-            jax.ShapeDtypeStruct((voxels, LANES), jnp.bfloat16),
+            jax.ShapeDtypeStruct((voxels, 2 * SLOT_TILE), jnp.bfloat16),
             jax.ShapeDtypeStruct((voxels // LANES, LANES), jnp.int32),
             jax.ShapeDtypeStruct((marks, LANES), jnp.int32),
             jax.ShapeDtypeStruct((early_rows, lanes), jnp.bfloat16),
@@ -347,9 +368,10 @@
         + [
             pltpu.VMEM(filters.shape, jnp.float32),
             pltpu.VMEM((voxels // LANES, LANES), jnp.int32),
-            pltpu.SemaphoreType.DMA((len(COPIES[0]) + 2,)),
+            pltpu.SemaphoreType.DMA((len(COPIES[0]), bases)),
+            pltpu.SemaphoreType.DMA((2,)),
         ],
-        compiler_params=pltpu.CompilerParams(vmem_limit_bytes=10 * MIB),
+        compiler_params=pltpu.CompilerParams(vmem_limit_bytes=8 * MIB),
         cost_estimate=cost(0, 2 * bases * depth * copied[0]),
         name="early",
     )(
@@ -367,14 +389,15 @@
         in_specs=[SMEM(), SMEM(), VMEM(), VMEM(), ANY()] + [VMEM()] * parts,
         out_specs=[VMEM()] * (1 + len(COPIES[1])),
         out_shape=[jax.ShapeDtypeStruct((time_len, lanes), jnp.bfloat16)] + room(1),
-        scratch_shapes=filter_scratch(time_len) + [pltpu.SemaphoreType.DMA((len(COPIES[1]),))],
-        compiler_params=pltpu.CompilerParams(vmem_limit_bytes=10 * MIB),
+        scratch_shapes=filter_scratch(time_len) + [pltpu.SemaphoreType.DMA((len(COPIES[1]), bases))],
+        compiler_params=pltpu.CompilerParams(vmem_limit_bytes=8 * MIB),
         cost_estimate=cost(0, 2 * bases * depth * copied[1]),
         name="design",
     )(order, place, early, filters, weights, *series)
     keep_pieces(1, pieces)
 
-    widths, terms, sent, got = [], [], [], []
+    half = time_block // 2
+    widths, sums, sent, got = [], [], [], []
     for c in range(CHUNKS):
         after = sent[max(c - 2, 0) : max(c - 1, 0)] + got[max(c - 3, 0) : max(c - 2, 0)]
         ahead = room(c + 2)
@@ -385,34 +408,55 @@
         for bit in range(bits):
             if bit > 0:
                 rows = own[-1].shape[0] // 2
-                send = sum(term[rows : 2 * rows].astype(jnp.float32) for term in own).astype(jnp.bfloat16)
-                if bit == 1:
+                send = added(own, rows, half if bit == bits - 1 else rows)
+                if bit == bits - 1:
                     sent.append(send)
             own.append(lax.ppermute(send, "chan", [(i, i ^ (1 << bit)) for i in range(parts)]))
-        terms.append(own)
+        sums.append(own)
         got.append(own[-1])
-
-    packed = []
-    for low, high in ((0, PACK_FIRST), (PACK_FIRST, CHUNKS)):
-        args = packed + [term for own in terms[low:high] for term in own]
+    def pack(low, high, second, packed, after=()):
+        terms, spots = [], []
+        for c in range(low, high):
+            own = sums[c][:-1]
+            terms += own + [late if second else got[c]]
+            spots.append([(half if second else 0, 0)] * len(own) + [(0, sum(widths[:c]) if second else 0)])
         here = widths[low:high]
-        room_here = send_cap if high == CHUNKS else spread * SLOT_TILE
-        packed = [
-            pl.pallas_call(
-                functools.partial(pack_kernel, spread, here, sum(widths[:low]) // VOX_BLOCK),
-                in_specs=[SMEM(), VMEM(), VMEM()] + [VMEM()] * len(args),
-                out_specs=VMEM(),
-                out_shape=jax.ShapeDtypeStruct((owners, time_block, room_here), jnp.bfloat16),
-                scratch_shapes=[
-                    pltpu.VMEM((time_block, sum(here)), jnp.bfloat16),
-                    pltpu.VMEM((owners, time_block, spread * SLOT_TILE), jnp.bfloat16),
-                ],
-                compiler_params=pltpu.CompilerParams(vmem_limit_bytes=14 * MIB),
-                name="pack",
-            )(starts, onehot, tiles, *args)
-        ]
-    received = lax.all_to_all(packed[0], "vox", split_axis=0, concat_axis=0, tiled=True)
-    return jnp.transpose(received, (0, 2, 1))
+        lanes_out = send_cap if high == CHUNKS else spread * SLOT_TILE
+        return pl.pallas_call(
+            functools.partial(pack_kernel, spread, here, spots, sum(widths[:low]) // VOX_BLOCK, len(after)),
+            in_specs=[SMEM(), VMEM(), VMEM()] + [VMEM()] * (len(packed) + len(terms)) + [ANY()] * len(after),
+            out_specs=VMEM(),
+            out_shape=jax.ShapeDtypeStruct((owners, half, lanes_out), jnp.bfloat16),
+            scratch_shapes=[
+                pltpu.VMEM((half, sum(here)), jnp.bfloat16),
+                pltpu.VMEM((owners, half, spread * SLOT_TILE), jnp.bfloat16),
+            ],
+            compiler_params=pltpu.CompilerParams(vmem_limit_bytes=8 * MIB),
+            cost_estimate=cost(2 * half * owners * VOX_BLOCK * sum(here), 4 * half * sum(here)),
+            name="pack",
+        )(starts, onehot, tiles, *packed, *terms, *after)
+
+    def deliver(packed):
+        return lax.all_to_all(packed, "vox", split_axis=0, concat_axis=0, tiled=True)
+
+    packed = pack(0, PACK_FIRST, False, [])
+    late_terms = [term for own in sums for term in own[:-1]]
+    late_send = pl.pallas_call(
+        functools.partial(late_kernel, bits, time_block + half),
+        in_specs=[VMEM()] * len(late_terms) + [ANY()] * 2,
+        out_specs=VMEM(),
+        out_shape=jax.ShapeDtypeStruct((half, voxels), jnp.bfloat16),
+        compiler_params=pltpu.CompilerParams(vmem_limit_bytes=6 * MIB),
+        name="late",
+    )(*late_terms, got[-1], packed)
+    late = lax.ppermute(late_send, "chan", [(i, i ^ (1 << (bits - 1))) for i in range(parts)])
+    one = deliver(pack(PACK_FIRST, CHUNKS, False, [packed], [late_send]))
+    two = deliver(pack(0, CHUNKS, True, []))
+    return jnp.transpose(jnp.concatenate([one, two], axis=1), (0, 2, 1))
+
+
+def added(terms, first, rows):
+    return sum(term[first : first + rows].astype(jnp.float32) for term in terms).astype(jnp.bfloat16)
 
 
 def solution(mesh):

time: 92.5 us -> 105 us (1.14)
  blocking collectives: 36.5 us -> 21.2 us
  Pallas kernels: 36 us -> 43.4 us
  local copies, waits for them, and re-layouts: 2.99 us -> 10.2 us
  starting transfers between devices: 9.65 us -> 16.7 us
  waiting for transfers between devices: 6.72 us -> 10.1 us
  other arithmetic: 0.18 us -> 2.32 us
    all_to_all x1, blocking collectives: 36.5 us -> 21.2 us  [deliver(): lax.all_to_all(packed, 'vox', split_axis=0, concat_axis=0, tiled=True)]
    unnamed x3 -> x32, local copies, waits for them, and re-layouts: 1.06 us -> 8.23 us
    ppermute x0 -> x1, waiting for transfers between devices: none -> 7.03 us  [shards(): lax.ppermute(late_send, 'chan', [(i, i ^ 1 << bits - 1) for i in range(pa...]
    all_to_all x0 -> x1, starting transfers between devices: none -> 5.98 us  [deliver(): lax.all_to_all(packed, 'vox', split_axis=0, concat_axis=0, tiled=True)]
    pallas_call x1, Pallas kernels: 7.34 us -> 11.6 us  [shards(): pl.pallas_call(functools.partial(early_kernel, owners, spread), in_specs=...]
    ppermute x10 -> x8, waiting for transfers between devices: 6.41 us -> 2.71 us  [shards(): lax.ppermute(send, 'chan', [(i, i ^ 1 << bit) for i in range(parts)])]
    pallas_call x5 -> x4, Pallas kernels: 16.9 us -> 19.3 us  [product(): pl.pallas_call(functools.partial(product_kernel, len(taken), len(after),...]
    transpose x0 -> x1, other arithmetic: none -> 2.23 us  [shards(): return jnp.transpose(jnp.concatenate([one, two], axis=1), (0, 2, 1))]
  transfers between devices with their start and end apart: 13 -> 13, of which waited for: 4 -> 3; matrix products, arithmetic and copies ran while one was open for 1% -> 1% of each run, Pallas kernels for 29% -> 31%
where the time goes in v7:
time: 105 us; the launch traced here: 104 us
  Pallas kernels  43.4 us (41%)
  blocking collectives  21.2 us (20%)
  starting transfers between devices  16.7 us (16%)
  local copies, waits for them, and re-layouts  10.2 us (10%)
  waiting for transfers between devices  10.1 us (10%)
  other arithmetic  2.32 us (2%)
    all_to_all x1, blocking collectives, deliver(): lax.all_to_all(packed, 'vox', split_axis=0, concat_axis=0, tiled=True)  21.2 us
    pallas_call x4, Pallas kernels, product(): pl.pallas_call(functools.partial(product_kernel, len(taken), len(after),...  19.3 us
    pallas_call x1, Pallas kernels, shards(): pl.pallas_call(functools.partial(early_kernel, owners, spread), in_specs=...  11.6 us
    unnamed x32, local copies, waits for them, and re-layouts  8.23 us
    pallas_call x3, Pallas kernels, pack(): pl.pallas_call(functools.partial(pack_kernel, spread, here, spots, sum(wi...  8.18 us
    ppermute x1, waiting for transfers between devices, shards(): lax.ppermute(late_send, 'chan', [(i, i ^ 1 << bits - 1) for i in range(pa...  7.03 us
    ppermute x8, starting transfers between devices, shards(): lax.ppermute(send, 'chan', [(i, i ^ 1 << bit) for i in range(parts)])  6.07 us
    all_to_all x1, starting transfers between devices, deliver(): lax.all_to_all(packed, 'vox', split_axis=0, concat_axis=0, tiled=True)  5.98 us
  transfers between devices with their start and end apart: 13, of which 3 were waited for; matrix products, arithmetic and copies ran while one was open for 1% of the time, Pallas kernels for 31%

profile of v7, /device:TPU:0, one launch (start us, length us, event | category | flops | bytes accessed | tf_op | source)
XLA Modules:
  0.0 104.1 jit_solution(3474006252237281336)
XLA Ops:
  0.0 1.2 %constant_dynamic-slice_fusion = (bf16[64,1408]{1,0:T(8,128)(2,1)S(1)}, bf16[64,1408]{1,0:T(8,128)(2,1)S(1)}, bf16[64,1408]{1,0:T(8,128)(2,1)S(1)}, bf16[64,1408]{1,0:T(8,128)(2,1)S(1)}) fusion(bf16[64,5632]{1,0:T(8,128)(2,1)} %param.5, s32[]{:T(128)S(6)} %select_n.15, s32[]{:T(128)S(6)} %select_n.13, s32[]{:T(128)S(6)} %select_n.12, s32[]{:T(128)S(6)} %select_n.14), kind=kLoop, calls=%fused_computation.6 | loop fusion | bytes 1441808 | tf_op jit(solution)/shard_map/dynamic_slice | solution.py:323
  1.2 2.4 %collective-permute-start.2 = (bf16[64,1408]{1,0:T(8,128)(2,1)S(1)}, bf16[64,1408]{1,0:T(8,128)(2,1)S(1)}, u32[]{:S(2)}, u32[]{:S(2)}) collective-permute-start(bf16[64,1408]{1,0:T(8,128)(2,1)S(1)} %get-tuple-element.45), channel_id=1, source_target_pairs={{0,24},{8,16},{16,8},{24,0},{1,25},{9,17},{17,9},{25,1},{2,26},{10... | collective-permute-start | bytes 540680 | tf_op jit(solution)/shard_map/ppermute | solution.py:325
  3.7 0.7 collective-permute-start
  4.4 0.7 pad_bitcast_fusion.table_ref
  5.4 11.6 %early.1 = (bf16[5120,256]{1,0:T(8,128)(2,1)S(1)}, s32[40,128]{1,0:T(8,128)S(1)}, s32[24,128]{1,0:T(8,128)S(1)}, bf16[96,4224]{1,0:T(8,128)(2,1)S(1)}, bf16[3,14...) custom-call(s32[4]{0:T(128)S(1)} %get-tuple-element.50.order_ref, ...), custom_call_target="tpu_custom_call" | custom-call | bytes 19464192 | tf_op jit(solution)/shard_map/early/pallas_call | solution.py:356
  17.1 4.2 %design.1 = (bf16[256,4224]{1,0:T(8,128)(2,1)S(1)}, bf16[3,1408,512]{2,1,0:T(8,128)(2,1)S(1)}, bf16[3,1408,512]{2,1,0:T(8,128)(2,1)S(1)}) custom-call(s32[4]{0:T(128)S(1)} %get-tuple-element.50.order_ref, s32[4]{0:T(128)S(1)} %get-tuple-element.49.place_ref, bf16[96,4224]{1,0:T(8,128)(2,1)S(1)} %get-tuple-element.28.early_ref, f32[3,16,1408]{2,1,0:T(8,128)S(1)} %bitcast.7, ...), custom_call_target="tpu_custom_call" | custom-call | bytes 8650752 | tf_op jit(solution)/shard_map/design/pallas_call | solution.py:387
  21.3 5.2 %product.4 = (bf16[128,1280]{1,0:T(8,128)(2,1)S(1)}, bf16[128,1280]{1,0:T(8,128)(2,1)S(1)}, bf16[3,1408,512]{2,1,0:T(8,128)(2,1)S(1)}) custom-call(bf16[256,4224]{1,0:T(8,128)(2,1)S(1)} %get-tuple-element.29.design_ref, bf16[3,1408,1280]{2,1,0:T(8,128)(2,1)S(1)} %get-tuple-element.30.refs_0_, bf16[3,1408,5120]{2,1,0:T(8,128)(2,1)} %refs_4_.1), custom_call_target="tpu_custom_call" | custom-call | flops 2768240640 | bytes 10813440 | tf_op jit(solution)/shard_map/product/pallas_call | solution.py:226
  26.9 5.9 %product.5 = (bf16[128,1536]{1,0:T(8,128)(2,1)S(1)}, bf16[128,1536]{1,0:T(8,128)(2,1)S(1)}, bf16[3,1408,512]{2,1,0:T(8,128)(2,1)S(1)}) custom-call(bf16[256,4224]{1,0:T(8,128)(2,1)S(1)} %get-tuple-element.29.design_ref, bf16[3,1408,1024]{2,1,0:T(8,128)(2,1)S(1)} %get-tuple-element.33.refs_0_, bf16[3,1408,512]{2,1,0:T(8,128)(2,1)S(1)} %get-tuple-element.34.refs_1_, ...), custom_call_target="tpu_custom_call" | custom-call | flops 3321888768 | bytes 12976128 | tf_op jit(solution)/shard_map/product/pallas_call | solution.py:226
  33.0 1.7 %collective-permute-start.4 = (bf16[32,1280]{1,0:T(8,128)(2,1)S(1)}, bf16[32,1280]{1,0:T(8,128)(2,1)S(1)}, u32[]{:S(2)}, u32[]{:S(2)}) collective-permute-start(bf16[32,1280]{1,0:T(8,128)(2,1)S(1)} %add_convert_fusion.2.refs_3_), channel_id=1, source_target_pairs={{0,16},{8,24},{16,0},{24,8},{1,17},{9,25},{17,1},{25,9},{2,18},{10... | collective-permute-start | bytes 245768 | tf_op jit(solution)/shard_map/ppermute | solution.py:414
  34.8 6.4 %product.6 = (bf16[128,1536]{1,0:T(8,128)(2,1)S(1)}, bf16[128,1536]{1,0:T(8,128)(2,1)S(1)}, bf16[3,1408,768]{2,1,0:T(8,128)(2,1)S(1)}) custom-call(bf16[256,4224]{1,0:T(8,128)(2,1)S(1)} %get-tuple-element.29.design_ref, bf16[3,1408,512]{2,1,0:T(8,128)(2,1)S(1)} %get-tuple-element.37.refs_0_, bf16[3,1408,512]{2,1,0:T(8,128)(2,1)S(1)} %get-tuple-element.38.refs_1_, ...), custom_call_target="tpu_custom_call" | custom-call | flops 3321888768 | bytes 12976128 | tf_op jit(solution)/shard_map/product/pallas_call | solution.py:226
  41.3 0.5 collective-permute-start.6
  41.8 1.9 %product.7 = (bf16[128,768]{1,0:T(8,128)(2,1)S(1)}, bf16[128,768]{1,0:T(8,128)(2,1)S(1)}) custom-call(bf16[256,4224]{1,0:T(8,128)(2,1)S(1)} %get-tuple-element.29.design_ref, bf16[3,1408,768]{2,1,0:T(8,128)(2,1)S(1)} %get-tuple-element.42.refs_0_, bf16[32,1536]{1,0:T(8,128)(2,1)S(1)} %add_convert_fusion.1.refs_1_, ...), custom_call_target="tpu_custom_call" | custom-call | flops 1660944384 | bytes 6488064 | tf_op jit(solution)/shard_map/product/pallas_call | solution.py:226
  43.9 1.7 %collective-permute-start.8 = (bf16[32,1536]{1,0:T(8,128)(2,1)S(1)}, bf16[32,1536]{1,0:T(8,128)(2,1)S(1)}, u32[]{:S(2)}, u32[]{:S(2)}) collective-permute-start(bf16[32,1536]{1,0:T(8,128)(2,1)S(1)} %add_convert_fusion), channel_id=1, source_target_pairs={{0,16},{8,24},{16,0},{24,8},{1,17},{9,25},{17,1},{25,9},{2,18},{10... | collective-permute-start | bytes 294920 | tf_op jit(solution)/shard_map/ppermute | solution.py:414
  45.7 1.2 %collective-permute-start.10 = (bf16[32,768]{1,0:T(8,128)(2,1)S(1)}, bf16[32,768]{1,0:T(8,128)(2,1)S(1)}, u32[]{:S(2)}, u32[]{:S(2)}) collective-permute-start(bf16[32,768]{1,0:T(8,128)(2,1)S(1)} %add_convert_fusion.3), channel_id=1, source_target_pairs={{0,16},{8,24},{16,0},{24,8},{1,17},{9,25},{17,1},{25,9},{2,18},{10... | collective-permute-start | bytes 147464 | tf_op jit(solution)/shard_map/ppermute | solution.py:414
  46.9 2.7 %collective-permute-done.8.refs_8_ = bf16[32,1536]{1,0:T(8,128)(2,1)S(1)} collective-permute-done((bf16[32,1536]{1,0:T(8,128)(2,1)S(1)}, bf16[32,1536]{1,0:T(8,128)(2,1)S(1)}, u32[]{:S(2)}, u32[]{:S(2)}) %collective-permute-start.8) | collective-permute-done | bytes 98336 | tf_op jit(solution)/shard_map/ppermute | solution.py:414
  49.6 3.3 %pack.3.refs_9_.refs_0_ = bf16[8,32,1664]{2,1,0:T(8,128)(2,1)S(1)} custom-call(s32[24,128]{1,0:T(8,128)S(1)} %get-tuple-element.25.start_ref, bf16[5120,256]{1,0:T(8,128)(2,1)S(1)} %get-tuple-element.26.onehot_ref, s32[40,128]{1,0:T(8,128)S(1)} %get-tuple-element.27.tile_ref, bf16[128,1280]{1,0:T(8,128)(2,1)S(1)} %get-tuple-element.31.refs_0_, ...), custom_call_target="tpu_custom_call" | custom-call | flops 570425344 | bytes 557056 | tf_op jit(solution)/shard_map/pack/pallas_call | solution.py:425
  53.1 1.2 %pack.4 = bf16[8,32,1280]{2,1,0:T(8,128)(2,1)S(1)} custom-call(s32[24,128]{1,0:T(8,128)S(1)} %get-tuple-element.25.start_ref, bf16[5120,256]{1,0:T(8,128)(2,1)S(1)} %get-tuple-element.26.onehot_ref, s32[40,128]{1,0:T(8,128)S(1)} %get-tuple-element.27.tile_ref, bf16[8,32,1664]{2,1,0:T(8,128)(2,1)S(1)} %pack.3.refs_9_.refs_0_, ...), custom_call_target="tpu_custom_call" | custom-call | flops 100663296 | bytes 98304 | tf_op jit(solution)/shard_map/pack/pallas_call | solution.py:425
  54.3 0.8 copy-done.8
  55.2 0.7 copy-done.14
  55.9 6.0 %all-to-all-start = ((bf16[8,32,1280]{2,1,0:T(8,128)(2,1)}), bf16[8,32,1280]{2,1,0:T(8,128)(2,1)}, u32[]{:S(2)}, u32[]{:S(2)}) async-start(bf16[8,32,1280]{2,1,0:T(8,128)(2,1)} %copy-done.8), calls=%async_computation | async-start | bytes 1310720 | tf_op jit(solution)/shard_map/all_to_all | solution.py:440
  61.9 1.5 %collective-permute-start.11 = (bf16[32,5120]{1,0:T(8,128)(2,1)}, bf16[32,5120]{1,0:T(8,128)(2,1)S(1)}, u32[]{:S(2)}, u32[]{:S(2)}) collective-permute-start(bf16[32,5120]{1,0:T(8,128)(2,1)} %copy-done.14), channel_id=1, source_target_pairs={{0,16},{8,24},{16,0},{24,8},{1,17},{9,25},{17,1},{25,9},{2,18},{10... | collective-permute-start | bytes 983048 | tf_op jit(solution)/shard_map/ppermute | solution.py:452
  63.4 7.0 %collective-permute-done.11.refs_2_.refs_5_.refs_8_.refs_11_ = bf16[32,5120]{1,0:T(8,128)(2,1)S(1)} collective-permute-done((bf16[32,5120]{1,0:T(8,128)(2,1)}, bf16[32,5120]{1,0:T(8,128)(2,1)S(1)}, u32[]{:S(2)}, u32[]{:S(2)}) %collective-permute-start.11) | collective-permute-done | bytes 327712 | tf_op jit(solution)/shard_map/ppermute | solution.py:452
  70.4 1.0 copy-done.1
  71.4 1.0 copy-done.3
  72.4 1.0 copy-done.5
  73.4 1.0 copy-done.7
  74.3 0.9 copy-done.11
  75.3 0.9 copy-done.13
  76.2 3.6 %pack.5 = bf16[8,32,1280]{2,1,0:T(8,128)(2,1)S(1)} custom-call(s32[24,128]{1,0:T(8,128)S(1)} %get-tuple-element.25.start_ref, bf16[5120,256]{1,0:T(8,128)(2,1)S(1)} %get-tuple-element.26.onehot_ref, s32[40,128]{1,0:T(8,128)S(1)} %get-tuple-element.27.tile_ref, bf16[128,1280]{1,0:T(8,128)(2,1)S(1)} %copy-done.5, bf16[128,1280]{1,0:T(8,128)(2,1)S(1)} %copy-done.7, ...), custom_call_target="tpu_custom_call" | custom-call | flops 671088640 | bytes 655360 | tf_op jit(solution)/shard_map/pack/pallas_call | solution.py:425
  79.9 0.8 copy-done.9
  80.7 21.2 %all_to_all.10 = bf16[8,32,1280]{2,1,0:T(8,128)(2,1)S(1)} all-to-all(bf16[8,32,1280]{2,1,0:T(8,128)(2,1)} %copy-done.9), channel_id=1, replica_groups=mesh['chan'=4,'vox'=8] {'vox'}, dimensions={0} | all-to-all | bytes 1310720 | tf_op jit(solution)/shard_map/all_to_all | solution.py:440
  101.8 2.2 %maximum_bitcast_fusion = bf16[8,1280,64]{1,2,0:T(8,128)(2,1)} fusion(bf16[8,32,1280]{2,1,0:T(8,128)(2,1)S(1)} %all_to_all.10, bf16[8,32,1280]{2,1,0:T(8,128)(2,1)} %all-to-all-done), kind=kLoop, calls=%fused_computation | loop fusion | flops 2621440 | bytes 2621440 | tf_op jit(solution)/shard_map/transpose | solution.py:455
  (45 shorter events, 1.4 us)
Async XLA Ops:
  1.2 15.8 %collective-permute-start.2 = (bf16[64,1408]{1,0:T(8,128)(2,1)S(1)}, bf16[64,1408]{1,0:T(8,128)(2,1)S(1)}, u32[]{:S(2)}, u32[]{:S(2)}) collective-permute-start(bf16[64,1408]{1,0:T(8,128)(2,1)S(1)} %get-tuple-element.45), channel_id=1, source_target_pairs={{0,24},{8,16},{16,8},{24,0},{1,25},{9,17},{17,9},{25,1},{2,26},{10... | collective-permute-start | bytes 540680 | tf_op jit(solution)/shard_map/ppermute | solution.py:325
  3.7 1.7 %collective-permute-start = (bf16[64,1408]{1,0:T(8,128)(2,1)S(1)}, bf16[64,1408]{1,0:T(8,128)(2,1)S(1)}, u32[]{:S(2)}, u32[]{:S(2)}) collective-permute-start(bf16[64,1408]{1,0:T(8,128)(2,1)S(1)} %get-tuple-element.46), channel_id=1, source_target_pairs={{0,8},{8,0},{16,24},{24,16},{1,9},{9,1},{17,25},{25,17},{2,10},{10... | collective-permute-start | bytes 540680 | tf_op jit(solution)/shard_map/ppermute | solution.py:325
  4.4 12.7 %collective-permute-start.1 = (bf16[64,1408]{1,0:T(8,128)(2,1)S(1)}, bf16[64,1408]{1,0:T(8,128)(2,1)S(1)}, u32[]{:S(2)}, u32[]{:S(2)}) collective-permute-start(bf16[64,1408]{1,0:T(8,128)(2,1)S(1)} %get-tuple-element.48), channel_id=1, source_target_pairs={{0,16},{8,24},{16,0},{24,8},{1,17},{9,25},{17,1},{25,9},{2,18},{10... | collective-permute-start | bytes 540680 | tf_op jit(solution)/shard_map/ppermute | solution.py:325
  5.4 11.7 %copy-start.15 = (f32[3,1408,16]{1,2,0:T(8,128)S(1)}, f32[3,1408,16]{1,2,0:T(8,128)}, u32[]{:S(2)}) copy-start(f32[3,1408,16]{1,2,0:T(8,128)} %param.6) | copy-start | bytes 811012
  26.5 26.5 %copy-start.4 = (bf16[128,1280]{1,0:T(8,128)(2,1)}, bf16[128,1280]{1,0:T(8,128)(2,1)S(1)}, u32[]{:S(2)}) copy-start(bf16[128,1280]{1,0:T(8,128)(2,1)S(1)} %get-tuple-element.31.refs_0_) | copy-start | bytes 983044
  26.5 6.5 %collective-permute-start.3 = (bf16[128,1280]{1,0:T(8,128)(2,1)S(1)}, bf16[128,1280]{1,0:T(8,128)(2,1)S(1)}, u32[]{:S(2)}, u32[]{:S(2)}) collective-permute-start(bf16[128,1280]{1,0:T(8,128)(2,1)S(1)} %get-tuple-element.32), channel_id=1, source_target_pairs={{0,8},{8,0},{16,24},{24,16},{1,9},{9,1},{17,25},{25,17},{2,10},{10... | collective-permute-start | bytes 983048 | tf_op jit(solution)/shard_map/ppermute | solution.py:414
  32.8 8.4 %collective-permute-start.5 = (bf16[128,1536]{1,0:T(8,128)(2,1)S(1)}, bf16[128,1536]{1,0:T(8,128)(2,1)S(1)}, u32[]{:S(2)}, u32[]{:S(2)}) collective-permute-start(bf16[128,1536]{1,0:T(8,128)(2,1)S(1)} %get-tuple-element.36), channel_id=1, source_target_pairs={{0,8},{8,0},{16,24},{24,16},{1,9},{9,1},{17,25},{25,17},{2,10},{10... | collective-permute-start | bytes 1179656 | tf_op jit(solution)/shard_map/ppermute | solution.py:414
  33.0 19.9 %copy-start.6 = (bf16[128,1280]{1,0:T(8,128)(2,1)}, bf16[128,1280]{1,0:T(8,128)(2,1)S(1)}, u32[]{:S(2)}) copy-start(bf16[128,1280]{1,0:T(8,128)(2,1)S(1)} %collective-permute-done.3.refs_1_) | copy-start | bytes 983044
  33.0 8.8 %collective-permute-start.4 = (bf16[32,1280]{1,0:T(8,128)(2,1)S(1)}, bf16[32,1280]{1,0:T(8,128)(2,1)S(1)}, u32[]{:S(2)}, u32[]{:S(2)}) collective-permute-start(bf16[32,1280]{1,0:T(8,128)(2,1)S(1)} %add_convert_fusion.2.refs_3_), channel_id=1, source_target_pairs={{0,16},{8,24},{16,0},{24,8},{1,17},{9,25},{17,1},{25,9},{2,18},{10... | collective-permute-start | bytes 245768 | tf_op jit(solution)/shard_map/ppermute | solution.py:414
  41.1 11.8 %copy-start = (bf16[128,1536]{1,0:T(8,128)(2,1)}, bf16[128,1536]{1,0:T(8,128)(2,1)S(1)}, u32[]{:S(2)}) copy-start(bf16[128,1536]{1,0:T(8,128)(2,1)S(1)} %get-tuple-element.40.refs_6_.refs_4_) | copy-start | bytes 1179652
  41.2 2.8 %collective-permute-start.7 = (bf16[128,1536]{1,0:T(8,128)(2,1)S(1)}, bf16[128,1536]{1,0:T(8,128)(2,1)S(1)}, u32[]{:S(2)}, u32[]{:S(2)}) collective-permute-start(bf16[128,1536]{1,0:T(8,128)(2,1)S(1)} %get-tuple-element.41), channel_id=1, source_target_pairs={{0,8},{8,0},{16,24},{24,16},{1,9},{9,1},{17,25},{25,17},{2,10},{10... | collective-permute-start | bytes 1179656 | tf_op jit(solution)/shard_map/ppermute | solution.py:414
  41.3 5.6 %collective-permute-start.6 = (bf16[32,1536]{1,0:T(8,128)(2,1)S(1)}, bf16[32,1536]{1,0:T(8,128)(2,1)S(1)}, u32[]{:S(2)}, u32[]{:S(2)}) collective-permute-start(bf16[32,1536]{1,0:T(8,128)(2,1)S(1)} %add_convert_fusion.1.refs_1_), channel_id=1, source_target_pairs={{0,16},{8,24},{16,0},{24,8},{1,17},{9,25},{17,1},{25,9},{2,18},{10... | collective-permute-start | bytes 294920 | tf_op jit(solution)/shard_map/ppermute | solution.py:414
  43.8 9.3 %copy-start.10 = (bf16[128,768]{1,0:T(8,128)(2,1)}, bf16[128,768]{1,0:T(8,128)(2,1)S(1)}, u32[]{:S(2)}) copy-start(bf16[128,768]{1,0:T(8,128)(2,1)S(1)} %get-tuple-element.43.refs_6_.refs_1_.refs_9_) | copy-start | bytes 589828
  43.8 1.9 %collective-permute-start.9 = (bf16[128,768]{1,0:T(8,128)(2,1)S(1)}, bf16[128,768]{1,0:T(8,128)(2,1)S(1)}, u32[]{:S(2)}, u32[]{:S(2)}) collective-permute-start(bf16[128,768]{1,0:T(8,128)(2,1)S(1)} %get-tuple-element.44), channel_id=1, source_target_pairs={{0,8},{8,0},{16,24},{24,16},{1,9},{9,1},{17,25},{25,17},{2,10},{10... | collective-permute-start | bytes 589832 | tf_op jit(solution)/shard_map/ppermute | solution.py:414
  43.9 9.0 %copy-start.2 = (bf16[128,1536]{1,0:T(8,128)(2,1)}, bf16[128,1536]{1,0:T(8,128)(2,1)S(1)}, u32[]{:S(2)}) copy-start(bf16[128,1536]{1,0:T(8,128)(2,1)S(1)} %collective-permute-done.7.refs_7_.refs_5_) | copy-start | bytes 1179652
  43.9 5.7 %collective-permute-start.8 = (bf16[32,1536]{1,0:T(8,128)(2,1)S(1)}, bf16[32,1536]{1,0:T(8,128)(2,1)S(1)}, u32[]{:S(2)}, u32[]{:S(2)}) collective-permute-start(bf16[32,1536]{1,0:T(8,128)(2,1)S(1)} %add_convert_fusion), channel_id=1, source_target_pairs={{0,16},{8,24},{16,0},{24,8},{1,17},{9,25},{17,1},{25,9},{2,18},{10... | collective-permute-start | bytes 294920 | tf_op jit(solution)/shard_map/ppermute | solution.py:414
  45.7 7.4 %copy-start.12 = (bf16[128,768]{1,0:T(8,128)(2,1)}, bf16[128,768]{1,0:T(8,128)(2,1)S(1)}, u32[]{:S(2)}) copy-start(bf16[128,768]{1,0:T(8,128)(2,1)S(1)} %collective-permute-done.9.refs_7_.refs_2_.refs_10_) | copy-start | bytes 589828
  45.7 7.2 %collective-permute-start.10 = (bf16[32,768]{1,0:T(8,128)(2,1)S(1)}, bf16[32,768]{1,0:T(8,128)(2,1)S(1)}, u32[]{:S(2)}, u32[]{:S(2)}) collective-permute-start(bf16[32,768]{1,0:T(8,128)(2,1)S(1)} %add_convert_fusion.3), channel_id=1, source_target_pairs={{0,16},{8,24},{16,0},{24,8},{1,17},{9,25},{17,1},{25,9},{2,18},{10... | collective-permute-start | bytes 147464 | tf_op jit(solution)/shard_map/ppermute | solution.py:414
  54.3 0.8 copy-start.8
  55.2 0.7 copy-start.14
  55.9 24.8 %all-to-all-start = ((bf16[8,32,1280]{2,1,0:T(8,128)(2,1)}), bf16[8,32,1280]{2,1,0:T(8,128)(2,1)}, u32[]{:S(2)}, u32[]{:S(2)}) async-start(bf16[8,32,1280]{2,1,0:T(8,128)(2,1)} %copy-done.8), calls=%async_computation | async-start | bytes 1310720 | tf_op jit(solution)/shard_map/all_to_all | solution.py:440
  61.9 8.5 %collective-permute-start.11 = (bf16[32,5120]{1,0:T(8,128)(2,1)}, bf16[32,5120]{1,0:T(8,128)(2,1)S(1)}, u32[]{:S(2)}, u32[]{:S(2)}) collective-permute-start(bf16[32,5120]{1,0:T(8,128)(2,1)} %copy-done.14), channel_id=1, source_target_pairs={{0,16},{8,24},{16,0},{24,8},{1,17},{9,25},{17,1},{25,9},{2,18},{10... | collective-permute-start | bytes 983048 | tf_op jit(solution)/shard_map/ppermute | solution.py:452
  70.4 1.0 copy-start.1
  71.4 1.0 copy-start.3
  72.4 1.0 copy-start.5
  73.4 1.0 copy-start.7
  74.3 0.9 copy-start.11
  75.3 0.9 copy-start.13
  79.8 0.8 copy-start.9

commit v8 on v7

--- a/solution.py
+++ b/solution.py
@@ -16,7 +16,7 @@
 ROWS = 32
 CHUNKS = 4
 COPIES = (((0, 5), (1, 4)), ((1, 2), (2, 2)), ((2, 2),), ((2, 2),), ((3, 3),))
-PACK_FIRST = 3
+PACK_FIRST = 2
 MIB = 1 << 20
 
 VMEM = functools.partial(pl.BlockSpec, memory_space=pltpu.VMEM)
@@ -30,9 +30,12 @@
     for i, ref in enumerate(piece_refs):
         if ref.shape[1] > depth:
             ref[:, depth:, :] = jnp.zeros_like(ref[:, depth:, :])
-        for b in range(ref.shape[0]):
+        for j, at in enumerate(range(0, ref.shape[2], COLUMNS)):
+            size = min(COLUMNS, ref.shape[2] - at)
             copy = pltpu.make_async_copy(
-                weight_ref.at[b, :, pl.ds(first, ref.shape[2])], ref.at[b, pl.ds(0, depth), :], sems.at[i, b]
+                weight_ref.at[:, :, pl.ds(first + at, size)],
+                ref.at[:, pl.ds(0, depth), pl.ds(at, size)],
+                sems.at[i, j],
             )
             copy.start()
             copies.append(copy)
@@ -228,25 +231,32 @@
         in_specs=[VMEM()] * (1 + len(taken)) + [ANY()] * (len(after) + bool(ahead)),
         out_specs=[VMEM()] * (2 + len(ahead)),
         out_shape=[half, half] + ahead,
-        scratch_shapes=[pltpu.SemaphoreType.DMA((len(ahead), weights.shape[0]))] if ahead else [],
+        scratch_shapes=[pltpu.SemaphoreType.DMA((len(ahead), 4))] if ahead else [],
         compiler_params=pltpu.CompilerParams(vmem_limit_bytes=8 * MIB),
         cost_estimate=cost(2 * time_len * lanes * width, 2 * lanes * width),
         name="product",
     )(design, *taken, *after, *([weights] if ahead else []))
 
 
-def late_kernel(each, first, *refs):
-    out_ref, at = refs[-1], 0
-    for c in range(0, len(refs) - 3, each):
-        terms, width = refs[c : c + each], refs[c].shape[1]
-        total = sum(term[first : first + out_ref.shape[0], :].astype(jnp.float32) for term in terms)
+def add_rows(terms, each, first, out_ref):
+    at, rows = 0, out_ref.shape[0]
+    for c in range(0, len(terms), each):
+        chunk, width = terms[c : c + each], terms[c].shape[1]
+        total = sum(term[first : first + rows, :].astype(jnp.float32) for term in chunk)
         out_ref[:, at : at + width] = total.astype(jnp.bfloat16)
         at += width
 
 
-def pack_kernel(spread, widths, places, first, extra, start_ref, onehot_ref, tile_ref, *refs):
-    *terms, out_ref, summed, packed = refs
-    terms = terms[: len(terms) - extra]
+def pack_kernel(spread, widths, places, first, later, start_ref, onehot_ref, tile_ref, *refs):
+    if later:
+        count, each = later
+        *terms, out_ref, send_ref, keep_ref, summed, packed = refs
+        rows = packed.shape[1]
+        add_rows(terms[-count:], each, 3 * rows, send_ref)
+        add_rows(terms[-count:], each, rows, keep_ref)
+        terms = terms[:-count]
+    else:
+        *terms, out_ref, summed, packed = refs
     owners, rows = packed.shape[:2]
     if first:
         packed[...] = terms.pop(0)[...]
@@ -368,7 +378,7 @@
         + [
             pltpu.VMEM(filters.shape, jnp.float32),
             pltpu.VMEM((voxels // LANES, LANES), jnp.int32),
-            pltpu.SemaphoreType.DMA((len(COPIES[0]), bases)),
+            pltpu.SemaphoreType.DMA((len(COPIES[0]), 4)),
             pltpu.SemaphoreType.DMA((2,)),
         ],
         compiler_params=pltpu.CompilerParams(vmem_limit_bytes=8 * MIB),
@@ -389,7 +399,7 @@
         in_specs=[SMEM(), SMEM(), VMEM(), VMEM(), ANY()] + [VMEM()] * parts,
         out_specs=[VMEM()] * (1 + len(COPIES[1])),
         out_shape=[jax.ShapeDtypeStruct((time_len, lanes), jnp.bfloat16)] + room(1),
-        scratch_shapes=filter_scratch(time_len) + [pltpu.SemaphoreType.DMA((len(COPIES[1]), bases))],
+        scratch_shapes=filter_scratch(time_len) + [pltpu.SemaphoreType.DMA((len(COPIES[1]), 4))],
         compiler_params=pltpu.CompilerParams(vmem_limit_bytes=8 * MIB),
         cost_estimate=cost(0, 2 * bases * depth * copied[1]),
         name="design",
@@ -414,19 +424,17 @@
             own.append(lax.ppermute(send, "chan", [(i, i ^ (1 << bit)) for i in range(parts)]))
         sums.append(own)
         got.append(own[-1])
-    def pack(low, high, second, packed, after=()):
-        terms, spots = [], []
-        for c in range(low, high):
-            own = sums[c][:-1]
-            terms += own + [late if second else got[c]]
-            spots.append([(half if second else 0, 0)] * len(own) + [(0, sum(widths[:c]) if second else 0)])
-        here = widths[low:high]
-        lanes_out = send_cap if high == CHUNKS else spread * SLOT_TILE
+    def pack(chunks, terms, spots, packed=(), later=()):
+        here = [widths[c] for c in chunks]
+        lanes_out = send_cap if chunks[-1] == CHUNKS - 1 else spread * SLOT_TILE
+        spec = (len(later), bits) if later else None
         return pl.pallas_call(
-            functools.partial(pack_kernel, spread, here, spots, sum(widths[:low]) // VOX_BLOCK, len(after)),
-            in_specs=[SMEM(), VMEM(), VMEM()] + [VMEM()] * (len(packed) + len(terms)) + [ANY()] * len(after),
-            out_specs=VMEM(),
-            out_shape=jax.ShapeDtypeStruct((owners, half, lanes_out), jnp.bfloat16),
+            functools.partial(pack_kernel, spread, here, spots, sum(widths[: chunks[0]]) // VOX_BLOCK, spec),
+            in_specs=[SMEM(), VMEM(), VMEM()] + [VMEM()] * (len(packed) + len(terms) + len(later)),
+            out_specs=[VMEM()] * (3 if later else 1),
+            out_shape=[jax.ShapeDtypeStruct((owners, half, lanes_out), jnp.bfloat16)]
+            + ([jax.ShapeDtypeStruct((half, voxels), jnp.bfloat16)] if later else [])
+            + ([pltpu.VMEM((half, voxels), jnp.bfloat16)] if later else []),
             scratch_shapes=[
                 pltpu.VMEM((half, sum(here)), jnp.bfloat16),
                 pltpu.VMEM((owners, half, spread * SLOT_TILE), jnp.bfloat16),
@@ -434,24 +442,22 @@
             compiler_params=pltpu.CompilerParams(vmem_limit_bytes=8 * MIB),
             cost_estimate=cost(2 * half * owners * VOX_BLOCK * sum(here), 4 * half * sum(here)),
             name="pack",
-        )(starts, onehot, tiles, *packed, *terms, *after)
+        )(starts, onehot, tiles, *packed, *terms, *later)
 
     def deliver(packed):
         return lax.all_to_all(packed, "vox", split_axis=0, concat_axis=0, tiled=True)
 
-    packed = pack(0, PACK_FIRST, False, [])
-    late_terms = [term for own in sums for term in own[:-1]]
-    late_send = pl.pallas_call(
-        functools.partial(late_kernel, bits, time_block + half),
-        in_specs=[VMEM()] * len(late_terms) + [ANY()] * 2,
-        out_specs=VMEM(),
-        out_shape=jax.ShapeDtypeStruct((half, voxels), jnp.bfloat16),
-        compiler_params=pltpu.CompilerParams(vmem_limit_bytes=6 * MIB),
-        name="late",
-    )(*late_terms, got[-1], packed)
+    def early_terms(chunks):
+        return [term for c in chunks for term in sums[c]], [[(0, 0)] * len(sums[c]) for c in chunks]
+
+    low, high = range(PACK_FIRST), range(PACK_FIRST, CHUNKS)
+    packed, late_send, late_own = pack(low, *early_terms(low), later=[term for own in sums for term in own[:-1]])
     late = lax.ppermute(late_send, "chan", [(i, i ^ (1 << (bits - 1))) for i in range(parts)])
-    one = deliver(pack(PACK_FIRST, CHUNKS, False, [packed], [late_send]))
-    two = deliver(pack(0, CHUNKS, True, []))
+    one = deliver(*pack(high, *early_terms(high), packed=[packed]))
+    starting = [sum(widths[:c]) for c in range(CHUNKS)]
+    two = deliver(
+        *pack(range(CHUNKS), [late_own, late] * CHUNKS, [[(0, first)] * 2 for first in starting])
+    )
     return jnp.transpose(jnp.concatenate([one, two], axis=1), (0, 2, 1))
 
 

time: 105 us -> 100 us (0.952)
  local copies, waits for them, and re-layouts: 10.2 us -> 3.62 us
  waiting for transfers between devices: 10.1 us -> 12.1 us
    unnamed x32 -> x6, local copies, waits for them, and re-layouts: 8.23 us -> 1.69 us
    all_to_all x1, waiting for transfers between devices: 0.01 us -> 3.78 us  [deliver(): lax.all_to_all(packed, 'vox', split_axis=0, concat_axis=0, tiled=True)]
    ppermute x8, waiting for transfers between devices: 2.71 us -> 0.65 us  [shards(): lax.ppermute(send, 'chan', [(i, i ^ 1 << bit) for i in range(parts)])]
  transfers between devices with their start and end apart: 13 -> 13, of which waited for: 3 -> 4; matrix products, arithmetic and copies ran while one was open for 1% -> 1% of each run, Pallas kernels for 31% -> 32%
where the time goes in v8:
time: 100 us; the launch traced here: 99.6 us
  Pallas kernels  43.2 us (43%)
  blocking collectives  21.5 us (22%)
  starting transfers between devices  16.7 us (17%)
  waiting for transfers between devices  12.1 us (12%)
  local copies, waits for them, and re-layouts  3.62 us (4%)
  other arithmetic  2.32 us (2%)
    all_to_all x1, blocking collectives, deliver(): lax.all_to_all(packed, 'vox', split_axis=0, concat_axis=0, tiled=True)  21.5 us
    pallas_call x4, Pallas kernels, product(): pl.pallas_call(functools.partial(product_kernel, len(taken), len(after),...  19 us
    pallas_call x1, Pallas kernels, shards(): pl.pallas_call(functools.partial(early_kernel, owners, spread), in_specs=...  11.6 us
    pallas_call x3, Pallas kernels, pack(): pl.pallas_call(functools.partial(pack_kernel, spread, here, spots, sum(wi...  8.39 us
    ppermute x1, waiting for transfers between devices, shards(): lax.ppermute(late_send, 'chan', [(i, i ^ 1 << bits - 1) for i in range(pa...  7.35 us
    ppermute x8, starting transfers between devices, shards(): lax.ppermute(send, 'chan', [(i, i ^ 1 << bit) for i in range(parts)])  6.08 us
    all_to_all x1, starting transfers between devices, deliver(): lax.all_to_all(packed, 'vox', split_axis=0, concat_axis=0, tiled=True)  5.94 us
    pallas_call x1, Pallas kernels, shards(): pl.pallas_call(functools.partial(design_kernel, parts, firsts[1]), in_spe...  4.21 us
  transfers between devices with their start and end apart: 13, of which 4 were waited for; matrix products, arithmetic and copies ran while one was open for 1% of the time, Pallas kernels for 32%

profile of v8, /device:TPU:0, one launch (start us, length us, event | category | flops | bytes accessed | tf_op | source)
XLA Modules:
  0.0 99.6 jit_solution(292226527034249465)
XLA Ops:
  0.0 1.2 %constant_dynamic-slice_fusion = (bf16[64,1408]{1,0:T(8,128)(2,1)S(1)}, bf16[64,1408]{1,0:T(8,128)(2,1)S(1)}, bf16[64,1408]{1,0:T(8,128)(2,1)S(1)}, bf16[64,1408]{1,0:T(8,128)(2,1)S(1)}) fusion(bf16[64,5632]{1,0:T(8,128)(2,1)} %param.5, s32[]{:T(128)S(6)} %select_n.15, s32[]{:T(128)S(6)} %select_n.13, s32[]{:T(128)S(6)} %select_n.12, s32[]{:T(128)S(6)} %select_n.14), kind=kLoop, calls=%fused_computation.6 | loop fusion | bytes 1441808 | tf_op jit(solution)/shard_map/dynamic_slice | solution.py:333
  1.2 2.4 %collective-permute-start.2 = (bf16[64,1408]{1,0:T(8,128)(2,1)S(1)}, bf16[64,1408]{1,0:T(8,128)(2,1)S(1)}, u32[]{:S(2)}, u32[]{:S(2)}) collective-permute-start(bf16[64,1408]{1,0:T(8,128)(2,1)S(1)} %get-tuple-element.51), channel_id=1, source_target_pairs={{0,24},{8,16},{16,8},{24,0},{1,25},{9,17},{17,9},{25,1},{2,26},{10... | collective-permute-start | bytes 540680 | tf_op jit(solution)/shard_map/ppermute | solution.py:335
  3.7 0.7 collective-permute-start
  4.4 0.0 collective-permute-start.1
  4.4 0.7 pad_bitcast_fusion.table_ref
  5.1 0.3 collective-permute-done.pair_ref.refs_1_
  5.4 11.6 %early.1 = (bf16[5120,256]{1,0:T(8,128)(2,1)S(1)}, s32[40,128]{1,0:T(8,128)S(1)}, s32[24,128]{1,0:T(8,128)S(1)}, bf16[96,4224]{1,0:T(8,128)(2,1)S(1)}, bf16[3,14...) custom-call(s32[4]{0:T(128)S(1)} %get-tuple-element.56.order_ref, ...), custom_call_target="tpu_custom_call" | custom-call | bytes 19464192 | tf_op jit(solution)/shard_map/early/pallas_call | solution.py:366
  17.0 4.2 %design.1 = (bf16[256,4224]{1,0:T(8,128)(2,1)S(1)}, bf16[3,1408,512]{2,1,0:T(8,128)(2,1)S(1)}, bf16[3,1408,512]{2,1,0:T(8,128)(2,1)S(1)}) custom-call(s32[4]{0:T(128)S(1)} %get-tuple-element.56.order_ref, s32[4]{0:T(128)S(1)} %get-tuple-element.55.place_ref, bf16[96,4224]{1,0:T(8,128)(2,1)S(1)} %get-tuple-element.31.early_ref, f32[3,16,1408]{2,1,0:T(8,128)S(1)} %bitcast.7, ...), custom_call_target="tpu_custom_call" | custom-call | bytes 8650752 | tf_op jit(solution)/shard_map/design/pallas_call | solution.py:397
  21.3 5.0 %product.4 = (bf16[128,1280]{1,0:T(8,128)(2,1)S(1)}, bf16[128,1280]{1,0:T(8,128)(2,1)S(1)}, bf16[3,1408,512]{2,1,0:T(8,128)(2,1)S(1)}) custom-call(bf16[256,4224]{1,0:T(8,128)(2,1)S(1)} %get-tuple-element.32.design_ref, bf16[3,1408,1280]{2,1,0:T(8,128)(2,1)S(1)} %get-tuple-element.33.refs_0_, bf16[3,1408,5120]{2,1,0:T(8,128)(2,1)} %refs_4_.1), custom_call_target="tpu_custom_call" | custom-call | flops 2768240640 | bytes 10813440 | tf_op jit(solution)/shard_map/product/pallas_call | solution.py:229
  26.3 0.4 collective-permute-start.3
  26.8 5.8 %product.5 = (bf16[128,1536]{1,0:T(8,128)(2,1)S(1)}, bf16[128,1536]{1,0:T(8,128)(2,1)S(1)}, bf16[3,1408,512]{2,1,0:T(8,128)(2,1)S(1)}) custom-call(bf16[256,4224]{1,0:T(8,128)(2,1)S(1)} %get-tuple-element.32.design_ref, bf16[3,1408,1024]{2,1,0:T(8,128)(2,1)S(1)} %get-tuple-element.36.refs_0_, bf16[3,1408,512]{2,1,0:T(8,128)(2,1)S(1)} %get-tuple-element.37.refs_1_, ...), custom_call_target="tpu_custom_call" | custom-call | flops 3321888768 | bytes 12976128 | tf_op jit(solution)/shard_map/product/pallas_call | solution.py:229
  32.5 0.2 collective-permute-start.5
  32.7 1.7 %collective-permute-start.4 = (bf16[32,1280]{1,0:T(8,128)(2,1)S(1)}, bf16[32,1280]{1,0:T(8,128)(2,1)S(1)}, u32[]{:S(2)}, u32[]{:S(2)}) collective-permute-start(bf16[32,1280]{1,0:T(8,128)(2,1)S(1)} %add_convert_fusion.2.refs_3_), channel_id=1, source_target_pairs={{0,16},{8,24},{16,0},{24,8},{1,17},{9,25},{17,1},{25,9},{2,18},{10... | collective-permute-start | bytes 245768 | tf_op jit(solution)/shard_map/ppermute | solution.py:424
  34.5 6.3 %product.6 = (bf16[128,1536]{1,0:T(8,128)(2,1)S(1)}, bf16[128,1536]{1,0:T(8,128)(2,1)S(1)}, bf16[3,1408,768]{2,1,0:T(8,128)(2,1)S(1)}) custom-call(bf16[256,4224]{1,0:T(8,128)(2,1)S(1)} %get-tuple-element.32.design_ref, bf16[3,1408,512]{2,1,0:T(8,128)(2,1)S(1)} %get-tuple-element.40.refs_0_, bf16[3,1408,512]{2,1,0:T(8,128)(2,1)S(1)} %get-tuple-element.41.refs_1_, ...), custom_call_target="tpu_custom_call" | custom-call | flops 3321888768 | bytes 12976128 | tf_op jit(solution)/shard_map/product/pallas_call | solution.py:229
  40.8 0.1 collective-permute-start.7
  41.0 0.5 collective-permute-start.6
  41.5 1.9 %product.7 = (bf16[128,768]{1,0:T(8,128)(2,1)S(1)}, bf16[128,768]{1,0:T(8,128)(2,1)S(1)}) custom-call(bf16[256,4224]{1,0:T(8,128)(2,1)S(1)} %get-tuple-element.32.design_ref, bf16[3,1408,768]{2,1,0:T(8,128)(2,1)S(1)} %get-tuple-element.45.refs_0_, bf16[32,1536]{1,0:T(8,128)(2,1)S(1)} %add_convert_fusion.1.refs_1_, ...), custom_call_target="tpu_custom_call" | custom-call | flops 1660944384 | bytes 6488064 | tf_op jit(solution)/shard_map/product/pallas_call | solution.py:229
  43.3 0.2 collective-permute-start.8
  43.6 1.7 %collective-permute-start.9 = (bf16[32,1536]{1,0:T(8,128)(2,1)S(1)}, bf16[32,1536]{1,0:T(8,128)(2,1)S(1)}, u32[]{:S(2)}, u32[]{:S(2)}) collective-permute-start(bf16[32,1536]{1,0:T(8,128)(2,1)S(1)} %add_convert_fusion), channel_id=1, source_target_pairs={{0,16},{8,24},{16,0},{24,8},{1,17},{9,25},{17,1},{25,9},{2,18},{10... | collective-permute-start | bytes 294920 | tf_op jit(solution)/shard_map/ppermute | solution.py:424
  45.3 1.2 %collective-permute-start.10 = (bf16[32,768]{1,0:T(8,128)(2,1)S(1)}, bf16[32,768]{1,0:T(8,128)(2,1)S(1)}, u32[]{:S(2)}, u32[]{:S(2)}) collective-permute-start(bf16[32,768]{1,0:T(8,128)(2,1)S(1)} %add_convert_fusion.3), channel_id=1, source_target_pairs={{0,16},{8,24},{16,0},{24,8},{1,17},{9,25},{17,1},{25,9},{2,18},{10... | collective-permute-start | bytes 147464 | tf_op jit(solution)/shard_map/ppermute | solution.py:424
  46.5 2.6 %pack.3 = (bf16[8,32,1664]{2,1,0:T(8,128)(2,1)S(1)}, bf16[32,5120]{1,0:T(8,128)(2,1)S(1)}, bf16[32,5120]{1,0:T(8,128)(2,1)S(1)}) custom-call(s32[24,128]{1,0:T(8,128)S(1)} %get-tuple-element.28.start_ref, bf16[5120,256]{1,0:T(8,128)(2,1)S(1)} %get-tuple-element.29.onehot_ref, s32[40,128]{1,0:T(8,128)S(1)} %get-tuple-element.30.tile_ref, ...), custom_call_target="tpu_custom_call" | custom-call | flops 369098752 | bytes 360448 | tf_op jit(solution)/shard_map/pack/pallas_call | solution.py:431
  49.1 0.6 collective-permute-done.10.refs_6_
  49.8 2.2 %pack.4 = bf16[8,32,1280]{2,1,0:T(8,128)(2,1)S(1)} custom-call(s32[24,128]{1,0:T(8,128)S(1)} %get-tuple-element.28.start_ref, bf16[5120,256]{1,0:T(8,128)(2,1)S(1)} %get-tuple-element.29.onehot_ref, s32[40,128]{1,0:T(8,128)S(1)} %get-tuple-element.30.tile_ref, bf16[8,32,1664]{2,1,0:T(8,128)(2,1)S(1)} %get-tuple-element.48.refs_0_, ...), custom_call_target="tpu_custom_call" | custom-call | flops 301989888 | bytes 294912 | tf_op jit(solution)/shard_map/pack/pallas_call | solution.py:431
  52.0 0.9 copy-done
  52.8 5.9 %all-to-all-start = ((bf16[8,32,1280]{2,1,0:T(8,128)(2,1)}), bf16[8,32,1280]{2,1,0:T(8,128)(2,1)}, u32[]{:S(2)}, u32[]{:S(2)}) async-start(bf16[8,32,1280]{2,1,0:T(8,128)(2,1)} %copy-done), calls=%async_computation | async-start | bytes 1310720 | tf_op jit(solution)/shard_map/all_to_all | solution.py:448
  58.8 1.5 %collective-permute-start.11 = (bf16[32,5120]{1,0:T(8,128)(2,1)S(1)}, bf16[32,5120]{1,0:T(8,128)(2,1)S(1)}, u32[]{:S(2)}, u32[]{:S(2)}) collective-permute-start(bf16[32,5120]{1,0:T(8,128)(2,1)S(1)} %get-tuple-element.50), channel_id=1, source_target_pairs={{0,16},{8,24},{16,0},{24,8},{1,17},{9,25},{17,1},{25,9},{2,18},{10... | collective-permute-start | bytes 983048 | tf_op jit(solution)/shard_map/ppermute | solution.py:455
  60.3 7.3 %collective-permute-done.11.refs_1_.refs_3_.refs_5_.refs_7_ = bf16[32,5120]{1,0:T(8,128)(2,1)S(1)} collective-permute-done((bf16[32,5120]{1,0:T(8,128)(2,1)S(1)}, bf16[32,5120]{1,0:T(8,128)(2,1)S(1)}, u32[]{:S(2)}, u32[]{:S(2)}) %collective-permute-start.11) | collective-permute-done | bytes 327712 | tf_op jit(solution)/shard_map/ppermute | solution.py:455
  67.6 3.6 %pack.5 = bf16[8,32,1280]{2,1,0:T(8,128)(2,1)S(1)} custom-call(s32[24,128]{1,0:T(8,128)S(1)} %get-tuple-element.28.start_ref, bf16[5120,256]{1,0:T(8,128)(2,1)S(1)} %get-tuple-element.29.onehot_ref, s32[40,128]{1,0:T(8,128)S(1)} %get-tuple-element.30.tile_ref, bf16[32,5120]{1,0:T(8,128)(2,1)S(1)} %get-tuple-element.49.refs_0_.refs_2_.refs_4_.refs_6_, ...), custom_call_target="tpu_custom_call" | custom-call | flops 671088640 | bytes 655360 | tf_op jit(solution)/shard_map/pack/pallas_call | solution.py:431
  71.3 0.8 copy-done.1
  72.1 3.8 %all-to-all-done = bf16[8,32,1280]{2,1,0:T(8,128)(2,1)} async-done(((bf16[8,32,1280]{2,1,0:T(8,128)(2,1)}), bf16[8,32,1280]{2,1,0:T(8,128)(2,1)}, u32[]{:S(2)}, u32[]{:S(2)}) %all-to-all-start) | async-done | bytes 655392 | tf_op jit(solution)/shard_map/all_to_all | solution.py:448
  75.9 21.5 %all_to_all.10 = bf16[8,32,1280]{2,1,0:T(8,128)(2,1)S(1)} all-to-all(bf16[8,32,1280]{2,1,0:T(8,128)(2,1)} %copy-done.1), channel_id=1, replica_groups=mesh['chan'=4,'vox'=8] {'vox'}, dimensions={0} | all-to-all | bytes 1310720 | tf_op jit(solution)/shard_map/all_to_all | solution.py:448
  97.3 2.2 %maximum_bitcast_fusion = bf16[8,1280,64]{1,2,0:T(8,128)(2,1)} fusion(bf16[8,32,1280]{2,1,0:T(8,128)(2,1)S(1)} %all_to_all.10, bf16[8,32,1280]{2,1,0:T(8,128)(2,1)} %all-to-all-done), kind=kLoop, calls=%fused_computation | loop fusion | flops 2621440 | bytes 2621440 | tf_op jit(solution)/shard_map/transpose | solution.py:461
  (18 shorter events, 0.1 us)
Async XLA Ops:
  1.2 15.8 %collective-permute-start.2 = (bf16[64,1408]{1,0:T(8,128)(2,1)S(1)}, bf16[64,1408]{1,0:T(8,128)(2,1)S(1)}, u32[]{:S(2)}, u32[]{:S(2)}) collective-permute-start(bf16[64,1408]{1,0:T(8,128)(2,1)S(1)} %get-tuple-element.51), channel_id=1, source_target_pairs={{0,24},{8,16},{16,8},{24,0},{1,25},{9,17},{17,9},{25,1},{2,26},{10... | collective-permute-start | bytes 540680 | tf_op jit(solution)/shard_map/ppermute | solution.py:335
  3.7 1.7 %collective-permute-start = (bf16[64,1408]{1,0:T(8,128)(2,1)S(1)}, bf16[64,1408]{1,0:T(8,128)(2,1)S(1)}, u32[]{:S(2)}, u32[]{:S(2)}) collective-permute-start(bf16[64,1408]{1,0:T(8,128)(2,1)S(1)} %get-tuple-element.52), channel_id=1, source_target_pairs={{0,8},{8,0},{16,24},{24,16},{1,9},{9,1},{17,25},{25,17},{2,10},{10... | collective-permute-start | bytes 540680 | tf_op jit(solution)/shard_map/ppermute | solution.py:335
  4.4 12.7 %collective-permute-start.1 = (bf16[64,1408]{1,0:T(8,128)(2,1)S(1)}, bf16[64,1408]{1,0:T(8,128)(2,1)S(1)}, u32[]{:S(2)}, u32[]{:S(2)}) collective-permute-start(bf16[64,1408]{1,0:T(8,128)(2,1)S(1)} %get-tuple-element.54), channel_id=1, source_target_pairs={{0,16},{8,24},{16,0},{24,8},{1,17},{9,25},{17,1},{25,9},{2,18},{10... | collective-permute-start | bytes 540680 | tf_op jit(solution)/shard_map/ppermute | solution.py:335
  5.4 11.6 %copy-start.2 = (f32[3,1408,16]{1,2,0:T(8,128)S(1)}, f32[3,1408,16]{1,2,0:T(8,128)}, u32[]{:S(2)}) copy-start(f32[3,1408,16]{1,2,0:T(8,128)} %param.6) | copy-start | bytes 811012
  26.3 6.4 %collective-permute-start.3 = (bf16[128,1280]{1,0:T(8,128)(2,1)S(1)}, bf16[128,1280]{1,0:T(8,128)(2,1)S(1)}, u32[]{:S(2)}, u32[]{:S(2)}) collective-permute-start(bf16[128,1280]{1,0:T(8,128)(2,1)S(1)} %get-tuple-element.35), channel_id=1, source_target_pairs={{0,8},{8,0},{16,24},{24,16},{1,9},{9,1},{17,25},{25,17},{2,10},{10... | collective-permute-start | bytes 983048 | tf_op jit(solution)/shard_map/ppermute | solution.py:424
  32.5 8.4 %collective-permute-start.5 = (bf16[128,1536]{1,0:T(8,128)(2,1)S(1)}, bf16[128,1536]{1,0:T(8,128)(2,1)S(1)}, u32[]{:S(2)}, u32[]{:S(2)}) collective-permute-start(bf16[128,1536]{1,0:T(8,128)(2,1)S(1)} %get-tuple-element.39), channel_id=1, source_target_pairs={{0,8},{8,0},{16,24},{24,16},{1,9},{9,1},{17,25},{25,17},{2,10},{10... | collective-permute-start | bytes 1179656 | tf_op jit(solution)/shard_map/ppermute | solution.py:424
  32.7 8.7 %collective-permute-start.4 = (bf16[32,1280]{1,0:T(8,128)(2,1)S(1)}, bf16[32,1280]{1,0:T(8,128)(2,1)S(1)}, u32[]{:S(2)}, u32[]{:S(2)}) collective-permute-start(bf16[32,1280]{1,0:T(8,128)(2,1)S(1)} %add_convert_fusion.2.refs_3_), channel_id=1, source_target_pairs={{0,16},{8,24},{16,0},{24,8},{1,17},{9,25},{17,1},{25,9},{2,18},{10... | collective-permute-start | bytes 245768 | tf_op jit(solution)/shard_map/ppermute | solution.py:424
  40.8 2.8 %collective-permute-start.7 = (bf16[128,1536]{1,0:T(8,128)(2,1)S(1)}, bf16[128,1536]{1,0:T(8,128)(2,1)S(1)}, u32[]{:S(2)}, u32[]{:S(2)}) collective-permute-start(bf16[128,1536]{1,0:T(8,128)(2,1)S(1)} %get-tuple-element.44), channel_id=1, source_target_pairs={{0,8},{8,0},{16,24},{24,16},{1,9},{9,1},{17,25},{25,17},{2,10},{10... | collective-permute-start | bytes 1179656 | tf_op jit(solution)/shard_map/ppermute | solution.py:424
  41.0 5.6 %collective-permute-start.6 = (bf16[32,1536]{1,0:T(8,128)(2,1)S(1)}, bf16[32,1536]{1,0:T(8,128)(2,1)S(1)}, u32[]{:S(2)}, u32[]{:S(2)}) collective-permute-start(bf16[32,1536]{1,0:T(8,128)(2,1)S(1)} %add_convert_fusion.1.refs_1_), channel_id=1, source_target_pairs={{0,16},{8,24},{16,0},{24,8},{1,17},{9,25},{17,1},{25,9},{2,18},{10... | collective-permute-start | bytes 294920 | tf_op jit(solution)/shard_map/ppermute | solution.py:424
  43.3 2.0 %collective-permute-start.8 = (bf16[128,768]{1,0:T(8,128)(2,1)S(1)}, bf16[128,768]{1,0:T(8,128)(2,1)S(1)}, u32[]{:S(2)}, u32[]{:S(2)}) collective-permute-start(bf16[128,768]{1,0:T(8,128)(2,1)S(1)} %get-tuple-element.47), channel_id=1, source_target_pairs={{0,8},{8,0},{16,24},{24,16},{1,9},{9,1},{17,25},{25,17},{2,10},{10... | collective-permute-start | bytes 589832 | tf_op jit(solution)/shard_map/ppermute | solution.py:424
  43.6 6.2 %collective-permute-start.9 = (bf16[32,1536]{1,0:T(8,128)(2,1)S(1)}, bf16[32,1536]{1,0:T(8,128)(2,1)S(1)}, u32[]{:S(2)}, u32[]{:S(2)}) collective-permute-start(bf16[32,1536]{1,0:T(8,128)(2,1)S(1)} %add_convert_fusion), channel_id=1, source_target_pairs={{0,16},{8,24},{16,0},{24,8},{1,17},{9,25},{17,1},{25,9},{2,18},{10... | collective-permute-start | bytes 294920 | tf_op jit(solution)/shard_map/ppermute | solution.py:424
  45.3 4.4 %collective-permute-start.10 = (bf16[32,768]{1,0:T(8,128)(2,1)S(1)}, bf16[32,768]{1,0:T(8,128)(2,1)S(1)}, u32[]{:S(2)}, u32[]{:S(2)}) collective-permute-start(bf16[32,768]{1,0:T(8,128)(2,1)S(1)} %add_convert_fusion.3), channel_id=1, source_target_pairs={{0,16},{8,24},{16,0},{24,8},{1,17},{9,25},{17,1},{25,9},{2,18},{10... | collective-permute-start | bytes 147464 | tf_op jit(solution)/shard_map/ppermute | solution.py:424
  52.0 0.9 copy-start
  52.8 23.0 %all-to-all-start = ((bf16[8,32,1280]{2,1,0:T(8,128)(2,1)}), bf16[8,32,1280]{2,1,0:T(8,128)(2,1)}, u32[]{:S(2)}, u32[]{:S(2)}) async-start(bf16[8,32,1280]{2,1,0:T(8,128)(2,1)} %copy-done), calls=%async_computation | async-start | bytes 1310720 | tf_op jit(solution)/shard_map/all_to_all | solution.py:448
  58.8 8.8 %collective-permute-start.11 = (bf16[32,5120]{1,0:T(8,128)(2,1)S(1)}, bf16[32,5120]{1,0:T(8,128)(2,1)S(1)}, u32[]{:S(2)}, u32[]{:S(2)}) collective-permute-start(bf16[32,5120]{1,0:T(8,128)(2,1)S(1)} %get-tuple-element.50), channel_id=1, source_target_pairs={{0,16},{8,24},{16,0},{24,8},{1,17},{9,25},{17,1},{25,9},{2,18},{10... | collective-permute-start | bytes 983048 | tf_op jit(solution)/shard_map/ppermute | solution.py:455
  71.2 0.8 copy-start.1

commit v9 on v8

--- a/solution.py
+++ b/solution.py
@@ -15,7 +15,7 @@
 COLUMNS = 512
 ROWS = 32
 CHUNKS = 4
-COPIES = (((0, 5), (1, 4)), ((1, 2), (2, 2)), ((2, 2),), ((2, 2),), ((3, 3),))
+COPIES = (((0, 4), (1, 5)), ((1, 1), (2, 4)), (), ((2, 2), (3, 1)), ((3, 2), (3, 1)))
 PACK_FIRST = 2
 MIB = 1 << 20
 
@@ -30,15 +30,11 @@
     for i, ref in enumerate(piece_refs):
         if ref.shape[1] > depth:
             ref[:, depth:, :] = jnp.zeros_like(ref[:, depth:, :])
-        for j, at in enumerate(range(0, ref.shape[2], COLUMNS)):
-            size = min(COLUMNS, ref.shape[2] - at)
-            copy = pltpu.make_async_copy(
-                weight_ref.at[:, :, pl.ds(first + at, size)],
-                ref.at[:, pl.ds(0, depth), pl.ds(at, size)],
-                sems.at[i, j],
-            )
-            copy.start()
-            copies.append(copy)
+        copy = pltpu.make_async_copy(
+            weight_ref.at[:, :, pl.ds(first, ref.shape[2])], ref.at[:, pl.ds(0, depth), :], sems.at[i]
+        )
+        copy.start()
+        copies.append(copy)
         first += ref.shape[2]
     return copies
 
@@ -52,7 +48,7 @@
     return pl.CostEstimate(flops=flops, bytes_accessed=read, transcendentals=0)
 
 
-def places(owners, spread, parcel_ref, table_ref, onehot_ref, tile_ref, start_ref):
+def places(owners, spread, parcel_ref, table_ref, inner_ref, tile_ref, start_ref):
     rows = parcel_ref.shape[0]
     parcel = parcel_ref[...]
     high, low = parcel >> 7, parcel & 127
@@ -89,13 +85,7 @@
     slots = slots.astype(jnp.int32)
     start_ref[...] = starts.astype(jnp.int32)
     tile_ref[...] = owner * spread + (slots >> 7)
-    inner = (slots - (bases.astype(jnp.int32) & -SLOT_TILE)) & (2 * SLOT_TILE - 1)
-    for row in range(rows):
-        line = jnp.broadcast_to(inner[row : row + 1, :], (LANES, LANES)).T
-        for side in range(2):
-            hit = jnp.where(line == lane + side * LANES, 1.0, 0.0)
-            at = slice(side * LANES, (side + 1) * LANES)
-            onehot_ref[row * LANES : (row + 1) * LANES, at] = hit.astype(jnp.bfloat16)
+    inner_ref[...] = (slots - (bases.astype(jnp.int32) & -SLOT_TILE)) & (2 * SLOT_TILE - 1)
 
 
 def clear_lead(shifted):
@@ -130,7 +120,7 @@
 
 
 def early_kernel(owners, spread, order_ref, own_ref, pair_ref, parcel_hbm, table_ref, filter_hbm, weight_ref, *refs):
-    onehot_ref, tile_ref, start_ref, design_ref, *piece_refs, plain, shifted, filter_ref, parcel_ref, sems, small_sems = refs
+    inner_ref, tile_ref, start_ref, design_ref, *piece_refs, plain, shifted, filter_ref, parcel_ref, sems, small_sems = refs
     load_filter = pltpu.make_async_copy(filter_hbm, filter_ref, small_sems.at[0])
     load_parcel = pltpu.make_async_copy(parcel_hbm, parcel_ref, small_sems.at[1])
     load_filter.start()
@@ -156,7 +146,7 @@
 
     lax.fori_loop(0, width // LANES, columns, 0)
     load_parcel.wait()
-    places(owners, spread, parcel_ref, table_ref, onehot_ref, tile_ref, start_ref)
+    places(owners, spread, parcel_ref, table_ref, inner_ref, tile_ref, start_ref)
     wait_all(copies)
 
 
@@ -231,7 +221,7 @@
         in_specs=[VMEM()] * (1 + len(taken)) + [ANY()] * (len(after) + bool(ahead)),
         out_specs=[VMEM()] * (2 + len(ahead)),
         out_shape=[half, half] + ahead,
-        scratch_shapes=[pltpu.SemaphoreType.DMA((len(ahead), 4))] if ahead else [],
+        scratch_shapes=[pltpu.SemaphoreType.DMA((len(ahead),))] if ahead else [],
         compiler_params=pltpu.CompilerParams(vmem_limit_bytes=8 * MIB),
         cost_estimate=cost(2 * time_len * lanes * width, 2 * lanes * width),
         name="product",
@@ -247,16 +237,17 @@
         at += width
 
 
-def pack_kernel(spread, widths, places, first, later, start_ref, onehot_ref, tile_ref, *refs):
+def pack_kernel(spread, widths, places, first, later, outs, order_ref, start_ref, inner_ref, tile_ref, *refs):
+    *refs, summed, packed = refs
     if later:
         count, each = later
-        *terms, out_ref, send_ref, keep_ref, summed, packed = refs
+        *refs, send_ref, keep_ref = refs
+    terms, out_refs = refs[: len(refs) - outs], refs[len(refs) - outs :]
+    if later:
         rows = packed.shape[1]
         add_rows(terms[-count:], each, 3 * rows, send_ref)
         add_rows(terms[-count:], each, rows, keep_ref)
         terms = terms[:-count]
-    else:
-        *terms, out_ref, summed, packed = refs
     owners, rows = packed.shape[:2]
     if first:
         packed[...] = terms.pop(0)[...]
@@ -270,19 +261,25 @@
         summed[:, at : at + width] = total.astype(jnp.bfloat16)
         at += width
     step = VOX_BLOCK // LANES
+    slot_rows = lax.broadcasted_iota(jnp.int32, (2 * SLOT_TILE, VOX_BLOCK), 0)
 
     def moves(index, far):
         block = first + index
         values = summed[:, pl.ds(pl.multiple_of(index * VOX_BLOCK, VOX_BLOCK), VOX_BLOCK)]
-        onehot = onehot_ref[pl.ds(pl.multiple_of(block * VOX_BLOCK, VOX_BLOCK), VOX_BLOCK), :]
-        tiles = jnp.concatenate([tile_ref[pl.ds(block * step + i, 1), :] for i in range(step)], axis=1)
+        tiles, inner = (
+            jnp.concatenate([ref[pl.ds(block * step + i, 1), :] for i in range(step)], axis=1)
+            for ref in (tile_ref, inner_ref)
+        )
+        onehot = jnp.where(inner == slot_rows, 1.0, 0.0).astype(jnp.bfloat16)
         low = [start_ref[block, o] >> 7 for o in range(owners)]
         chosen = []
         for o in range(owners):
             tile = tiles - (o * spread + low[o])
             hit = jnp.where((tile == 2) if far else ((tile == 0) | (tile == 1)), 1.0, 0.0)
             chosen.append(values * hit.astype(jnp.bfloat16))
-        moved = jnp.dot(jnp.concatenate(chosen, axis=0), onehot, preferred_element_type=jnp.float32)
+        moved = lax.dot_general(
+            jnp.concatenate(chosen, axis=0), onehot, (((1,), (1,)), ((), ())), preferred_element_type=jnp.float32
+        )
         moved = moved.astype(jnp.bfloat16)
         out = []
         for o in range(owners):
@@ -317,7 +314,11 @@
     lax.fori_loop(0, count // 2, two, 0)
     if count % 2:
         blocks([count - 1])
-    out_ref[...] = packed[:, :, : out_ref.shape[2]]
+    if outs == 1:
+        out_refs[0][...] = packed[...]
+    else:
+        for d, ref in enumerate(out_refs):
+            ref[...] = packed[order_ref[d], :, : ref.shape[1]]
 
 
 def shards(features, hrf_filters, weights, voxel_parcel, parcel_owner):
@@ -363,12 +364,12 @@
     place = sum(((order >> bit) & 1) << (bits - 1 - bit) for bit in range(bits)).astype(jnp.int32)
 
     early_rows = 2 * time_block - ROWS
-    onehot, tiles, starts, early, *pieces = pl.pallas_call(
+    inner, tiles, starts, early, *pieces = pl.pallas_call(
         functools.partial(early_kernel, owners, spread),
         in_specs=[SMEM(), VMEM(), VMEM(), HBM(), VMEM(), HBM(), ANY()],
         out_specs=[VMEM()] * (4 + len(COPIES[0])),
         out_shape=[
-            jax.ShapeDtypeStruct((voxels, 2 * SLOT_TILE), jnp.bfloat16),
+            jax.ShapeDtypeStruct((voxels // LANES, LANES), jnp.int32),
             jax.ShapeDtypeStruct((voxels // LANES, LANES), jnp.int32),
             jax.ShapeDtypeStruct((marks, LANES), jnp.int32),
             jax.ShapeDtypeStruct((early_rows, lanes), jnp.bfloat16),
@@ -378,7 +379,7 @@
         + [
             pltpu.VMEM(filters.shape, jnp.float32),
             pltpu.VMEM((voxels // LANES, LANES), jnp.int32),
-            pltpu.SemaphoreType.DMA((len(COPIES[0]), 4)),
+            pltpu.SemaphoreType.DMA((len(COPIES[0]),)),
             pltpu.SemaphoreType.DMA((2,)),
         ],
         compiler_params=pltpu.CompilerParams(vmem_limit_bytes=8 * MIB),
@@ -399,7 +400,7 @@
         in_specs=[SMEM(), SMEM(), VMEM(), VMEM(), ANY()] + [VMEM()] * parts,
         out_specs=[VMEM()] * (1 + len(COPIES[1])),
         out_shape=[jax.ShapeDtypeStruct((time_len, lanes), jnp.bfloat16)] + room(1),
-        scratch_shapes=filter_scratch(time_len) + [pltpu.SemaphoreType.DMA((len(COPIES[1]), 4))],
+        scratch_shapes=filter_scratch(time_len) + [pltpu.SemaphoreType.DMA((len(COPIES[1]),))],
         compiler_params=pltpu.CompilerParams(vmem_limit_bytes=8 * MIB),
         cost_estimate=cost(0, 2 * bases * depth * copied[1]),
         name="design",
@@ -424,41 +425,87 @@
             own.append(lax.ppermute(send, "chan", [(i, i ^ (1 << bit)) for i in range(parts)]))
         sums.append(own)
         got.append(own[-1])
+    here = lax.axis_index("vox")
+    targets = jnp.arange(owners, dtype=jnp.int32) ^ here
+
     def pack(chunks, terms, spots, packed=(), later=()):
-        here = [widths[c] for c in chunks]
-        lanes_out = send_cap if chunks[-1] == CHUNKS - 1 else spread * SLOT_TILE
+        sizes = [widths[c] for c in chunks]
         spec = (len(later), bits) if later else None
+        if chunks[-1] == CHUNKS - 1:
+            outs = [jax.ShapeDtypeStruct((half, send_cap), jnp.bfloat16)] * owners
+        else:
+            outs = [jax.ShapeDtypeStruct((owners, half, spread * SLOT_TILE), jnp.bfloat16)]
+        more = []
+        if later:
+            more = [jax.ShapeDtypeStruct((half, voxels), jnp.bfloat16), pltpu.VMEM((half, voxels), jnp.bfloat16)]
         return pl.pallas_call(
-            functools.partial(pack_kernel, spread, here, spots, sum(widths[: chunks[0]]) // VOX_BLOCK, spec),
-            in_specs=[SMEM(), VMEM(), VMEM()] + [VMEM()] * (len(packed) + len(terms) + len(later)),
-            out_specs=[VMEM()] * (3 if later else 1),
-            out_shape=[jax.ShapeDtypeStruct((owners, half, lanes_out), jnp.bfloat16)]
-            + ([jax.ShapeDtypeStruct((half, voxels), jnp.bfloat16)] if later else [])
-            + ([pltpu.VMEM((half, voxels), jnp.bfloat16)] if later else []),
+            functools.partial(
+                pack_kernel, spread, sizes, spots, sum(widths[: chunks[0]]) // VOX_BLOCK, spec, len(outs)
+            ),
+            in_specs=[SMEM(), SMEM(), VMEM(), VMEM()] + [VMEM()] * (len(packed) + len(terms) + len(later)),
+            out_specs=[VMEM()] * (len(outs) + len(more)),
+            out_shape=outs + more,
             scratch_shapes=[
-                pltpu.VMEM((half, sum(here)), jnp.bfloat16),
+                pltpu.VMEM((half, sum(sizes)), jnp.bfloat16),
                 pltpu.VMEM((owners, half, spread * SLOT_TILE), jnp.bfloat16),
             ],
             compiler_params=pltpu.CompilerParams(vmem_limit_bytes=8 * MIB),
-            cost_estimate=cost(2 * half * owners * VOX_BLOCK * sum(here), 4 * half * sum(here)),
+            cost_estimate=cost(2 * half * owners * VOX_BLOCK * sum(sizes), 4 * half * sum(sizes)),
             name="pack",
-        )(starts, onehot, tiles, *packed, *terms, *later)
+        )(targets, starts, inner, tiles, *packed, *terms, *later)
 
     def deliver(packed):
-        return lax.all_to_all(packed, "vox", split_axis=0, concat_axis=0, tiled=True)
+        got = list(packed)
+        far, near = range(owners - 1, owners // 2 - 1, -1), range(owners // 2 - 1, -1, -1)
+        for d in [d for pair in zip(far, near) for d in pair if d]:
+            got[d] = lax.ppermute(packed[d], "vox", [(i, i ^ d) for i in range(owners)])
+        return got
 
     def early_terms(chunks):
         return [term for c in chunks for term in sums[c]], [[(0, 0)] * len(sums[c]) for c in chunks]
 
     low, high = range(PACK_FIRST), range(PACK_FIRST, CHUNKS)
-    packed, late_send, late_own = pack(low, *early_terms(low), later=[term for own in sums for term in own[:-1]])
+    packed = pack(low, *early_terms(low))
+    *one, late_send, late_own = pack(
+        high, *early_terms(high), packed=packed, later=[term for own in sums for term in own[:-1]]
+    )
     late = lax.ppermute(late_send, "chan", [(i, i ^ (1 << (bits - 1))) for i in range(parts)])
-    one = deliver(*pack(high, *early_terms(high), packed=[packed]))
+    one = deliver(one)
     starting = [sum(widths[:c]) for c in range(CHUNKS)]
-    two = deliver(
-        *pack(range(CHUNKS), [late_own, late] * CHUNKS, [[(0, first)] * 2 for first in starting])
-    )
-    return jnp.transpose(jnp.concatenate([one, two], axis=1), (0, 2, 1))
+    two = pack(range(CHUNKS), [late_own, late] * CHUNKS, [[(0, first)] * 2 for first in starting])
+    two = pl.pallas_call(
+        gate_kernel,
+        in_specs=[ANY()] * (2 * owners),
+        out_specs=[ANY()] * owners,
+        out_shape=[jax.ShapeDtypeStruct((half, send_cap), jnp.bfloat16)] * owners,
+        input_output_aliases={i: i for i in range(owners)},
+        name="gate",
+    )(*two, *one)
+    two = deliver(two)
+    owned = pl.pallas_call(
+        functools.partial(assemble_kernel, owners),
+        in_specs=[SMEM()] + [ANY()] * (2 * owners),
+        out_specs=HBM(),
+        out_shape=jax.ShapeDtypeStruct((owners, time_block, send_cap), jnp.bfloat16),
+        scratch_shapes=[pltpu.SemaphoreType.DMA((2 * owners,))],
+        name="assemble",
+    )(targets, *one, *two)
+    return jnp.transpose(owned, (0, 2, 1))
+
+
+def gate_kernel(*refs):
+    pass
+
+
+def assemble_kernel(owners, order_ref, *refs):
+    *parts, out_ref, sems = refs
+    half = out_ref.shape[1] // 2
+    copies = []
+    for i, ref in enumerate(parts):
+        rows = pl.ds(i // owners * half, half)
+        copies.append(pltpu.make_async_copy(ref, out_ref.at[order_ref[i % owners], rows, :], sems.at[i]))
+        copies[-1].start()
+    wait_all(copies)
 
 
 def added(terms, first, rows):

time: 100 us -> 127 us (1.27)
  Pallas kernels: 43.2 us -> 74.9 us
  blocking collectives: 21.5 us -> 0 us
  starting transfers between devices: 16.7 us -> 35.1 us
  local copies, waits for them, and re-layouts: 3.62 us -> 8.34 us
  waiting for transfers between devices: 12.1 us -> 8.14 us
  other arithmetic: 2.32 us -> 0.1 us
    pallas_call x3 -> x5, Pallas kernels: 8.39 us -> 50.6 us  [the longest x1 41.6 us: shards(): pl.pallas_call(functools.partial(assemble_kernel, owners), in_specs=[SMEM...]
    ppermute x0 -> x14, starting transfers between devices: none -> 23.3 us  [deliver(): got[d] = lax.ppermute(packed[d], 'vox', [(i, i ^ d) for i in range(owners)])]
    all_to_all x1 -> x0, blocking collectives: 21.5 us -> none  [deliver(): lax.all_to_all(packed, 'vox', split_axis=0, concat_axis=0, tiled=True)]
    ppermute x1, waiting for transfers between devices: 7.35 us -> 0.01 us  [shards(): lax.ppermute(late_send, 'chan', [(i, i ^ 1 << bits - 1) for i in range(pa...]
    ppermute x0 -> x14, waiting for transfers between devices: none -> 6.9 us  [deliver(): got[d] = lax.ppermute(packed[d], 'vox', [(i, i ^ d) for i in range(owners)])]
    pallas_call x4, Pallas kernels: 19 us -> 12.2 us  [product(): pl.pallas_call(functools.partial(product_kernel, len(taken), len(after),...]
    all_to_all x1 -> x0, starting transfers between devices: 5.94 us -> none  [deliver(): lax.all_to_all(packed, 'vox', split_axis=0, concat_axis=0, tiled=True)]
    unnamed x6 -> x50, local copies, waits for them, and re-layouts: 1.69 us -> 6.4 us
  transfers between devices with their start and end apart: 13 -> 26, of which waited for: 4 -> 4; matrix products, arithmetic and copies ran while one was open for 1% -> 1% of each run, Pallas kernels for 32% -> 18%
where the time goes in v9:
time: 127 us
  Pallas kernels  74.9 us (59%)
  starting transfers between devices  35.1 us (28%)
  local copies, waits for them, and re-layouts  8.34 us (7%)
  waiting for transfers between devices  8.14 us (6%)
    pallas_call x1, Pallas kernels, shards(): pl.pallas_call(functools.partial(assemble_kernel, owners), in_specs=[SMEM...  41.6 us
    ppermute x14, starting transfers between devices, deliver(): got[d] = lax.ppermute(packed[d], 'vox', [(i, i ^ d) for i in range(owners)])  23.3 us
    pallas_call x4, Pallas kernels, product(): pl.pallas_call(functools.partial(product_kernel, len(taken), len(after),...  12.2 us
    pallas_call x3, Pallas kernels, pack(): pl.pallas_call(functools.partial(pack_kernel, spread, sizes, spots, sum(w...  8.99 us
    pallas_call x1, Pallas kernels, shards(): pl.pallas_call(functools.partial(early_kernel, owners, spread), in_specs=...  7.24 us
    ppermute x14, waiting for transfers between devices, deliver(): got[d] = lax.ppermute(packed[d], 'vox', [(i, i ^ d) for i in range(owners)])  6.9 us
    ppermute x8, starting transfers between devices, shards(): lax.ppermute(send, 'chan', [(i, i ^ 1 << bit) for i in range(parts)])  6.76 us
    unnamed x50, local copies, waits for them, and re-layouts  6.4 us
  transfers between devices with their start and end apart: 26, of which 4 were waited for; matrix products, arithmetic and copies ran while one was open for 1% of the time, Pallas kernels for 18%

profile of v9, /device:TPU:0, one launch (start us, length us, event | category | flops | bytes accessed | tf_op | source)
XLA Modules:
  0.0 126.9 jit_solution(3134461757848367588)
XLA Ops:
  0.0 1.2 constant_dynamic-slice_fusion
  1.2 2.4 %collective-permute-start.2 = (bf16[64,1408]{1,0:T(8,128)(2,1)S(1)}, bf16[64,1408]{1,0:T(8,128)(2,1)S(1)}, u32[]{:S(2)}, u32[]{:S(2)}) collective-permute-start(bf16[64,1408]{1,0:T(8,128)(2,1)S(1)} %get-tuple-element.99), channel_id=1, source_target_pairs={{0,24},{8,16},{16,8},{24,0},{1,25},{9,17},{17,9},{25,1},{2,26},{10... | collective-permute-start | bytes 540680 | tf_op jit(solution)/shard_map/ppermute | solution.py:336
  4.4 0.7 pad_bitcast_fusion.table_ref
  5.4 7.2 %early.1 = (s32[40,128]{1,0:T(8,128)S(1)}, s32[40,128]{1,0:T(8,128)S(1)}, s32[24,128]{1,0:T(8,128)S(1)}, bf16[96,4224]{1,0:T(8,128)(2,1)S(1)}, bf16[3,1408,1024]...) custom-call(s32[4]{0:T(128)S(1)} %get-tuple-element.104.order_ref, ...), custom_call_target="tpu_custom_call" | custom-call | bytes 19464192 | tf_op jit(solution)/shard_map/early/pallas_call | solution.py:367
  12.7 4.9 %design.1 = (bf16[256,4224]{1,0:T(8,128)(2,1)S(1)}, bf16[3,1408,256]{2,1,0:T(8,128)(2,1)S(1)}, bf16[3,1408,1024]{2,1,0:T(8,128)(2,1)S(1)}) custom-call(s32[4]{0:T(128)S(1)} %get-tuple-element.104.order_ref, s32[4]{0:T(128)S(1)} %get-tuple-element.103.place_ref, bf16[96,4224]{1,0:T(8,128)(2,1)S(1)} %get-tuple-element.55.early_ref, ...), custom_call_target="tpu_custom_call" | custom-call | bytes 10813440 | tf_op jit(solution)/shard_map/design/pallas_call | solution.py:398
  17.6 2.5 %product.4 = (bf16[128,1024]{1,0:T(8,128)(2,1)S(1)}, bf16[128,1024]{1,0:T(8,128)(2,1)S(1)}) custom-call(bf16[256,4224]{1,0:T(8,128)(2,1)S(1)} %get-tuple-element.56.design_ref, bf16[3,1408,1024]{2,1,0:T(8,128)(2,1)S(1)} %get-tuple-element.57.refs_0_), custom_call_target="tpu_custom_call" | custom-call | flops 2214592512 | bytes 8650752 | tf_op jit(solution)/shard_map/product/pallas_call | solution.py:219
  20.5 3.6 %product.5 = (bf16[128,1536]{1,0:T(8,128)(2,1)S(1)}, bf16[128,1536]{1,0:T(8,128)(2,1)S(1)}, bf16[3,1408,512]{2,1,0:T(8,128)(2,1)S(1)}, bf16[3,1408,256]{2,1,0:T(8,128)(2,1)S(1)}) custom-call(bf16[256,4224]{1,0:T(8,128)(2,1)S(1)} %get-tuple-element.56.design_ref, bf16[3,1408,1280]{2,1,0:T(8,128)(2,1)S(1)} %get-tuple-element.60.refs_0_, ...), custom_call_target="tpu_custom_call" | custom-call | flops 3321888768 | bytes 12976128 | tf_op jit(solution)/shard_map/product/pallas_call | solution.py:219
  24.4 2.3 %collective-permute-start.4 = (bf16[32,1024]{1,0:T(8,128)(2,1)S(1)}, bf16[32,1024]{1,0:T(8,128)(2,1)S(1)}, u32[]{:S(2)}, u32[]{:S(2)}) collective-permute-start(bf16[32,1024]{1,0:T(8,128)(2,1)S(1)} %add_convert_fusion.3.refs_2_), channel_id=1, source_target_pairs={{0,16},{8,24},{16,0},{24,8},{1,17},{9,25},{17,1},{25,9},{2,18},{10... | collective-permute-start | bytes 196616 | tf_op jit(solution)/shard_map/ppermute | solution.py:425
  26.7 3.7 %product.6 = (bf16[128,1536]{1,0:T(8,128)(2,1)S(1)}, bf16[128,1536]{1,0:T(8,128)(2,1)S(1)}, bf16[3,1408,512]{2,1,0:T(8,128)(2,1)S(1)}, bf16[3,1408,256]{2,1,0:T(8,128)(2,1)S(1)}) custom-call(bf16[256,4224]{1,0:T(8,128)(2,1)S(1)} %get-tuple-element.56.design_ref, bf16[3,1408,1024]{2,1,0:T(8,128)(2,1)S(1)} %get-tuple-element.64.refs_0_, ...), custom_call_target="tpu_custom_call" | custom-call | flops 3321888768 | bytes 12976128 | tf_op jit(solution)/shard_map/product/pallas_call | solution.py:219
  30.7 2.5 %product.7 = (bf16[128,1024]{1,0:T(8,128)(2,1)S(1)}, bf16[128,1024]{1,0:T(8,128)(2,1)S(1)}) custom-call(bf16[256,4224]{1,0:T(8,128)(2,1)S(1)} %get-tuple-element.56.design_ref, bf16[3,1408,256]{2,1,0:T(8,128)(2,1)S(1)} %get-tuple-element.68.refs_0_, bf16[3,1408,512]{2,1,0:T(8,128)(2,1)S(1)} %get-tuple-element.69.refs_1_, ...), custom_call_target="tpu_custom_call" | custom-call | flops 2214592512 | bytes 8650752 | tf_op jit(solution)/shard_map/product/pallas_call | solution.py:219
  33.6 1.8 %collective-permute-start.8 = (bf16[32,1536]{1,0:T(8,128)(2,1)S(1)}, bf16[32,1536]{1,0:T(8,128)(2,1)S(1)}, u32[]{:S(2)}, u32[]{:S(2)}) collective-permute-start(bf16[32,1536]{1,0:T(8,128)(2,1)S(1)} %add_convert_fusion), channel_id=1, source_target_pairs={{0,16},{8,24},{16,0},{24,8},{1,17},{9,25},{17,1},{25,9},{2,18},{10... | collective-permute-start | bytes 294920 | tf_op jit(solution)/shard_map/ppermute | solution.py:425
  35.5 1.3 %collective-permute-start.10 = (bf16[32,1024]{1,0:T(8,128)(2,1)S(1)}, bf16[32,1024]{1,0:T(8,128)(2,1)S(1)}, u32[]{:S(2)}, u32[]{:S(2)}) collective-permute-start(bf16[32,1024]{1,0:T(8,128)(2,1)S(1)} %add_convert_fusion.2), channel_id=1, source_target_pairs={{0,16},{8,24},{16,0},{24,8},{1,17},{9,25},{17,1},{25,9},{2,18},{10... | collective-permute-start | bytes 196616 | tf_op jit(solution)/shard_map/ppermute | solution.py:425
  36.8 2.4 %pack.3.refs_0_ = bf16[8,32,1664]{2,1,0:T(8,128)(2,1)S(1)} custom-call(s32[8]{0:T(128)S(1)} %iota_xor_fusion.1.order_ref, s32[24,128]{1,0:T(8,128)S(1)} %get-tuple-element.52.start_ref, s32[40,128]{1,0:T(8,128)S(1)} %get-tuple-element.53.inner_ref, s32[40,128]{1,0:T(8,128)S(1)} %get-tuple-element.54.tile_ref, ...), custom_call_target="tpu_custom_call" | custom-call | flops 335544320 | bytes 327680 | tf_op jit(solution)/shard_map/pack/pallas_call | solution.py:441
  39.2 0.9 collective-permute-done.10.refs_6_
  40.1 2.6 %pack.4 = (bf16[32,1280]{1,0:T(8,128)(2,1)S(1)}, bf16[32,1280]{1,0:T(8,128)(2,1)S(1)}, bf16[32,1280]{1,0:T(8,128)(2,1)S(1)}, bf16[32,1280]{1,0:T(8,128)(2,1)S(1)...) custom-call(s32[8]{0:T(128)S(1)} %iota_xor_fusion.1.order_ref, ...), custom_call_target="tpu_custom_call" | custom-call | flops 335544320 | bytes 327680 | tf_op jit(solution)/shard_map/pack/pallas_call | solution.py:441
  42.7 1.8 %collective-permute-start.18 = (bf16[32,5120]{1,0:T(8,128)(2,1)S(1)}, bf16[32,5120]{1,0:T(8,128)(2,1)S(1)}, u32[]{:S(2)}, u32[]{:S(2)}) collective-permute-start(bf16[32,5120]{1,0:T(8,128)(2,1)S(1)} %get-tuple-element.82), channel_id=1, source_target_pairs={{0,16},{8,24},{16,0},{24,8},{1,17},{9,25},{17,1},{25,9},{2,18},{10... | collective-permute-start | bytes 983048 | tf_op jit(solution)/shard_map/ppermute | solution.py:472
  44.5 1.5 %collective-permute-start.11 = (bf16[32,1280]{1,0:T(8,128)(2,1)S(1)}, bf16[32,1280]{1,0:T(8,128)(2,1)S(1)}, u32[]{:S(2)}, u32[]{:S(2)}) collective-permute-start(bf16[32,1280]{1,0:T(8,128)(2,1)S(1)} %get-tuple-element.74), channel_id=1, source_target_pairs={{0,1},{1,0},{2,3},{3,2},{4,5},{5,4},{6,7},{7,6},{8,9},{9,8},{10,11... | collective-permute-start | bytes 245768 | tf_op jit(solution)/shard_map/ppermute | solution.py:461
  46.0 1.6 %collective-permute-start.12 = (bf16[32,1280]{1,0:T(8,128)(2,1)S(1)}, bf16[32,1280]{1,0:T(8,128)(2,1)S(1)}, u32[]{:S(2)}, u32[]{:S(2)}) collective-permute-start(bf16[32,1280]{1,0:T(8,128)(2,1)S(1)} %get-tuple-element.75), channel_id=1, source_target_pairs={{0,2},{1,3},{2,0},{3,1},{4,6},{5,7},{6,4},{7,5},{8,10},{9,11},{10,... | collective-permute-start | bytes 245768 | tf_op jit(solution)/shard_map/ppermute | solution.py:461
  48.0 2.6 %collective-permute-start.14 = (bf16[32,1280]{1,0:T(8,128)(2,1)S(1)}, bf16[32,1280]{1,0:T(8,128)(2,1)S(1)}, u32[]{:S(2)}, u32[]{:S(2)}) collective-permute-start(bf16[32,1280]{1,0:T(8,128)(2,1)S(1)} %get-tuple-element.77), channel_id=1, source_target_pairs={{0,4},{1,5},{2,6},{3,7},{4,0},{5,1},{6,2},{7,3},{8,12},{9,13},{10,... | collective-permute-start | bytes 245768 | tf_op jit(solution)/shard_map/ppermute | solution.py:461
  50.6 2.8 %collective-permute-start.15 = (bf16[32,1280]{1,0:T(8,128)(2,1)S(1)}, bf16[32,1280]{1,0:T(8,128)(2,1)S(1)}, u32[]{:S(2)}, u32[]{:S(2)}) collective-permute-start(bf16[32,1280]{1,0:T(8,128)(2,1)S(1)} %get-tuple-element.78), channel_id=1, source_target_pairs={{0,5},{1,4},{2,7},{3,6},{4,1},{5,0},{6,3},{7,2},{8,13},{9,12},{10,... | collective-permute-start | bytes 245768 | tf_op jit(solution)/shard_map/ppermute | solution.py:461
  53.4 2.1 %collective-permute-start.16 = (bf16[32,1280]{1,0:T(8,128)(2,1)S(1)}, bf16[32,1280]{1,0:T(8,128)(2,1)S(1)}, u32[]{:S(2)}, u32[]{:S(2)}) collective-permute-start(bf16[32,1280]{1,0:T(8,128)(2,1)S(1)} %get-tuple-element.79), channel_id=1, source_target_pairs={{0,6},{1,7},{2,4},{3,5},{4,2},{5,3},{6,0},{7,1},{8,14},{9,15},{10,... | collective-permute-start | bytes 245768 | tf_op jit(solution)/shard_map/ppermute | solution.py:461
  55.5 1.2 collective-permute-start.17
  56.7 4.0 %pack.5 = (bf16[32,1280]{1,0:T(8,128)(2,1)S(1)}, bf16[32,1280]{1,0:T(8,128)(2,1)S(1)}, bf16[32,1280]{1,0:T(8,128)(2,1)S(1)}, bf16[32,1280]{1,0:T(8,128)(2,1)S(1)...) custom-call(s32[8]{0:T(128)S(1)} %iota_xor_fusion.1.order_ref, ...), custom_call_target="tpu_custom_call" | custom-call | flops 671088640 | bytes 655360 | tf_op jit(solution)/shard_map/pack/pallas_call | solution.py:441
  66.5 2.0 %collective-permute-start.19 = (bf16[32,1280]{1,0:T(8,128)(2,1)}, bf16[32,1280]{1,0:T(8,128)(2,1)S(1)}, u32[]{:S(2)}, u32[]{:S(2)}) collective-permute-start(bf16[32,1280]{1,0:T(8,128)(2,1)} %get-tuple-element.92), channel_id=1, source_target_pairs={{0,1},{1,0},{2,3},{3,2},{4,5},{5,4},{6,7},{7,6},{8,9},{9,8},{10,11... | collective-permute-start | bytes 245768 | tf_op jit(solution)/shard_map/ppermute | solution.py:461
  68.5 1.5 %collective-permute-start.21 = (bf16[32,1280]{1,0:T(8,128)(2,1)}, bf16[32,1280]{1,0:T(8,128)(2,1)S(1)}, u32[]{:S(2)}, u32[]{:S(2)}) collective-permute-start(bf16[32,1280]{1,0:T(8,128)(2,1)} %get-tuple-element.94), channel_id=1, source_target_pairs={{0,3},{1,2},{2,1},{3,0},{4,7},{5,6},{6,5},{7,4},{8,11},{9,10},{10,... | collective-permute-start | bytes 245768 | tf_op jit(solution)/shard_map/ppermute | solution.py:461
  70.0 1.6 %collective-permute-start.22 = (bf16[32,1280]{1,0:T(8,128)(2,1)}, bf16[32,1280]{1,0:T(8,128)(2,1)S(1)}, u32[]{:S(2)}, u32[]{:S(2)}) collective-permute-start(bf16[32,1280]{1,0:T(8,128)(2,1)} %get-tuple-element.95), channel_id=1, source_target_pairs={{0,4},{1,5},{2,6},{3,7},{4,0},{5,1},{6,2},{7,3},{8,12},{9,13},{10,... | collective-permute-start | bytes 245768 | tf_op jit(solution)/shard_map/ppermute | solution.py:461
  71.6 2.7 %collective-permute-start.23 = (bf16[32,1280]{1,0:T(8,128)(2,1)}, bf16[32,1280]{1,0:T(8,128)(2,1)S(1)}, u32[]{:S(2)}, u32[]{:S(2)}) collective-permute-start(bf16[32,1280]{1,0:T(8,128)(2,1)} %get-tuple-element.96), channel_id=1, source_target_pairs={{0,5},{1,4},{2,7},{3,6},{4,1},{5,0},{6,3},{7,2},{8,13},{9,12},{10,... | collective-permute-start | bytes 245768 | tf_op jit(solution)/shard_map/ppermute | solution.py:461
  74.3 2.1 %collective-permute-start.24 = (bf16[32,1280]{1,0:T(8,128)(2,1)}, bf16[32,1280]{1,0:T(8,128)(2,1)S(1)}, u32[]{:S(2)}, u32[]{:S(2)}) collective-permute-start(bf16[32,1280]{1,0:T(8,128)(2,1)} %get-tuple-element.97), channel_id=1, source_target_pairs={{0,6},{1,7},{2,4},{3,5},{4,2},{5,3},{6,0},{7,1},{8,14},{9,15},{10,... | collective-permute-start | bytes 245768 | tf_op jit(solution)/shard_map/ppermute | solution.py:461
  76.4 1.2 collective-permute-start.25
  77.7 3.2 %collective-permute-done.22.refs_12_ = bf16[32,1280]{1,0:T(8,128)(2,1)S(1)} collective-permute-done((bf16[32,1280]{1,0:T(8,128)(2,1)}, bf16[32,1280]{1,0:T(8,128)(2,1)S(1)}, u32[]{:S(2)}, u32[]{:S(2)}) %collective-permute-start.22) | collective-permute-done | bytes 81952 | tf_op jit(solution)/shard_map/ppermute | solution.py:461
  80.9 3.7 %collective-permute-done.23.refs_13_ = bf16[32,1280]{1,0:T(8,128)(2,1)S(1)} collective-permute-done((bf16[32,1280]{1,0:T(8,128)(2,1)}, bf16[32,1280]{1,0:T(8,128)(2,1)S(1)}, u32[]{:S(2)}, u32[]{:S(2)}) %collective-permute-start.23) | collective-permute-done | bytes 81952 | tf_op jit(solution)/shard_map/ppermute | solution.py:461
  85.3 41.6 %assemble.1 = bf16[8,64,1280]{2,1,0:T(8,128)(2,1)} custom-call(s32[8]{0:T(128)} %copy-done.10, bf16[32,1280]{1,0:T(8,128)(2,1)} %copy-done.1, bf16[32,1280]{1,0:T(8,128)(2,1)} %copy-done.11, bf16[32,1280]{1,0:T(8,128)(2,1)} %copy-done.12, bf16[32,1280]{1,0:T(8,128)(2,1)} %copy-done.13, bf16[32,1280]{1,0:T(8,128)(2,1)} %copy-done.14, ...), custom_call_target="tpu_custom_call" | custom-call | tf_op jit(solution)/shard_map/assemble/pallas_call | solution.py:485
  (89 shorter events, 9.3 us)
Async XLA Ops:
  1.2 11.4 %collective-permute-start.2 = (bf16[64,1408]{1,0:T(8,128)(2,1)S(1)}, bf16[64,1408]{1,0:T(8,128)(2,1)S(1)}, u32[]{:S(2)}, u32[]{:S(2)}) collective-permute-start(bf16[64,1408]{1,0:T(8,128)(2,1)S(1)} %get-tuple-element.99), channel_id=1, source_target_pairs={{0,24},{8,16},{16,8},{24,0},{1,25},{9,17},{17,9},{25,1},{2,26},{10... | collective-permute-start | bytes 540680 | tf_op jit(solution)/shard_map/ppermute | solution.py:336
  3.7 1.7 %collective-permute-start = (bf16[64,1408]{1,0:T(8,128)(2,1)S(1)}, bf16[64,1408]{1,0:T(8,128)(2,1)S(1)}, u32[]{:S(2)}, u32[]{:S(2)}) collective-permute-start(bf16[64,1408]{1,0:T(8,128)(2,1)S(1)} %get-tuple-element.100), channel_id=1, source_target_pairs={{0,8},{8,0},{16,24},{24,16},{1,9},{9,1},{17,25},{25,17},{2,10},{10... | collective-permute-start | bytes 540680 | tf_op jit(solution)/shard_map/ppermute | solution.py:336
  4.4 8.3 %collective-permute-start.1 = (bf16[64,1408]{1,0:T(8,128)(2,1)S(1)}, bf16[64,1408]{1,0:T(8,128)(2,1)S(1)}, u32[]{:S(2)}, u32[]{:S(2)}) collective-permute-start(bf16[64,1408]{1,0:T(8,128)(2,1)S(1)} %get-tuple-element.102), channel_id=1, source_target_pairs={{0,16},{8,24},{16,0},{24,8},{1,17},{9,25},{17,1},{25,9},{2,18},{10... | collective-permute-start | bytes 540680 | tf_op jit(solution)/shard_map/ppermute | solution.py:336
  20.1 4.3 %collective-permute-start.3 = (bf16[128,1024]{1,0:T(8,128)(2,1)S(1)}, bf16[128,1024]{1,0:T(8,128)(2,1)S(1)}, u32[]{:S(2)}, u32[]{:S(2)}) collective-permute-start(bf16[128,1024]{1,0:T(8,128)(2,1)S(1)} %get-tuple-element.59), channel_id=1, source_target_pairs={{0,8},{8,0},{16,24},{24,16},{1,9},{9,1},{17,25},{25,17},{2,10},{10... | collective-permute-start | bytes 786440 | tf_op jit(solution)/shard_map/ppermute | solution.py:425
  24.1 6.3 %collective-permute-start.5 = (bf16[128,1536]{1,0:T(8,128)(2,1)S(1)}, bf16[128,1536]{1,0:T(8,128)(2,1)S(1)}, u32[]{:S(2)}, u32[]{:S(2)}) collective-permute-start(bf16[128,1536]{1,0:T(8,128)(2,1)S(1)} %get-tuple-element.63), channel_id=1, source_target_pairs={{0,8},{8,0},{16,24},{24,16},{1,9},{9,1},{17,25},{25,17},{2,10},{10... | collective-permute-start | bytes 1179656 | tf_op jit(solution)/shard_map/ppermute | solution.py:425
  24.4 6.3 %collective-permute-start.4 = (bf16[32,1024]{1,0:T(8,128)(2,1)S(1)}, bf16[32,1024]{1,0:T(8,128)(2,1)S(1)}, u32[]{:S(2)}, u32[]{:S(2)}) collective-permute-start(bf16[32,1024]{1,0:T(8,128)(2,1)S(1)} %add_convert_fusion.3.refs_2_), channel_id=1, source_target_pairs={{0,16},{8,24},{16,0},{24,8},{1,17},{9,25},{17,1},{25,9},{2,18},{10... | collective-permute-start | bytes 196616 | tf_op jit(solution)/shard_map/ppermute | solution.py:425
  30.4 3.2 %collective-permute-start.7 = (bf16[128,1536]{1,0:T(8,128)(2,1)S(1)}, bf16[128,1536]{1,0:T(8,128)(2,1)S(1)}, u32[]{:S(2)}, u32[]{:S(2)}) collective-permute-start(bf16[128,1536]{1,0:T(8,128)(2,1)S(1)} %get-tuple-element.67), channel_id=1, source_target_pairs={{0,8},{8,0},{16,24},{24,16},{1,9},{9,1},{17,25},{25,17},{2,10},{10... | collective-permute-start | bytes 1179656 | tf_op jit(solution)/shard_map/ppermute | solution.py:425
  30.5 6.3 %collective-permute-start.6 = (bf16[32,1536]{1,0:T(8,128)(2,1)S(1)}, bf16[32,1536]{1,0:T(8,128)(2,1)S(1)}, u32[]{:S(2)}, u32[]{:S(2)}) collective-permute-start(bf16[32,1536]{1,0:T(8,128)(2,1)S(1)} %add_convert_fusion.1.refs_3_), channel_id=1, source_target_pairs={{0,16},{8,24},{16,0},{24,8},{1,17},{9,25},{17,1},{25,9},{2,18},{10... | collective-permute-start | bytes 294920 | tf_op jit(solution)/shard_map/ppermute | solution.py:425
  33.1 2.3 %collective-permute-start.9 = (bf16[128,1024]{1,0:T(8,128)(2,1)S(1)}, bf16[128,1024]{1,0:T(8,128)(2,1)S(1)}, u32[]{:S(2)}, u32[]{:S(2)}) collective-permute-start(bf16[128,1024]{1,0:T(8,128)(2,1)S(1)} %get-tuple-element.72), channel_id=1, source_target_pairs={{0,8},{8,0},{16,24},{24,16},{1,9},{9,1},{17,25},{25,17},{2,10},{10... | collective-permute-start | bytes 786440 | tf_op jit(solution)/shard_map/ppermute | solution.py:425
  33.6 6.5 %collective-permute-start.8 = (bf16[32,1536]{1,0:T(8,128)(2,1)S(1)}, bf16[32,1536]{1,0:T(8,128)(2,1)S(1)}, u32[]{:S(2)}, u32[]{:S(2)}) collective-permute-start(bf16[32,1536]{1,0:T(8,128)(2,1)S(1)} %add_convert_fusion), channel_id=1, source_target_pairs={{0,16},{8,24},{16,0},{24,8},{1,17},{9,25},{17,1},{25,9},{2,18},{10... | collective-permute-start | bytes 294920 | tf_op jit(solution)/shard_map/ppermute | solution.py:425
  35.5 4.6 %collective-permute-start.10 = (bf16[32,1024]{1,0:T(8,128)(2,1)S(1)}, bf16[32,1024]{1,0:T(8,128)(2,1)S(1)}, u32[]{:S(2)}, u32[]{:S(2)}) collective-permute-start(bf16[32,1024]{1,0:T(8,128)(2,1)S(1)} %add_convert_fusion.2), channel_id=1, source_target_pairs={{0,16},{8,24},{16,0},{24,8},{1,17},{9,25},{17,1},{25,9},{2,18},{10... | collective-permute-start | bytes 196616 | tf_op jit(solution)/shard_map/ppermute | solution.py:425
  36.8 23.9 %copy-start.10 = (s32[8]{0:T(128)}, s32[8]{0:T(128)S(1)}, u32[]{:S(2)}) copy-start(s32[8]{0:T(128)S(1)} %iota_xor_fusion.1.order_ref) | copy-start | bytes 100
  42.7 18.0 %copy-start.1 = (bf16[32,1280]{1,0:T(8,128)(2,1)}, bf16[32,1280]{1,0:T(8,128)(2,1)S(1)}, u32[]{:S(2)}) copy-start(bf16[32,1280]{1,0:T(8,128)(2,1)S(1)} %get-tuple-element.73.refs_8_.refs_0_) | copy-start | bytes 245764
  42.7 12.8 %collective-permute-start.18 = (bf16[32,5120]{1,0:T(8,128)(2,1)S(1)}, bf16[32,5120]{1,0:T(8,128)(2,1)S(1)}, u32[]{:S(2)}, u32[]{:S(2)}) collective-permute-start(bf16[32,5120]{1,0:T(8,128)(2,1)S(1)} %get-tuple-element.82), channel_id=1, source_target_pairs={{0,16},{8,24},{16,0},{24,8},{1,17},{9,25},{17,1},{25,9},{2,18},{10... | collective-permute-start | bytes 983048 | tf_op jit(solution)/shard_map/ppermute | solution.py:472
  44.5 6.1 %collective-permute-start.11 = (bf16[32,1280]{1,0:T(8,128)(2,1)S(1)}, bf16[32,1280]{1,0:T(8,128)(2,1)S(1)}, u32[]{:S(2)}, u32[]{:S(2)}) collective-permute-start(bf16[32,1280]{1,0:T(8,128)(2,1)S(1)} %get-tuple-element.74), channel_id=1, source_target_pairs={{0,1},{1,0},{2,3},{3,2},{4,5},{5,4},{6,7},{7,6},{8,9},{9,8},{10,11... | collective-permute-start | bytes 245768 | tf_op jit(solution)/shard_map/ppermute | solution.py:461
  46.0 7.3 %collective-permute-start.12 = (bf16[32,1280]{1,0:T(8,128)(2,1)S(1)}, bf16[32,1280]{1,0:T(8,128)(2,1)S(1)}, u32[]{:S(2)}, u32[]{:S(2)}) collective-permute-start(bf16[32,1280]{1,0:T(8,128)(2,1)S(1)} %get-tuple-element.75), channel_id=1, source_target_pairs={{0,2},{1,3},{2,0},{3,1},{4,6},{5,7},{6,4},{7,5},{8,10},{9,11},{10,... | collective-permute-start | bytes 245768 | tf_op jit(solution)/shard_map/ppermute | solution.py:461
  47.6 18.1 %collective-permute-start.13 = (bf16[32,1280]{1,0:T(8,128)(2,1)S(1)}, bf16[32,1280]{1,0:T(8,128)(2,1)S(1)}, u32[]{:S(2)}, u32[]{:S(2)}) collective-permute-start(bf16[32,1280]{1,0:T(8,128)(2,1)S(1)} %get-tuple-element.76), channel_id=1, source_target_pairs={{0,3},{1,2},{2,1},{3,0},{4,7},{5,6},{6,5},{7,4},{8,11},{9,10},{10,... | collective-permute-start | bytes 245768 | tf_op jit(solution)/shard_map/ppermute | solution.py:461
  48.0 17.7 %collective-permute-start.14 = (bf16[32,1280]{1,0:T(8,128)(2,1)S(1)}, bf16[32,1280]{1,0:T(8,128)(2,1)S(1)}, u32[]{:S(2)}, u32[]{:S(2)}) collective-permute-start(bf16[32,1280]{1,0:T(8,128)(2,1)S(1)} %get-tuple-element.77), channel_id=1, source_target_pairs={{0,4},{1,5},{2,6},{3,7},{4,0},{5,1},{6,2},{7,3},{8,12},{9,13},{10,... | collective-permute-start | bytes 245768 | tf_op jit(solution)/shard_map/ppermute | solution.py:461
  50.6 15.2 %copy-start.11 = (bf16[32,1280]{1,0:T(8,128)(2,1)}, bf16[32,1280]{1,0:T(8,128)(2,1)S(1)}, u32[]{:S(2)}) copy-start(bf16[32,1280]{1,0:T(8,128)(2,1)S(1)} %collective-permute-done.11.refs_9_.refs_1_) | copy-start | bytes 245764
  50.6 15.1 %collective-permute-start.15 = (bf16[32,1280]{1,0:T(8,128)(2,1)S(1)}, bf16[32,1280]{1,0:T(8,128)(2,1)S(1)}, u32[]{:S(2)}, u32[]{:S(2)}) collective-permute-start(bf16[32,1280]{1,0:T(8,128)(2,1)S(1)} %get-tuple-element.78), channel_id=1, source_target_pairs={{0,5},{1,4},{2,7},{3,6},{4,1},{5,0},{6,3},{7,2},{8,13},{9,12},{10,... | collective-permute-start | bytes 245768 | tf_op jit(solution)/shard_map/ppermute | solution.py:461
  53.4 12.4 %copy-start.12 = (bf16[32,1280]{1,0:T(8,128)(2,1)}, bf16[32,1280]{1,0:T(8,128)(2,1)S(1)}, u32[]{:S(2)}) copy-start(bf16[32,1280]{1,0:T(8,128)(2,1)S(1)} %collective-permute-done.12.refs_10_.refs_2_) | copy-start | bytes 245764
  53.4 12.4 %collective-permute-start.16 = (bf16[32,1280]{1,0:T(8,128)(2,1)S(1)}, bf16[32,1280]{1,0:T(8,128)(2,1)S(1)}, u32[]{:S(2)}, u32[]{:S(2)}) collective-permute-start(bf16[32,1280]{1,0:T(8,128)(2,1)S(1)} %get-tuple-element.79), channel_id=1, source_target_pairs={{0,6},{1,7},{2,4},{3,5},{4,2},{5,3},{6,0},{7,1},{8,14},{9,15},{10,... | collective-permute-start | bytes 245768 | tf_op jit(solution)/shard_map/ppermute | solution.py:461
  55.5 10.3 %collective-permute-start.17 = (bf16[32,1280]{1,0:T(8,128)(2,1)S(1)}, bf16[32,1280]{1,0:T(8,128)(2,1)S(1)}, u32[]{:S(2)}, u32[]{:S(2)}) collective-permute-start(bf16[32,1280]{1,0:T(8,128)(2,1)S(1)} %get-tuple-element.80), channel_id=1, source_target_pairs={{0,7},{1,6},{2,5},{3,4},{4,3},{5,2},{6,1},{7,0},{8,15},{9,14},{10,... | collective-permute-start | bytes 245768 | tf_op jit(solution)/shard_map/ppermute | solution.py:461
  66.5 7.9 %collective-permute-start.19 = (bf16[32,1280]{1,0:T(8,128)(2,1)}, bf16[32,1280]{1,0:T(8,128)(2,1)S(1)}, u32[]{:S(2)}, u32[]{:S(2)}) collective-permute-start(bf16[32,1280]{1,0:T(8,128)(2,1)} %get-tuple-element.92), channel_id=1, source_target_pairs={{0,1},{1,0},{2,3},{3,2},{4,5},{5,4},{6,7},{7,6},{8,9},{9,8},{10,11... | collective-permute-start | bytes 245768 | tf_op jit(solution)/shard_map/ppermute | solution.py:461
  68.5 7.9 %collective-permute-start.20 = (bf16[32,1280]{1,0:T(8,128)(2,1)}, bf16[32,1280]{1,0:T(8,128)(2,1)S(1)}, u32[]{:S(2)}, u32[]{:S(2)}) collective-permute-start(bf16[32,1280]{1,0:T(8,128)(2,1)} %get-tuple-element.93), channel_id=1, source_target_pairs={{0,2},{1,3},{2,0},{3,1},{4,6},{5,7},{6,4},{7,5},{8,10},{9,11},{10,... | collective-permute-start | bytes 245768 | tf_op jit(solution)/shard_map/ppermute | solution.py:461
  68.5 9.2 %collective-permute-start.21 = (bf16[32,1280]{1,0:T(8,128)(2,1)}, bf16[32,1280]{1,0:T(8,128)(2,1)S(1)}, u32[]{:S(2)}, u32[]{:S(2)}) collective-permute-start(bf16[32,1280]{1,0:T(8,128)(2,1)} %get-tuple-element.94), channel_id=1, source_target_pairs={{0,3},{1,2},{2,1},{3,0},{4,7},{5,6},{6,5},{7,4},{8,11},{9,10},{10,... | collective-permute-start | bytes 245768 | tf_op jit(solution)/shard_map/ppermute | solution.py:461
  70.0 10.9 %collective-permute-start.22 = (bf16[32,1280]{1,0:T(8,128)(2,1)}, bf16[32,1280]{1,0:T(8,128)(2,1)S(1)}, u32[]{:S(2)}, u32[]{:S(2)}) collective-permute-start(bf16[32,1280]{1,0:T(8,128)(2,1)} %get-tuple-element.95), channel_id=1, source_target_pairs={{0,4},{1,5},{2,6},{3,7},{4,0},{5,1},{6,2},{7,3},{8,12},{9,13},{10,... | collective-permute-start | bytes 245768 | tf_op jit(solution)/shard_map/ppermute | solution.py:461
  71.6 12.9 %collective-permute-start.23 = (bf16[32,1280]{1,0:T(8,128)(2,1)}, bf16[32,1280]{1,0:T(8,128)(2,1)S(1)}, u32[]{:S(2)}, u32[]{:S(2)}) collective-permute-start(bf16[32,1280]{1,0:T(8,128)(2,1)} %get-tuple-element.96), channel_id=1, source_target_pairs={{0,5},{1,4},{2,7},{3,6},{4,1},{5,0},{6,3},{7,2},{8,13},{9,12},{10,... | collective-permute-start | bytes 245768 | tf_op jit(solution)/shard_map/ppermute | solution.py:461
  74.3 10.2 %copy-start.18 = (bf16[32,1280]{1,0:T(8,128)(2,1)}, bf16[32,1280]{1,0:T(8,128)(2,1)S(1)}, u32[]{:S(2)}) copy-start(bf16[32,1280]{1,0:T(8,128)(2,1)S(1)} %collective-permute-done.19.refs_9_) | copy-start | bytes 245764
  74.3 10.2 %collective-permute-start.24 = (bf16[32,1280]{1,0:T(8,128)(2,1)}, bf16[32,1280]{1,0:T(8,128)(2,1)S(1)}, u32[]{:S(2)}, u32[]{:S(2)}) collective-permute-start(bf16[32,1280]{1,0:T(8,128)(2,1)} %get-tuple-element.97), channel_id=1, source_target_pairs={{0,6},{1,7},{2,4},{3,5},{4,2},{5,3},{6,0},{7,1},{8,14},{9,15},{10,... | collective-permute-start | bytes 245768 | tf_op jit(solution)/shard_map/ppermute | solution.py:461
  76.4 8.2 %copy-start.19 = (bf16[32,1280]{1,0:T(8,128)(2,1)}, bf16[32,1280]{1,0:T(8,128)(2,1)S(1)}, u32[]{:S(2)}) copy-start(bf16[32,1280]{1,0:T(8,128)(2,1)S(1)} %collective-permute-done.20.refs_10_) | copy-start | bytes 245764
  76.4 8.1 %collective-permute-start.25 = (bf16[32,1280]{1,0:T(8,128)(2,1)}, bf16[32,1280]{1,0:T(8,128)(2,1)S(1)}, u32[]{:S(2)}, u32[]{:S(2)}) collective-permute-start(bf16[32,1280]{1,0:T(8,128)(2,1)} %get-tuple-element.98), channel_id=1, source_target_pairs={{0,7},{1,6},{2,5},{3,4},{4,3},{5,2},{6,1},{7,0},{8,15},{9,14},{10,... | collective-permute-start | bytes 245768 | tf_op jit(solution)/shard_map/ppermute | solution.py:461
  (19 other events, 28.3 us)

commit v10 on v9

--- a/solution.py
+++ b/solution.py
@@ -475,16 +475,15 @@
     two = pack(range(CHUNKS), [late_own, late] * CHUNKS, [[(0, first)] * 2 for first in starting])
     two = pl.pallas_call(
         gate_kernel,
-        in_specs=[ANY()] * (2 * owners),
-        out_specs=[ANY()] * owners,
+        in_specs=[VMEM()] * (2 * owners),
+        out_specs=[VMEM()] * owners,
         out_shape=[jax.ShapeDtypeStruct((half, send_cap), jnp.bfloat16)] * owners,
-        input_output_aliases={i: i for i in range(owners)},
         name="gate",
     )(*two, *one)
     two = deliver(two)
     owned = pl.pallas_call(
         functools.partial(assemble_kernel, owners),
-        in_specs=[SMEM()] + [ANY()] * (2 * owners),
+        in_specs=[SMEM()] + [VMEM()] * (2 * owners),
         out_specs=HBM(),
         out_shape=jax.ShapeDtypeStruct((owners, time_block, send_cap), jnp.bfloat16),
         scratch_shapes=[pltpu.SemaphoreType.DMA((2 * owners,))],
@@ -494,7 +493,9 @@
 
 
 def gate_kernel(*refs):
-    pass
+    count = len(refs) // 3
+    for given, out in zip(refs[:count], refs[2 * count :]):
+        out[...] = given[...]
 
 
 def assemble_kernel(owners, order_ref, *refs):

time: 127 us -> 90.4 us (0.71)
  Pallas kernels: 74.9 us -> 38.1 us
    pallas_call x1, Pallas kernels: 41.6 us -> 2.56 us  [shards(): pl.pallas_call(functools.partial(assemble_kernel, owners), in_specs=[SMEM...]
    pallas_call x1, Pallas kernels: 0.01 us -> 2.22 us  [shards(): pl.pallas_call(gate_kernel, in_specs=[VMEM()] * (2 * owners), out_specs=[...]
  transfers between devices with their start and end apart: 26 -> 26, of which waited for: 4 -> 4; matrix products, arithmetic and copies ran while one was open for 1% -> 1% of each run, Pallas kernels for 18% -> 26%
where the time goes in v10:
time: 90.4 us; the launch traced here: 90.1 us
  Pallas kernels  38.1 us (42%)
  starting transfers between devices  35.1 us (39%)
  local copies, waits for them, and re-layouts  8.31 us (9%)
  waiting for transfers between devices  8.11 us (9%)
    ppermute x14, starting transfers between devices, deliver(): got[d] = lax.ppermute(packed[d], 'vox', [(i, i ^ d) for i in range(owners)])  23.4 us
    pallas_call x4, Pallas kernels, product(): pl.pallas_call(functools.partial(product_kernel, len(taken), len(after),...  12.2 us
    pallas_call x3, Pallas kernels, pack(): pl.pallas_call(functools.partial(pack_kernel, spread, sizes, spots, sum(w...  8.99 us
    pallas_call x1, Pallas kernels, shards(): pl.pallas_call(functools.partial(early_kernel, owners, spread), in_specs=...  7.24 us
    ppermute x14, waiting for transfers between devices, deliver(): got[d] = lax.ppermute(packed[d], 'vox', [(i, i ^ d) for i in range(owners)])  6.87 us
    ppermute x8, starting transfers between devices, shards(): lax.ppermute(send, 'chan', [(i, i ^ 1 << bit) for i in range(parts)])  6.76 us
    unnamed x50, local copies, waits for them, and re-layouts  6.38 us
    pallas_call x1, Pallas kernels, shards(): pl.pallas_call(functools.partial(design_kernel, parts, firsts[1]), in_spe...  4.9 us
  transfers between devices with their start and end apart: 26, of which 4 were waited for; matrix products, arithmetic and copies ran while one was open for 1% of the time, Pallas kernels for 26%

profile of v10, /device:TPU:0, one launch (start us, length us, event | category | flops | bytes accessed | tf_op | source)
XLA Modules:
  0.0 90.1 jit_solution(153504722958725813)
XLA Ops:
  0.0 1.2 %constant_dynamic-slice_fusion = (bf16[64,1408]{1,0:T(8,128)(2,1)S(1)}, bf16[64,1408]{1,0:T(8,128)(2,1)S(1)}, bf16[64,1408]{1,0:T(8,128)(2,1)S(1)}, bf16[64,1408]{1,0:T(8,128)(2,1)S(1)}) fusion(bf16[64,5632]{1,0:T(8,128)(2,1)} %param.5, s32[]{:T(128)S(6)} %select_n.15, s32[]{:T(128)S(6)} %select_n.13, s32[]{:T(128)S(6)} %select_n.12, s32[]{:T(128)S(6)} %select_n.14), kind=kLoop, calls=%fused_computation.5 | loop fusion | bytes 1441808 | tf_op jit(solution)/shard_map/dynamic_slice | solution.py:334
  1.2 2.4 %collective-permute-start.2 = (bf16[64,1408]{1,0:T(8,128)(2,1)S(1)}, bf16[64,1408]{1,0:T(8,128)(2,1)S(1)}, u32[]{:S(2)}, u32[]{:S(2)}) collective-permute-start(bf16[64,1408]{1,0:T(8,128)(2,1)S(1)} %get-tuple-element.99), channel_id=1, source_target_pairs={{0,24},{8,16},{16,8},{24,0},{1,25},{9,17},{17,9},{25,1},{2,26},{10... | collective-permute-start | bytes 540680 | tf_op jit(solution)/shard_map/ppermute | solution.py:336
  5.4 7.2 %early.1 = (s32[40,128]{1,0:T(8,128)S(1)}, s32[40,128]{1,0:T(8,128)S(1)}, s32[24,128]{1,0:T(8,128)S(1)}, bf16[96,4224]{1,0:T(8,128)(2,1)S(1)}, bf16[3,1408,1024]...) custom-call(s32[4]{0:T(128)S(1)} %get-tuple-element.104.order_ref, ...), custom_call_target="tpu_custom_call" | custom-call | bytes 19464192 | tf_op jit(solution)/shard_map/early/pallas_call | solution.py:367
  12.7 4.9 %design.1 = (bf16[256,4224]{1,0:T(8,128)(2,1)S(1)}, bf16[3,1408,256]{2,1,0:T(8,128)(2,1)S(1)}, bf16[3,1408,1024]{2,1,0:T(8,128)(2,1)S(1)}) custom-call(s32[4]{0:T(128)S(1)} %get-tuple-element.104.order_ref, s32[4]{0:T(128)S(1)} %get-tuple-element.103.place_ref, bf16[96,4224]{1,0:T(8,128)(2,1)S(1)} %get-tuple-element.55.early_ref, ...), custom_call_target="tpu_custom_call" | custom-call | bytes 10813440 | tf_op jit(solution)/shard_map/design/pallas_call | solution.py:398
  17.6 2.5 %product.4 = (bf16[128,1024]{1,0:T(8,128)(2,1)S(1)}, bf16[128,1024]{1,0:T(8,128)(2,1)S(1)}) custom-call(bf16[256,4224]{1,0:T(8,128)(2,1)S(1)} %get-tuple-element.56.design_ref, bf16[3,1408,1024]{2,1,0:T(8,128)(2,1)S(1)} %get-tuple-element.57.refs_0_), custom_call_target="tpu_custom_call" | custom-call | flops 2214592512 | bytes 8650752 | tf_op jit(solution)/shard_map/product/pallas_call | solution.py:219
  20.5 3.6 %product.5 = (bf16[128,1536]{1,0:T(8,128)(2,1)S(1)}, bf16[128,1536]{1,0:T(8,128)(2,1)S(1)}, bf16[3,1408,512]{2,1,0:T(8,128)(2,1)S(1)}, bf16[3,1408,256]{2,1,0:T(8,128)(2,1)S(1)}) custom-call(bf16[256,4224]{1,0:T(8,128)(2,1)S(1)} %get-tuple-element.56.design_ref, bf16[3,1408,1280]{2,1,0:T(8,128)(2,1)S(1)} %get-tuple-element.60.refs_0_, ...), custom_call_target="tpu_custom_call" | custom-call | flops 3321888768 | bytes 12976128 | tf_op jit(solution)/shard_map/product/pallas_call | solution.py:219
  24.4 2.3 %collective-permute-start.4 = (bf16[32,1024]{1,0:T(8,128)(2,1)S(1)}, bf16[32,1024]{1,0:T(8,128)(2,1)S(1)}, u32[]{:S(2)}, u32[]{:S(2)}) collective-permute-start(bf16[32,1024]{1,0:T(8,128)(2,1)S(1)} %add_convert_fusion.3.refs_2_), channel_id=1, source_target_pairs={{0,16},{8,24},{16,0},{24,8},{1,17},{9,25},{17,1},{25,9},{2,18},{10... | collective-permute-start | bytes 196616 | tf_op jit(solution)/shard_map/ppermute | solution.py:425
  26.7 3.7 %product.6 = (bf16[128,1536]{1,0:T(8,128)(2,1)S(1)}, bf16[128,1536]{1,0:T(8,128)(2,1)S(1)}, bf16[3,1408,512]{2,1,0:T(8,128)(2,1)S(1)}, bf16[3,1408,256]{2,1,0:T(8,128)(2,1)S(1)}) custom-call(bf16[256,4224]{1,0:T(8,128)(2,1)S(1)} %get-tuple-element.56.design_ref, bf16[3,1408,1024]{2,1,0:T(8,128)(2,1)S(1)} %get-tuple-element.64.refs_0_, ...), custom_call_target="tpu_custom_call" | custom-call | flops 3321888768 | bytes 12976128 | tf_op jit(solution)/shard_map/product/pallas_call | solution.py:219
  30.7 2.5 %product.7 = (bf16[128,1024]{1,0:T(8,128)(2,1)S(1)}, bf16[128,1024]{1,0:T(8,128)(2,1)S(1)}) custom-call(bf16[256,4224]{1,0:T(8,128)(2,1)S(1)} %get-tuple-element.56.design_ref, bf16[3,1408,256]{2,1,0:T(8,128)(2,1)S(1)} %get-tuple-element.68.refs_0_, bf16[3,1408,512]{2,1,0:T(8,128)(2,1)S(1)} %get-tuple-element.69.refs_1_, ...), custom_call_target="tpu_custom_call" | custom-call | flops 2214592512 | bytes 8650752 | tf_op jit(solution)/shard_map/product/pallas_call | solution.py:219
  33.6 1.8 %collective-permute-start.8 = (bf16[32,1536]{1,0:T(8,128)(2,1)S(1)}, bf16[32,1536]{1,0:T(8,128)(2,1)S(1)}, u32[]{:S(2)}, u32[]{:S(2)}) collective-permute-start(bf16[32,1536]{1,0:T(8,128)(2,1)S(1)} %add_convert_fusion), channel_id=1, source_target_pairs={{0,16},{8,24},{16,0},{24,8},{1,17},{9,25},{17,1},{25,9},{2,18},{10... | collective-permute-start | bytes 294920 | tf_op jit(solution)/shard_map/ppermute | solution.py:425
  35.5 1.3 %collective-permute-start.10 = (bf16[32,1024]{1,0:T(8,128)(2,1)S(1)}, bf16[32,1024]{1,0:T(8,128)(2,1)S(1)}, u32[]{:S(2)}, u32[]{:S(2)}) collective-permute-start(bf16[32,1024]{1,0:T(8,128)(2,1)S(1)} %add_convert_fusion.2), channel_id=1, source_target_pairs={{0,16},{8,24},{16,0},{24,8},{1,17},{9,25},{17,1},{25,9},{2,18},{10... | collective-permute-start | bytes 196616 | tf_op jit(solution)/shard_map/ppermute | solution.py:425
  36.8 2.4 %pack.3.refs_0_ = bf16[8,32,1664]{2,1,0:T(8,128)(2,1)S(1)} custom-call(s32[8]{0:T(128)S(1)} %iota_xor_fusion.1.order_ref, s32[24,128]{1,0:T(8,128)S(1)} %get-tuple-element.52.start_ref, s32[40,128]{1,0:T(8,128)S(1)} %get-tuple-element.53.inner_ref, s32[40,128]{1,0:T(8,128)S(1)} %get-tuple-element.54.tile_ref, ...), custom_call_target="tpu_custom_call" | custom-call | flops 335544320 | bytes 327680 | tf_op jit(solution)/shard_map/pack/pallas_call | solution.py:441
  39.2 0.9 collective-permute-done.10.refs_6_
  40.1 2.6 %pack.4 = (bf16[32,1280]{1,0:T(8,128)(2,1)S(1)}, bf16[32,1280]{1,0:T(8,128)(2,1)S(1)}, bf16[32,1280]{1,0:T(8,128)(2,1)S(1)}, bf16[32,1280]{1,0:T(8,128)(2,1)S(1)...) custom-call(s32[8]{0:T(128)S(1)} %iota_xor_fusion.1.order_ref, ...), custom_call_target="tpu_custom_call" | custom-call | flops 335544320 | bytes 327680 | tf_op jit(solution)/shard_map/pack/pallas_call | solution.py:441
  42.7 1.8 %collective-permute-start.18 = (bf16[32,5120]{1,0:T(8,128)(2,1)S(1)}, bf16[32,5120]{1,0:T(8,128)(2,1)S(1)}, u32[]{:S(2)}, u32[]{:S(2)}) collective-permute-start(bf16[32,5120]{1,0:T(8,128)(2,1)S(1)} %get-tuple-element.82), channel_id=1, source_target_pairs={{0,16},{8,24},{16,0},{24,8},{1,17},{9,25},{17,1},{25,9},{2,18},{10... | collective-permute-start | bytes 983048 | tf_op jit(solution)/shard_map/ppermute | solution.py:472
  44.5 1.5 %collective-permute-start.11 = (bf16[32,1280]{1,0:T(8,128)(2,1)S(1)}, bf16[32,1280]{1,0:T(8,128)(2,1)S(1)}, u32[]{:S(2)}, u32[]{:S(2)}) collective-permute-start(bf16[32,1280]{1,0:T(8,128)(2,1)S(1)} %get-tuple-element.74), channel_id=1, source_target_pairs={{0,1},{1,0},{2,3},{3,2},{4,5},{5,4},{6,7},{7,6},{8,9},{9,8},{10,11... | collective-permute-start | bytes 245768 | tf_op jit(solution)/shard_map/ppermute | solution.py:461
  46.0 1.6 %collective-permute-start.12 = (bf16[32,1280]{1,0:T(8,128)(2,1)S(1)}, bf16[32,1280]{1,0:T(8,128)(2,1)S(1)}, u32[]{:S(2)}, u32[]{:S(2)}) collective-permute-start(bf16[32,1280]{1,0:T(8,128)(2,1)S(1)} %get-tuple-element.75), channel_id=1, source_target_pairs={{0,2},{1,3},{2,0},{3,1},{4,6},{5,7},{6,4},{7,5},{8,10},{9,11},{10,... | collective-permute-start | bytes 245768 | tf_op jit(solution)/shard_map/ppermute | solution.py:461
  48.0 2.6 %collective-permute-start.14 = (bf16[32,1280]{1,0:T(8,128)(2,1)S(1)}, bf16[32,1280]{1,0:T(8,128)(2,1)S(1)}, u32[]{:S(2)}, u32[]{:S(2)}) collective-permute-start(bf16[32,1280]{1,0:T(8,128)(2,1)S(1)} %get-tuple-element.77), channel_id=1, source_target_pairs={{0,4},{1,5},{2,6},{3,7},{4,0},{5,1},{6,2},{7,3},{8,12},{9,13},{10,... | collective-permute-start | bytes 245768 | tf_op jit(solution)/shard_map/ppermute | solution.py:461
  50.6 2.8 %collective-permute-start.15 = (bf16[32,1280]{1,0:T(8,128)(2,1)S(1)}, bf16[32,1280]{1,0:T(8,128)(2,1)S(1)}, u32[]{:S(2)}, u32[]{:S(2)}) collective-permute-start(bf16[32,1280]{1,0:T(8,128)(2,1)S(1)} %get-tuple-element.78), channel_id=1, source_target_pairs={{0,5},{1,4},{2,7},{3,6},{4,1},{5,0},{6,3},{7,2},{8,13},{9,12},{10,... | collective-permute-start | bytes 245768 | tf_op jit(solution)/shard_map/ppermute | solution.py:461
  53.4 2.1 %collective-permute-start.16 = (bf16[32,1280]{1,0:T(8,128)(2,1)S(1)}, bf16[32,1280]{1,0:T(8,128)(2,1)S(1)}, u32[]{:S(2)}, u32[]{:S(2)}) collective-permute-start(bf16[32,1280]{1,0:T(8,128)(2,1)S(1)} %get-tuple-element.79), channel_id=1, source_target_pairs={{0,6},{1,7},{2,4},{3,5},{4,2},{5,3},{6,0},{7,1},{8,14},{9,15},{10,... | collective-permute-start | bytes 245768 | tf_op jit(solution)/shard_map/ppermute | solution.py:461
  55.5 1.2 %collective-permute-start.17 = (bf16[32,1280]{1,0:T(8,128)(2,1)S(1)}, bf16[32,1280]{1,0:T(8,128)(2,1)S(1)}, u32[]{:S(2)}, u32[]{:S(2)}) collective-permute-start(bf16[32,1280]{1,0:T(8,128)(2,1)S(1)} %get-tuple-element.80), channel_id=1, source_target_pairs={{0,7},{1,6},{2,5},{3,4},{4,3},{5,2},{6,1},{7,0},{8,15},{9,14},{10,... | collective-permute-start | bytes 245768 | tf_op jit(solution)/shard_map/ppermute | solution.py:461
  56.7 4.0 %pack.5 = (bf16[32,1280]{1,0:T(8,128)(2,1)S(1)}, bf16[32,1280]{1,0:T(8,128)(2,1)S(1)}, bf16[32,1280]{1,0:T(8,128)(2,1)S(1)}, bf16[32,1280]{1,0:T(8,128)(2,1)S(1)...) custom-call(s32[8]{0:T(128)S(1)} %iota_xor_fusion.1.order_ref, ...), custom_call_target="tpu_custom_call" | custom-call | flops 671088640 | bytes 655360 | tf_op jit(solution)/shard_map/pack/pallas_call | solution.py:441
  66.5 2.2 %gate.1 = (bf16[32,1280]{1,0:T(8,128)(2,1)}, bf16[32,1280]{1,0:T(8,128)(2,1)}, bf16[32,1280]{1,0:T(8,128)(2,1)}, bf16[32,1280]{1,0:T(8,128)(2,1)}, bf16[32,1280]...) custom-call(bf16[32,1280]{1,0:T(8,128)(2,1)} %copy-done.2, ...), custom_call_target="tpu_custom_call" | custom-call | tf_op jit(solution)/shard_map/gate/pallas_call | solution.py:476
  68.7 2.0 %collective-permute-start.19 = (bf16[32,1280]{1,0:T(8,128)(2,1)}, bf16[32,1280]{1,0:T(8,128)(2,1)S(1)}, u32[]{:S(2)}, u32[]{:S(2)}) collective-permute-start(bf16[32,1280]{1,0:T(8,128)(2,1)} %get-tuple-element.92), channel_id=1, source_target_pairs={{0,1},{1,0},{2,3},{3,2},{4,5},{5,4},{6,7},{7,6},{8,9},{9,8},{10,11... | collective-permute-start | bytes 245768 | tf_op jit(solution)/shard_map/ppermute | solution.py:461
  70.8 1.5 %collective-permute-start.21 = (bf16[32,1280]{1,0:T(8,128)(2,1)}, bf16[32,1280]{1,0:T(8,128)(2,1)S(1)}, u32[]{:S(2)}, u32[]{:S(2)}) collective-permute-start(bf16[32,1280]{1,0:T(8,128)(2,1)} %get-tuple-element.94), channel_id=1, source_target_pairs={{0,3},{1,2},{2,1},{3,0},{4,7},{5,6},{6,5},{7,4},{8,11},{9,10},{10,... | collective-permute-start | bytes 245768 | tf_op jit(solution)/shard_map/ppermute | solution.py:461
  72.3 1.6 %collective-permute-start.22 = (bf16[32,1280]{1,0:T(8,128)(2,1)}, bf16[32,1280]{1,0:T(8,128)(2,1)S(1)}, u32[]{:S(2)}, u32[]{:S(2)}) collective-permute-start(bf16[32,1280]{1,0:T(8,128)(2,1)} %get-tuple-element.95), channel_id=1, source_target_pairs={{0,4},{1,5},{2,6},{3,7},{4,0},{5,1},{6,2},{7,3},{8,12},{9,13},{10,... | collective-permute-start | bytes 245768 | tf_op jit(solution)/shard_map/ppermute | solution.py:461
  73.9 2.7 %collective-permute-start.23 = (bf16[32,1280]{1,0:T(8,128)(2,1)}, bf16[32,1280]{1,0:T(8,128)(2,1)S(1)}, u32[]{:S(2)}, u32[]{:S(2)}) collective-permute-start(bf16[32,1280]{1,0:T(8,128)(2,1)} %get-tuple-element.96), channel_id=1, source_target_pairs={{0,5},{1,4},{2,7},{3,6},{4,1},{5,0},{6,3},{7,2},{8,13},{9,12},{10,... | collective-permute-start | bytes 245768 | tf_op jit(solution)/shard_map/ppermute | solution.py:461
  76.6 2.1 %collective-permute-start.24 = (bf16[32,1280]{1,0:T(8,128)(2,1)}, bf16[32,1280]{1,0:T(8,128)(2,1)S(1)}, u32[]{:S(2)}, u32[]{:S(2)}) collective-permute-start(bf16[32,1280]{1,0:T(8,128)(2,1)} %get-tuple-element.97), channel_id=1, source_target_pairs={{0,6},{1,7},{2,4},{3,5},{4,2},{5,3},{6,0},{7,1},{8,14},{9,15},{10,... | collective-permute-start | bytes 245768 | tf_op jit(solution)/shard_map/ppermute | solution.py:461
  78.8 1.2 %collective-permute-start.25 = (bf16[32,1280]{1,0:T(8,128)(2,1)}, bf16[32,1280]{1,0:T(8,128)(2,1)S(1)}, u32[]{:S(2)}, u32[]{:S(2)}) collective-permute-start(bf16[32,1280]{1,0:T(8,128)(2,1)} %get-tuple-element.98), channel_id=1, source_target_pairs={{0,7},{1,6},{2,5},{3,4},{4,3},{5,2},{6,1},{7,0},{8,15},{9,14},{10,... | collective-permute-start | bytes 245768 | tf_op jit(solution)/shard_map/ppermute | solution.py:461
  80.0 3.2 %collective-permute-done.22.refs_12_ = bf16[32,1280]{1,0:T(8,128)(2,1)S(1)} collective-permute-done((bf16[32,1280]{1,0:T(8,128)(2,1)}, bf16[32,1280]{1,0:T(8,128)(2,1)S(1)}, u32[]{:S(2)}, u32[]{:S(2)}) %collective-permute-start.22) | collective-permute-done | bytes 81952 | tf_op jit(solution)/shard_map/ppermute | solution.py:461
  83.2 3.6 %collective-permute-done.23.refs_13_ = bf16[32,1280]{1,0:T(8,128)(2,1)S(1)} collective-permute-done((bf16[32,1280]{1,0:T(8,128)(2,1)}, bf16[32,1280]{1,0:T(8,128)(2,1)S(1)}, u32[]{:S(2)}, u32[]{:S(2)}) %collective-permute-start.23) | collective-permute-done | bytes 81952 | tf_op jit(solution)/shard_map/ppermute | solution.py:461
  87.5 2.6 %assemble.1 = bf16[8,64,1280]{2,1,0:T(8,128)(2,1)} custom-call(s32[8]{0:T(128)} %copy-done.10, bf16[32,1280]{1,0:T(8,128)(2,1)} %copy-done.1, bf16[32,1280]{1,0:T(8,128)(2,1)} %copy-done.11, bf16[32,1280]{1,0:T(8,128)(2,1)} %copy-done.12, bf16[32,1280]{1,0:T(8,128)(2,1)} %copy-done.13, bf16[32,1280]{1,0:T(8,128)(2,1)} %copy-done.14, ...), custom_call_target="tpu_custom_call" | custom-call | tf_op jit(solution)/shard_map/assemble/pallas_call | solution.py:484
  (89 shorter events, 10.0 us)
Async XLA Ops:
  1.2 11.4 %collective-permute-start.2 = (bf16[64,1408]{1,0:T(8,128)(2,1)S(1)}, bf16[64,1408]{1,0:T(8,128)(2,1)S(1)}, u32[]{:S(2)}, u32[]{:S(2)}) collective-permute-start(bf16[64,1408]{1,0:T(8,128)(2,1)S(1)} %get-tuple-element.99), channel_id=1, source_target_pairs={{0,24},{8,16},{16,8},{24,0},{1,25},{9,17},{17,9},{25,1},{2,26},{10... | collective-permute-start | bytes 540680 | tf_op jit(solution)/shard_map/ppermute | solution.py:336
  3.7 1.7 %collective-permute-start = (bf16[64,1408]{1,0:T(8,128)(2,1)S(1)}, bf16[64,1408]{1,0:T(8,128)(2,1)S(1)}, u32[]{:S(2)}, u32[]{:S(2)}) collective-permute-start(bf16[64,1408]{1,0:T(8,128)(2,1)S(1)} %get-tuple-element.100), channel_id=1, source_target_pairs={{0,8},{8,0},{16,24},{24,16},{1,9},{9,1},{17,25},{25,17},{2,10},{10... | collective-permute-start | bytes 540680 | tf_op jit(solution)/shard_map/ppermute | solution.py:336
  4.4 8.3 %collective-permute-start.1 = (bf16[64,1408]{1,0:T(8,128)(2,1)S(1)}, bf16[64,1408]{1,0:T(8,128)(2,1)S(1)}, u32[]{:S(2)}, u32[]{:S(2)}) collective-permute-start(bf16[64,1408]{1,0:T(8,128)(2,1)S(1)} %get-tuple-element.102), channel_id=1, source_target_pairs={{0,16},{8,24},{16,0},{24,8},{1,17},{9,25},{17,1},{25,9},{2,18},{10... | collective-permute-start | bytes 540680 | tf_op jit(solution)/shard_map/ppermute | solution.py:336
  20.1 4.3 %collective-permute-start.3 = (bf16[128,1024]{1,0:T(8,128)(2,1)S(1)}, bf16[128,1024]{1,0:T(8,128)(2,1)S(1)}, u32[]{:S(2)}, u32[]{:S(2)}) collective-permute-start(bf16[128,1024]{1,0:T(8,128)(2,1)S(1)} %get-tuple-element.59), channel_id=1, source_target_pairs={{0,8},{8,0},{16,24},{24,16},{1,9},{9,1},{17,25},{25,17},{2,10},{10... | collective-permute-start | bytes 786440 | tf_op jit(solution)/shard_map/ppermute | solution.py:425
  24.1 6.3 %collective-permute-start.5 = (bf16[128,1536]{1,0:T(8,128)(2,1)S(1)}, bf16[128,1536]{1,0:T(8,128)(2,1)S(1)}, u32[]{:S(2)}, u32[]{:S(2)}) collective-permute-start(bf16[128,1536]{1,0:T(8,128)(2,1)S(1)} %get-tuple-element.63), channel_id=1, source_target_pairs={{0,8},{8,0},{16,24},{24,16},{1,9},{9,1},{17,25},{25,17},{2,10},{10... | collective-permute-start | bytes 1179656 | tf_op jit(solution)/shard_map/ppermute | solution.py:425
  24.4 6.3 %collective-permute-start.4 = (bf16[32,1024]{1,0:T(8,128)(2,1)S(1)}, bf16[32,1024]{1,0:T(8,128)(2,1)S(1)}, u32[]{:S(2)}, u32[]{:S(2)}) collective-permute-start(bf16[32,1024]{1,0:T(8,128)(2,1)S(1)} %add_convert_fusion.3.refs_2_), channel_id=1, source_target_pairs={{0,16},{8,24},{16,0},{24,8},{1,17},{9,25},{17,1},{25,9},{2,18},{10... | collective-permute-start | bytes 196616 | tf_op jit(solution)/shard_map/ppermute | solution.py:425
  30.4 3.2 %collective-permute-start.7 = (bf16[128,1536]{1,0:T(8,128)(2,1)S(1)}, bf16[128,1536]{1,0:T(8,128)(2,1)S(1)}, u32[]{:S(2)}, u32[]{:S(2)}) collective-permute-start(bf16[128,1536]{1,0:T(8,128)(2,1)S(1)} %get-tuple-element.67), channel_id=1, source_target_pairs={{0,8},{8,0},{16,24},{24,16},{1,9},{9,1},{17,25},{25,17},{2,10},{10... | collective-permute-start | bytes 1179656 | tf_op jit(solution)/shard_map/ppermute | solution.py:425
  30.5 6.3 %collective-permute-start.6 = (bf16[32,1536]{1,0:T(8,128)(2,1)S(1)}, bf16[32,1536]{1,0:T(8,128)(2,1)S(1)}, u32[]{:S(2)}, u32[]{:S(2)}) collective-permute-start(bf16[32,1536]{1,0:T(8,128)(2,1)S(1)} %add_convert_fusion.1.refs_3_), channel_id=1, source_target_pairs={{0,16},{8,24},{16,0},{24,8},{1,17},{9,25},{17,1},{25,9},{2,18},{10... | collective-permute-start | bytes 294920 | tf_op jit(solution)/shard_map/ppermute | solution.py:425
  33.1 2.3 %collective-permute-start.9 = (bf16[128,1024]{1,0:T(8,128)(2,1)S(1)}, bf16[128,1024]{1,0:T(8,128)(2,1)S(1)}, u32[]{:S(2)}, u32[]{:S(2)}) collective-permute-start(bf16[128,1024]{1,0:T(8,128)(2,1)S(1)} %get-tuple-element.72), channel_id=1, source_target_pairs={{0,8},{8,0},{16,24},{24,16},{1,9},{9,1},{17,25},{25,17},{2,10},{10... | collective-permute-start | bytes 786440 | tf_op jit(solution)/shard_map/ppermute | solution.py:425
  33.6 6.5 %collective-permute-start.8 = (bf16[32,1536]{1,0:T(8,128)(2,1)S(1)}, bf16[32,1536]{1,0:T(8,128)(2,1)S(1)}, u32[]{:S(2)}, u32[]{:S(2)}) collective-permute-start(bf16[32,1536]{1,0:T(8,128)(2,1)S(1)} %add_convert_fusion), channel_id=1, source_target_pairs={{0,16},{8,24},{16,0},{24,8},{1,17},{9,25},{17,1},{25,9},{2,18},{10... | collective-permute-start | bytes 294920 | tf_op jit(solution)/shard_map/ppermute | solution.py:425
  35.5 4.6 %collective-permute-start.10 = (bf16[32,1024]{1,0:T(8,128)(2,1)S(1)}, bf16[32,1024]{1,0:T(8,128)(2,1)S(1)}, u32[]{:S(2)}, u32[]{:S(2)}) collective-permute-start(bf16[32,1024]{1,0:T(8,128)(2,1)S(1)} %add_convert_fusion.2), channel_id=1, source_target_pairs={{0,16},{8,24},{16,0},{24,8},{1,17},{9,25},{17,1},{25,9},{2,18},{10... | collective-permute-start | bytes 196616 | tf_op jit(solution)/shard_map/ppermute | solution.py:425
  36.8 23.9 %copy-start.10 = (s32[8]{0:T(128)}, s32[8]{0:T(128)S(1)}, u32[]{:S(2)}) copy-start(s32[8]{0:T(128)S(1)} %iota_xor_fusion.1.order_ref) | copy-start | bytes 100
  42.7 18.0 %copy-start.1 = (bf16[32,1280]{1,0:T(8,128)(2,1)}, bf16[32,1280]{1,0:T(8,128)(2,1)S(1)}, u32[]{:S(2)}) copy-start(bf16[32,1280]{1,0:T(8,128)(2,1)S(1)} %get-tuple-element.73.refs_8_.refs_0_) | copy-start | bytes 245764
  42.7 12.8 %collective-permute-start.18 = (bf16[32,5120]{1,0:T(8,128)(2,1)S(1)}, bf16[32,5120]{1,0:T(8,128)(2,1)S(1)}, u32[]{:S(2)}, u32[]{:S(2)}) collective-permute-start(bf16[32,5120]{1,0:T(8,128)(2,1)S(1)} %get-tuple-element.82), channel_id=1, source_target_pairs={{0,16},{8,24},{16,0},{24,8},{1,17},{9,25},{17,1},{25,9},{2,18},{10... | collective-permute-start | bytes 983048 | tf_op jit(solution)/shard_map/ppermute | solution.py:472
  44.5 6.1 %collective-permute-start.11 = (bf16[32,1280]{1,0:T(8,128)(2,1)S(1)}, bf16[32,1280]{1,0:T(8,128)(2,1)S(1)}, u32[]{:S(2)}, u32[]{:S(2)}) collective-permute-start(bf16[32,1280]{1,0:T(8,128)(2,1)S(1)} %get-tuple-element.74), channel_id=1, source_target_pairs={{0,1},{1,0},{2,3},{3,2},{4,5},{5,4},{6,7},{7,6},{8,9},{9,8},{10,11... | collective-permute-start | bytes 245768 | tf_op jit(solution)/shard_map/ppermute | solution.py:461
  46.0 7.3 %collective-permute-start.12 = (bf16[32,1280]{1,0:T(8,128)(2,1)S(1)}, bf16[32,1280]{1,0:T(8,128)(2,1)S(1)}, u32[]{:S(2)}, u32[]{:S(2)}) collective-permute-start(bf16[32,1280]{1,0:T(8,128)(2,1)S(1)} %get-tuple-element.75), channel_id=1, source_target_pairs={{0,2},{1,3},{2,0},{3,1},{4,6},{5,7},{6,4},{7,5},{8,10},{9,11},{10,... | collective-permute-start | bytes 245768 | tf_op jit(solution)/shard_map/ppermute | solution.py:461
  47.6 18.1 %collective-permute-start.13 = (bf16[32,1280]{1,0:T(8,128)(2,1)S(1)}, bf16[32,1280]{1,0:T(8,128)(2,1)S(1)}, u32[]{:S(2)}, u32[]{:S(2)}) collective-permute-start(bf16[32,1280]{1,0:T(8,128)(2,1)S(1)} %get-tuple-element.76), channel_id=1, source_target_pairs={{0,3},{1,2},{2,1},{3,0},{4,7},{5,6},{6,5},{7,4},{8,11},{9,10},{10,... | collective-permute-start | bytes 245768 | tf_op jit(solution)/shard_map/ppermute | solution.py:461
  48.0 17.7 %collective-permute-start.14 = (bf16[32,1280]{1,0:T(8,128)(2,1)S(1)}, bf16[32,1280]{1,0:T(8,128)(2,1)S(1)}, u32[]{:S(2)}, u32[]{:S(2)}) collective-permute-start(bf16[32,1280]{1,0:T(8,128)(2,1)S(1)} %get-tuple-element.77), channel_id=1, source_target_pairs={{0,4},{1,5},{2,6},{3,7},{4,0},{5,1},{6,2},{7,3},{8,12},{9,13},{10,... | collective-permute-start | bytes 245768 | tf_op jit(solution)/shard_map/ppermute | solution.py:461
  50.6 15.2 %copy-start.11 = (bf16[32,1280]{1,0:T(8,128)(2,1)}, bf16[32,1280]{1,0:T(8,128)(2,1)S(1)}, u32[]{:S(2)}) copy-start(bf16[32,1280]{1,0:T(8,128)(2,1)S(1)} %collective-permute-done.11.refs_9_.refs_1_) | copy-start | bytes 245764
  50.6 15.2 %collective-permute-start.15 = (bf16[32,1280]{1,0:T(8,128)(2,1)S(1)}, bf16[32,1280]{1,0:T(8,128)(2,1)S(1)}, u32[]{:S(2)}, u32[]{:S(2)}) collective-permute-start(bf16[32,1280]{1,0:T(8,128)(2,1)S(1)} %get-tuple-element.78), channel_id=1, source_target_pairs={{0,5},{1,4},{2,7},{3,6},{4,1},{5,0},{6,3},{7,2},{8,13},{9,12},{10,... | collective-permute-start | bytes 245768 | tf_op jit(solution)/shard_map/ppermute | solution.py:461
  53.4 12.4 %copy-start.12 = (bf16[32,1280]{1,0:T(8,128)(2,1)}, bf16[32,1280]{1,0:T(8,128)(2,1)S(1)}, u32[]{:S(2)}) copy-start(bf16[32,1280]{1,0:T(8,128)(2,1)S(1)} %collective-permute-done.12.refs_10_.refs_2_) | copy-start | bytes 245764
  53.4 12.4 %collective-permute-start.16 = (bf16[32,1280]{1,0:T(8,128)(2,1)S(1)}, bf16[32,1280]{1,0:T(8,128)(2,1)S(1)}, u32[]{:S(2)}, u32[]{:S(2)}) collective-permute-start(bf16[32,1280]{1,0:T(8,128)(2,1)S(1)} %get-tuple-element.79), channel_id=1, source_target_pairs={{0,6},{1,7},{2,4},{3,5},{4,2},{5,3},{6,0},{7,1},{8,14},{9,15},{10,... | collective-permute-start | bytes 245768 | tf_op jit(solution)/shard_map/ppermute | solution.py:461
  55.5 10.3 %collective-permute-start.17 = (bf16[32,1280]{1,0:T(8,128)(2,1)S(1)}, bf16[32,1280]{1,0:T(8,128)(2,1)S(1)}, u32[]{:S(2)}, u32[]{:S(2)}) collective-permute-start(bf16[32,1280]{1,0:T(8,128)(2,1)S(1)} %get-tuple-element.80), channel_id=1, source_target_pairs={{0,7},{1,6},{2,5},{3,4},{4,3},{5,2},{6,1},{7,0},{8,15},{9,14},{10,... | collective-permute-start | bytes 245768 | tf_op jit(solution)/shard_map/ppermute | solution.py:461
  68.7 7.9 %collective-permute-start.19 = (bf16[32,1280]{1,0:T(8,128)(2,1)}, bf16[32,1280]{1,0:T(8,128)(2,1)S(1)}, u32[]{:S(2)}, u32[]{:S(2)}) collective-permute-start(bf16[32,1280]{1,0:T(8,128)(2,1)} %get-tuple-element.92), channel_id=1, source_target_pairs={{0,1},{1,0},{2,3},{3,2},{4,5},{5,4},{6,7},{7,6},{8,9},{9,8},{10,11... | collective-permute-start | bytes 245768 | tf_op jit(solution)/shard_map/ppermute | solution.py:461
  70.8 8.0 %collective-permute-start.20 = (bf16[32,1280]{1,0:T(8,128)(2,1)}, bf16[32,1280]{1,0:T(8,128)(2,1)S(1)}, u32[]{:S(2)}, u32[]{:S(2)}) collective-permute-start(bf16[32,1280]{1,0:T(8,128)(2,1)} %get-tuple-element.93), channel_id=1, source_target_pairs={{0,2},{1,3},{2,0},{3,1},{4,6},{5,7},{6,4},{7,5},{8,10},{9,11},{10,... | collective-permute-start | bytes 245768 | tf_op jit(solution)/shard_map/ppermute | solution.py:461
  70.8 9.2 %collective-permute-start.21 = (bf16[32,1280]{1,0:T(8,128)(2,1)}, bf16[32,1280]{1,0:T(8,128)(2,1)S(1)}, u32[]{:S(2)}, u32[]{:S(2)}) collective-permute-start(bf16[32,1280]{1,0:T(8,128)(2,1)} %get-tuple-element.94), channel_id=1, source_target_pairs={{0,3},{1,2},{2,1},{3,0},{4,7},{5,6},{6,5},{7,4},{8,11},{9,10},{10,... | collective-permute-start | bytes 245768 | tf_op jit(solution)/shard_map/ppermute | solution.py:461
  72.3 10.9 %collective-permute-start.22 = (bf16[32,1280]{1,0:T(8,128)(2,1)}, bf16[32,1280]{1,0:T(8,128)(2,1)S(1)}, u32[]{:S(2)}, u32[]{:S(2)}) collective-permute-start(bf16[32,1280]{1,0:T(8,128)(2,1)} %get-tuple-element.95), channel_id=1, source_target_pairs={{0,4},{1,5},{2,6},{3,7},{4,0},{5,1},{6,2},{7,3},{8,12},{9,13},{10,... | collective-permute-start | bytes 245768 | tf_op jit(solution)/shard_map/ppermute | solution.py:461
  73.9 12.9 %collective-permute-start.23 = (bf16[32,1280]{1,0:T(8,128)(2,1)}, bf16[32,1280]{1,0:T(8,128)(2,1)S(1)}, u32[]{:S(2)}, u32[]{:S(2)}) collective-permute-start(bf16[32,1280]{1,0:T(8,128)(2,1)} %get-tuple-element.96), channel_id=1, source_target_pairs={{0,5},{1,4},{2,7},{3,6},{4,1},{5,0},{6,3},{7,2},{8,13},{9,12},{10,... | collective-permute-start | bytes 245768 | tf_op jit(solution)/shard_map/ppermute | solution.py:461
  76.6 10.2 %copy-start.18 = (bf16[32,1280]{1,0:T(8,128)(2,1)}, bf16[32,1280]{1,0:T(8,128)(2,1)S(1)}, u32[]{:S(2)}) copy-start(bf16[32,1280]{1,0:T(8,128)(2,1)S(1)} %collective-permute-done.19.refs_9_) | copy-start | bytes 245764
  76.6 10.2 %collective-permute-start.24 = (bf16[32,1280]{1,0:T(8,128)(2,1)}, bf16[32,1280]{1,0:T(8,128)(2,1)S(1)}, u32[]{:S(2)}, u32[]{:S(2)}) collective-permute-start(bf16[32,1280]{1,0:T(8,128)(2,1)} %get-tuple-element.97), channel_id=1, source_target_pairs={{0,6},{1,7},{2,4},{3,5},{4,2},{5,3},{6,0},{7,1},{8,14},{9,15},{10,... | collective-permute-start | bytes 245768 | tf_op jit(solution)/shard_map/ppermute | solution.py:461
  78.8 8.1 %copy-start.19 = (bf16[32,1280]{1,0:T(8,128)(2,1)}, bf16[32,1280]{1,0:T(8,128)(2,1)S(1)}, u32[]{:S(2)}) copy-start(bf16[32,1280]{1,0:T(8,128)(2,1)S(1)} %collective-permute-done.20.refs_10_) | copy-start | bytes 245764
  78.8 8.1 %collective-permute-start.25 = (bf16[32,1280]{1,0:T(8,128)(2,1)}, bf16[32,1280]{1,0:T(8,128)(2,1)S(1)}, u32[]{:S(2)}, u32[]{:S(2)}) collective-permute-start(bf16[32,1280]{1,0:T(8,128)(2,1)} %get-tuple-element.98), channel_id=1, source_target_pairs={{0,7},{1,6},{2,5},{3,4},{4,3},{5,2},{6,1},{7,0},{8,15},{9,14},{10,... | collective-permute-start | bytes 245768 | tf_op jit(solution)/shard_map/ppermute | solution.py:461
  (19 other events, 28.2 us)

commit v11 on v10

--- a/solution.py
+++ b/solution.py
@@ -17,6 +17,7 @@
 CHUNKS = 4
 COPIES = (((0, 4), (1, 5)), ((1, 1), (2, 4)), (), ((2, 2), (3, 1)), ((3, 2), (3, 1)))
 PACK_FIRST = 2
+GATE = 4
 MIB = 1 << 20
 
 VMEM = functools.partial(pl.BlockSpec, memory_space=pltpu.VMEM)
@@ -432,7 +433,7 @@
         sizes = [widths[c] for c in chunks]
         spec = (len(later), bits) if later else None
         if chunks[-1] == CHUNKS - 1:
-            outs = [jax.ShapeDtypeStruct((half, send_cap), jnp.bfloat16)] * owners
+            outs = [pltpu.VMEM((half, send_cap), jnp.bfloat16)] * owners
         else:
             outs = [jax.ShapeDtypeStruct((owners, half, spread * SLOT_TILE), jnp.bfloat16)]
         more = []
@@ -454,10 +455,12 @@
             name="pack",
         )(targets, starts, inner, tiles, *packed, *terms, *later)
 
+    far, near = range(owners - 1, owners // 2 - 1, -1), range(owners // 2 - 1, -1, -1)
+    turns = [d for pair in zip(far, near) for d in pair if d]
+
     def deliver(packed):
         got = list(packed)
-        far, near = range(owners - 1, owners // 2 - 1, -1), range(owners // 2 - 1, -1, -1)
-        for d in [d for pair in zip(far, near) for d in pair if d]:
+        for d in turns:
             got[d] = lax.ppermute(packed[d], "vox", [(i, i ^ d) for i in range(owners)])
         return got
 
@@ -475,36 +478,39 @@
     two = pack(range(CHUNKS), [late_own, late] * CHUNKS, [[(0, first)] * 2 for first in starting])
     two = pl.pallas_call(
         gate_kernel,
-        in_specs=[VMEM()] * (2 * owners),
+        in_specs=[VMEM()] * (owners + GATE),
         out_specs=[VMEM()] * owners,
-        out_shape=[jax.ShapeDtypeStruct((half, send_cap), jnp.bfloat16)] * owners,
+        out_shape=[pltpu.VMEM((half, send_cap), jnp.bfloat16)] * owners,
         name="gate",
-    )(*two, *one)
+    )(*two, *(one[d] for d in turns[:GATE]))
     two = deliver(two)
-    owned = pl.pallas_call(
-        functools.partial(assemble_kernel, owners),
-        in_specs=[SMEM()] + [VMEM()] * (2 * owners),
-        out_specs=HBM(),
-        out_shape=jax.ShapeDtypeStruct((owners, time_block, send_cap), jnp.bfloat16),
-        scratch_shapes=[pltpu.SemaphoreType.DMA((2 * owners,))],
-        name="assemble",
-    )(targets, *one, *two)
+    owned = None
+    for first, got in ((0, one), (half, two)):
+        given = [] if owned is None else [owned]
+        owned = pl.pallas_call(
+            functools.partial(assemble_kernel, owners, first),
+            in_specs=[SMEM()] + [VMEM()] * owners + [HBM()] * len(given),
+            out_specs=HBM(),
+            out_shape=jax.ShapeDtypeStruct((owners, time_block, send_cap), jnp.bfloat16),
+            scratch_shapes=[pltpu.SemaphoreType.DMA((owners,))],
+            input_output_aliases={1 + owners: 0} if given else {},
+            name="assemble",
+        )(targets, *got, *given)
     return jnp.transpose(owned, (0, 2, 1))
 
 
 def gate_kernel(*refs):
-    count = len(refs) // 3
-    for given, out in zip(refs[:count], refs[2 * count :]):
+    count = (len(refs) - GATE) // 2
+    for given, out in zip(refs[:count], refs[count + GATE :]):
         out[...] = given[...]
 
 
-def assemble_kernel(owners, order_ref, *refs):
-    *parts, out_ref, sems = refs
-    half = out_ref.shape[1] // 2
+def assemble_kernel(owners, first, order_ref, *refs):
+    parts, (out_ref, sems) = refs[:owners], refs[-2:]
     copies = []
     for i, ref in enumerate(parts):
-        rows = pl.ds(i // owners * half, half)
-        copies.append(pltpu.make_async_copy(ref, out_ref.at[order_ref[i % owners], rows, :], sems.at[i]))
+        rows = pl.ds(first, ref.shape[0])
+        copies.append(pltpu.make_async_copy(ref, out_ref.at[order_ref[i], rows, :], sems.at[i]))
         copies[-1].start()
     wait_all(copies)
 

time: 90.4 us -> 88.9 us (0.983)
  starting transfers between devices: 35.1 us -> 33.9 us
    ppermute x14, waiting for transfers between devices: 6.87 us -> 5.12 us  [deliver(): got[d] = lax.ppermute(packed[d], 'vox', [(i, i ^ d) for i in range(owners)])]
    ppermute x14, starting transfers between devices: 23.4 us -> 22.2 us  [deliver(): got[d] = lax.ppermute(packed[d], 'vox', [(i, i ^ d) for i in range(owners)])]
    pallas_call x2 -> x3, Pallas kernels: 4.78 us -> 5.47 us  [the longest x2 4.16 us: shards(): pl.pallas_call(functools.partial(assemble_kernel, owners, first), in_spec...]
    unnamed x50 -> x52, local copies, waits for them, and re-layouts: 6.38 us -> 6.32 us
  transfers between devices with their start and end apart: 26 -> 26, of which waited for: 4 -> 6; matrix products, arithmetic and copies ran while one was open for 1% -> 1% of each run, Pallas kernels for 26% -> 30%
where the time goes in v11:
time: 88.9 us; the launch traced here: 88.6 us
  Pallas kernels  38.8 us (44%)
  starting transfers between devices  33.9 us (38%)
  local copies, waits for them, and re-layouts  8.25 us (9%)
  waiting for transfers between devices  7.22 us (8%)
    ppermute x14, starting transfers between devices, deliver(): got[d] = lax.ppermute(packed[d], 'vox', [(i, i ^ d) for i in range(owners)])  22.2 us
    pallas_call x4, Pallas kernels, product(): pl.pallas_call(functools.partial(product_kernel, len(taken), len(after),...  12.2 us
    pallas_call x3, Pallas kernels, pack(): pl.pallas_call(functools.partial(pack_kernel, spread, sizes, spots, sum(w...  9.02 us
    pallas_call x1, Pallas kernels, shards(): pl.pallas_call(functools.partial(early_kernel, owners, spread), in_specs=...  7.24 us
    ppermute x8, starting transfers between devices, shards(): lax.ppermute(send, 'chan', [(i, i ^ 1 << bit) for i in range(parts)])  6.76 us
    unnamed x52, local copies, waits for them, and re-layouts  6.32 us
    ppermute x14, waiting for transfers between devices, deliver(): got[d] = lax.ppermute(packed[d], 'vox', [(i, i ^ d) for i in range(owners)])  5.12 us
    pallas_call x1, Pallas kernels, shards(): pl.pallas_call(functools.partial(design_kernel, parts, firsts[1]), in_spe...  4.9 us
  transfers between devices with their start and end apart: 26, of which 6 were waited for; matrix products, arithmetic and copies ran while one was open for 1% of the time, Pallas kernels for 30%

profile of v11, /device:TPU:0, one launch (start us, length us, event | category | flops | bytes accessed | tf_op | source)
XLA Modules:
  0.0 88.6 jit_solution(9299619075007018538)
XLA Ops:
  0.0 1.2 %constant_dynamic-slice_fusion = (bf16[64,1408]{1,0:T(8,128)(2,1)S(1)}, bf16[64,1408]{1,0:T(8,128)(2,1)S(1)}, bf16[64,1408]{1,0:T(8,128)(2,1)S(1)}, bf16[64,1408]{1,0:T(8,128)(2,1)S(1)}) fusion(bf16[64,5632]{1,0:T(8,128)(2,1)} %param.5, s32[]{:T(128)S(6)} %select_n.15, s32[]{:T(128)S(6)} %select_n.13, s32[]{:T(128)S(6)} %select_n.12, s32[]{:T(128)S(6)} %select_n.14), kind=kLoop, calls=%fused_computation.5 | loop fusion | bytes 1441808 | tf_op jit(solution)/shard_map/dynamic_slice | solution.py:335
  1.2 2.4 %collective-permute-start.2 = (bf16[64,1408]{1,0:T(8,128)(2,1)S(1)}, bf16[64,1408]{1,0:T(8,128)(2,1)S(1)}, u32[]{:S(2)}, u32[]{:S(2)}) collective-permute-start(bf16[64,1408]{1,0:T(8,128)(2,1)S(1)} %get-tuple-element.99), channel_id=1, source_target_pairs={{0,24},{8,16},{16,8},{24,0},{1,25},{9,17},{17,9},{25,1},{2,26},{10... | collective-permute-start | bytes 540680 | tf_op jit(solution)/shard_map/ppermute | solution.py:337
  5.4 7.2 %early.1 = (s32[40,128]{1,0:T(8,128)S(1)}, s32[40,128]{1,0:T(8,128)S(1)}, s32[24,128]{1,0:T(8,128)S(1)}, bf16[96,4224]{1,0:T(8,128)(2,1)S(1)}, bf16[3,1408,1024]...) custom-call(s32[4]{0:T(128)S(1)} %get-tuple-element.104.order_ref, ...), custom_call_target="tpu_custom_call" | custom-call | bytes 19464192 | tf_op jit(solution)/shard_map/early/pallas_call | solution.py:368
  12.7 4.9 %design.1 = (bf16[256,4224]{1,0:T(8,128)(2,1)S(1)}, bf16[3,1408,256]{2,1,0:T(8,128)(2,1)S(1)}, bf16[3,1408,1024]{2,1,0:T(8,128)(2,1)S(1)}) custom-call(s32[4]{0:T(128)S(1)} %get-tuple-element.104.order_ref, s32[4]{0:T(128)S(1)} %get-tuple-element.103.place_ref, bf16[96,4224]{1,0:T(8,128)(2,1)S(1)} %get-tuple-element.55.early_ref, ...), custom_call_target="tpu_custom_call" | custom-call | bytes 10813440 | tf_op jit(solution)/shard_map/design/pallas_call | solution.py:399
  17.6 2.5 %product.4 = (bf16[128,1024]{1,0:T(8,128)(2,1)S(1)}, bf16[128,1024]{1,0:T(8,128)(2,1)S(1)}) custom-call(bf16[256,4224]{1,0:T(8,128)(2,1)S(1)} %get-tuple-element.56.design_ref, bf16[3,1408,1024]{2,1,0:T(8,128)(2,1)S(1)} %get-tuple-element.57.refs_0_), custom_call_target="tpu_custom_call" | custom-call | flops 2214592512 | bytes 8650752 | tf_op jit(solution)/shard_map/product/pallas_call | solution.py:220
  20.5 3.6 %product.5 = (bf16[128,1536]{1,0:T(8,128)(2,1)S(1)}, bf16[128,1536]{1,0:T(8,128)(2,1)S(1)}, bf16[3,1408,512]{2,1,0:T(8,128)(2,1)S(1)}, bf16[3,1408,256]{2,1,0:T(8,128)(2,1)S(1)}) custom-call(bf16[256,4224]{1,0:T(8,128)(2,1)S(1)} %get-tuple-element.56.design_ref, bf16[3,1408,1280]{2,1,0:T(8,128)(2,1)S(1)} %get-tuple-element.60.refs_0_, ...), custom_call_target="tpu_custom_call" | custom-call | flops 3321888768 | bytes 12976128 | tf_op jit(solution)/shard_map/product/pallas_call | solution.py:220
  24.4 2.3 %collective-permute-start.4 = (bf16[32,1024]{1,0:T(8,128)(2,1)S(1)}, bf16[32,1024]{1,0:T(8,128)(2,1)S(1)}, u32[]{:S(2)}, u32[]{:S(2)}) collective-permute-start(bf16[32,1024]{1,0:T(8,128)(2,1)S(1)} %add_convert_fusion.3.refs_2_), channel_id=1, source_target_pairs={{0,16},{8,24},{16,0},{24,8},{1,17},{9,25},{17,1},{25,9},{2,18},{10... | collective-permute-start | bytes 196616 | tf_op jit(solution)/shard_map/ppermute | solution.py:426
  26.7 3.7 %product.6 = (bf16[128,1536]{1,0:T(8,128)(2,1)S(1)}, bf16[128,1536]{1,0:T(8,128)(2,1)S(1)}, bf16[3,1408,512]{2,1,0:T(8,128)(2,1)S(1)}, bf16[3,1408,256]{2,1,0:T(8,128)(2,1)S(1)}) custom-call(bf16[256,4224]{1,0:T(8,128)(2,1)S(1)} %get-tuple-element.56.design_ref, bf16[3,1408,1024]{2,1,0:T(8,128)(2,1)S(1)} %get-tuple-element.64.refs_0_, ...), custom_call_target="tpu_custom_call" | custom-call | flops 3321888768 | bytes 12976128 | tf_op jit(solution)/shard_map/product/pallas_call | solution.py:220
  30.7 2.5 %product.7 = (bf16[128,1024]{1,0:T(8,128)(2,1)S(1)}, bf16[128,1024]{1,0:T(8,128)(2,1)S(1)}) custom-call(bf16[256,4224]{1,0:T(8,128)(2,1)S(1)} %get-tuple-element.56.design_ref, bf16[3,1408,256]{2,1,0:T(8,128)(2,1)S(1)} %get-tuple-element.68.refs_0_, bf16[3,1408,512]{2,1,0:T(8,128)(2,1)S(1)} %get-tuple-element.69.refs_1_, ...), custom_call_target="tpu_custom_call" | custom-call | flops 2214592512 | bytes 8650752 | tf_op jit(solution)/shard_map/product/pallas_call | solution.py:220
  33.6 1.8 %collective-permute-start.8 = (bf16[32,1536]{1,0:T(8,128)(2,1)S(1)}, bf16[32,1536]{1,0:T(8,128)(2,1)S(1)}, u32[]{:S(2)}, u32[]{:S(2)}) collective-permute-start(bf16[32,1536]{1,0:T(8,128)(2,1)S(1)} %add_convert_fusion), channel_id=1, source_target_pairs={{0,16},{8,24},{16,0},{24,8},{1,17},{9,25},{17,1},{25,9},{2,18},{10... | collective-permute-start | bytes 294920 | tf_op jit(solution)/shard_map/ppermute | solution.py:426
  35.5 1.3 %collective-permute-start.10 = (bf16[32,1024]{1,0:T(8,128)(2,1)S(1)}, bf16[32,1024]{1,0:T(8,128)(2,1)S(1)}, u32[]{:S(2)}, u32[]{:S(2)}) collective-permute-start(bf16[32,1024]{1,0:T(8,128)(2,1)S(1)} %add_convert_fusion.2), channel_id=1, source_target_pairs={{0,16},{8,24},{16,0},{24,8},{1,17},{9,25},{17,1},{25,9},{2,18},{10... | collective-permute-start | bytes 196616 | tf_op jit(solution)/shard_map/ppermute | solution.py:426
  36.8 2.4 %pack.3.refs_0_ = bf16[8,32,1664]{2,1,0:T(8,128)(2,1)S(1)} custom-call(s32[8]{0:T(128)S(1)} %iota_xor_fusion.1.order_ref, s32[24,128]{1,0:T(8,128)S(1)} %get-tuple-element.52.start_ref, s32[40,128]{1,0:T(8,128)S(1)} %get-tuple-element.53.inner_ref, s32[40,128]{1,0:T(8,128)S(1)} %get-tuple-element.54.tile_ref, ...), custom_call_target="tpu_custom_call" | custom-call | flops 335544320 | bytes 327680 | tf_op jit(solution)/shard_map/pack/pallas_call | solution.py:442
  39.2 0.9 %collective-permute-done.10.refs_6_ = bf16[32,1024]{1,0:T(8,128)(2,1)S(1)} collective-permute-done((bf16[32,1024]{1,0:T(8,128)(2,1)S(1)}, bf16[32,1024]{1,0:T(8,128)(2,1)S(1)}, u32[]{:S(2)}, u32[]{:S(2)}) %collective-permute-start.10) | collective-permute-done | bytes 65568 | tf_op jit(solution)/shard_map/ppermute | solution.py:426
  40.1 2.6 %pack.4 = (bf16[32,1280]{1,0:T(8,128)(2,1)S(1)}, bf16[32,1280]{1,0:T(8,128)(2,1)S(1)}, bf16[32,1280]{1,0:T(8,128)(2,1)S(1)}, bf16[32,1280]{1,0:T(8,128)(2,1)S(1)...) custom-call(s32[8]{0:T(128)S(1)} %iota_xor_fusion.1.order_ref, ...), custom_call_target="tpu_custom_call" | custom-call | flops 335544320 | bytes 327680 | tf_op jit(solution)/shard_map/pack/pallas_call | solution.py:442
  42.7 1.8 %collective-permute-start.11 = (bf16[32,5120]{1,0:T(8,128)(2,1)S(1)}, bf16[32,5120]{1,0:T(8,128)(2,1)S(1)}, u32[]{:S(2)}, u32[]{:S(2)}) collective-permute-start(bf16[32,5120]{1,0:T(8,128)(2,1)S(1)} %get-tuple-element.74), channel_id=1, source_target_pairs={{0,16},{8,24},{16,0},{24,8},{1,17},{9,25},{17,1},{25,9},{2,18},{10... | collective-permute-start | bytes 983048 | tf_op jit(solution)/shard_map/ppermute | solution.py:475
  44.5 4.5 %collective-permute-start.12 = (bf16[32,1280]{1,0:T(8,128)(2,1)S(1)}, bf16[32,1280]{1,0:T(8,128)(2,1)S(1)}, u32[]{:S(2)}, u32[]{:S(2)}) collective-permute-start(bf16[32,1280]{1,0:T(8,128)(2,1)S(1)} %get-tuple-element.83), channel_id=1, source_target_pairs={{0,7},{1,6},{2,5},{3,4},{4,3},{5,2},{6,1},{7,0},{8,15},{9,14},{10,... | collective-permute-start | bytes 245768 | tf_op jit(solution)/shard_map/ppermute | solution.py:464
  49.9 1.2 %collective-permute-start.15 = (bf16[32,1280]{1,0:T(8,128)(2,1)S(1)}, bf16[32,1280]{1,0:T(8,128)(2,1)S(1)}, u32[]{:S(2)}, u32[]{:S(2)}) collective-permute-start(bf16[32,1280]{1,0:T(8,128)(2,1)S(1)} %get-tuple-element.86), channel_id=1, source_target_pairs={{0,2},{1,3},{2,0},{3,1},{4,6},{5,7},{6,4},{7,5},{8,10},{9,11},{10,... | collective-permute-start | bytes 245768 | tf_op jit(solution)/shard_map/ppermute | solution.py:464
  51.1 0.9 collective-permute-done.11.refs_1_.refs_3_.refs_5_.refs_7_
  51.9 1.7 %collective-permute-start.23 = (bf16[32,1280]{1,0:T(8,128)(2,1)S(1)}, bf16[32,1280]{1,0:T(8,128)(2,1)S(1)}, u32[]{:S(2)}, u32[]{:S(2)}) collective-permute-start(bf16[32,1280]{1,0:T(8,128)(2,1)S(1)} %get-tuple-element.96), channel_id=1, source_target_pairs={{0,1},{1,0},{2,3},{3,2},{4,5},{5,4},{6,7},{7,6},{8,9},{9,8},{10,11... | collective-permute-start | bytes 245768 | tf_op jit(solution)/shard_map/ppermute | solution.py:464
  53.7 4.0 %pack.5 = (bf16[32,1280]{1,0:T(8,128)(2,1)S(1)}, bf16[32,1280]{1,0:T(8,128)(2,1)S(1)}, bf16[32,1280]{1,0:T(8,128)(2,1)S(1)}, bf16[32,1280]{1,0:T(8,128)(2,1)S(1)...) custom-call(s32[8]{0:T(128)S(1)} %iota_xor_fusion.1.order_ref, ...), custom_call_target="tpu_custom_call" | custom-call | flops 671088640 | bytes 655360 | tf_op jit(solution)/shard_map/pack/pallas_call | solution.py:442
  62.7 2.6 %collective-permute-start.24 = (bf16[32,1280]{1,0:T(8,128)(2,1)S(1)}, bf16[32,1280]{1,0:T(8,128)(2,1)S(1)}, u32[]{:S(2)}, u32[]{:S(2)}) collective-permute-start(bf16[32,1280]{1,0:T(8,128)(2,1)S(1)} %get-tuple-element.97), channel_id=1, source_target_pairs={{0,4},{1,5},{2,6},{3,7},{4,0},{5,1},{6,2},{7,3},{8,12},{9,13},{10,... | collective-permute-start | bytes 245768 | tf_op jit(solution)/shard_map/ppermute | solution.py:464
  66.1 1.3 %gate.1 = (bf16[32,1280]{1,0:T(8,128)(2,1)S(1)}, bf16[32,1280]{1,0:T(8,128)(2,1)S(1)}, bf16[32,1280]{1,0:T(8,128)(2,1)S(1)}, bf16[32,1280]{1,0:T(8,128)(2,1)S(1)...) custom-call(bf16[32,1280]{1,0:T(8,128)(2,1)} %copy-done.3, ...), custom_call_target="tpu_custom_call" | custom-call | tf_op jit(solution)/shard_map/gate/pallas_call | solution.py:479
  67.4 1.8 %collective-permute-start.16 = (bf16[32,1280]{1,0:T(8,128)(2,1)S(1)}, bf16[32,1280]{1,0:T(8,128)(2,1)S(1)}, u32[]{:S(2)}, u32[]{:S(2)}) collective-permute-start(bf16[32,1280]{1,0:T(8,128)(2,1)S(1)} %get-tuple-element.88), channel_id=1, source_target_pairs={{0,1},{1,0},{2,3},{3,2},{4,5},{5,4},{6,7},{7,6},{8,9},{9,8},{10,11... | collective-permute-start | bytes 245768 | tf_op jit(solution)/shard_map/ppermute | solution.py:464
  69.2 1.5 %collective-permute-start.17 = (bf16[32,1280]{1,0:T(8,128)(2,1)S(1)}, bf16[32,1280]{1,0:T(8,128)(2,1)S(1)}, u32[]{:S(2)}, u32[]{:S(2)}) collective-permute-start(bf16[32,1280]{1,0:T(8,128)(2,1)S(1)} %get-tuple-element.89), channel_id=1, source_target_pairs={{0,2},{1,3},{2,0},{3,1},{4,6},{5,7},{6,4},{7,5},{8,10},{9,11},{10,... | collective-permute-start | bytes 245768 | tf_op jit(solution)/shard_map/ppermute | solution.py:464
  70.9 2.8 %collective-permute-start.19 = (bf16[32,1280]{1,0:T(8,128)(2,1)S(1)}, bf16[32,1280]{1,0:T(8,128)(2,1)S(1)}, u32[]{:S(2)}, u32[]{:S(2)}) collective-permute-start(bf16[32,1280]{1,0:T(8,128)(2,1)S(1)} %get-tuple-element.91), channel_id=1, source_target_pairs={{0,4},{1,5},{2,6},{3,7},{4,0},{5,1},{6,2},{7,3},{8,12},{9,13},{10,... | collective-permute-start | bytes 245768 | tf_op jit(solution)/shard_map/ppermute | solution.py:464
  73.7 1.3 %collective-permute-start.20 = (bf16[32,1280]{1,0:T(8,128)(2,1)S(1)}, bf16[32,1280]{1,0:T(8,128)(2,1)S(1)}, u32[]{:S(2)}, u32[]{:S(2)}) collective-permute-start(bf16[32,1280]{1,0:T(8,128)(2,1)S(1)} %get-tuple-element.92), channel_id=1, source_target_pairs={{0,5},{1,4},{2,7},{3,6},{4,1},{5,0},{6,3},{7,2},{8,13},{9,12},{10,... | collective-permute-start | bytes 245768 | tf_op jit(solution)/shard_map/ppermute | solution.py:464
  75.1 3.6 %collective-permute-start.21 = (bf16[32,1280]{1,0:T(8,128)(2,1)S(1)}, bf16[32,1280]{1,0:T(8,128)(2,1)S(1)}, u32[]{:S(2)}, u32[]{:S(2)}) collective-permute-start(bf16[32,1280]{1,0:T(8,128)(2,1)S(1)} %get-tuple-element.93), channel_id=1, source_target_pairs={{0,6},{1,7},{2,4},{3,5},{4,2},{5,3},{6,0},{7,1},{8,14},{9,15},{10,... | collective-permute-start | bytes 245768 | tf_op jit(solution)/shard_map/ppermute | solution.py:464
  78.7 2.1 %assemble.2.refs_8_ = bf16[8,64,1280]{2,1,0:T(8,128)(2,1)} custom-call(s32[8]{0:T(128)} %copy-done.11, bf16[32,1280]{1,0:T(8,128)(2,1)} %copy-done.1, bf16[32,1280]{1,0:T(8,128)(2,1)} %copy-done.16, bf16[32,1280]{1,0:T(8,128)(2,1)} %copy-done.15, bf16[32,1280]{1,0:T(8,128)(2,1)} %copy-done.13, bf16[32,1280]{1,0:T(8,128)(2,1)} %copy-done.17, ...), custom_call_target="tpu_custom_call" | custom-call | tf_op jit(solution)/shard_map/assemble/pallas_call | solution.py:490
  80.8 1.4 %collective-permute-done.19.refs_4_ = bf16[32,1280]{1,0:T(8,128)(2,1)S(1)} collective-permute-done((bf16[32,1280]{1,0:T(8,128)(2,1)S(1)}, bf16[32,1280]{1,0:T(8,128)(2,1)S(1)}, u32[]{:S(2)}, u32[]{:S(2)}) %collective-permute-start.19) | collective-permute-done | bytes 81952 | tf_op jit(solution)/shard_map/ppermute | solution.py:464
  82.2 2.7 %collective-permute-done.20.refs_5_ = bf16[32,1280]{1,0:T(8,128)(2,1)S(1)} collective-permute-done((bf16[32,1280]{1,0:T(8,128)(2,1)S(1)}, bf16[32,1280]{1,0:T(8,128)(2,1)S(1)}, u32[]{:S(2)}, u32[]{:S(2)}) %collective-permute-start.20) | collective-permute-done | bytes 81952 | tf_op jit(solution)/shard_map/ppermute | solution.py:464
  84.8 1.1 %collective-permute-done.22.refs_7_ = bf16[32,1280]{1,0:T(8,128)(2,1)S(1)} collective-permute-done((bf16[32,1280]{1,0:T(8,128)(2,1)S(1)}, bf16[32,1280]{1,0:T(8,128)(2,1)S(1)}, u32[]{:S(2)}, u32[]{:S(2)}) %collective-permute-start.22) | collective-permute-done | bytes 81952 | tf_op jit(solution)/shard_map/ppermute | solution.py:464
  86.5 2.1 %assemble.3 = bf16[8,64,1280]{2,1,0:T(8,128)(2,1)} custom-call(s32[8]{0:T(128)} %copy-done.11, bf16[32,1280]{1,0:T(8,128)(2,1)} %copy-done.2, bf16[32,1280]{1,0:T(8,128)(2,1)} %copy-done.19, bf16[32,1280]{1,0:T(8,128)(2,1)} %copy-done.20, bf16[32,1280]{1,0:T(8,128)(2,1)} %copy-done.21, bf16[32,1280]{1,0:T(8,128)(2,1)} %copy-done.22, ...), custom_call_target="tpu_custom_call", output_to_operand_aliasing={{}: (9, {})} | custom-call | tf_op jit(solution)/shard_map/assemble/pallas_call | solution.py:490
  (92 shorter events, 10.7 us)
Async XLA Ops:
  1.2 11.4 %collective-permute-start.2 = (bf16[64,1408]{1,0:T(8,128)(2,1)S(1)}, bf16[64,1408]{1,0:T(8,128)(2,1)S(1)}, u32[]{:S(2)}, u32[]{:S(2)}) collective-permute-start(bf16[64,1408]{1,0:T(8,128)(2,1)S(1)} %get-tuple-element.99), channel_id=1, source_target_pairs={{0,24},{8,16},{16,8},{24,0},{1,25},{9,17},{17,9},{25,1},{2,26},{10... | collective-permute-start | bytes 540680 | tf_op jit(solution)/shard_map/ppermute | solution.py:337
  3.7 1.7 %collective-permute-start = (bf16[64,1408]{1,0:T(8,128)(2,1)S(1)}, bf16[64,1408]{1,0:T(8,128)(2,1)S(1)}, u32[]{:S(2)}, u32[]{:S(2)}) collective-permute-start(bf16[64,1408]{1,0:T(8,128)(2,1)S(1)} %get-tuple-element.100), channel_id=1, source_target_pairs={{0,8},{8,0},{16,24},{24,16},{1,9},{9,1},{17,25},{25,17},{2,10},{10... | collective-permute-start | bytes 540680 | tf_op jit(solution)/shard_map/ppermute | solution.py:337
  4.4 8.3 %collective-permute-start.1 = (bf16[64,1408]{1,0:T(8,128)(2,1)S(1)}, bf16[64,1408]{1,0:T(8,128)(2,1)S(1)}, u32[]{:S(2)}, u32[]{:S(2)}) collective-permute-start(bf16[64,1408]{1,0:T(8,128)(2,1)S(1)} %get-tuple-element.102), channel_id=1, source_target_pairs={{0,16},{8,24},{16,0},{24,8},{1,17},{9,25},{17,1},{25,9},{2,18},{10... | collective-permute-start | bytes 540680 | tf_op jit(solution)/shard_map/ppermute | solution.py:337
  20.1 4.3 %collective-permute-start.3 = (bf16[128,1024]{1,0:T(8,128)(2,1)S(1)}, bf16[128,1024]{1,0:T(8,128)(2,1)S(1)}, u32[]{:S(2)}, u32[]{:S(2)}) collective-permute-start(bf16[128,1024]{1,0:T(8,128)(2,1)S(1)} %get-tuple-element.59), channel_id=1, source_target_pairs={{0,8},{8,0},{16,24},{24,16},{1,9},{9,1},{17,25},{25,17},{2,10},{10... | collective-permute-start | bytes 786440 | tf_op jit(solution)/shard_map/ppermute | solution.py:426
  24.1 6.3 %collective-permute-start.5 = (bf16[128,1536]{1,0:T(8,128)(2,1)S(1)}, bf16[128,1536]{1,0:T(8,128)(2,1)S(1)}, u32[]{:S(2)}, u32[]{:S(2)}) collective-permute-start(bf16[128,1536]{1,0:T(8,128)(2,1)S(1)} %get-tuple-element.63), channel_id=1, source_target_pairs={{0,8},{8,0},{16,24},{24,16},{1,9},{9,1},{17,25},{25,17},{2,10},{10... | collective-permute-start | bytes 1179656 | tf_op jit(solution)/shard_map/ppermute | solution.py:426
  24.4 6.3 %collective-permute-start.4 = (bf16[32,1024]{1,0:T(8,128)(2,1)S(1)}, bf16[32,1024]{1,0:T(8,128)(2,1)S(1)}, u32[]{:S(2)}, u32[]{:S(2)}) collective-permute-start(bf16[32,1024]{1,0:T(8,128)(2,1)S(1)} %add_convert_fusion.3.refs_2_), channel_id=1, source_target_pairs={{0,16},{8,24},{16,0},{24,8},{1,17},{9,25},{17,1},{25,9},{2,18},{10... | collective-permute-start | bytes 196616 | tf_op jit(solution)/shard_map/ppermute | solution.py:426
  30.4 3.2 %collective-permute-start.7 = (bf16[128,1536]{1,0:T(8,128)(2,1)S(1)}, bf16[128,1536]{1,0:T(8,128)(2,1)S(1)}, u32[]{:S(2)}, u32[]{:S(2)}) collective-permute-start(bf16[128,1536]{1,0:T(8,128)(2,1)S(1)} %get-tuple-element.67), channel_id=1, source_target_pairs={{0,8},{8,0},{16,24},{24,16},{1,9},{9,1},{17,25},{25,17},{2,10},{10... | collective-permute-start | bytes 1179656 | tf_op jit(solution)/shard_map/ppermute | solution.py:426
  30.5 6.3 %collective-permute-start.6 = (bf16[32,1536]{1,0:T(8,128)(2,1)S(1)}, bf16[32,1536]{1,0:T(8,128)(2,1)S(1)}, u32[]{:S(2)}, u32[]{:S(2)}) collective-permute-start(bf16[32,1536]{1,0:T(8,128)(2,1)S(1)} %add_convert_fusion.1.refs_3_), channel_id=1, source_target_pairs={{0,16},{8,24},{16,0},{24,8},{1,17},{9,25},{17,1},{25,9},{2,18},{10... | collective-permute-start | bytes 294920 | tf_op jit(solution)/shard_map/ppermute | solution.py:426
  33.1 2.3 %collective-permute-start.9 = (bf16[128,1024]{1,0:T(8,128)(2,1)S(1)}, bf16[128,1024]{1,0:T(8,128)(2,1)S(1)}, u32[]{:S(2)}, u32[]{:S(2)}) collective-permute-start(bf16[128,1024]{1,0:T(8,128)(2,1)S(1)} %get-tuple-element.72), channel_id=1, source_target_pairs={{0,8},{8,0},{16,24},{24,16},{1,9},{9,1},{17,25},{25,17},{2,10},{10... | collective-permute-start | bytes 786440 | tf_op jit(solution)/shard_map/ppermute | solution.py:426
  33.6 6.5 %collective-permute-start.8 = (bf16[32,1536]{1,0:T(8,128)(2,1)S(1)}, bf16[32,1536]{1,0:T(8,128)(2,1)S(1)}, u32[]{:S(2)}, u32[]{:S(2)}) collective-permute-start(bf16[32,1536]{1,0:T(8,128)(2,1)S(1)} %add_convert_fusion), channel_id=1, source_target_pairs={{0,16},{8,24},{16,0},{24,8},{1,17},{9,25},{17,1},{25,9},{2,18},{10... | collective-permute-start | bytes 294920 | tf_op jit(solution)/shard_map/ppermute | solution.py:426
  35.5 4.6 %collective-permute-start.10 = (bf16[32,1024]{1,0:T(8,128)(2,1)S(1)}, bf16[32,1024]{1,0:T(8,128)(2,1)S(1)}, u32[]{:S(2)}, u32[]{:S(2)}) collective-permute-start(bf16[32,1024]{1,0:T(8,128)(2,1)S(1)} %add_convert_fusion.2), channel_id=1, source_target_pairs={{0,16},{8,24},{16,0},{24,8},{1,17},{9,25},{17,1},{25,9},{2,18},{10... | collective-permute-start | bytes 196616 | tf_op jit(solution)/shard_map/ppermute | solution.py:426
  36.8 20.9 %copy-start.11 = (s32[8]{0:T(128)}, s32[8]{0:T(128)S(1)}, u32[]{:S(2)}) copy-start(s32[8]{0:T(128)S(1)} %iota_xor_fusion.1.order_ref) | copy-start | bytes 100
  42.7 15.0 %copy-start.1 = (bf16[32,1280]{1,0:T(8,128)(2,1)}, bf16[32,1280]{1,0:T(8,128)(2,1)S(1)}, u32[]{:S(2)}) copy-start(bf16[32,1280]{1,0:T(8,128)(2,1)S(1)} %get-tuple-element.95.refs_0_) | copy-start | bytes 245764
  42.7 9.2 %collective-permute-start.11 = (bf16[32,5120]{1,0:T(8,128)(2,1)S(1)}, bf16[32,5120]{1,0:T(8,128)(2,1)S(1)}, u32[]{:S(2)}, u32[]{:S(2)}) collective-permute-start(bf16[32,5120]{1,0:T(8,128)(2,1)S(1)} %get-tuple-element.74), channel_id=1, source_target_pairs={{0,16},{8,24},{16,0},{24,8},{1,17},{9,25},{17,1},{25,9},{2,18},{10... | collective-permute-start | bytes 983048 | tf_op jit(solution)/shard_map/ppermute | solution.py:475
  44.5 18.2 %collective-permute-start.12 = (bf16[32,1280]{1,0:T(8,128)(2,1)S(1)}, bf16[32,1280]{1,0:T(8,128)(2,1)S(1)}, u32[]{:S(2)}, u32[]{:S(2)}) collective-permute-start(bf16[32,1280]{1,0:T(8,128)(2,1)S(1)} %get-tuple-element.83), channel_id=1, source_target_pairs={{0,7},{1,6},{2,5},{3,4},{4,3},{5,2},{6,1},{7,0},{8,15},{9,14},{10,... | collective-permute-start | bytes 245768 | tf_op jit(solution)/shard_map/ppermute | solution.py:464
  49.1 16.2 %collective-permute-start.13 = (bf16[32,1280]{1,0:T(8,128)(2,1)S(1)}, bf16[32,1280]{1,0:T(8,128)(2,1)S(1)}, u32[]{:S(2)}, u32[]{:S(2)}) collective-permute-start(bf16[32,1280]{1,0:T(8,128)(2,1)S(1)} %get-tuple-element.84), channel_id=1, source_target_pairs={{0,3},{1,2},{2,1},{3,0},{4,7},{5,6},{6,5},{7,4},{8,11},{9,10},{10,... | collective-permute-start | bytes 245768 | tf_op jit(solution)/shard_map/ppermute | solution.py:464
  49.1 16.3 %collective-permute-start.14 = (bf16[32,1280]{1,0:T(8,128)(2,1)S(1)}, bf16[32,1280]{1,0:T(8,128)(2,1)S(1)}, u32[]{:S(2)}, u32[]{:S(2)}) collective-permute-start(bf16[32,1280]{1,0:T(8,128)(2,1)S(1)} %get-tuple-element.85), channel_id=1, source_target_pairs={{0,6},{1,7},{2,4},{3,5},{4,2},{5,3},{6,0},{7,1},{8,14},{9,15},{10,... | collective-permute-start | bytes 245768 | tf_op jit(solution)/shard_map/ppermute | solution.py:464
  49.9 15.5 %collective-permute-start.15 = (bf16[32,1280]{1,0:T(8,128)(2,1)S(1)}, bf16[32,1280]{1,0:T(8,128)(2,1)S(1)}, u32[]{:S(2)}, u32[]{:S(2)}) collective-permute-start(bf16[32,1280]{1,0:T(8,128)(2,1)S(1)} %get-tuple-element.86), channel_id=1, source_target_pairs={{0,2},{1,3},{2,0},{3,1},{4,6},{5,7},{6,4},{7,5},{8,10},{9,11},{10,... | collective-permute-start | bytes 245768 | tf_op jit(solution)/shard_map/ppermute | solution.py:464
  51.9 18.8 %collective-permute-start.23 = (bf16[32,1280]{1,0:T(8,128)(2,1)S(1)}, bf16[32,1280]{1,0:T(8,128)(2,1)S(1)}, u32[]{:S(2)}, u32[]{:S(2)}) collective-permute-start(bf16[32,1280]{1,0:T(8,128)(2,1)S(1)} %get-tuple-element.96), channel_id=1, source_target_pairs={{0,1},{1,0},{2,3},{3,2},{4,5},{5,4},{6,7},{7,6},{8,9},{9,8},{10,11... | collective-permute-start | bytes 245768 | tf_op jit(solution)/shard_map/ppermute | solution.py:464
  62.7 8.2 %collective-permute-start.24 = (bf16[32,1280]{1,0:T(8,128)(2,1)S(1)}, bf16[32,1280]{1,0:T(8,128)(2,1)S(1)}, u32[]{:S(2)}, u32[]{:S(2)}) collective-permute-start(bf16[32,1280]{1,0:T(8,128)(2,1)S(1)} %get-tuple-element.97), channel_id=1, source_target_pairs={{0,4},{1,5},{2,6},{3,7},{4,0},{5,1},{6,2},{7,3},{8,12},{9,13},{10,... | collective-permute-start | bytes 245768 | tf_op jit(solution)/shard_map/ppermute | solution.py:464
  65.3 8.4 %collective-permute-start.25 = (bf16[32,1280]{1,0:T(8,128)(2,1)S(1)}, bf16[32,1280]{1,0:T(8,128)(2,1)S(1)}, u32[]{:S(2)}, u32[]{:S(2)}) collective-permute-start(bf16[32,1280]{1,0:T(8,128)(2,1)S(1)} %get-tuple-element.98), channel_id=1, source_target_pairs={{0,5},{1,4},{2,7},{3,6},{4,1},{5,0},{6,3},{7,2},{8,13},{9,12},{10,... | collective-permute-start | bytes 245768 | tf_op jit(solution)/shard_map/ppermute | solution.py:464
  67.4 18.5 %copy-start.2 = (bf16[32,1280]{1,0:T(8,128)(2,1)}, bf16[32,1280]{1,0:T(8,128)(2,1)S(1)}, u32[]{:S(2)}) copy-start(bf16[32,1280]{1,0:T(8,128)(2,1)S(1)} %get-tuple-element.87.refs_0_) | copy-start | bytes 245764
  67.4 7.7 %collective-permute-start.16 = (bf16[32,1280]{1,0:T(8,128)(2,1)S(1)}, bf16[32,1280]{1,0:T(8,128)(2,1)S(1)}, u32[]{:S(2)}, u32[]{:S(2)}) collective-permute-start(bf16[32,1280]{1,0:T(8,128)(2,1)S(1)} %get-tuple-element.88), channel_id=1, source_target_pairs={{0,1},{1,0},{2,3},{3,2},{4,5},{5,4},{6,7},{7,6},{8,9},{9,8},{10,11... | collective-permute-start | bytes 245768 | tf_op jit(solution)/shard_map/ppermute | solution.py:464
  69.2 9.5 %collective-permute-start.17 = (bf16[32,1280]{1,0:T(8,128)(2,1)S(1)}, bf16[32,1280]{1,0:T(8,128)(2,1)S(1)}, u32[]{:S(2)}, u32[]{:S(2)}) collective-permute-start(bf16[32,1280]{1,0:T(8,128)(2,1)S(1)} %get-tuple-element.89), channel_id=1, source_target_pairs={{0,2},{1,3},{2,0},{3,1},{4,6},{5,7},{6,4},{7,5},{8,10},{9,11},{10,... | collective-permute-start | bytes 245768 | tf_op jit(solution)/shard_map/ppermute | solution.py:464
  70.7 8.0 %copy-start.16 = (bf16[32,1280]{1,0:T(8,128)(2,1)}, bf16[32,1280]{1,0:T(8,128)(2,1)S(1)}, u32[]{:S(2)}) copy-start(bf16[32,1280]{1,0:T(8,128)(2,1)S(1)} %collective-permute-done.23.refs_1_) | copy-start | bytes 245764
  70.7 10.1 %collective-permute-start.18 = (bf16[32,1280]{1,0:T(8,128)(2,1)S(1)}, bf16[32,1280]{1,0:T(8,128)(2,1)S(1)}, u32[]{:S(2)}, u32[]{:S(2)}) collective-permute-start(bf16[32,1280]{1,0:T(8,128)(2,1)S(1)} %get-tuple-element.90), channel_id=1, source_target_pairs={{0,3},{1,2},{2,1},{3,0},{4,7},{5,6},{6,5},{7,4},{8,11},{9,10},{10,... | collective-permute-start | bytes 245768 | tf_op jit(solution)/shard_map/ppermute | solution.py:464
  70.9 7.8 %copy-start.17 = (bf16[32,1280]{1,0:T(8,128)(2,1)}, bf16[32,1280]{1,0:T(8,128)(2,1)S(1)}, u32[]{:S(2)}) copy-start(bf16[32,1280]{1,0:T(8,128)(2,1)S(1)} %collective-permute-done.24.refs_4_) | copy-start | bytes 245764
  70.9 11.2 %collective-permute-start.19 = (bf16[32,1280]{1,0:T(8,128)(2,1)S(1)}, bf16[32,1280]{1,0:T(8,128)(2,1)S(1)}, u32[]{:S(2)}, u32[]{:S(2)}) collective-permute-start(bf16[32,1280]{1,0:T(8,128)(2,1)S(1)} %get-tuple-element.91), channel_id=1, source_target_pairs={{0,4},{1,5},{2,6},{3,7},{4,0},{5,1},{6,2},{7,3},{8,12},{9,13},{10,... | collective-permute-start | bytes 245768 | tf_op jit(solution)/shard_map/ppermute | solution.py:464
  73.7 11.1 %collective-permute-start.20 = (bf16[32,1280]{1,0:T(8,128)(2,1)S(1)}, bf16[32,1280]{1,0:T(8,128)(2,1)S(1)}, u32[]{:S(2)}, u32[]{:S(2)}) collective-permute-start(bf16[32,1280]{1,0:T(8,128)(2,1)S(1)} %get-tuple-element.92), channel_id=1, source_target_pairs={{0,5},{1,4},{2,7},{3,6},{4,1},{5,0},{6,3},{7,2},{8,13},{9,12},{10,... | collective-permute-start | bytes 245768 | tf_op jit(solution)/shard_map/ppermute | solution.py:464
  75.1 10.8 %copy-start.19 = (bf16[32,1280]{1,0:T(8,128)(2,1)}, bf16[32,1280]{1,0:T(8,128)(2,1)S(1)}, u32[]{:S(2)}) copy-start(bf16[32,1280]{1,0:T(8,128)(2,1)S(1)} %collective-permute-done.16.refs_1_) | copy-start | bytes 245764
  75.1 9.8 %collective-permute-start.21 = (bf16[32,1280]{1,0:T(8,128)(2,1)S(1)}, bf16[32,1280]{1,0:T(8,128)(2,1)S(1)}, u32[]{:S(2)}, u32[]{:S(2)}) collective-permute-start(bf16[32,1280]{1,0:T(8,128)(2,1)S(1)} %get-tuple-element.93), channel_id=1, source_target_pairs={{0,6},{1,7},{2,4},{3,5},{4,2},{5,3},{6,0},{7,1},{8,14},{9,15},{10,... | collective-permute-start | bytes 245768 | tf_op jit(solution)/shard_map/ppermute | solution.py:464
  78.7 7.2 %collective-permute-start.22 = (bf16[32,1280]{1,0:T(8,128)(2,1)S(1)}, bf16[32,1280]{1,0:T(8,128)(2,1)S(1)}, u32[]{:S(2)}, u32[]{:S(2)}) collective-permute-start(bf16[32,1280]{1,0:T(8,128)(2,1)S(1)} %get-tuple-element.94), channel_id=1, source_target_pairs={{0,7},{1,6},{2,5},{3,4},{4,3},{5,2},{6,1},{7,0},{8,15},{9,14},{10,... | collective-permute-start | bytes 245768 | tf_op jit(solution)/shard_map/ppermute | solution.py:464
  (20 other events, 40.9 us)

commit v12 on v11

--- a/solution.py
+++ b/solution.py
@@ -481,6 +481,7 @@
         in_specs=[VMEM()] * (owners + GATE),
         out_specs=[VMEM()] * owners,
         out_shape=[pltpu.VMEM((half, send_cap), jnp.bfloat16)] * owners,
+        compiler_params=pltpu.CompilerParams(vmem_limit_bytes=4 * MIB),
         name="gate",
     )(*two, *(one[d] for d in turns[:GATE]))
     two = deliver(two)
@@ -494,6 +495,7 @@
             out_shape=jax.ShapeDtypeStruct((owners, time_block, send_cap), jnp.bfloat16),
             scratch_shapes=[pltpu.SemaphoreType.DMA((owners,))],
             input_output_aliases={1 + owners: 0} if given else {},
+            compiler_params=pltpu.CompilerParams(vmem_limit_bytes=4 * MIB),
             name="assemble",
         )(targets, *got, *given)
     return jnp.transpose(owned, (0, 2, 1))

time: 88.9 us -> 81.2 us (0.913)
  local copies, waits for them, and re-layouts: 8.25 us -> 1.94 us
  Pallas kernels: 38.8 us -> 36.3 us
  waiting for transfers between devices: 7.22 us -> 9.51 us
  starting transfers between devices: 33.9 us -> 33 us
    unnamed x52 -> x2, local copies, waits for them, and re-layouts: 6.32 us -> 0.01 us
    ppermute x14, waiting for transfers between devices: 5.12 us -> 7.37 us  [deliver(): got[d] = lax.ppermute(packed[d], 'vox', [(i, i ^ d) for i in range(owners)])]
    pallas_call x2, Pallas kernels: 4.16 us -> 2.87 us  [shards(): pl.pallas_call(functools.partial(assemble_kernel, owners, first), in_spec...]
    pallas_call x1, Pallas kernels: 1.31 us -> 0.04 us  [shards(): pl.pallas_call(gate_kernel, in_specs=[VMEM()] * (owners + GATE), out_spec...]
    ppermute x14, starting transfers between devices: 22.2 us -> 21.2 us  [deliver(): got[d] = lax.ppermute(packed[d], 'vox', [(i, i ^ d) for i in range(owners)])]
  transfers between devices with their start and end apart: 26 -> 26, of which waited for: 6 -> 8; matrix products, arithmetic and copies ran while one was open for 1% -> 1% of each run, Pallas kernels for 30% -> 31%
where the time goes in v12:
time: 81.2 us; the launch traced here: 81 us
  Pallas kernels  36.3 us (45%)
  starting transfers between devices  33 us (41%)
  waiting for transfers between devices  9.51 us (12%)
  local copies, waits for them, and re-layouts  1.94 us (2%)
    ppermute x14, starting transfers between devices, deliver(): got[d] = lax.ppermute(packed[d], 'vox', [(i, i ^ d) for i in range(owners)])  21.2 us
    pallas_call x4, Pallas kernels, product(): pl.pallas_call(functools.partial(product_kernel, len(taken), len(after),...  12.2 us
    pallas_call x3, Pallas kernels, pack(): pl.pallas_call(functools.partial(pack_kernel, spread, sizes, spots, sum(w...  9.05 us
    ppermute x14, waiting for transfers between devices, deliver(): got[d] = lax.ppermute(packed[d], 'vox', [(i, i ^ d) for i in range(owners)])  7.37 us
    pallas_call x1, Pallas kernels, shards(): pl.pallas_call(functools.partial(early_kernel, owners, spread), in_specs=...  7.24 us
    ppermute x8, starting transfers between devices, shards(): lax.ppermute(send, 'chan', [(i, i ^ 1 << bit) for i in range(parts)])  6.76 us
    pallas_call x1, Pallas kernels, shards(): pl.pallas_call(functools.partial(design_kernel, parts, firsts[1]), in_spe...  4.9 us
    ppermute x3, starting transfers between devices, shards(): lax.ppermute(series[d], 'chan', [(i, i ^ d) for i in range(parts)])  3.16 us
  transfers between devices with their start and end apart: 26, of which 8 were waited for; matrix products, arithmetic and copies ran while one was open for 1% of the time, Pallas kernels for 31%

profile of v12, /device:TPU:0, one launch (start us, length us, event | category | flops | bytes accessed | tf_op | source)
XLA Modules:
  0.0 81.0 jit_solution(2726439357004957786)
XLA Ops:
  0.0 1.2 %constant_dynamic-slice_fusion = (bf16[64,1408]{1,0:T(8,128)(2,1)S(1)}, bf16[64,1408]{1,0:T(8,128)(2,1)S(1)}, bf16[64,1408]{1,0:T(8,128)(2,1)S(1)}, bf16[64,1408]{1,0:T(8,128)(2,1)S(1)}) fusion(bf16[64,5632]{1,0:T(8,128)(2,1)} %param.5, s32[]{:T(128)S(6)} %select_n.15, s32[]{:T(128)S(6)} %select_n.13, s32[]{:T(128)S(6)} %select_n.12, s32[]{:T(128)S(6)} %select_n.14), kind=kLoop, calls=%fused_computation.5 | loop fusion | bytes 1441808 | tf_op jit(solution)/shard_map/dynamic_slice | solution.py:335
  1.2 2.4 %collective-permute-start.2 = (bf16[64,1408]{1,0:T(8,128)(2,1)S(1)}, bf16[64,1408]{1,0:T(8,128)(2,1)S(1)}, u32[]{:S(2)}, u32[]{:S(2)}) collective-permute-start(bf16[64,1408]{1,0:T(8,128)(2,1)S(1)} %get-tuple-element.99), channel_id=1, source_target_pairs={{0,24},{8,16},{16,8},{24,0},{1,25},{9,17},{17,9},{25,1},{2,26},{10... | collective-permute-start | bytes 540680 | tf_op jit(solution)/shard_map/ppermute | solution.py:337
  5.4 7.2 %early.1 = (s32[40,128]{1,0:T(8,128)S(1)}, s32[40,128]{1,0:T(8,128)S(1)}, s32[24,128]{1,0:T(8,128)S(1)}, bf16[96,4224]{1,0:T(8,128)(2,1)S(1)}, bf16[3,1408,1024]...) custom-call(s32[4]{0:T(128)S(1)} %get-tuple-element.104.order_ref, ...), custom_call_target="tpu_custom_call" | custom-call | bytes 19464192 | tf_op jit(solution)/shard_map/early/pallas_call | solution.py:368
  12.7 4.9 %design.1 = (bf16[256,4224]{1,0:T(8,128)(2,1)S(1)}, bf16[3,1408,256]{2,1,0:T(8,128)(2,1)S(1)}, bf16[3,1408,1024]{2,1,0:T(8,128)(2,1)S(1)}) custom-call(s32[4]{0:T(128)S(1)} %get-tuple-element.104.order_ref, s32[4]{0:T(128)S(1)} %get-tuple-element.103.place_ref, bf16[96,4224]{1,0:T(8,128)(2,1)S(1)} %get-tuple-element.55.early_ref, ...), custom_call_target="tpu_custom_call" | custom-call | bytes 10813440 | tf_op jit(solution)/shard_map/design/pallas_call | solution.py:399
  17.6 2.5 %product.4 = (bf16[128,1024]{1,0:T(8,128)(2,1)S(1)}, bf16[128,1024]{1,0:T(8,128)(2,1)S(1)}) custom-call(bf16[256,4224]{1,0:T(8,128)(2,1)S(1)} %get-tuple-element.56.design_ref, bf16[3,1408,1024]{2,1,0:T(8,128)(2,1)S(1)} %get-tuple-element.57.refs_0_), custom_call_target="tpu_custom_call" | custom-call | flops 2214592512 | bytes 8650752 | tf_op jit(solution)/shard_map/product/pallas_call | solution.py:220
  20.5 3.6 %product.5 = (bf16[128,1536]{1,0:T(8,128)(2,1)S(1)}, bf16[128,1536]{1,0:T(8,128)(2,1)S(1)}, bf16[3,1408,512]{2,1,0:T(8,128)(2,1)S(1)}, bf16[3,1408,256]{2,1,0:T(8,128)(2,1)S(1)}) custom-call(bf16[256,4224]{1,0:T(8,128)(2,1)S(1)} %get-tuple-element.56.design_ref, bf16[3,1408,1280]{2,1,0:T(8,128)(2,1)S(1)} %get-tuple-element.60.refs_0_, ...), custom_call_target="tpu_custom_call" | custom-call | flops 3321888768 | bytes 12976128 | tf_op jit(solution)/shard_map/product/pallas_call | solution.py:220
  24.4 2.3 %collective-permute-start.4 = (bf16[32,1024]{1,0:T(8,128)(2,1)S(1)}, bf16[32,1024]{1,0:T(8,128)(2,1)S(1)}, u32[]{:S(2)}, u32[]{:S(2)}) collective-permute-start(bf16[32,1024]{1,0:T(8,128)(2,1)S(1)} %add_convert_fusion.3.refs_2_), channel_id=1, source_target_pairs={{0,16},{8,24},{16,0},{24,8},{1,17},{9,25},{17,1},{25,9},{2,18},{10... | collective-permute-start | bytes 196616 | tf_op jit(solution)/shard_map/ppermute | solution.py:426
  26.7 3.7 %product.6 = (bf16[128,1536]{1,0:T(8,128)(2,1)S(1)}, bf16[128,1536]{1,0:T(8,128)(2,1)S(1)}, bf16[3,1408,512]{2,1,0:T(8,128)(2,1)S(1)}, bf16[3,1408,256]{2,1,0:T(8,128)(2,1)S(1)}) custom-call(bf16[256,4224]{1,0:T(8,128)(2,1)S(1)} %get-tuple-element.56.design_ref, bf16[3,1408,1024]{2,1,0:T(8,128)(2,1)S(1)} %get-tuple-element.64.refs_0_, ...), custom_call_target="tpu_custom_call" | custom-call | flops 3321888768 | bytes 12976128 | tf_op jit(solution)/shard_map/product/pallas_call | solution.py:220
  30.7 2.5 %product.7 = (bf16[128,1024]{1,0:T(8,128)(2,1)S(1)}, bf16[128,1024]{1,0:T(8,128)(2,1)S(1)}) custom-call(bf16[256,4224]{1,0:T(8,128)(2,1)S(1)} %get-tuple-element.56.design_ref, bf16[3,1408,256]{2,1,0:T(8,128)(2,1)S(1)} %get-tuple-element.68.refs_0_, bf16[3,1408,512]{2,1,0:T(8,128)(2,1)S(1)} %get-tuple-element.69.refs_1_, ...), custom_call_target="tpu_custom_call" | custom-call | flops 2214592512 | bytes 8650752 | tf_op jit(solution)/shard_map/product/pallas_call | solution.py:220
  33.6 1.8 %collective-permute-start.8 = (bf16[32,1536]{1,0:T(8,128)(2,1)S(1)}, bf16[32,1536]{1,0:T(8,128)(2,1)S(1)}, u32[]{:S(2)}, u32[]{:S(2)}) collective-permute-start(bf16[32,1536]{1,0:T(8,128)(2,1)S(1)} %add_convert_fusion), channel_id=1, source_target_pairs={{0,16},{8,24},{16,0},{24,8},{1,17},{9,25},{17,1},{25,9},{2,18},{10... | collective-permute-start | bytes 294920 | tf_op jit(solution)/shard_map/ppermute | solution.py:426
  35.5 1.3 %collective-permute-start.10 = (bf16[32,1024]{1,0:T(8,128)(2,1)S(1)}, bf16[32,1024]{1,0:T(8,128)(2,1)S(1)}, u32[]{:S(2)}, u32[]{:S(2)}) collective-permute-start(bf16[32,1024]{1,0:T(8,128)(2,1)S(1)} %add_convert_fusion.2), channel_id=1, source_target_pairs={{0,16},{8,24},{16,0},{24,8},{1,17},{9,25},{17,1},{25,9},{2,18},{10... | collective-permute-start | bytes 196616 | tf_op jit(solution)/shard_map/ppermute | solution.py:426
  36.8 2.4 %pack.3.refs_0_ = bf16[8,32,1664]{2,1,0:T(8,128)(2,1)S(1)} custom-call(s32[8]{0:T(128)S(1)} %iota_xor_fusion.1.order_ref, s32[24,128]{1,0:T(8,128)S(1)} %get-tuple-element.52.start_ref, s32[40,128]{1,0:T(8,128)S(1)} %get-tuple-element.53.inner_ref, s32[40,128]{1,0:T(8,128)S(1)} %get-tuple-element.54.tile_ref, ...), custom_call_target="tpu_custom_call" | custom-call | flops 335544320 | bytes 327680 | tf_op jit(solution)/shard_map/pack/pallas_call | solution.py:442
  40.1 2.6 %pack.4 = (bf16[32,1280]{1,0:T(8,128)(2,1)S(1)}, bf16[32,1280]{1,0:T(8,128)(2,1)S(1)}, bf16[32,1280]{1,0:T(8,128)(2,1)S(1)}, bf16[32,1280]{1,0:T(8,128)(2,1)S(1)...) custom-call(s32[8]{0:T(128)S(1)} %iota_xor_fusion.1.order_ref, ...), custom_call_target="tpu_custom_call" | custom-call | flops 335544320 | bytes 327680 | tf_op jit(solution)/shard_map/pack/pallas_call | solution.py:442
  42.7 1.8 %collective-permute-start.11 = (bf16[32,5120]{1,0:T(8,128)(2,1)S(1)}, bf16[32,5120]{1,0:T(8,128)(2,1)S(1)}, u32[]{:S(2)}, u32[]{:S(2)}) collective-permute-start(bf16[32,5120]{1,0:T(8,128)(2,1)S(1)} %get-tuple-element.74), channel_id=1, source_target_pairs={{0,16},{8,24},{16,0},{24,8},{1,17},{9,25},{17,1},{25,9},{2,18},{10... | collective-permute-start | bytes 983048 | tf_op jit(solution)/shard_map/ppermute | solution.py:475
  44.5 4.5 %collective-permute-start.12 = (bf16[32,1280]{1,0:T(8,128)(2,1)S(1)}, bf16[32,1280]{1,0:T(8,128)(2,1)S(1)}, u32[]{:S(2)}, u32[]{:S(2)}) collective-permute-start(bf16[32,1280]{1,0:T(8,128)(2,1)S(1)} %get-tuple-element.83), channel_id=1, source_target_pairs={{0,7},{1,6},{2,5},{3,4},{4,3},{5,2},{6,1},{7,0},{8,15},{9,14},{10,... | collective-permute-start | bytes 245768 | tf_op jit(solution)/shard_map/ppermute | solution.py:464
  49.9 1.1 %collective-permute-start.15 = (bf16[32,1280]{1,0:T(8,128)(2,1)S(1)}, bf16[32,1280]{1,0:T(8,128)(2,1)S(1)}, u32[]{:S(2)}, u32[]{:S(2)}) collective-permute-start(bf16[32,1280]{1,0:T(8,128)(2,1)S(1)} %get-tuple-element.86), channel_id=1, source_target_pairs={{0,2},{1,3},{2,0},{3,1},{4,6},{5,7},{6,4},{7,5},{8,10},{9,11},{10,... | collective-permute-start | bytes 245768 | tf_op jit(solution)/shard_map/ppermute | solution.py:464
  51.9 1.7 %collective-permute-start.23 = (bf16[32,1280]{1,0:T(8,128)(2,1)S(1)}, bf16[32,1280]{1,0:T(8,128)(2,1)S(1)}, u32[]{:S(2)}, u32[]{:S(2)}) collective-permute-start(bf16[32,1280]{1,0:T(8,128)(2,1)S(1)} %get-tuple-element.96), channel_id=1, source_target_pairs={{0,1},{1,0},{2,3},{3,2},{4,5},{5,4},{6,7},{7,6},{8,9},{9,8},{10,11... | collective-permute-start | bytes 245768 | tf_op jit(solution)/shard_map/ppermute | solution.py:464
  53.6 4.0 %pack.5 = (bf16[32,1280]{1,0:T(8,128)(2,1)S(1)}, bf16[32,1280]{1,0:T(8,128)(2,1)S(1)}, bf16[32,1280]{1,0:T(8,128)(2,1)S(1)}, bf16[32,1280]{1,0:T(8,128)(2,1)S(1)...) custom-call(s32[8]{0:T(128)S(1)} %iota_xor_fusion.1.order_ref, ...), custom_call_target="tpu_custom_call" | custom-call | flops 671088640 | bytes 655360 | tf_op jit(solution)/shard_map/pack/pallas_call | solution.py:442
  57.7 2.6 %collective-permute-start.24 = (bf16[32,1280]{1,0:T(8,128)(2,1)S(1)}, bf16[32,1280]{1,0:T(8,128)(2,1)S(1)}, u32[]{:S(2)}, u32[]{:S(2)}) collective-permute-start(bf16[32,1280]{1,0:T(8,128)(2,1)S(1)} %get-tuple-element.97), channel_id=1, source_target_pairs={{0,4},{1,5},{2,6},{3,7},{4,0},{5,1},{6,2},{7,3},{8,12},{9,13},{10,... | collective-permute-start | bytes 245768 | tf_op jit(solution)/shard_map/ppermute | solution.py:464
  60.4 1.8 %collective-permute-start.16 = (bf16[32,1280]{1,0:T(8,128)(2,1)S(1)}, bf16[32,1280]{1,0:T(8,128)(2,1)S(1)}, u32[]{:S(2)}, u32[]{:S(2)}) collective-permute-start(bf16[32,1280]{1,0:T(8,128)(2,1)S(1)} %get-tuple-element.88), channel_id=1, source_target_pairs={{0,1},{1,0},{2,3},{3,2},{4,5},{5,4},{6,7},{7,6},{8,9},{9,8},{10,11... | collective-permute-start | bytes 245768 | tf_op jit(solution)/shard_map/ppermute | solution.py:464
  62.2 1.5 %collective-permute-start.17 = (bf16[32,1280]{1,0:T(8,128)(2,1)S(1)}, bf16[32,1280]{1,0:T(8,128)(2,1)S(1)}, u32[]{:S(2)}, u32[]{:S(2)}) collective-permute-start(bf16[32,1280]{1,0:T(8,128)(2,1)S(1)} %get-tuple-element.89), channel_id=1, source_target_pairs={{0,2},{1,3},{2,0},{3,1},{4,6},{5,7},{6,4},{7,5},{8,10},{9,11},{10,... | collective-permute-start | bytes 245768 | tf_op jit(solution)/shard_map/ppermute | solution.py:464
  64.0 1.6 %collective-permute-done.24.refs_4_ = bf16[32,1280]{1,0:T(8,128)(2,1)S(1)} collective-permute-done((bf16[32,1280]{1,0:T(8,128)(2,1)S(1)}, bf16[32,1280]{1,0:T(8,128)(2,1)S(1)}, u32[]{:S(2)}, u32[]{:S(2)}) %collective-permute-start.24) | collective-permute-done | bytes 81952 | tf_op jit(solution)/shard_map/ppermute | solution.py:464
  65.6 1.2 %collective-permute-start.19 = (bf16[32,1280]{1,0:T(8,128)(2,1)S(1)}, bf16[32,1280]{1,0:T(8,128)(2,1)S(1)}, u32[]{:S(2)}, u32[]{:S(2)}) collective-permute-start(bf16[32,1280]{1,0:T(8,128)(2,1)S(1)} %get-tuple-element.91), channel_id=1, source_target_pairs={{0,4},{1,5},{2,6},{3,7},{4,0},{5,1},{6,2},{7,3},{8,12},{9,13},{10,... | collective-permute-start | bytes 245768 | tf_op jit(solution)/shard_map/ppermute | solution.py:464
  66.8 1.2 %collective-permute-done.25.refs_5_ = bf16[32,1280]{1,0:T(8,128)(2,1)S(1)} collective-permute-done((bf16[32,1280]{1,0:T(8,128)(2,1)S(1)}, bf16[32,1280]{1,0:T(8,128)(2,1)S(1)}, u32[]{:S(2)}, u32[]{:S(2)}) %collective-permute-start.25) | collective-permute-done | bytes 81952 | tf_op jit(solution)/shard_map/ppermute | solution.py:464
  68.0 1.2 %collective-permute-start.20 = (bf16[32,1280]{1,0:T(8,128)(2,1)S(1)}, bf16[32,1280]{1,0:T(8,128)(2,1)S(1)}, u32[]{:S(2)}, u32[]{:S(2)}) collective-permute-start(bf16[32,1280]{1,0:T(8,128)(2,1)S(1)} %get-tuple-element.92), channel_id=1, source_target_pairs={{0,5},{1,4},{2,7},{3,6},{4,1},{5,0},{6,3},{7,2},{8,13},{9,12},{10,... | collective-permute-start | bytes 245768 | tf_op jit(solution)/shard_map/ppermute | solution.py:464
  69.2 3.2 %collective-permute-start.21 = (bf16[32,1280]{1,0:T(8,128)(2,1)S(1)}, bf16[32,1280]{1,0:T(8,128)(2,1)S(1)}, u32[]{:S(2)}, u32[]{:S(2)}) collective-permute-start(bf16[32,1280]{1,0:T(8,128)(2,1)S(1)} %get-tuple-element.93), channel_id=1, source_target_pairs={{0,6},{1,7},{2,4},{3,5},{4,2},{5,3},{6,0},{7,1},{8,14},{9,15},{10,... | collective-permute-start | bytes 245768 | tf_op jit(solution)/shard_map/ppermute | solution.py:464
  72.3 1.2 %collective-permute-start.22 = (bf16[32,1280]{1,0:T(8,128)(2,1)S(1)}, bf16[32,1280]{1,0:T(8,128)(2,1)S(1)}, u32[]{:S(2)}, u32[]{:S(2)}) collective-permute-start(bf16[32,1280]{1,0:T(8,128)(2,1)S(1)} %get-tuple-element.94), channel_id=1, source_target_pairs={{0,7},{1,6},{2,5},{3,4},{4,3},{5,2},{6,1},{7,0},{8,15},{9,14},{10,... | collective-permute-start | bytes 245768 | tf_op jit(solution)/shard_map/ppermute | solution.py:464
  73.6 1.4 %assemble.2.refs_8_ = bf16[8,64,1280]{2,1,0:T(8,128)(2,1)} custom-call(s32[8]{0:T(128)S(1)} %iota_xor_fusion.1.order_ref, bf16[32,1280]{1,0:T(8,128)(2,1)S(1)} %get-tuple-element.95.refs_0_, bf16[32,1280]{1,0:T(8,128)(2,1)S(1)} %collective-permute-done.23.refs_1_, bf16[32,1280]{1,0:T(8,128)(2,1)S(1)} %collective-permute-done.15.refs_11_.refs_2_, ...), custom_call_target="tpu_custom_call" | custom-call | tf_op jit(solution)/shard_map/assemble/pallas_call | solution.py:491
  75.0 1.7 %collective-permute-done.19.refs_4_ = bf16[32,1280]{1,0:T(8,128)(2,1)S(1)} collective-permute-done((bf16[32,1280]{1,0:T(8,128)(2,1)S(1)}, bf16[32,1280]{1,0:T(8,128)(2,1)S(1)}, u32[]{:S(2)}, u32[]{:S(2)}) %collective-permute-start.19) | collective-permute-done | bytes 81952 | tf_op jit(solution)/shard_map/ppermute | solution.py:464
  76.7 1.6 %collective-permute-done.20.refs_5_ = bf16[32,1280]{1,0:T(8,128)(2,1)S(1)} collective-permute-done((bf16[32,1280]{1,0:T(8,128)(2,1)S(1)}, bf16[32,1280]{1,0:T(8,128)(2,1)S(1)}, u32[]{:S(2)}, u32[]{:S(2)}) %collective-permute-start.20) | collective-permute-done | bytes 81952 | tf_op jit(solution)/shard_map/ppermute | solution.py:464
  78.4 1.2 %collective-permute-done.22.refs_7_ = bf16[32,1280]{1,0:T(8,128)(2,1)S(1)} collective-permute-done((bf16[32,1280]{1,0:T(8,128)(2,1)S(1)}, bf16[32,1280]{1,0:T(8,128)(2,1)S(1)}, u32[]{:S(2)}, u32[]{:S(2)}) %collective-permute-start.22) | collective-permute-done | bytes 81952 | tf_op jit(solution)/shard_map/ppermute | solution.py:464
  79.6 1.4 %assemble.3 = bf16[8,64,1280]{2,1,0:T(8,128)(2,1)} custom-call(s32[8]{0:T(128)S(1)} %iota_xor_fusion.1.order_ref, bf16[32,1280]{1,0:T(8,128)(2,1)S(1)} %get-tuple-element.87.refs_0_, bf16[32,1280]{1,0:T(8,128)(2,1)S(1)} %collective-permute-done.16.refs_1_, bf16[32,1280]{1,0:T(8,128)(2,1)S(1)} %collective-permute-done.17.refs_2_, ...), custom_call_target="tpu_custom_call", output_to_operand_aliasing={{}: (9, {})} | custom-call | tf_op jit(solution)/shard_map/assemble/pallas_call | solution.py:491
  (42 shorter events, 6.2 us)
Async XLA Ops:
  1.2 11.4 %collective-permute-start.2 = (bf16[64,1408]{1,0:T(8,128)(2,1)S(1)}, bf16[64,1408]{1,0:T(8,128)(2,1)S(1)}, u32[]{:S(2)}, u32[]{:S(2)}) collective-permute-start(bf16[64,1408]{1,0:T(8,128)(2,1)S(1)} %get-tuple-element.99), channel_id=1, source_target_pairs={{0,24},{8,16},{16,8},{24,0},{1,25},{9,17},{17,9},{25,1},{2,26},{10... | collective-permute-start | bytes 540680 | tf_op jit(solution)/shard_map/ppermute | solution.py:337
  3.7 1.7 %collective-permute-start = (bf16[64,1408]{1,0:T(8,128)(2,1)S(1)}, bf16[64,1408]{1,0:T(8,128)(2,1)S(1)}, u32[]{:S(2)}, u32[]{:S(2)}) collective-permute-start(bf16[64,1408]{1,0:T(8,128)(2,1)S(1)} %get-tuple-element.100), channel_id=1, source_target_pairs={{0,8},{8,0},{16,24},{24,16},{1,9},{9,1},{17,25},{25,17},{2,10},{10... | collective-permute-start | bytes 540680 | tf_op jit(solution)/shard_map/ppermute | solution.py:337
  4.4 8.3 %collective-permute-start.1 = (bf16[64,1408]{1,0:T(8,128)(2,1)S(1)}, bf16[64,1408]{1,0:T(8,128)(2,1)S(1)}, u32[]{:S(2)}, u32[]{:S(2)}) collective-permute-start(bf16[64,1408]{1,0:T(8,128)(2,1)S(1)} %get-tuple-element.102), channel_id=1, source_target_pairs={{0,16},{8,24},{16,0},{24,8},{1,17},{9,25},{17,1},{25,9},{2,18},{10... | collective-permute-start | bytes 540680 | tf_op jit(solution)/shard_map/ppermute | solution.py:337
  5.4 7.3 %copy-start = (f32[3,1408,16]{1,2,0:T(8,128)S(1)}, f32[3,1408,16]{1,2,0:T(8,128)}, u32[]{:S(2)}) copy-start(f32[3,1408,16]{1,2,0:T(8,128)} %param.6) | copy-start | bytes 811012
  20.1 4.3 %collective-permute-start.3 = (bf16[128,1024]{1,0:T(8,128)(2,1)S(1)}, bf16[128,1024]{1,0:T(8,128)(2,1)S(1)}, u32[]{:S(2)}, u32[]{:S(2)}) collective-permute-start(bf16[128,1024]{1,0:T(8,128)(2,1)S(1)} %get-tuple-element.59), channel_id=1, source_target_pairs={{0,8},{8,0},{16,24},{24,16},{1,9},{9,1},{17,25},{25,17},{2,10},{10... | collective-permute-start | bytes 786440 | tf_op jit(solution)/shard_map/ppermute | solution.py:426
  24.1 6.3 %collective-permute-start.5 = (bf16[128,1536]{1,0:T(8,128)(2,1)S(1)}, bf16[128,1536]{1,0:T(8,128)(2,1)S(1)}, u32[]{:S(2)}, u32[]{:S(2)}) collective-permute-start(bf16[128,1536]{1,0:T(8,128)(2,1)S(1)} %get-tuple-element.63), channel_id=1, source_target_pairs={{0,8},{8,0},{16,24},{24,16},{1,9},{9,1},{17,25},{25,17},{2,10},{10... | collective-permute-start | bytes 1179656 | tf_op jit(solution)/shard_map/ppermute | solution.py:426
  24.4 6.3 %collective-permute-start.4 = (bf16[32,1024]{1,0:T(8,128)(2,1)S(1)}, bf16[32,1024]{1,0:T(8,128)(2,1)S(1)}, u32[]{:S(2)}, u32[]{:S(2)}) collective-permute-start(bf16[32,1024]{1,0:T(8,128)(2,1)S(1)} %add_convert_fusion.3.refs_2_), channel_id=1, source_target_pairs={{0,16},{8,24},{16,0},{24,8},{1,17},{9,25},{17,1},{25,9},{2,18},{10... | collective-permute-start | bytes 196616 | tf_op jit(solution)/shard_map/ppermute | solution.py:426
  30.4 3.2 %collective-permute-start.7 = (bf16[128,1536]{1,0:T(8,128)(2,1)S(1)}, bf16[128,1536]{1,0:T(8,128)(2,1)S(1)}, u32[]{:S(2)}, u32[]{:S(2)}) collective-permute-start(bf16[128,1536]{1,0:T(8,128)(2,1)S(1)} %get-tuple-element.67), channel_id=1, source_target_pairs={{0,8},{8,0},{16,24},{24,16},{1,9},{9,1},{17,25},{25,17},{2,10},{10... | collective-permute-start | bytes 1179656 | tf_op jit(solution)/shard_map/ppermute | solution.py:426
  30.5 6.3 %collective-permute-start.6 = (bf16[32,1536]{1,0:T(8,128)(2,1)S(1)}, bf16[32,1536]{1,0:T(8,128)(2,1)S(1)}, u32[]{:S(2)}, u32[]{:S(2)}) collective-permute-start(bf16[32,1536]{1,0:T(8,128)(2,1)S(1)} %add_convert_fusion.1.refs_3_), channel_id=1, source_target_pairs={{0,16},{8,24},{16,0},{24,8},{1,17},{9,25},{17,1},{25,9},{2,18},{10... | collective-permute-start | bytes 294920 | tf_op jit(solution)/shard_map/ppermute | solution.py:426
  33.1 2.3 %collective-permute-start.9 = (bf16[128,1024]{1,0:T(8,128)(2,1)S(1)}, bf16[128,1024]{1,0:T(8,128)(2,1)S(1)}, u32[]{:S(2)}, u32[]{:S(2)}) collective-permute-start(bf16[128,1024]{1,0:T(8,128)(2,1)S(1)} %get-tuple-element.72), channel_id=1, source_target_pairs={{0,8},{8,0},{16,24},{24,16},{1,9},{9,1},{17,25},{25,17},{2,10},{10... | collective-permute-start | bytes 786440 | tf_op jit(solution)/shard_map/ppermute | solution.py:426
  33.6 6.5 %collective-permute-start.8 = (bf16[32,1536]{1,0:T(8,128)(2,1)S(1)}, bf16[32,1536]{1,0:T(8,128)(2,1)S(1)}, u32[]{:S(2)}, u32[]{:S(2)}) collective-permute-start(bf16[32,1536]{1,0:T(8,128)(2,1)S(1)} %add_convert_fusion), channel_id=1, source_target_pairs={{0,16},{8,24},{16,0},{24,8},{1,17},{9,25},{17,1},{25,9},{2,18},{10... | collective-permute-start | bytes 294920 | tf_op jit(solution)/shard_map/ppermute | solution.py:426
  35.5 4.6 %collective-permute-start.10 = (bf16[32,1024]{1,0:T(8,128)(2,1)S(1)}, bf16[32,1024]{1,0:T(8,128)(2,1)S(1)}, u32[]{:S(2)}, u32[]{:S(2)}) collective-permute-start(bf16[32,1024]{1,0:T(8,128)(2,1)S(1)} %add_convert_fusion.2), channel_id=1, source_target_pairs={{0,16},{8,24},{16,0},{24,8},{1,17},{9,25},{17,1},{25,9},{2,18},{10... | collective-permute-start | bytes 196616 | tf_op jit(solution)/shard_map/ppermute | solution.py:426
  42.7 9.2 %collective-permute-start.11 = (bf16[32,5120]{1,0:T(8,128)(2,1)S(1)}, bf16[32,5120]{1,0:T(8,128)(2,1)S(1)}, u32[]{:S(2)}, u32[]{:S(2)}) collective-permute-start(bf16[32,5120]{1,0:T(8,128)(2,1)S(1)} %get-tuple-element.74), channel_id=1, source_target_pairs={{0,16},{8,24},{16,0},{24,8},{1,17},{9,25},{17,1},{25,9},{2,18},{10... | collective-permute-start | bytes 983048 | tf_op jit(solution)/shard_map/ppermute | solution.py:475
  44.5 13.1 %collective-permute-start.12 = (bf16[32,1280]{1,0:T(8,128)(2,1)S(1)}, bf16[32,1280]{1,0:T(8,128)(2,1)S(1)}, u32[]{:S(2)}, u32[]{:S(2)}) collective-permute-start(bf16[32,1280]{1,0:T(8,128)(2,1)S(1)} %get-tuple-element.83), channel_id=1, source_target_pairs={{0,7},{1,6},{2,5},{3,4},{4,3},{5,2},{6,1},{7,0},{8,15},{9,14},{10,... | collective-permute-start | bytes 245768 | tf_op jit(solution)/shard_map/ppermute | solution.py:464
  49.1 11.2 %collective-permute-start.13 = (bf16[32,1280]{1,0:T(8,128)(2,1)S(1)}, bf16[32,1280]{1,0:T(8,128)(2,1)S(1)}, u32[]{:S(2)}, u32[]{:S(2)}) collective-permute-start(bf16[32,1280]{1,0:T(8,128)(2,1)S(1)} %get-tuple-element.84), channel_id=1, source_target_pairs={{0,3},{1,2},{2,1},{3,0},{4,7},{5,6},{6,5},{7,4},{8,11},{9,10},{10,... | collective-permute-start | bytes 245768 | tf_op jit(solution)/shard_map/ppermute | solution.py:464
  49.1 11.3 %collective-permute-start.14 = (bf16[32,1280]{1,0:T(8,128)(2,1)S(1)}, bf16[32,1280]{1,0:T(8,128)(2,1)S(1)}, u32[]{:S(2)}, u32[]{:S(2)}) collective-permute-start(bf16[32,1280]{1,0:T(8,128)(2,1)S(1)} %get-tuple-element.85), channel_id=1, source_target_pairs={{0,6},{1,7},{2,4},{3,5},{4,2},{5,3},{6,0},{7,1},{8,14},{9,15},{10,... | collective-permute-start | bytes 245768 | tf_op jit(solution)/shard_map/ppermute | solution.py:464
  49.9 10.5 %collective-permute-start.15 = (bf16[32,1280]{1,0:T(8,128)(2,1)S(1)}, bf16[32,1280]{1,0:T(8,128)(2,1)S(1)}, u32[]{:S(2)}, u32[]{:S(2)}) collective-permute-start(bf16[32,1280]{1,0:T(8,128)(2,1)S(1)} %get-tuple-element.86), channel_id=1, source_target_pairs={{0,2},{1,3},{2,0},{3,1},{4,6},{5,7},{6,4},{7,5},{8,10},{9,11},{10,... | collective-permute-start | bytes 245768 | tf_op jit(solution)/shard_map/ppermute | solution.py:464
  51.9 11.8 %collective-permute-start.23 = (bf16[32,1280]{1,0:T(8,128)(2,1)S(1)}, bf16[32,1280]{1,0:T(8,128)(2,1)S(1)}, u32[]{:S(2)}, u32[]{:S(2)}) collective-permute-start(bf16[32,1280]{1,0:T(8,128)(2,1)S(1)} %get-tuple-element.96), channel_id=1, source_target_pairs={{0,1},{1,0},{2,3},{3,2},{4,5},{5,4},{6,7},{7,6},{8,9},{9,8},{10,11... | collective-permute-start | bytes 245768 | tf_op jit(solution)/shard_map/ppermute | solution.py:464
  57.7 8.0 %collective-permute-start.24 = (bf16[32,1280]{1,0:T(8,128)(2,1)S(1)}, bf16[32,1280]{1,0:T(8,128)(2,1)S(1)}, u32[]{:S(2)}, u32[]{:S(2)}) collective-permute-start(bf16[32,1280]{1,0:T(8,128)(2,1)S(1)} %get-tuple-element.97), channel_id=1, source_target_pairs={{0,4},{1,5},{2,6},{3,7},{4,0},{5,1},{6,2},{7,3},{8,12},{9,13},{10,... | collective-permute-start | bytes 245768 | tf_op jit(solution)/shard_map/ppermute | solution.py:464
  60.3 7.7 %collective-permute-start.25 = (bf16[32,1280]{1,0:T(8,128)(2,1)S(1)}, bf16[32,1280]{1,0:T(8,128)(2,1)S(1)}, u32[]{:S(2)}, u32[]{:S(2)}) collective-permute-start(bf16[32,1280]{1,0:T(8,128)(2,1)S(1)} %get-tuple-element.98), channel_id=1, source_target_pairs={{0,5},{1,4},{2,7},{3,6},{4,1},{5,0},{6,3},{7,2},{8,13},{9,12},{10,... | collective-permute-start | bytes 245768 | tf_op jit(solution)/shard_map/ppermute | solution.py:464
  60.4 8.7 %collective-permute-start.16 = (bf16[32,1280]{1,0:T(8,128)(2,1)S(1)}, bf16[32,1280]{1,0:T(8,128)(2,1)S(1)}, u32[]{:S(2)}, u32[]{:S(2)}) collective-permute-start(bf16[32,1280]{1,0:T(8,128)(2,1)S(1)} %get-tuple-element.88), channel_id=1, source_target_pairs={{0,1},{1,0},{2,3},{3,2},{4,5},{5,4},{6,7},{7,6},{8,9},{9,8},{10,11... | collective-permute-start | bytes 245768 | tf_op jit(solution)/shard_map/ppermute | solution.py:464
  62.2 10.1 %collective-permute-start.17 = (bf16[32,1280]{1,0:T(8,128)(2,1)S(1)}, bf16[32,1280]{1,0:T(8,128)(2,1)S(1)}, u32[]{:S(2)}, u32[]{:S(2)}) collective-permute-start(bf16[32,1280]{1,0:T(8,128)(2,1)S(1)} %get-tuple-element.89), channel_id=1, source_target_pairs={{0,2},{1,3},{2,0},{3,1},{4,6},{5,7},{6,4},{7,5},{8,10},{9,11},{10,... | collective-permute-start | bytes 245768 | tf_op jit(solution)/shard_map/ppermute | solution.py:464
  63.8 11.2 %collective-permute-start.18 = (bf16[32,1280]{1,0:T(8,128)(2,1)S(1)}, bf16[32,1280]{1,0:T(8,128)(2,1)S(1)}, u32[]{:S(2)}, u32[]{:S(2)}) collective-permute-start(bf16[32,1280]{1,0:T(8,128)(2,1)S(1)} %get-tuple-element.90), channel_id=1, source_target_pairs={{0,3},{1,2},{2,1},{3,0},{4,7},{5,6},{6,5},{7,4},{8,11},{9,10},{10,... | collective-permute-start | bytes 245768 | tf_op jit(solution)/shard_map/ppermute | solution.py:464
  65.6 11.1 %collective-permute-start.19 = (bf16[32,1280]{1,0:T(8,128)(2,1)S(1)}, bf16[32,1280]{1,0:T(8,128)(2,1)S(1)}, u32[]{:S(2)}, u32[]{:S(2)}) collective-permute-start(bf16[32,1280]{1,0:T(8,128)(2,1)S(1)} %get-tuple-element.91), channel_id=1, source_target_pairs={{0,4},{1,5},{2,6},{3,7},{4,0},{5,1},{6,2},{7,3},{8,12},{9,13},{10,... | collective-permute-start | bytes 245768 | tf_op jit(solution)/shard_map/ppermute | solution.py:464
  68.0 10.4 %collective-permute-start.20 = (bf16[32,1280]{1,0:T(8,128)(2,1)S(1)}, bf16[32,1280]{1,0:T(8,128)(2,1)S(1)}, u32[]{:S(2)}, u32[]{:S(2)}) collective-permute-start(bf16[32,1280]{1,0:T(8,128)(2,1)S(1)} %get-tuple-element.92), channel_id=1, source_target_pairs={{0,5},{1,4},{2,7},{3,6},{4,1},{5,0},{6,3},{7,2},{8,13},{9,12},{10,... | collective-permute-start | bytes 245768 | tf_op jit(solution)/shard_map/ppermute | solution.py:464
  69.2 9.2 %collective-permute-start.21 = (bf16[32,1280]{1,0:T(8,128)(2,1)S(1)}, bf16[32,1280]{1,0:T(8,128)(2,1)S(1)}, u32[]{:S(2)}, u32[]{:S(2)}) collective-permute-start(bf16[32,1280]{1,0:T(8,128)(2,1)S(1)} %get-tuple-element.93), channel_id=1, source_target_pairs={{0,6},{1,7},{2,4},{3,5},{4,2},{5,3},{6,0},{7,1},{8,14},{9,15},{10,... | collective-permute-start | bytes 245768 | tf_op jit(solution)/shard_map/ppermute | solution.py:464
  72.3 7.2 %collective-permute-start.22 = (bf16[32,1280]{1,0:T(8,128)(2,1)S(1)}, bf16[32,1280]{1,0:T(8,128)(2,1)S(1)}, u32[]{:S(2)}, u32[]{:S(2)}) collective-permute-start(bf16[32,1280]{1,0:T(8,128)(2,1)S(1)} %get-tuple-element.94), channel_id=1, source_target_pairs={{0,7},{1,6},{2,5},{3,4},{4,3},{5,2},{6,1},{7,0},{8,15},{9,14},{10,... | collective-permute-start | bytes 245768 | tf_op jit(solution)/shard_map/ppermute | solution.py:464

commit v13 on v12

--- a/solution.py
+++ b/solution.py
@@ -15,9 +15,10 @@
 COLUMNS = 512
 ROWS = 32
 CHUNKS = 4
-COPIES = (((0, 4), (1, 5)), ((1, 1), (2, 4)), (), ((2, 2), (3, 1)), ((3, 2), (3, 1)))
-PACK_FIRST = 2
-GATE = 4
+COPIES = (((0, 4), (1, 6)), ((2, 2), (2, 2)), (), ((2, 2), (3, 1)), ((3, 2), (3, 1)))
+PACKS = (0, 2, 3, 4)
+PACK_STEP = 4
+GATE = 3
 MIB = 1 << 20
 
 VMEM = functools.partial(pl.BlockSpec, memory_space=pltpu.VMEM)
@@ -308,13 +309,13 @@
 
     count = sum(widths) // VOX_BLOCK
 
-    def two(i, carry):
-        blocks([2 * i, 2 * i + 1])
+    def some(i, carry):
+        blocks([PACK_STEP * i + j for j in range(PACK_STEP)])
         return carry
 
-    lax.fori_loop(0, count // 2, two, 0)
-    if count % 2:
-        blocks([count - 1])
+    lax.fori_loop(0, count // PACK_STEP, some, 0)
+    if count % PACK_STEP:
+        blocks(range(count - count % PACK_STEP, count))
     if outs == 1:
         out_refs[0][...] = packed[...]
     else:
@@ -455,8 +456,7 @@
             name="pack",
         )(targets, starts, inner, tiles, *packed, *terms, *later)
 
-    far, near = range(owners - 1, owners // 2 - 1, -1), range(owners // 2 - 1, -1, -1)
-    turns = [d for pair in zip(far, near) for d in pair if d]
+    turns = range(owners - 1, 0, -1)
 
     def deliver(packed):
         got = list(packed)
@@ -467,11 +467,12 @@
     def early_terms(chunks):
         return [term for c in chunks for term in sums[c]], [[(0, 0)] * len(sums[c]) for c in chunks]
 
-    low, high = range(PACK_FIRST), range(PACK_FIRST, CHUNKS)
-    packed = pack(low, *early_terms(low))
-    *one, late_send, late_own = pack(
-        high, *early_terms(high), packed=packed, later=[term for own in sums for term in own[:-1]]
-    )
+    packed = []
+    for low, high in zip(PACKS, PACKS[1:]):
+        chunks = range(low, high)
+        later = [term for own in sums for term in own[:-1]] if high == CHUNKS else []
+        packed = pack(chunks, *early_terms(chunks), packed=packed, later=later)
+    *one, late_send, late_own = packed
     late = lax.ppermute(late_send, "chan", [(i, i ^ (1 << (bits - 1))) for i in range(parts)])
     one = deliver(one)
     starting = [sum(widths[:c]) for c in range(CHUNKS)]

time: 81.2 us -> 79.1 us (0.974)
  waiting for transfers between devices: 9.51 us -> 6.16 us
  starting transfers between devices: 33 us -> 34.9 us
  Pallas kernels: 36.3 us -> 35.4 us
    ppermute x14, starting transfers between devices: 21.2 us -> 23.9 us  [deliver(): got[d] = lax.ppermute(packed[d], 'vox', [(i, i ^ d) for i in range(owners)])]
    ppermute x14, waiting for transfers between devices: 7.37 us -> 4.98 us  [deliver(): got[d] = lax.ppermute(packed[d], 'vox', [(i, i ^ d) for i in range(owners)])]
    pallas_call x3 -> x4, Pallas kernels: 9.05 us -> 8.04 us  [pack(): pl.pallas_call(functools.partial(pack_kernel, spread, sizes, spots, sum(w...]
  transfers between devices with their start and end apart: 26 -> 26, of which waited for: 8 -> 7; matrix products, arithmetic and copies ran while one was open for 1% -> 1% of each run, Pallas kernels for 31% -> 33%
where the time goes in v13:
time: 79.1 us; the launch traced here: 78.9 us
  Pallas kernels  35.4 us (45%)
  starting transfers between devices  34.9 us (44%)
  waiting for transfers between devices  6.16 us (8%)
  local copies, waits for them, and re-layouts  1.94 us (2%)
    ppermute x14, starting transfers between devices, deliver(): got[d] = lax.ppermute(packed[d], 'vox', [(i, i ^ d) for i in range(owners)])  23.9 us
    pallas_call x4, Pallas kernels, product(): pl.pallas_call(functools.partial(product_kernel, len(taken), len(after),...  12.3 us
    pallas_call x4, Pallas kernels, pack(): pl.pallas_call(functools.partial(pack_kernel, spread, sizes, spots, sum(w...  8.04 us
    pallas_call x1, Pallas kernels, shards(): pl.pallas_call(functools.partial(early_kernel, owners, spread), in_specs=...  7.9 us
    ppermute x8, starting transfers between devices, shards(): lax.ppermute(send, 'chan', [(i, i ^ 1 << bit) for i in range(parts)])  6.17 us
    ppermute x14, waiting for transfers between devices, deliver(): got[d] = lax.ppermute(packed[d], 'vox', [(i, i ^ d) for i in range(owners)])  4.98 us
    pallas_call x1, Pallas kernels, shards(): pl.pallas_call(functools.partial(design_kernel, parts, firsts[1]), in_spe...  4.26 us
    ppermute x3, starting transfers between devices, shards(): lax.ppermute(series[d], 'chan', [(i, i ^ d) for i in range(parts)])  3.16 us
  transfers between devices with their start and end apart: 26, of which 7 were waited for; matrix products, arithmetic and copies ran while one was open for 1% of the time, Pallas kernels for 33%

profile of v13, /device:TPU:0, one launch (start us, length us, event | category | flops | bytes accessed | tf_op | source)
XLA Modules:
  0.0 78.9 jit_solution(8996336405523713401)
XLA Ops:
  0.0 1.2 %constant_dynamic-slice_fusion = (bf16[64,1408]{1,0:T(8,128)(2,1)S(1)}, bf16[64,1408]{1,0:T(8,128)(2,1)S(1)}, bf16[64,1408]{1,0:T(8,128)(2,1)S(1)}, bf16[64,1408]{1,0:T(8,128)(2,1)S(1)}) fusion(bf16[64,5632]{1,0:T(8,128)(2,1)} %param.5, s32[]{:T(128)S(6)} %select_n.15, s32[]{:T(128)S(6)} %select_n.13, s32[]{:T(128)S(6)} %select_n.12, s32[]{:T(128)S(6)} %select_n.14), kind=kLoop, calls=%fused_computation.5 | loop fusion | bytes 1441808 | tf_op jit(solution)/shard_map/dynamic_slice | solution.py:336
  1.2 2.4 %collective-permute-start.2 = (bf16[64,1408]{1,0:T(8,128)(2,1)S(1)}, bf16[64,1408]{1,0:T(8,128)(2,1)S(1)}, u32[]{:S(2)}, u32[]{:S(2)}) collective-permute-start(bf16[64,1408]{1,0:T(8,128)(2,1)S(1)} %get-tuple-element.99), channel_id=1, source_target_pairs={{0,24},{8,16},{16,8},{24,0},{1,25},{9,17},{17,9},{25,1},{2,26},{10... | collective-permute-start | bytes 540680 | tf_op jit(solution)/shard_map/ppermute | solution.py:338
  4.4 0.7 pad_bitcast_fusion.table_ref
  5.4 7.9 %early.1 = (s32[40,128]{1,0:T(8,128)S(1)}, s32[40,128]{1,0:T(8,128)S(1)}, s32[24,128]{1,0:T(8,128)S(1)}, bf16[96,4224]{1,0:T(8,128)(2,1)S(1)}, bf16[3,1408,1024]...) custom-call(s32[4]{0:T(128)S(1)} %get-tuple-element.104.order_ref, ...), custom_call_target="tpu_custom_call" | custom-call | bytes 21626880 | tf_op jit(solution)/shard_map/early/pallas_call | solution.py:369
  13.4 4.3 %design.1 = (bf16[256,4224]{1,0:T(8,128)(2,1)S(1)}, bf16[3,1408,512]{2,1,0:T(8,128)(2,1)S(1)}, bf16[3,1408,512]{2,1,0:T(8,128)(2,1)S(1)}) custom-call(s32[4]{0:T(128)S(1)} %get-tuple-element.104.order_ref, s32[4]{0:T(128)S(1)} %get-tuple-element.103.place_ref, bf16[96,4224]{1,0:T(8,128)(2,1)S(1)} %get-tuple-element.55.early_ref, f32[3,16,1408]{2,1,0:T(8,128)S(1)} %bitcast.6, ...), custom_call_target="tpu_custom_call" | custom-call | bytes 8650752 | tf_op jit(solution)/shard_map/design/pallas_call | solution.py:400
  17.6 2.5 %product.4 = (bf16[128,1024]{1,0:T(8,128)(2,1)S(1)}, bf16[128,1024]{1,0:T(8,128)(2,1)S(1)}) custom-call(bf16[256,4224]{1,0:T(8,128)(2,1)S(1)} %get-tuple-element.56.design_ref, bf16[3,1408,1024]{2,1,0:T(8,128)(2,1)S(1)} %get-tuple-element.57.refs_0_), custom_call_target="tpu_custom_call" | custom-call | flops 2214592512 | bytes 8650752 | tf_op jit(solution)/shard_map/product/pallas_call | solution.py:221
  20.6 3.6 %product.5 = (bf16[128,1536]{1,0:T(8,128)(2,1)S(1)}, bf16[128,1536]{1,0:T(8,128)(2,1)S(1)}, bf16[3,1408,512]{2,1,0:T(8,128)(2,1)S(1)}, bf16[3,1408,256]{2,1,0:T(8,128)(2,1)S(1)}) custom-call(bf16[256,4224]{1,0:T(8,128)(2,1)S(1)} %get-tuple-element.56.design_ref, bf16[3,1408,1536]{2,1,0:T(8,128)(2,1)S(1)} %get-tuple-element.60.refs_0_, ...), custom_call_target="tpu_custom_call" | custom-call | flops 3321888768 | bytes 12976128 | tf_op jit(solution)/shard_map/product/pallas_call | solution.py:221
  24.5 1.7 %collective-permute-start.4 = (bf16[32,1024]{1,0:T(8,128)(2,1)S(1)}, bf16[32,1024]{1,0:T(8,128)(2,1)S(1)}, u32[]{:S(2)}, u32[]{:S(2)}) collective-permute-start(bf16[32,1024]{1,0:T(8,128)(2,1)S(1)} %add_convert_fusion.3.refs_3_), channel_id=1, source_target_pairs={{0,16},{8,24},{16,0},{24,8},{1,17},{9,25},{17,1},{25,9},{2,18},{10... | collective-permute-start | bytes 196616 | tf_op jit(solution)/shard_map/ppermute | solution.py:427
  26.2 3.7 %product.6 = (bf16[128,1536]{1,0:T(8,128)(2,1)S(1)}, bf16[128,1536]{1,0:T(8,128)(2,1)S(1)}, bf16[3,1408,512]{2,1,0:T(8,128)(2,1)S(1)}, bf16[3,1408,256]{2,1,0:T(8,128)(2,1)S(1)}) custom-call(bf16[256,4224]{1,0:T(8,128)(2,1)S(1)} %get-tuple-element.56.design_ref, bf16[3,1408,512]{2,1,0:T(8,128)(2,1)S(1)} %get-tuple-element.63.refs_0_, ...), custom_call_target="tpu_custom_call" | custom-call | flops 3321888768 | bytes 12976128 | tf_op jit(solution)/shard_map/product/pallas_call | solution.py:221
  30.5 2.5 %product.7 = (bf16[128,1024]{1,0:T(8,128)(2,1)S(1)}, bf16[128,1024]{1,0:T(8,128)(2,1)S(1)}) custom-call(bf16[256,4224]{1,0:T(8,128)(2,1)S(1)} %get-tuple-element.56.design_ref, bf16[3,1408,256]{2,1,0:T(8,128)(2,1)S(1)} %get-tuple-element.68.refs_0_, bf16[3,1408,512]{2,1,0:T(8,128)(2,1)S(1)} %get-tuple-element.69.refs_1_, ...), custom_call_target="tpu_custom_call" | custom-call | flops 2214592512 | bytes 8650752 | tf_op jit(solution)/shard_map/product/pallas_call | solution.py:221
  33.2 1.7 %collective-permute-start.8 = (bf16[32,1536]{1,0:T(8,128)(2,1)S(1)}, bf16[32,1536]{1,0:T(8,128)(2,1)S(1)}, u32[]{:S(2)}, u32[]{:S(2)}) collective-permute-start(bf16[32,1536]{1,0:T(8,128)(2,1)S(1)} %add_convert_fusion), channel_id=1, source_target_pairs={{0,16},{8,24},{16,0},{24,8},{1,17},{9,25},{17,1},{25,9},{2,18},{10... | collective-permute-start | bytes 294920 | tf_op jit(solution)/shard_map/ppermute | solution.py:427
  35.0 1.3 %collective-permute-start.10 = (bf16[32,1024]{1,0:T(8,128)(2,1)S(1)}, bf16[32,1024]{1,0:T(8,128)(2,1)S(1)}, u32[]{:S(2)}, u32[]{:S(2)}) collective-permute-start(bf16[32,1024]{1,0:T(8,128)(2,1)S(1)} %add_convert_fusion.2), channel_id=1, source_target_pairs={{0,16},{8,24},{16,0},{24,8},{1,17},{9,25},{17,1},{25,9},{2,18},{10... | collective-permute-start | bytes 196616 | tf_op jit(solution)/shard_map/ppermute | solution.py:427
  36.3 2.0 %pack.4.refs_0_ = bf16[8,32,1664]{2,1,0:T(8,128)(2,1)S(1)} custom-call(s32[8]{0:T(128)S(1)} %iota_xor_fusion.1.order_ref, s32[24,128]{1,0:T(8,128)S(1)} %get-tuple-element.52.start_ref, s32[40,128]{1,0:T(8,128)S(1)} %get-tuple-element.53.inner_ref, s32[40,128]{1,0:T(8,128)S(1)} %get-tuple-element.54.tile_ref, ...), custom_call_target="tpu_custom_call" | custom-call | flops 335544320 | bytes 327680 | tf_op jit(solution)/shard_map/pack/pallas_call | solution.py:443
  38.9 1.7 %pack.5.refs_0_ = bf16[8,32,1664]{2,1,0:T(8,128)(2,1)S(1)} custom-call(s32[8]{0:T(128)S(1)} %iota_xor_fusion.1.order_ref, s32[24,128]{1,0:T(8,128)S(1)} %get-tuple-element.52.start_ref, s32[40,128]{1,0:T(8,128)S(1)} %get-tuple-element.53.inner_ref, s32[40,128]{1,0:T(8,128)S(1)} %get-tuple-element.54.tile_ref, bf16[8,32,1664]{2,1,0:T(8,128)(2,1)S(1)} %pack.4.refs_0_, ...), custom_call_target="tpu_custom_call" | custom-call | flops 201326592 | bytes 196608 | tf_op jit(solution)/shard_map/pack/pallas_call | solution.py:443
  40.6 1.4 %pack.6 = (bf16[32,1280]{1,0:T(8,128)(2,1)S(1)}, bf16[32,1280]{1,0:T(8,128)(2,1)S(1)}, bf16[32,1280]{1,0:T(8,128)(2,1)S(1)}, bf16[32,1280]{1,0:T(8,128)(2,1)S(1)...) custom-call(s32[8]{0:T(128)S(1)} %iota_xor_fusion.1.order_ref, ...), custom_call_target="tpu_custom_call" | custom-call | flops 134217728 | bytes 131072 | tf_op jit(solution)/shard_map/pack/pallas_call | solution.py:443
  42.1 1.7 %collective-permute-start.11 = (bf16[32,5120]{1,0:T(8,128)(2,1)S(1)}, bf16[32,5120]{1,0:T(8,128)(2,1)S(1)}, u32[]{:S(2)}, u32[]{:S(2)}) collective-permute-start(bf16[32,5120]{1,0:T(8,128)(2,1)S(1)} %get-tuple-element.74), channel_id=1, source_target_pairs={{0,16},{8,24},{16,0},{24,8},{1,17},{9,25},{17,1},{25,9},{2,18},{10... | collective-permute-start | bytes 983048 | tf_op jit(solution)/shard_map/ppermute | solution.py:476
  43.8 4.6 %collective-permute-start.12 = (bf16[32,1280]{1,0:T(8,128)(2,1)S(1)}, bf16[32,1280]{1,0:T(8,128)(2,1)S(1)}, u32[]{:S(2)}, u32[]{:S(2)}) collective-permute-start(bf16[32,1280]{1,0:T(8,128)(2,1)S(1)} %get-tuple-element.83), channel_id=1, source_target_pairs={{0,7},{1,6},{2,5},{3,4},{4,3},{5,2},{6,1},{7,0},{8,15},{9,14},{10,... | collective-permute-start | bytes 245768 | tf_op jit(solution)/shard_map/ppermute | solution.py:464
  48.6 0.8 collective-permute-start.14
  49.3 1.5 %collective-permute-start.22 = (bf16[32,1280]{1,0:T(8,128)(2,1)S(1)}, bf16[32,1280]{1,0:T(8,128)(2,1)S(1)}, u32[]{:S(2)}, u32[]{:S(2)}) collective-permute-start(bf16[32,1280]{1,0:T(8,128)(2,1)S(1)} %get-tuple-element.95), channel_id=1, source_target_pairs={{0,1},{1,0},{2,3},{3,2},{4,5},{5,4},{6,7},{7,6},{8,9},{9,8},{10,11... | collective-permute-start | bytes 245768 | tf_op jit(solution)/shard_map/ppermute | solution.py:464
  51.1 3.1 %collective-permute-start.23 = (bf16[32,1280]{1,0:T(8,128)(2,1)S(1)}, bf16[32,1280]{1,0:T(8,128)(2,1)S(1)}, u32[]{:S(2)}, u32[]{:S(2)}) collective-permute-start(bf16[32,1280]{1,0:T(8,128)(2,1)S(1)} %get-tuple-element.96), channel_id=1, source_target_pairs={{0,2},{1,3},{2,0},{3,1},{4,6},{5,7},{6,4},{7,5},{8,10},{9,11},{10,... | collective-permute-start | bytes 245768 | tf_op jit(solution)/shard_map/ppermute | solution.py:464
  54.2 2.9 %pack.7 = (bf16[32,1280]{1,0:T(8,128)(2,1)S(1)}, bf16[32,1280]{1,0:T(8,128)(2,1)S(1)}, bf16[32,1280]{1,0:T(8,128)(2,1)S(1)}, bf16[32,1280]{1,0:T(8,128)(2,1)S(1)...) custom-call(s32[8]{0:T(128)S(1)} %iota_xor_fusion.1.order_ref, ...), custom_call_target="tpu_custom_call" | custom-call | flops 671088640 | bytes 655360 | tf_op jit(solution)/shard_map/pack/pallas_call | solution.py:443
  57.2 2.4 %collective-permute-start.25 = (bf16[32,1280]{1,0:T(8,128)(2,1)S(1)}, bf16[32,1280]{1,0:T(8,128)(2,1)S(1)}, u32[]{:S(2)}, u32[]{:S(2)}) collective-permute-start(bf16[32,1280]{1,0:T(8,128)(2,1)S(1)} %get-tuple-element.98), channel_id=1, source_target_pairs={{0,4},{1,5},{2,6},{3,7},{4,0},{5,1},{6,2},{7,3},{8,12},{9,13},{10,... | collective-permute-start | bytes 245768 | tf_op jit(solution)/shard_map/ppermute | solution.py:464
  60.2 1.6 %collective-permute-start.16 = (bf16[32,1280]{1,0:T(8,128)(2,1)S(1)}, bf16[32,1280]{1,0:T(8,128)(2,1)S(1)}, u32[]{:S(2)}, u32[]{:S(2)}) collective-permute-start(bf16[32,1280]{1,0:T(8,128)(2,1)S(1)} %get-tuple-element.88), channel_id=1, source_target_pairs={{0,2},{1,3},{2,0},{3,1},{4,6},{5,7},{6,4},{7,5},{8,10},{9,11},{10,... | collective-permute-start | bytes 245768 | tf_op jit(solution)/shard_map/ppermute | solution.py:464
  61.8 1.4 %collective-permute-start.17 = (bf16[32,1280]{1,0:T(8,128)(2,1)S(1)}, bf16[32,1280]{1,0:T(8,128)(2,1)S(1)}, u32[]{:S(2)}, u32[]{:S(2)}) collective-permute-start(bf16[32,1280]{1,0:T(8,128)(2,1)S(1)} %get-tuple-element.89), channel_id=1, source_target_pairs={{0,3},{1,2},{2,1},{3,0},{4,7},{5,6},{6,5},{7,4},{8,11},{9,10},{10,... | collective-permute-start | bytes 245768 | tf_op jit(solution)/shard_map/ppermute | solution.py:464
  63.2 1.5 %collective-permute-done.24.refs_3_ = bf16[32,1280]{1,0:T(8,128)(2,1)S(1)} collective-permute-done((bf16[32,1280]{1,0:T(8,128)(2,1)S(1)}, bf16[32,1280]{1,0:T(8,128)(2,1)S(1)}, u32[]{:S(2)}, u32[]{:S(2)}) %collective-permute-start.24) | collective-permute-done | bytes 81952 | tf_op jit(solution)/shard_map/ppermute | solution.py:464
  64.7 1.4 %collective-permute-start.19 = (bf16[32,1280]{1,0:T(8,128)(2,1)S(1)}, bf16[32,1280]{1,0:T(8,128)(2,1)S(1)}, u32[]{:S(2)}, u32[]{:S(2)}) collective-permute-start(bf16[32,1280]{1,0:T(8,128)(2,1)S(1)} %get-tuple-element.91), channel_id=1, source_target_pairs={{0,5},{1,4},{2,7},{3,6},{4,1},{5,0},{6,3},{7,2},{8,13},{9,12},{10,... | collective-permute-start | bytes 245768 | tf_op jit(solution)/shard_map/ppermute | solution.py:464
  66.1 3.9 %collective-permute-start.20 = (bf16[32,1280]{1,0:T(8,128)(2,1)S(1)}, bf16[32,1280]{1,0:T(8,128)(2,1)S(1)}, u32[]{:S(2)}, u32[]{:S(2)}) collective-permute-start(bf16[32,1280]{1,0:T(8,128)(2,1)S(1)} %get-tuple-element.92), channel_id=1, source_target_pairs={{0,6},{1,7},{2,4},{3,5},{4,2},{5,3},{6,0},{7,1},{8,14},{9,15},{10,... | collective-permute-start | bytes 245768 | tf_op jit(solution)/shard_map/ppermute | solution.py:464
  70.1 2.3 %collective-permute-start.21 = (bf16[32,1280]{1,0:T(8,128)(2,1)S(1)}, bf16[32,1280]{1,0:T(8,128)(2,1)S(1)}, u32[]{:S(2)}, u32[]{:S(2)}) collective-permute-start(bf16[32,1280]{1,0:T(8,128)(2,1)S(1)} %get-tuple-element.93), channel_id=1, source_target_pairs={{0,7},{1,6},{2,5},{3,4},{4,3},{5,2},{6,1},{7,0},{8,15},{9,14},{10,... | collective-permute-start | bytes 245768 | tf_op jit(solution)/shard_map/ppermute | solution.py:464
  72.4 1.4 %assemble.2.refs_8_ = bf16[8,64,1280]{2,1,0:T(8,128)(2,1)} custom-call(s32[8]{0:T(128)S(1)} %iota_xor_fusion.1.order_ref, bf16[32,1280]{1,0:T(8,128)(2,1)S(1)} %get-tuple-element.94.refs_0_, bf16[32,1280]{1,0:T(8,128)(2,1)S(1)} %collective-permute-done.22.refs_1_, bf16[32,1280]{1,0:T(8,128)(2,1)S(1)} %collective-permute-done.23.refs_2_, ...), custom_call_target="tpu_custom_call" | custom-call | tf_op jit(solution)/shard_map/assemble/pallas_call | solution.py:492
  74.4 1.2 %collective-permute-done.19.refs_5_ = bf16[32,1280]{1,0:T(8,128)(2,1)S(1)} collective-permute-done((bf16[32,1280]{1,0:T(8,128)(2,1)S(1)}, bf16[32,1280]{1,0:T(8,128)(2,1)S(1)}, u32[]{:S(2)}, u32[]{:S(2)}) %collective-permute-start.19) | collective-permute-done | bytes 81952 | tf_op jit(solution)/shard_map/ppermute | solution.py:464
  75.6 1.7 %collective-permute-done.21.refs_7_ = bf16[32,1280]{1,0:T(8,128)(2,1)S(1)} collective-permute-done((bf16[32,1280]{1,0:T(8,128)(2,1)S(1)}, bf16[32,1280]{1,0:T(8,128)(2,1)S(1)}, u32[]{:S(2)}, u32[]{:S(2)}) %collective-permute-start.21) | collective-permute-done | bytes 81952 | tf_op jit(solution)/shard_map/ppermute | solution.py:464
  77.3 1.4 %assemble.3 = bf16[8,64,1280]{2,1,0:T(8,128)(2,1)} custom-call(s32[8]{0:T(128)S(1)} %iota_xor_fusion.1.order_ref, bf16[32,1280]{1,0:T(8,128)(2,1)S(1)} %get-tuple-element.86.refs_0_, bf16[32,1280]{1,0:T(8,128)(2,1)S(1)} %collective-permute-done.15.refs_1_, bf16[32,1280]{1,0:T(8,128)(2,1)S(1)} %collective-permute-done.16.refs_2_, ...), custom_call_target="tpu_custom_call", output_to_operand_aliasing={{}: (9, {})} | custom-call | tf_op jit(solution)/shard_map/assemble/pallas_call | solution.py:492
  (43 shorter events, 4.9 us)
Async XLA Ops:
  1.2 12.1 %collective-permute-start.2 = (bf16[64,1408]{1,0:T(8,128)(2,1)S(1)}, bf16[64,1408]{1,0:T(8,128)(2,1)S(1)}, u32[]{:S(2)}, u32[]{:S(2)}) collective-permute-start(bf16[64,1408]{1,0:T(8,128)(2,1)S(1)} %get-tuple-element.99), channel_id=1, source_target_pairs={{0,24},{8,16},{16,8},{24,0},{1,25},{9,17},{17,9},{25,1},{2,26},{10... | collective-permute-start | bytes 540680 | tf_op jit(solution)/shard_map/ppermute | solution.py:338
  3.7 1.7 %collective-permute-start = (bf16[64,1408]{1,0:T(8,128)(2,1)S(1)}, bf16[64,1408]{1,0:T(8,128)(2,1)S(1)}, u32[]{:S(2)}, u32[]{:S(2)}) collective-permute-start(bf16[64,1408]{1,0:T(8,128)(2,1)S(1)} %get-tuple-element.100), channel_id=1, source_target_pairs={{0,8},{8,0},{16,24},{24,16},{1,9},{9,1},{17,25},{25,17},{2,10},{10... | collective-permute-start | bytes 540680 | tf_op jit(solution)/shard_map/ppermute | solution.py:338
  4.4 9.0 %collective-permute-start.1 = (bf16[64,1408]{1,0:T(8,128)(2,1)S(1)}, bf16[64,1408]{1,0:T(8,128)(2,1)S(1)}, u32[]{:S(2)}, u32[]{:S(2)}) collective-permute-start(bf16[64,1408]{1,0:T(8,128)(2,1)S(1)} %get-tuple-element.102), channel_id=1, source_target_pairs={{0,16},{8,24},{16,0},{24,8},{1,17},{9,25},{17,1},{25,9},{2,18},{10... | collective-permute-start | bytes 540680 | tf_op jit(solution)/shard_map/ppermute | solution.py:338
  5.4 7.9 %copy-start = (f32[3,1408,16]{1,2,0:T(8,128)S(1)}, f32[3,1408,16]{1,2,0:T(8,128)}, u32[]{:S(2)}) copy-start(f32[3,1408,16]{1,2,0:T(8,128)} %param.6) | copy-start | bytes 811012
  20.2 4.3 %collective-permute-start.3 = (bf16[128,1024]{1,0:T(8,128)(2,1)S(1)}, bf16[128,1024]{1,0:T(8,128)(2,1)S(1)}, u32[]{:S(2)}, u32[]{:S(2)}) collective-permute-start(bf16[128,1024]{1,0:T(8,128)(2,1)S(1)} %get-tuple-element.59), channel_id=1, source_target_pairs={{0,8},{8,0},{16,24},{24,16},{1,9},{9,1},{17,25},{25,17},{2,10},{10... | collective-permute-start | bytes 786440 | tf_op jit(solution)/shard_map/ppermute | solution.py:427
  24.2 5.7 %collective-permute-start.5 = (bf16[128,1536]{1,0:T(8,128)(2,1)S(1)}, bf16[128,1536]{1,0:T(8,128)(2,1)S(1)}, u32[]{:S(2)}, u32[]{:S(2)}) collective-permute-start(bf16[128,1536]{1,0:T(8,128)(2,1)S(1)} %get-tuple-element.62), channel_id=1, source_target_pairs={{0,8},{8,0},{16,24},{24,16},{1,9},{9,1},{17,25},{25,17},{2,10},{10... | collective-permute-start | bytes 1179656 | tf_op jit(solution)/shard_map/ppermute | solution.py:427
  24.5 6.0 %collective-permute-start.4 = (bf16[32,1024]{1,0:T(8,128)(2,1)S(1)}, bf16[32,1024]{1,0:T(8,128)(2,1)S(1)}, u32[]{:S(2)}, u32[]{:S(2)}) collective-permute-start(bf16[32,1024]{1,0:T(8,128)(2,1)S(1)} %add_convert_fusion.3.refs_3_), channel_id=1, source_target_pairs={{0,16},{8,24},{16,0},{24,8},{1,17},{9,25},{17,1},{25,9},{2,18},{10... | collective-permute-start | bytes 196616 | tf_op jit(solution)/shard_map/ppermute | solution.py:427
  29.9 3.3 %collective-permute-start.7 = (bf16[128,1536]{1,0:T(8,128)(2,1)S(1)}, bf16[128,1536]{1,0:T(8,128)(2,1)S(1)}, u32[]{:S(2)}, u32[]{:S(2)}) collective-permute-start(bf16[128,1536]{1,0:T(8,128)(2,1)S(1)} %get-tuple-element.67), channel_id=1, source_target_pairs={{0,8},{8,0},{16,24},{24,16},{1,9},{9,1},{17,25},{25,17},{2,10},{10... | collective-permute-start | bytes 1179656 | tf_op jit(solution)/shard_map/ppermute | solution.py:427
  30.0 6.3 %collective-permute-start.6 = (bf16[32,1536]{1,0:T(8,128)(2,1)S(1)}, bf16[32,1536]{1,0:T(8,128)(2,1)S(1)}, u32[]{:S(2)}, u32[]{:S(2)}) collective-permute-start(bf16[32,1536]{1,0:T(8,128)(2,1)S(1)} %add_convert_fusion.1.refs_3_), channel_id=1, source_target_pairs={{0,16},{8,24},{16,0},{24,8},{1,17},{9,25},{17,1},{25,9},{2,18},{10... | collective-permute-start | bytes 294920 | tf_op jit(solution)/shard_map/ppermute | solution.py:427
  33.0 2.0 %collective-permute-start.9 = (bf16[128,1024]{1,0:T(8,128)(2,1)S(1)}, bf16[128,1024]{1,0:T(8,128)(2,1)S(1)}, u32[]{:S(2)}, u32[]{:S(2)}) collective-permute-start(bf16[128,1024]{1,0:T(8,128)(2,1)S(1)} %get-tuple-element.72), channel_id=1, source_target_pairs={{0,8},{8,0},{16,24},{24,16},{1,9},{9,1},{17,25},{25,17},{2,10},{10... | collective-permute-start | bytes 786440 | tf_op jit(solution)/shard_map/ppermute | solution.py:427
  33.2 5.7 %collective-permute-start.8 = (bf16[32,1536]{1,0:T(8,128)(2,1)S(1)}, bf16[32,1536]{1,0:T(8,128)(2,1)S(1)}, u32[]{:S(2)}, u32[]{:S(2)}) collective-permute-start(bf16[32,1536]{1,0:T(8,128)(2,1)S(1)} %add_convert_fusion), channel_id=1, source_target_pairs={{0,16},{8,24},{16,0},{24,8},{1,17},{9,25},{17,1},{25,9},{2,18},{10... | collective-permute-start | bytes 294920 | tf_op jit(solution)/shard_map/ppermute | solution.py:427
  35.0 5.6 %collective-permute-start.10 = (bf16[32,1024]{1,0:T(8,128)(2,1)S(1)}, bf16[32,1024]{1,0:T(8,128)(2,1)S(1)}, u32[]{:S(2)}, u32[]{:S(2)}) collective-permute-start(bf16[32,1024]{1,0:T(8,128)(2,1)S(1)} %add_convert_fusion.2), channel_id=1, source_target_pairs={{0,16},{8,24},{16,0},{24,8},{1,17},{9,25},{17,1},{25,9},{2,18},{10... | collective-permute-start | bytes 196616 | tf_op jit(solution)/shard_map/ppermute | solution.py:427
  42.1 9.0 %collective-permute-start.11 = (bf16[32,5120]{1,0:T(8,128)(2,1)S(1)}, bf16[32,5120]{1,0:T(8,128)(2,1)S(1)}, u32[]{:S(2)}, u32[]{:S(2)}) collective-permute-start(bf16[32,5120]{1,0:T(8,128)(2,1)S(1)} %get-tuple-element.74), channel_id=1, source_target_pairs={{0,16},{8,24},{16,0},{24,8},{1,17},{9,25},{17,1},{25,9},{2,18},{10... | collective-permute-start | bytes 983048 | tf_op jit(solution)/shard_map/ppermute | solution.py:476
  43.8 13.3 %collective-permute-start.12 = (bf16[32,1280]{1,0:T(8,128)(2,1)S(1)}, bf16[32,1280]{1,0:T(8,128)(2,1)S(1)}, u32[]{:S(2)}, u32[]{:S(2)}) collective-permute-start(bf16[32,1280]{1,0:T(8,128)(2,1)S(1)} %get-tuple-element.83), channel_id=1, source_target_pairs={{0,7},{1,6},{2,5},{3,4},{4,3},{5,2},{6,1},{7,0},{8,15},{9,14},{10,... | collective-permute-start | bytes 245768 | tf_op jit(solution)/shard_map/ppermute | solution.py:464
  48.3 8.9 %collective-permute-start.13 = (bf16[32,1280]{1,0:T(8,128)(2,1)S(1)}, bf16[32,1280]{1,0:T(8,128)(2,1)S(1)}, u32[]{:S(2)}, u32[]{:S(2)}) collective-permute-start(bf16[32,1280]{1,0:T(8,128)(2,1)S(1)} %get-tuple-element.84), channel_id=1, source_target_pairs={{0,6},{1,7},{2,4},{3,5},{4,2},{5,3},{6,0},{7,1},{8,14},{9,15},{10,... | collective-permute-start | bytes 245768 | tf_op jit(solution)/shard_map/ppermute | solution.py:464
  48.6 11.1 %collective-permute-start.14 = (bf16[32,1280]{1,0:T(8,128)(2,1)S(1)}, bf16[32,1280]{1,0:T(8,128)(2,1)S(1)}, u32[]{:S(2)}, u32[]{:S(2)}) collective-permute-start(bf16[32,1280]{1,0:T(8,128)(2,1)S(1)} %get-tuple-element.85), channel_id=1, source_target_pairs={{0,5},{1,4},{2,7},{3,6},{4,1},{5,0},{6,3},{7,2},{8,13},{9,12},{10,... | collective-permute-start | bytes 245768 | tf_op jit(solution)/shard_map/ppermute | solution.py:464
  49.3 10.9 %collective-permute-start.22 = (bf16[32,1280]{1,0:T(8,128)(2,1)S(1)}, bf16[32,1280]{1,0:T(8,128)(2,1)S(1)}, u32[]{:S(2)}, u32[]{:S(2)}) collective-permute-start(bf16[32,1280]{1,0:T(8,128)(2,1)S(1)} %get-tuple-element.95), channel_id=1, source_target_pairs={{0,1},{1,0},{2,3},{3,2},{4,5},{5,4},{6,7},{7,6},{8,9},{9,8},{10,11... | collective-permute-start | bytes 245768 | tf_op jit(solution)/shard_map/ppermute | solution.py:464
  51.1 10.8 %collective-permute-start.23 = (bf16[32,1280]{1,0:T(8,128)(2,1)S(1)}, bf16[32,1280]{1,0:T(8,128)(2,1)S(1)}, u32[]{:S(2)}, u32[]{:S(2)}) collective-permute-start(bf16[32,1280]{1,0:T(8,128)(2,1)S(1)} %get-tuple-element.96), channel_id=1, source_target_pairs={{0,2},{1,3},{2,0},{3,1},{4,6},{5,7},{6,4},{7,5},{8,10},{9,11},{10,... | collective-permute-start | bytes 245768 | tf_op jit(solution)/shard_map/ppermute | solution.py:464
  57.1 7.6 %collective-permute-start.24 = (bf16[32,1280]{1,0:T(8,128)(2,1)S(1)}, bf16[32,1280]{1,0:T(8,128)(2,1)S(1)}, u32[]{:S(2)}, u32[]{:S(2)}) collective-permute-start(bf16[32,1280]{1,0:T(8,128)(2,1)S(1)} %get-tuple-element.97), channel_id=1, source_target_pairs={{0,3},{1,2},{2,1},{3,0},{4,7},{5,6},{6,5},{7,4},{8,11},{9,10},{10,... | collective-permute-start | bytes 245768 | tf_op jit(solution)/shard_map/ppermute | solution.py:464
  57.2 7.5 %collective-permute-start.25 = (bf16[32,1280]{1,0:T(8,128)(2,1)S(1)}, bf16[32,1280]{1,0:T(8,128)(2,1)S(1)}, u32[]{:S(2)}, u32[]{:S(2)}) collective-permute-start(bf16[32,1280]{1,0:T(8,128)(2,1)S(1)} %get-tuple-element.98), channel_id=1, source_target_pairs={{0,4},{1,5},{2,6},{3,7},{4,0},{5,1},{6,2},{7,3},{8,12},{9,13},{10,... | collective-permute-start | bytes 245768 | tf_op jit(solution)/shard_map/ppermute | solution.py:464
  59.7 6.4 %collective-permute-start.15 = (bf16[32,1280]{1,0:T(8,128)(2,1)S(1)}, bf16[32,1280]{1,0:T(8,128)(2,1)S(1)}, u32[]{:S(2)}, u32[]{:S(2)}) collective-permute-start(bf16[32,1280]{1,0:T(8,128)(2,1)S(1)} %get-tuple-element.87), channel_id=1, source_target_pairs={{0,1},{1,0},{2,3},{3,2},{4,5},{5,4},{6,7},{7,6},{8,9},{9,8},{10,11... | collective-permute-start | bytes 245768 | tf_op jit(solution)/shard_map/ppermute | solution.py:464
  60.2 9.8 %collective-permute-start.16 = (bf16[32,1280]{1,0:T(8,128)(2,1)S(1)}, bf16[32,1280]{1,0:T(8,128)(2,1)S(1)}, u32[]{:S(2)}, u32[]{:S(2)}) collective-permute-start(bf16[32,1280]{1,0:T(8,128)(2,1)S(1)} %get-tuple-element.88), channel_id=1, source_target_pairs={{0,2},{1,3},{2,0},{3,1},{4,6},{5,7},{6,4},{7,5},{8,10},{9,11},{10,... | collective-permute-start | bytes 245768 | tf_op jit(solution)/shard_map/ppermute | solution.py:464
  61.8 12.0 %collective-permute-start.17 = (bf16[32,1280]{1,0:T(8,128)(2,1)S(1)}, bf16[32,1280]{1,0:T(8,128)(2,1)S(1)}, u32[]{:S(2)}, u32[]{:S(2)}) collective-permute-start(bf16[32,1280]{1,0:T(8,128)(2,1)S(1)} %get-tuple-element.89), channel_id=1, source_target_pairs={{0,3},{1,2},{2,1},{3,0},{4,7},{5,6},{6,5},{7,4},{8,11},{9,10},{10,... | collective-permute-start | bytes 245768 | tf_op jit(solution)/shard_map/ppermute | solution.py:464
  64.7 9.7 %collective-permute-start.18 = (bf16[32,1280]{1,0:T(8,128)(2,1)S(1)}, bf16[32,1280]{1,0:T(8,128)(2,1)S(1)}, u32[]{:S(2)}, u32[]{:S(2)}) collective-permute-start(bf16[32,1280]{1,0:T(8,128)(2,1)S(1)} %get-tuple-element.90), channel_id=1, source_target_pairs={{0,4},{1,5},{2,6},{3,7},{4,0},{5,1},{6,2},{7,3},{8,12},{9,13},{10,... | collective-permute-start | bytes 245768 | tf_op jit(solution)/shard_map/ppermute | solution.py:464
  64.7 10.9 %collective-permute-start.19 = (bf16[32,1280]{1,0:T(8,128)(2,1)S(1)}, bf16[32,1280]{1,0:T(8,128)(2,1)S(1)}, u32[]{:S(2)}, u32[]{:S(2)}) collective-permute-start(bf16[32,1280]{1,0:T(8,128)(2,1)S(1)} %get-tuple-element.91), channel_id=1, source_target_pairs={{0,5},{1,4},{2,7},{3,6},{4,1},{5,0},{6,3},{7,2},{8,13},{9,12},{10,... | collective-permute-start | bytes 245768 | tf_op jit(solution)/shard_map/ppermute | solution.py:464
  66.1 9.5 %collective-permute-start.20 = (bf16[32,1280]{1,0:T(8,128)(2,1)S(1)}, bf16[32,1280]{1,0:T(8,128)(2,1)S(1)}, u32[]{:S(2)}, u32[]{:S(2)}) collective-permute-start(bf16[32,1280]{1,0:T(8,128)(2,1)S(1)} %get-tuple-element.92), channel_id=1, source_target_pairs={{0,6},{1,7},{2,4},{3,5},{4,2},{5,3},{6,0},{7,1},{8,14},{9,15},{10,... | collective-permute-start | bytes 245768 | tf_op jit(solution)/shard_map/ppermute | solution.py:464
  70.1 7.2 %collective-permute-start.21 = (bf16[32,1280]{1,0:T(8,128)(2,1)S(1)}, bf16[32,1280]{1,0:T(8,128)(2,1)S(1)}, u32[]{:S(2)}, u32[]{:S(2)}) collective-permute-start(bf16[32,1280]{1,0:T(8,128)(2,1)S(1)} %get-tuple-element.93), channel_id=1, source_target_pairs={{0,7},{1,6},{2,5},{3,4},{4,3},{5,2},{6,1},{7,0},{8,15},{9,14},{10,... | collective-permute-start | bytes 245768 | tf_op jit(solution)/shard_map/ppermute | solution.py:464

commit v14 on v13

--- a/solution.py
+++ b/solution.py
@@ -487,18 +487,21 @@
     )(*two, *(one[d] for d in turns[:GATE]))
     two = deliver(two)
     owned = None
-    for first, got in ((0, one), (half, two)):
+    everyone = [*turns, 0]
+    middle = owners // 2
+    for first, got, which in ((0, one, everyone), (half, two, [0, *turns[: middle - 1]]), (half, two, turns[middle - 1 :])):
         given = [] if owned is None else [owned]
+        count = len(which)
         owned = pl.pallas_call(
-            functools.partial(assemble_kernel, owners, first),
-            in_specs=[SMEM()] + [VMEM()] * owners + [HBM()] * len(given),
+            functools.partial(assemble_kernel, tuple(which), first),
+            in_specs=[SMEM()] + [VMEM()] * count + [HBM()] * len(given),
             out_specs=HBM(),
             out_shape=jax.ShapeDtypeStruct((owners, time_block, send_cap), jnp.bfloat16),
-            scratch_shapes=[pltpu.SemaphoreType.DMA((owners,))],
-            input_output_aliases={1 + owners: 0} if given else {},
+            scratch_shapes=[pltpu.SemaphoreType.DMA((count,))],
+            input_output_aliases={1 + count: 0} if given else {},
             compiler_params=pltpu.CompilerParams(vmem_limit_bytes=4 * MIB),
             name="assemble",
-        )(targets, *got, *given)
+        )(targets, *(got[d] for d in which), *given)
     return jnp.transpose(owned, (0, 2, 1))
 
 
@@ -508,12 +511,12 @@
         out[...] = given[...]
 
 
-def assemble_kernel(owners, first, order_ref, *refs):
-    parts, (out_ref, sems) = refs[:owners], refs[-2:]
+def assemble_kernel(which, first, order_ref, *refs):
+    parts, (out_ref, sems) = refs[: len(which)], refs[-2:]
     copies = []
-    for i, ref in enumerate(parts):
+    for i, (d, ref) in enumerate(zip(which, parts)):
         rows = pl.ds(first, ref.shape[0])
-        copies.append(pltpu.make_async_copy(ref, out_ref.at[order_ref[i], rows, :], sems.at[i]))
+        copies.append(pltpu.make_async_copy(ref, out_ref.at[order_ref[d], rows, :], sems.at[i]))
         copies[-1].start()
     wait_all(copies)
 

time: 79.1 us -> 79 us (level)
  Pallas kernels: 35.4 us -> 36.6 us
  starting transfers between devices: 34.9 us -> 33.8 us
    pallas_call x2 -> x3, Pallas kernels: 2.87 us -> 4.03 us  [shards(): pl.pallas_call(functools.partial(assemble_kernel, tuple(which), first), i...]
    ppermute x14, starting transfers between devices: 23.9 us -> 22.8 us  [deliver(): got[d] = lax.ppermute(packed[d], 'vox', [(i, i ^ d) for i in range(owners)])]
  transfers between devices with their start and end apart: 26 -> 26, of which waited for: 7 -> 5; matrix products, arithmetic and copies ran while one was open for 1% -> 1% of each run, Pallas kernels for 33% -> 34%
where the time goes in v14:
time: 79 us; the launch traced here: 78.9 us
  Pallas kernels  36.6 us (46%)
  starting transfers between devices  33.8 us (43%)
  waiting for transfers between devices  6.02 us (8%)
  local copies, waits for them, and re-layouts  1.94 us (2%)
    ppermute x14, starting transfers between devices, deliver(): got[d] = lax.ppermute(packed[d], 'vox', [(i, i ^ d) for i in range(owners)])  22.8 us
    pallas_call x4, Pallas kernels, product(): pl.pallas_call(functools.partial(product_kernel, len(taken), len(after),...  12.3 us
    pallas_call x4, Pallas kernels, pack(): pl.pallas_call(functools.partial(pack_kernel, spread, sizes, spots, sum(w...  8.06 us
    pallas_call x1, Pallas kernels, shards(): pl.pallas_call(functools.partial(early_kernel, owners, spread), in_specs=...  7.9 us
    ppermute x8, starting transfers between devices, shards(): lax.ppermute(send, 'chan', [(i, i ^ 1 << bit) for i in range(parts)])  6.17 us
    ppermute x14, waiting for transfers between devices, deliver(): got[d] = lax.ppermute(packed[d], 'vox', [(i, i ^ d) for i in range(owners)])  5.07 us
    pallas_call x1, Pallas kernels, shards(): pl.pallas_call(functools.partial(design_kernel, parts, firsts[1]), in_spe...  4.26 us
    pallas_call x3, Pallas kernels, shards(): pl.pallas_call(functools.partial(assemble_kernel, tuple(which), first), i...  4.03 us
  transfers between devices with their start and end apart: 26, of which 5 were waited for; matrix products, arithmetic and copies ran while one was open for 1% of the time, Pallas kernels for 34%

profile of v14, /device:TPU:0, one launch (start us, length us, event | category | flops | bytes accessed | tf_op | source)
XLA Modules:
  0.0 78.9 jit_solution(16014183984018620769)
XLA Ops:
  0.0 1.2 %constant_dynamic-slice_fusion = (bf16[64,1408]{1,0:T(8,128)(2,1)S(1)}, bf16[64,1408]{1,0:T(8,128)(2,1)S(1)}, bf16[64,1408]{1,0:T(8,128)(2,1)S(1)}, bf16[64,1408]{1,0:T(8,128)(2,1)S(1)}) fusion(bf16[64,5632]{1,0:T(8,128)(2,1)} %param.5, s32[]{:T(128)S(6)} %select_n.15, s32[]{:T(128)S(6)} %select_n.13, s32[]{:T(128)S(6)} %select_n.12, s32[]{:T(128)S(6)} %select_n.14), kind=kLoop, calls=%fused_computation.5 | loop fusion | bytes 1441808 | tf_op jit(solution)/shard_map/dynamic_slice | solution.py:336
  1.2 2.4 %collective-permute-start.2 = (bf16[64,1408]{1,0:T(8,128)(2,1)S(1)}, bf16[64,1408]{1,0:T(8,128)(2,1)S(1)}, u32[]{:S(2)}, u32[]{:S(2)}) collective-permute-start(bf16[64,1408]{1,0:T(8,128)(2,1)S(1)} %get-tuple-element.99), channel_id=1, source_target_pairs={{0,24},{8,16},{16,8},{24,0},{1,25},{9,17},{17,9},{25,1},{2,26},{10... | collective-permute-start | bytes 540680 | tf_op jit(solution)/shard_map/ppermute | solution.py:338
  4.4 0.7 pad_bitcast_fusion.table_ref
  5.4 7.9 %early.1 = (s32[40,128]{1,0:T(8,128)S(1)}, s32[40,128]{1,0:T(8,128)S(1)}, s32[24,128]{1,0:T(8,128)S(1)}, bf16[96,4224]{1,0:T(8,128)(2,1)S(1)}, bf16[3,1408,1024]...) custom-call(s32[4]{0:T(128)S(1)} %get-tuple-element.104.order_ref, ...), custom_call_target="tpu_custom_call" | custom-call | bytes 21626880 | tf_op jit(solution)/shard_map/early/pallas_call | solution.py:369
  13.4 4.3 %design.1 = (bf16[256,4224]{1,0:T(8,128)(2,1)S(1)}, bf16[3,1408,512]{2,1,0:T(8,128)(2,1)S(1)}, bf16[3,1408,512]{2,1,0:T(8,128)(2,1)S(1)}) custom-call(s32[4]{0:T(128)S(1)} %get-tuple-element.104.order_ref, s32[4]{0:T(128)S(1)} %get-tuple-element.103.place_ref, bf16[96,4224]{1,0:T(8,128)(2,1)S(1)} %get-tuple-element.55.early_ref, f32[3,16,1408]{2,1,0:T(8,128)S(1)} %bitcast.6, ...), custom_call_target="tpu_custom_call" | custom-call | bytes 8650752 | tf_op jit(solution)/shard_map/design/pallas_call | solution.py:400
  17.6 2.5 %product.4 = (bf16[128,1024]{1,0:T(8,128)(2,1)S(1)}, bf16[128,1024]{1,0:T(8,128)(2,1)S(1)}) custom-call(bf16[256,4224]{1,0:T(8,128)(2,1)S(1)} %get-tuple-element.56.design_ref, bf16[3,1408,1024]{2,1,0:T(8,128)(2,1)S(1)} %get-tuple-element.57.refs_0_), custom_call_target="tpu_custom_call" | custom-call | flops 2214592512 | bytes 8650752 | tf_op jit(solution)/shard_map/product/pallas_call | solution.py:221
  20.6 3.6 %product.5 = (bf16[128,1536]{1,0:T(8,128)(2,1)S(1)}, bf16[128,1536]{1,0:T(8,128)(2,1)S(1)}, bf16[3,1408,512]{2,1,0:T(8,128)(2,1)S(1)}, bf16[3,1408,256]{2,1,0:T(8,128)(2,1)S(1)}) custom-call(bf16[256,4224]{1,0:T(8,128)(2,1)S(1)} %get-tuple-element.56.design_ref, bf16[3,1408,1536]{2,1,0:T(8,128)(2,1)S(1)} %get-tuple-element.60.refs_0_, ...), custom_call_target="tpu_custom_call" | custom-call | flops 3321888768 | bytes 12976128 | tf_op jit(solution)/shard_map/product/pallas_call | solution.py:221
  24.5 1.7 %collective-permute-start.4 = (bf16[32,1024]{1,0:T(8,128)(2,1)S(1)}, bf16[32,1024]{1,0:T(8,128)(2,1)S(1)}, u32[]{:S(2)}, u32[]{:S(2)}) collective-permute-start(bf16[32,1024]{1,0:T(8,128)(2,1)S(1)} %add_convert_fusion.3.refs_3_), channel_id=1, source_target_pairs={{0,16},{8,24},{16,0},{24,8},{1,17},{9,25},{17,1},{25,9},{2,18},{10... | collective-permute-start | bytes 196616 | tf_op jit(solution)/shard_map/ppermute | solution.py:427
  26.2 3.7 %product.6 = (bf16[128,1536]{1,0:T(8,128)(2,1)S(1)}, bf16[128,1536]{1,0:T(8,128)(2,1)S(1)}, bf16[3,1408,512]{2,1,0:T(8,128)(2,1)S(1)}, bf16[3,1408,256]{2,1,0:T(8,128)(2,1)S(1)}) custom-call(bf16[256,4224]{1,0:T(8,128)(2,1)S(1)} %get-tuple-element.56.design_ref, bf16[3,1408,512]{2,1,0:T(8,128)(2,1)S(1)} %get-tuple-element.63.refs_0_, ...), custom_call_target="tpu_custom_call" | custom-call | flops 3321888768 | bytes 12976128 | tf_op jit(solution)/shard_map/product/pallas_call | solution.py:221
  30.5 2.5 %product.7 = (bf16[128,1024]{1,0:T(8,128)(2,1)S(1)}, bf16[128,1024]{1,0:T(8,128)(2,1)S(1)}) custom-call(bf16[256,4224]{1,0:T(8,128)(2,1)S(1)} %get-tuple-element.56.design_ref, bf16[3,1408,256]{2,1,0:T(8,128)(2,1)S(1)} %get-tuple-element.68.refs_0_, bf16[3,1408,512]{2,1,0:T(8,128)(2,1)S(1)} %get-tuple-element.69.refs_1_, ...), custom_call_target="tpu_custom_call" | custom-call | flops 2214592512 | bytes 8650752 | tf_op jit(solution)/shard_map/product/pallas_call | solution.py:221
  33.2 1.7 %collective-permute-start.8 = (bf16[32,1536]{1,0:T(8,128)(2,1)S(1)}, bf16[32,1536]{1,0:T(8,128)(2,1)S(1)}, u32[]{:S(2)}, u32[]{:S(2)}) collective-permute-start(bf16[32,1536]{1,0:T(8,128)(2,1)S(1)} %add_convert_fusion), channel_id=1, source_target_pairs={{0,16},{8,24},{16,0},{24,8},{1,17},{9,25},{17,1},{25,9},{2,18},{10... | collective-permute-start | bytes 294920 | tf_op jit(solution)/shard_map/ppermute | solution.py:427
  35.0 1.3 %collective-permute-start.10 = (bf16[32,1024]{1,0:T(8,128)(2,1)S(1)}, bf16[32,1024]{1,0:T(8,128)(2,1)S(1)}, u32[]{:S(2)}, u32[]{:S(2)}) collective-permute-start(bf16[32,1024]{1,0:T(8,128)(2,1)S(1)} %add_convert_fusion.2), channel_id=1, source_target_pairs={{0,16},{8,24},{16,0},{24,8},{1,17},{9,25},{17,1},{25,9},{2,18},{10... | collective-permute-start | bytes 196616 | tf_op jit(solution)/shard_map/ppermute | solution.py:427
  36.3 2.0 %pack.4.refs_0_ = bf16[8,32,1664]{2,1,0:T(8,128)(2,1)S(1)} custom-call(s32[8]{0:T(128)S(1)} %iota_xor_fusion.1.order_ref, s32[24,128]{1,0:T(8,128)S(1)} %get-tuple-element.52.start_ref, s32[40,128]{1,0:T(8,128)S(1)} %get-tuple-element.53.inner_ref, s32[40,128]{1,0:T(8,128)S(1)} %get-tuple-element.54.tile_ref, ...), custom_call_target="tpu_custom_call" | custom-call | flops 335544320 | bytes 327680 | tf_op jit(solution)/shard_map/pack/pallas_call | solution.py:443
  38.9 1.7 %pack.5.refs_0_ = bf16[8,32,1664]{2,1,0:T(8,128)(2,1)S(1)} custom-call(s32[8]{0:T(128)S(1)} %iota_xor_fusion.1.order_ref, s32[24,128]{1,0:T(8,128)S(1)} %get-tuple-element.52.start_ref, s32[40,128]{1,0:T(8,128)S(1)} %get-tuple-element.53.inner_ref, s32[40,128]{1,0:T(8,128)S(1)} %get-tuple-element.54.tile_ref, bf16[8,32,1664]{2,1,0:T(8,128)(2,1)S(1)} %pack.4.refs_0_, ...), custom_call_target="tpu_custom_call" | custom-call | flops 201326592 | bytes 196608 | tf_op jit(solution)/shard_map/pack/pallas_call | solution.py:443
  40.6 1.4 %pack.6 = (bf16[32,1280]{1,0:T(8,128)(2,1)S(1)}, bf16[32,1280]{1,0:T(8,128)(2,1)S(1)}, bf16[32,1280]{1,0:T(8,128)(2,1)S(1)}, bf16[32,1280]{1,0:T(8,128)(2,1)S(1)...) custom-call(s32[8]{0:T(128)S(1)} %iota_xor_fusion.1.order_ref, ...), custom_call_target="tpu_custom_call" | custom-call | flops 134217728 | bytes 131072 | tf_op jit(solution)/shard_map/pack/pallas_call | solution.py:443
  42.1 1.7 %collective-permute-start.11 = (bf16[32,5120]{1,0:T(8,128)(2,1)S(1)}, bf16[32,5120]{1,0:T(8,128)(2,1)S(1)}, u32[]{:S(2)}, u32[]{:S(2)}) collective-permute-start(bf16[32,5120]{1,0:T(8,128)(2,1)S(1)} %get-tuple-element.74), channel_id=1, source_target_pairs={{0,16},{8,24},{16,0},{24,8},{1,17},{9,25},{17,1},{25,9},{2,18},{10... | collective-permute-start | bytes 983048 | tf_op jit(solution)/shard_map/ppermute | solution.py:476
  43.8 4.6 %collective-permute-start.12 = (bf16[32,1280]{1,0:T(8,128)(2,1)S(1)}, bf16[32,1280]{1,0:T(8,128)(2,1)S(1)}, u32[]{:S(2)}, u32[]{:S(2)}) collective-permute-start(bf16[32,1280]{1,0:T(8,128)(2,1)S(1)} %get-tuple-element.83), channel_id=1, source_target_pairs={{0,7},{1,6},{2,5},{3,4},{4,3},{5,2},{6,1},{7,0},{8,15},{9,14},{10,... | collective-permute-start | bytes 245768 | tf_op jit(solution)/shard_map/ppermute | solution.py:464
  48.6 0.7 collective-permute-start.14
  49.3 2.1 %collective-permute-start.22 = (bf16[32,1280]{1,0:T(8,128)(2,1)S(1)}, bf16[32,1280]{1,0:T(8,128)(2,1)S(1)}, u32[]{:S(2)}, u32[]{:S(2)}) collective-permute-start(bf16[32,1280]{1,0:T(8,128)(2,1)S(1)} %get-tuple-element.94), channel_id=1, source_target_pairs={{0,4},{1,5},{2,6},{3,7},{4,0},{5,1},{6,2},{7,3},{8,12},{9,13},{10,... | collective-permute-start | bytes 245768 | tf_op jit(solution)/shard_map/ppermute | solution.py:464
  51.4 2.2 %collective-permute-start.23 = (bf16[32,1280]{1,0:T(8,128)(2,1)S(1)}, bf16[32,1280]{1,0:T(8,128)(2,1)S(1)}, u32[]{:S(2)}, u32[]{:S(2)}) collective-permute-start(bf16[32,1280]{1,0:T(8,128)(2,1)S(1)} %get-tuple-element.95), channel_id=1, source_target_pairs={{0,3},{1,2},{2,1},{3,0},{4,7},{5,6},{6,5},{7,4},{8,11},{9,10},{10,... | collective-permute-start | bytes 245768 | tf_op jit(solution)/shard_map/ppermute | solution.py:464
  53.6 2.9 %pack.7 = (bf16[32,1280]{1,0:T(8,128)(2,1)S(1)}, bf16[32,1280]{1,0:T(8,128)(2,1)S(1)}, bf16[32,1280]{1,0:T(8,128)(2,1)S(1)}, bf16[32,1280]{1,0:T(8,128)(2,1)S(1)...) custom-call(s32[8]{0:T(128)S(1)} %iota_xor_fusion.1.order_ref, ...), custom_call_target="tpu_custom_call" | custom-call | flops 671088640 | bytes 655360 | tf_op jit(solution)/shard_map/pack/pallas_call | solution.py:443
  56.6 0.8 %collective-permute-start.24 = (bf16[32,1280]{1,0:T(8,128)(2,1)S(1)}, bf16[32,1280]{1,0:T(8,128)(2,1)S(1)}, u32[]{:S(2)}, u32[]{:S(2)}) collective-permute-start(bf16[32,1280]{1,0:T(8,128)(2,1)S(1)} %get-tuple-element.96), channel_id=1, source_target_pairs={{0,2},{1,3},{2,0},{3,1},{4,6},{5,7},{6,4},{7,5},{8,10},{9,11},{10,... | collective-permute-start | bytes 245768 | tf_op jit(solution)/shard_map/ppermute | solution.py:464
  57.9 2.2 %collective-permute-done.14.refs_10_.refs_2_ = bf16[32,1280]{1,0:T(8,128)(2,1)S(1)} collective-permute-done((bf16[32,1280]{1,0:T(8,128)(2,1)S(1)}, bf16[32,1280]{1,0:T(8,128)(2,1)S(1)}, u32[]{:S(2)}, u32[]{:S(2)}) %collective-permute-start.14) | collective-permute-done | bytes 81952 | tf_op jit(solution)/shard_map/ppermute | solution.py:464
  60.1 4.2 %collective-permute-start.19 = (bf16[32,1280]{1,0:T(8,128)(2,1)S(1)}, bf16[32,1280]{1,0:T(8,128)(2,1)S(1)}, u32[]{:S(2)}, u32[]{:S(2)}) collective-permute-start(bf16[32,1280]{1,0:T(8,128)(2,1)S(1)} %get-tuple-element.91), channel_id=1, source_target_pairs={{0,7},{1,6},{2,5},{3,4},{4,3},{5,2},{6,1},{7,0},{8,15},{9,14},{10,... | collective-permute-start | bytes 245768 | tf_op jit(solution)/shard_map/ppermute | solution.py:464
  64.4 0.9 %collective-permute-start.20 = (bf16[32,1280]{1,0:T(8,128)(2,1)S(1)}, bf16[32,1280]{1,0:T(8,128)(2,1)S(1)}, u32[]{:S(2)}, u32[]{:S(2)}) collective-permute-start(bf16[32,1280]{1,0:T(8,128)(2,1)S(1)} %get-tuple-element.92), channel_id=1, source_target_pairs={{0,6},{1,7},{2,4},{3,5},{4,2},{5,3},{6,0},{7,1},{8,14},{9,15},{10,... | collective-permute-start | bytes 245768 | tf_op jit(solution)/shard_map/ppermute | solution.py:464
  65.3 3.4 %collective-permute-start.16 = (bf16[32,1280]{1,0:T(8,128)(2,1)S(1)}, bf16[32,1280]{1,0:T(8,128)(2,1)S(1)}, u32[]{:S(2)}, u32[]{:S(2)}) collective-permute-start(bf16[32,1280]{1,0:T(8,128)(2,1)S(1)} %get-tuple-element.87), channel_id=1, source_target_pairs={{0,3},{1,2},{2,1},{3,0},{4,7},{5,6},{6,5},{7,4},{8,11},{9,10},{10,... | collective-permute-start | bytes 245768 | tf_op jit(solution)/shard_map/ppermute | solution.py:464
  68.7 1.0 %collective-permute-start.21 = (bf16[32,1280]{1,0:T(8,128)(2,1)S(1)}, bf16[32,1280]{1,0:T(8,128)(2,1)S(1)}, u32[]{:S(2)}, u32[]{:S(2)}) collective-permute-start(bf16[32,1280]{1,0:T(8,128)(2,1)S(1)} %get-tuple-element.93), channel_id=1, source_target_pairs={{0,5},{1,4},{2,7},{3,6},{4,1},{5,0},{6,3},{7,2},{8,13},{9,12},{10,... | collective-permute-start | bytes 245768 | tf_op jit(solution)/shard_map/ppermute | solution.py:464
  69.7 1.4 %collective-permute-start.17 = (bf16[32,1280]{1,0:T(8,128)(2,1)S(1)}, bf16[32,1280]{1,0:T(8,128)(2,1)S(1)}, u32[]{:S(2)}, u32[]{:S(2)}) collective-permute-start(bf16[32,1280]{1,0:T(8,128)(2,1)S(1)} %get-tuple-element.88), channel_id=1, source_target_pairs={{0,2},{1,3},{2,0},{3,1},{4,6},{5,7},{6,4},{7,5},{8,10},{9,11},{10,... | collective-permute-start | bytes 245768 | tf_op jit(solution)/shard_map/ppermute | solution.py:464
  71.8 1.4 %assemble.3.refs_4_ = bf16[8,64,1280]{2,1,0:T(8,128)(2,1)} custom-call(s32[8]{0:T(128)S(1)} %iota_xor_fusion.1.order_ref, bf16[32,1280]{1,0:T(8,128)(2,1)S(1)} %collective-permute-done.12.refs_8_.refs_0_, bf16[32,1280]{1,0:T(8,128)(2,1)S(1)} %collective-permute-done.13.refs_9_.refs_1_, bf16[32,1280]{1,0:T(8,128)(2,1)S(1)} %collective-permute-done.14.refs_10_.refs_2_, ...), custom_call_target="tpu_custom_call" | custom-call | tf_op jit(solution)/shard_map/assemble/pallas_call | solution.py:495
  73.3 2.8 %collective-permute-done.21.refs_3_ = bf16[32,1280]{1,0:T(8,128)(2,1)S(1)} collective-permute-done((bf16[32,1280]{1,0:T(8,128)(2,1)S(1)}, bf16[32,1280]{1,0:T(8,128)(2,1)S(1)}, u32[]{:S(2)}, u32[]{:S(2)}) %collective-permute-start.21) | collective-permute-done | bytes 81952 | tf_op jit(solution)/shard_map/ppermute | solution.py:464
  76.1 1.3 %assemble.4.refs_4_ = bf16[8,64,1280]{2,1,0:T(8,128)(2,1)} custom-call(s32[8]{0:T(128)S(1)} %iota_xor_fusion.1.order_ref, bf16[32,1280]{1,0:T(8,128)(2,1)S(1)} %get-tuple-element.90.refs_0_, bf16[32,1280]{1,0:T(8,128)(2,1)S(1)} %collective-permute-done.19.refs_1_, ...), custom_call_target="tpu_custom_call", output_to_operand_aliasing={{}: (5, {})} | custom-call | tf_op jit(solution)/shard_map/assemble/pallas_call | solution.py:495
  77.4 1.3 %assemble.5 = bf16[8,64,1280]{2,1,0:T(8,128)(2,1)} custom-call(s32[8]{0:T(128)S(1)} %iota_xor_fusion.1.order_ref, bf16[32,1280]{1,0:T(8,128)(2,1)S(1)} %collective-permute-done.15.refs_0_, bf16[32,1280]{1,0:T(8,128)(2,1)S(1)} %collective-permute-done.16.refs_1_, ...), custom_call_target="tpu_custom_call", output_to_operand_aliasing={{}: (5, {})} | custom-call | tf_op jit(solution)/shard_map/assemble/pallas_call | solution.py:495
  (44 shorter events, 4.6 us)
Async XLA Ops:
  1.2 12.1 %collective-permute-start.2 = (bf16[64,1408]{1,0:T(8,128)(2,1)S(1)}, bf16[64,1408]{1,0:T(8,128)(2,1)S(1)}, u32[]{:S(2)}, u32[]{:S(2)}) collective-permute-start(bf16[64,1408]{1,0:T(8,128)(2,1)S(1)} %get-tuple-element.99), channel_id=1, source_target_pairs={{0,24},{8,16},{16,8},{24,0},{1,25},{9,17},{17,9},{25,1},{2,26},{10... | collective-permute-start | bytes 540680 | tf_op jit(solution)/shard_map/ppermute | solution.py:338
  3.7 1.7 %collective-permute-start = (bf16[64,1408]{1,0:T(8,128)(2,1)S(1)}, bf16[64,1408]{1,0:T(8,128)(2,1)S(1)}, u32[]{:S(2)}, u32[]{:S(2)}) collective-permute-start(bf16[64,1408]{1,0:T(8,128)(2,1)S(1)} %get-tuple-element.100), channel_id=1, source_target_pairs={{0,8},{8,0},{16,24},{24,16},{1,9},{9,1},{17,25},{25,17},{2,10},{10... | collective-permute-start | bytes 540680 | tf_op jit(solution)/shard_map/ppermute | solution.py:338
  4.4 9.0 %collective-permute-start.1 = (bf16[64,1408]{1,0:T(8,128)(2,1)S(1)}, bf16[64,1408]{1,0:T(8,128)(2,1)S(1)}, u32[]{:S(2)}, u32[]{:S(2)}) collective-permute-start(bf16[64,1408]{1,0:T(8,128)(2,1)S(1)} %get-tuple-element.102), channel_id=1, source_target_pairs={{0,16},{8,24},{16,0},{24,8},{1,17},{9,25},{17,1},{25,9},{2,18},{10... | collective-permute-start | bytes 540680 | tf_op jit(solution)/shard_map/ppermute | solution.py:338
  5.4 7.9 %copy-start = (f32[3,1408,16]{1,2,0:T(8,128)S(1)}, f32[3,1408,16]{1,2,0:T(8,128)}, u32[]{:S(2)}) copy-start(f32[3,1408,16]{1,2,0:T(8,128)} %param.6) | copy-start | bytes 811012
  20.2 4.3 %collective-permute-start.3 = (bf16[128,1024]{1,0:T(8,128)(2,1)S(1)}, bf16[128,1024]{1,0:T(8,128)(2,1)S(1)}, u32[]{:S(2)}, u32[]{:S(2)}) collective-permute-start(bf16[128,1024]{1,0:T(8,128)(2,1)S(1)} %get-tuple-element.59), channel_id=1, source_target_pairs={{0,8},{8,0},{16,24},{24,16},{1,9},{9,1},{17,25},{25,17},{2,10},{10... | collective-permute-start | bytes 786440 | tf_op jit(solution)/shard_map/ppermute | solution.py:427
  24.2 5.7 %collective-permute-start.5 = (bf16[128,1536]{1,0:T(8,128)(2,1)S(1)}, bf16[128,1536]{1,0:T(8,128)(2,1)S(1)}, u32[]{:S(2)}, u32[]{:S(2)}) collective-permute-start(bf16[128,1536]{1,0:T(8,128)(2,1)S(1)} %get-tuple-element.62), channel_id=1, source_target_pairs={{0,8},{8,0},{16,24},{24,16},{1,9},{9,1},{17,25},{25,17},{2,10},{10... | collective-permute-start | bytes 1179656 | tf_op jit(solution)/shard_map/ppermute | solution.py:427
  24.5 6.0 %collective-permute-start.4 = (bf16[32,1024]{1,0:T(8,128)(2,1)S(1)}, bf16[32,1024]{1,0:T(8,128)(2,1)S(1)}, u32[]{:S(2)}, u32[]{:S(2)}) collective-permute-start(bf16[32,1024]{1,0:T(8,128)(2,1)S(1)} %add_convert_fusion.3.refs_3_), channel_id=1, source_target_pairs={{0,16},{8,24},{16,0},{24,8},{1,17},{9,25},{17,1},{25,9},{2,18},{10... | collective-permute-start | bytes 196616 | tf_op jit(solution)/shard_map/ppermute | solution.py:427
  29.9 3.3 %collective-permute-start.7 = (bf16[128,1536]{1,0:T(8,128)(2,1)S(1)}, bf16[128,1536]{1,0:T(8,128)(2,1)S(1)}, u32[]{:S(2)}, u32[]{:S(2)}) collective-permute-start(bf16[128,1536]{1,0:T(8,128)(2,1)S(1)} %get-tuple-element.67), channel_id=1, source_target_pairs={{0,8},{8,0},{16,24},{24,16},{1,9},{9,1},{17,25},{25,17},{2,10},{10... | collective-permute-start | bytes 1179656 | tf_op jit(solution)/shard_map/ppermute | solution.py:427
  30.0 6.3 %collective-permute-start.6 = (bf16[32,1536]{1,0:T(8,128)(2,1)S(1)}, bf16[32,1536]{1,0:T(8,128)(2,1)S(1)}, u32[]{:S(2)}, u32[]{:S(2)}) collective-permute-start(bf16[32,1536]{1,0:T(8,128)(2,1)S(1)} %add_convert_fusion.1.refs_3_), channel_id=1, source_target_pairs={{0,16},{8,24},{16,0},{24,8},{1,17},{9,25},{17,1},{25,9},{2,18},{10... | collective-permute-start | bytes 294920 | tf_op jit(solution)/shard_map/ppermute | solution.py:427
  33.0 2.0 %collective-permute-start.9 = (bf16[128,1024]{1,0:T(8,128)(2,1)S(1)}, bf16[128,1024]{1,0:T(8,128)(2,1)S(1)}, u32[]{:S(2)}, u32[]{:S(2)}) collective-permute-start(bf16[128,1024]{1,0:T(8,128)(2,1)S(1)} %get-tuple-element.72), channel_id=1, source_target_pairs={{0,8},{8,0},{16,24},{24,16},{1,9},{9,1},{17,25},{25,17},{2,10},{10... | collective-permute-start | bytes 786440 | tf_op jit(solution)/shard_map/ppermute | solution.py:427
  33.2 5.7 %collective-permute-start.8 = (bf16[32,1536]{1,0:T(8,128)(2,1)S(1)}, bf16[32,1536]{1,0:T(8,128)(2,1)S(1)}, u32[]{:S(2)}, u32[]{:S(2)}) collective-permute-start(bf16[32,1536]{1,0:T(8,128)(2,1)S(1)} %add_convert_fusion), channel_id=1, source_target_pairs={{0,16},{8,24},{16,0},{24,8},{1,17},{9,25},{17,1},{25,9},{2,18},{10... | collective-permute-start | bytes 294920 | tf_op jit(solution)/shard_map/ppermute | solution.py:427
  35.0 5.7 %collective-permute-start.10 = (bf16[32,1024]{1,0:T(8,128)(2,1)S(1)}, bf16[32,1024]{1,0:T(8,128)(2,1)S(1)}, u32[]{:S(2)}, u32[]{:S(2)}) collective-permute-start(bf16[32,1024]{1,0:T(8,128)(2,1)S(1)} %add_convert_fusion.2), channel_id=1, source_target_pairs={{0,16},{8,24},{16,0},{24,8},{1,17},{9,25},{17,1},{25,9},{2,18},{10... | collective-permute-start | bytes 196616 | tf_op jit(solution)/shard_map/ppermute | solution.py:427
  42.1 9.4 %collective-permute-start.11 = (bf16[32,5120]{1,0:T(8,128)(2,1)S(1)}, bf16[32,5120]{1,0:T(8,128)(2,1)S(1)}, u32[]{:S(2)}, u32[]{:S(2)}) collective-permute-start(bf16[32,5120]{1,0:T(8,128)(2,1)S(1)} %get-tuple-element.74), channel_id=1, source_target_pairs={{0,16},{8,24},{16,0},{24,8},{1,17},{9,25},{17,1},{25,9},{2,18},{10... | collective-permute-start | bytes 983048 | tf_op jit(solution)/shard_map/ppermute | solution.py:476
  43.8 12.8 %collective-permute-start.12 = (bf16[32,1280]{1,0:T(8,128)(2,1)S(1)}, bf16[32,1280]{1,0:T(8,128)(2,1)S(1)}, u32[]{:S(2)}, u32[]{:S(2)}) collective-permute-start(bf16[32,1280]{1,0:T(8,128)(2,1)S(1)} %get-tuple-element.83), channel_id=1, source_target_pairs={{0,7},{1,6},{2,5},{3,4},{4,3},{5,2},{6,1},{7,0},{8,15},{9,14},{10,... | collective-permute-start | bytes 245768 | tf_op jit(solution)/shard_map/ppermute | solution.py:464
  48.4 9.1 %collective-permute-start.13 = (bf16[32,1280]{1,0:T(8,128)(2,1)S(1)}, bf16[32,1280]{1,0:T(8,128)(2,1)S(1)}, u32[]{:S(2)}, u32[]{:S(2)}) collective-permute-start(bf16[32,1280]{1,0:T(8,128)(2,1)S(1)} %get-tuple-element.84), channel_id=1, source_target_pairs={{0,6},{1,7},{2,4},{3,5},{4,2},{5,3},{6,0},{7,1},{8,14},{9,15},{10,... | collective-permute-start | bytes 245768 | tf_op jit(solution)/shard_map/ppermute | solution.py:464
  48.6 11.5 %collective-permute-start.14 = (bf16[32,1280]{1,0:T(8,128)(2,1)S(1)}, bf16[32,1280]{1,0:T(8,128)(2,1)S(1)}, u32[]{:S(2)}, u32[]{:S(2)}) collective-permute-start(bf16[32,1280]{1,0:T(8,128)(2,1)S(1)} %get-tuple-element.85), channel_id=1, source_target_pairs={{0,5},{1,4},{2,7},{3,6},{4,1},{5,0},{6,3},{7,2},{8,13},{9,12},{10,... | collective-permute-start | bytes 245768 | tf_op jit(solution)/shard_map/ppermute | solution.py:464
  49.3 15.1 %collective-permute-start.22 = (bf16[32,1280]{1,0:T(8,128)(2,1)S(1)}, bf16[32,1280]{1,0:T(8,128)(2,1)S(1)}, u32[]{:S(2)}, u32[]{:S(2)}) collective-permute-start(bf16[32,1280]{1,0:T(8,128)(2,1)S(1)} %get-tuple-element.94), channel_id=1, source_target_pairs={{0,4},{1,5},{2,6},{3,7},{4,0},{5,1},{6,2},{7,3},{8,12},{9,13},{10,... | collective-permute-start | bytes 245768 | tf_op jit(solution)/shard_map/ppermute | solution.py:464
  51.4 13.9 %collective-permute-start.23 = (bf16[32,1280]{1,0:T(8,128)(2,1)S(1)}, bf16[32,1280]{1,0:T(8,128)(2,1)S(1)}, u32[]{:S(2)}, u32[]{:S(2)}) collective-permute-start(bf16[32,1280]{1,0:T(8,128)(2,1)S(1)} %get-tuple-element.95), channel_id=1, source_target_pairs={{0,3},{1,2},{2,1},{3,0},{4,7},{5,6},{6,5},{7,4},{8,11},{9,10},{10,... | collective-permute-start | bytes 245768 | tf_op jit(solution)/shard_map/ppermute | solution.py:464
  56.6 8.7 %collective-permute-start.24 = (bf16[32,1280]{1,0:T(8,128)(2,1)S(1)}, bf16[32,1280]{1,0:T(8,128)(2,1)S(1)}, u32[]{:S(2)}, u32[]{:S(2)}) collective-permute-start(bf16[32,1280]{1,0:T(8,128)(2,1)S(1)} %get-tuple-element.96), channel_id=1, source_target_pairs={{0,2},{1,3},{2,0},{3,1},{4,6},{5,7},{6,4},{7,5},{8,10},{9,11},{10,... | collective-permute-start | bytes 245768 | tf_op jit(solution)/shard_map/ppermute | solution.py:464
  57.4 11.3 %collective-permute-start.25 = (bf16[32,1280]{1,0:T(8,128)(2,1)S(1)}, bf16[32,1280]{1,0:T(8,128)(2,1)S(1)}, u32[]{:S(2)}, u32[]{:S(2)}) collective-permute-start(bf16[32,1280]{1,0:T(8,128)(2,1)S(1)} %get-tuple-element.97), channel_id=1, source_target_pairs={{0,1},{1,0},{2,3},{3,2},{4,5},{5,4},{6,7},{7,6},{8,9},{9,8},{10,11... | collective-permute-start | bytes 245768 | tf_op jit(solution)/shard_map/ppermute | solution.py:464
  60.1 9.6 %collective-permute-start.19 = (bf16[32,1280]{1,0:T(8,128)(2,1)S(1)}, bf16[32,1280]{1,0:T(8,128)(2,1)S(1)}, u32[]{:S(2)}, u32[]{:S(2)}) collective-permute-start(bf16[32,1280]{1,0:T(8,128)(2,1)S(1)} %get-tuple-element.91), channel_id=1, source_target_pairs={{0,7},{1,6},{2,5},{3,4},{4,3},{5,2},{6,1},{7,0},{8,15},{9,14},{10,... | collective-permute-start | bytes 245768 | tf_op jit(solution)/shard_map/ppermute | solution.py:464
  64.4 6.9 %collective-permute-start.20 = (bf16[32,1280]{1,0:T(8,128)(2,1)S(1)}, bf16[32,1280]{1,0:T(8,128)(2,1)S(1)}, u32[]{:S(2)}, u32[]{:S(2)}) collective-permute-start(bf16[32,1280]{1,0:T(8,128)(2,1)S(1)} %get-tuple-element.92), channel_id=1, source_target_pairs={{0,6},{1,7},{2,4},{3,5},{4,2},{5,3},{6,0},{7,1},{8,14},{9,15},{10,... | collective-permute-start | bytes 245768 | tf_op jit(solution)/shard_map/ppermute | solution.py:464
  65.3 12.1 %collective-permute-start.15 = (bf16[32,1280]{1,0:T(8,128)(2,1)S(1)}, bf16[32,1280]{1,0:T(8,128)(2,1)S(1)}, u32[]{:S(2)}, u32[]{:S(2)}) collective-permute-start(bf16[32,1280]{1,0:T(8,128)(2,1)S(1)} %get-tuple-element.86), channel_id=1, source_target_pairs={{0,4},{1,5},{2,6},{3,7},{4,0},{5,1},{6,2},{7,3},{8,12},{9,13},{10,... | collective-permute-start | bytes 245768 | tf_op jit(solution)/shard_map/ppermute | solution.py:464
  65.3 12.1 %collective-permute-start.16 = (bf16[32,1280]{1,0:T(8,128)(2,1)S(1)}, bf16[32,1280]{1,0:T(8,128)(2,1)S(1)}, u32[]{:S(2)}, u32[]{:S(2)}) collective-permute-start(bf16[32,1280]{1,0:T(8,128)(2,1)S(1)} %get-tuple-element.87), channel_id=1, source_target_pairs={{0,3},{1,2},{2,1},{3,0},{4,7},{5,6},{6,5},{7,4},{8,11},{9,10},{10,... | collective-permute-start | bytes 245768 | tf_op jit(solution)/shard_map/ppermute | solution.py:464
  68.7 7.3 %collective-permute-start.21 = (bf16[32,1280]{1,0:T(8,128)(2,1)S(1)}, bf16[32,1280]{1,0:T(8,128)(2,1)S(1)}, u32[]{:S(2)}, u32[]{:S(2)}) collective-permute-start(bf16[32,1280]{1,0:T(8,128)(2,1)S(1)} %get-tuple-element.93), channel_id=1, source_target_pairs={{0,5},{1,4},{2,7},{3,6},{4,1},{5,0},{6,3},{7,2},{8,13},{9,12},{10,... | collective-permute-start | bytes 245768 | tf_op jit(solution)/shard_map/ppermute | solution.py:464
  69.7 7.6 %collective-permute-start.17 = (bf16[32,1280]{1,0:T(8,128)(2,1)S(1)}, bf16[32,1280]{1,0:T(8,128)(2,1)S(1)}, u32[]{:S(2)}, u32[]{:S(2)}) collective-permute-start(bf16[32,1280]{1,0:T(8,128)(2,1)S(1)} %get-tuple-element.88), channel_id=1, source_target_pairs={{0,2},{1,3},{2,0},{3,1},{4,6},{5,7},{6,4},{7,5},{8,10},{9,11},{10,... | collective-permute-start | bytes 245768 | tf_op jit(solution)/shard_map/ppermute | solution.py:464
  71.3 6.1 %collective-permute-start.18 = (bf16[32,1280]{1,0:T(8,128)(2,1)S(1)}, bf16[32,1280]{1,0:T(8,128)(2,1)S(1)}, u32[]{:S(2)}, u32[]{:S(2)}) collective-permute-start(bf16[32,1280]{1,0:T(8,128)(2,1)S(1)} %get-tuple-element.89), channel_id=1, source_target_pairs={{0,1},{1,0},{2,3},{3,2},{4,5},{5,4},{6,7},{7,6},{8,9},{9,8},{10,11... | collective-permute-start | bytes 245768 | tf_op jit(solution)/shard_map/ppermute | solution.py:464

commit v15 on v14

--- a/solution.py
+++ b/solution.py
@@ -18,7 +18,7 @@
 COPIES = (((0, 4), (1, 6)), ((2, 2), (2, 2)), (), ((2, 2), (3, 1)), ((3, 2), (3, 1)))
 PACKS = (0, 2, 3, 4)
 PACK_STEP = 4
-GATE = 3
+GATE = 2
 MIB = 1 << 20
 
 VMEM = functools.partial(pl.BlockSpec, memory_space=pltpu.VMEM)
@@ -488,8 +488,7 @@
     two = deliver(two)
     owned = None
     everyone = [*turns, 0]
-    middle = owners // 2
-    for first, got, which in ((0, one, everyone), (half, two, [0, *turns[: middle - 1]]), (half, two, turns[middle - 1 :])):
+    for first, got, which in ((0, one, everyone), (half, two, everyone)):
         given = [] if owned is None else [owned]
         count = len(which)
         owned = pl.pallas_call(

time: 79 us -> 78.5 us (level)
  Pallas kernels: 36.6 us -> 35.4 us
    pallas_call x3 -> x2, Pallas kernels: 4.03 us -> 2.88 us  [shards(): pl.pallas_call(functools.partial(assemble_kernel, tuple(which), first), i...]
  transfers between devices with their start and end apart: 26 -> 26, of which waited for: 5 -> 7; matrix products, arithmetic and copies ran while one was open for 1% -> 1% of each run, Pallas kernels for 34% -> 33%
where the time goes in v15:
time: 78.5 us; the launch traced here: 78.3 us
  Pallas kernels  35.4 us (45%)
  starting transfers between devices  33.9 us (43%)
  waiting for transfers between devices  6.54 us (8%)
  local copies, waits for them, and re-layouts  1.94 us (2%)
    ppermute x14, starting transfers between devices, deliver(): got[d] = lax.ppermute(packed[d], 'vox', [(i, i ^ d) for i in range(owners)])  22.9 us
    pallas_call x4, Pallas kernels, product(): pl.pallas_call(functools.partial(product_kernel, len(taken), len(after),...  12.3 us
    pallas_call x4, Pallas kernels, pack(): pl.pallas_call(functools.partial(pack_kernel, spread, sizes, spots, sum(w...  8.07 us
    pallas_call x1, Pallas kernels, shards(): pl.pallas_call(functools.partial(early_kernel, owners, spread), in_specs=...  7.9 us
    ppermute x8, starting transfers between devices, shards(): lax.ppermute(send, 'chan', [(i, i ^ 1 << bit) for i in range(parts)])  6.17 us
    ppermute x14, waiting for transfers between devices, deliver(): got[d] = lax.ppermute(packed[d], 'vox', [(i, i ^ d) for i in range(owners)])  5.59 us
    pallas_call x1, Pallas kernels, shards(): pl.pallas_call(functools.partial(design_kernel, parts, firsts[1]), in_spe...  4.26 us
    ppermute x3, starting transfers between devices, shards(): lax.ppermute(series[d], 'chan', [(i, i ^ d) for i in range(parts)])  3.16 us
  transfers between devices with their start and end apart: 26, of which 7 were waited for; matrix products, arithmetic and copies ran while one was open for 1% of the time, Pallas kernels for 33%

profile of v15, /device:TPU:0, one launch (start us, length us, event | category | flops | bytes accessed | tf_op | source)
XLA Modules:
  0.0 78.3 jit_solution(12032211179616273082)
XLA Ops:
  0.0 1.2 %constant_dynamic-slice_fusion = (bf16[64,1408]{1,0:T(8,128)(2,1)S(1)}, bf16[64,1408]{1,0:T(8,128)(2,1)S(1)}, bf16[64,1408]{1,0:T(8,128)(2,1)S(1)}, bf16[64,1408]{1,0:T(8,128)(2,1)S(1)}) fusion(bf16[64,5632]{1,0:T(8,128)(2,1)} %param.5, s32[]{:T(128)S(6)} %select_n.15, s32[]{:T(128)S(6)} %select_n.13, s32[]{:T(128)S(6)} %select_n.12, s32[]{:T(128)S(6)} %select_n.14), kind=kLoop, calls=%fused_computation.5 | loop fusion | bytes 1441808 | tf_op jit(solution)/shard_map/dynamic_slice | solution.py:336
  1.2 2.4 %collective-permute-start.2 = (bf16[64,1408]{1,0:T(8,128)(2,1)S(1)}, bf16[64,1408]{1,0:T(8,128)(2,1)S(1)}, u32[]{:S(2)}, u32[]{:S(2)}) collective-permute-start(bf16[64,1408]{1,0:T(8,128)(2,1)S(1)} %get-tuple-element.99), channel_id=1, source_target_pairs={{0,24},{8,16},{16,8},{24,0},{1,25},{9,17},{17,9},{25,1},{2,26},{10... | collective-permute-start | bytes 540680 | tf_op jit(solution)/shard_map/ppermute | solution.py:338
  5.4 7.9 %early.1 = (s32[40,128]{1,0:T(8,128)S(1)}, s32[40,128]{1,0:T(8,128)S(1)}, s32[24,128]{1,0:T(8,128)S(1)}, bf16[96,4224]{1,0:T(8,128)(2,1)S(1)}, bf16[3,1408,1024]...) custom-call(s32[4]{0:T(128)S(1)} %get-tuple-element.104.order_ref, ...), custom_call_target="tpu_custom_call" | custom-call | bytes 21626880 | tf_op jit(solution)/shard_map/early/pallas_call | solution.py:369
  13.4 4.3 %design.1 = (bf16[256,4224]{1,0:T(8,128)(2,1)S(1)}, bf16[3,1408,512]{2,1,0:T(8,128)(2,1)S(1)}, bf16[3,1408,512]{2,1,0:T(8,128)(2,1)S(1)}) custom-call(s32[4]{0:T(128)S(1)} %get-tuple-element.104.order_ref, s32[4]{0:T(128)S(1)} %get-tuple-element.103.place_ref, bf16[96,4224]{1,0:T(8,128)(2,1)S(1)} %get-tuple-element.55.early_ref, f32[3,16,1408]{2,1,0:T(8,128)S(1)} %bitcast.6, ...), custom_call_target="tpu_custom_call" | custom-call | bytes 8650752 | tf_op jit(solution)/shard_map/design/pallas_call | solution.py:400
  17.6 2.5 %product.4 = (bf16[128,1024]{1,0:T(8,128)(2,1)S(1)}, bf16[128,1024]{1,0:T(8,128)(2,1)S(1)}) custom-call(bf16[256,4224]{1,0:T(8,128)(2,1)S(1)} %get-tuple-element.56.design_ref, bf16[3,1408,1024]{2,1,0:T(8,128)(2,1)S(1)} %get-tuple-element.57.refs_0_), custom_call_target="tpu_custom_call" | custom-call | flops 2214592512 | bytes 8650752 | tf_op jit(solution)/shard_map/product/pallas_call | solution.py:221
  20.6 3.6 %product.5 = (bf16[128,1536]{1,0:T(8,128)(2,1)S(1)}, bf16[128,1536]{1,0:T(8,128)(2,1)S(1)}, bf16[3,1408,512]{2,1,0:T(8,128)(2,1)S(1)}, bf16[3,1408,256]{2,1,0:T(8,128)(2,1)S(1)}) custom-call(bf16[256,4224]{1,0:T(8,128)(2,1)S(1)} %get-tuple-element.56.design_ref, bf16[3,1408,1536]{2,1,0:T(8,128)(2,1)S(1)} %get-tuple-element.60.refs_0_, ...), custom_call_target="tpu_custom_call" | custom-call | flops 3321888768 | bytes 12976128 | tf_op jit(solution)/shard_map/product/pallas_call | solution.py:221
  24.5 1.7 %collective-permute-start.4 = (bf16[32,1024]{1,0:T(8,128)(2,1)S(1)}, bf16[32,1024]{1,0:T(8,128)(2,1)S(1)}, u32[]{:S(2)}, u32[]{:S(2)}) collective-permute-start(bf16[32,1024]{1,0:T(8,128)(2,1)S(1)} %add_convert_fusion.3.refs_3_), channel_id=1, source_target_pairs={{0,16},{8,24},{16,0},{24,8},{1,17},{9,25},{17,1},{25,9},{2,18},{10... | collective-permute-start | bytes 196616 | tf_op jit(solution)/shard_map/ppermute | solution.py:427
  26.2 3.7 %product.6 = (bf16[128,1536]{1,0:T(8,128)(2,1)S(1)}, bf16[128,1536]{1,0:T(8,128)(2,1)S(1)}, bf16[3,1408,512]{2,1,0:T(8,128)(2,1)S(1)}, bf16[3,1408,256]{2,1,0:T(8,128)(2,1)S(1)}) custom-call(bf16[256,4224]{1,0:T(8,128)(2,1)S(1)} %get-tuple-element.56.design_ref, bf16[3,1408,512]{2,1,0:T(8,128)(2,1)S(1)} %get-tuple-element.63.refs_0_, ...), custom_call_target="tpu_custom_call" | custom-call | flops 3321888768 | bytes 12976128 | tf_op jit(solution)/shard_map/product/pallas_call | solution.py:221
  30.5 2.5 %product.7 = (bf16[128,1024]{1,0:T(8,128)(2,1)S(1)}, bf16[128,1024]{1,0:T(8,128)(2,1)S(1)}) custom-call(bf16[256,4224]{1,0:T(8,128)(2,1)S(1)} %get-tuple-element.56.design_ref, bf16[3,1408,256]{2,1,0:T(8,128)(2,1)S(1)} %get-tuple-element.68.refs_0_, bf16[3,1408,512]{2,1,0:T(8,128)(2,1)S(1)} %get-tuple-element.69.refs_1_, ...), custom_call_target="tpu_custom_call" | custom-call | flops 2214592512 | bytes 8650752 | tf_op jit(solution)/shard_map/product/pallas_call | solution.py:221
  33.2 1.7 %collective-permute-start.8 = (bf16[32,1536]{1,0:T(8,128)(2,1)S(1)}, bf16[32,1536]{1,0:T(8,128)(2,1)S(1)}, u32[]{:S(2)}, u32[]{:S(2)}) collective-permute-start(bf16[32,1536]{1,0:T(8,128)(2,1)S(1)} %add_convert_fusion), channel_id=1, source_target_pairs={{0,16},{8,24},{16,0},{24,8},{1,17},{9,25},{17,1},{25,9},{2,18},{10... | collective-permute-start | bytes 294920 | tf_op jit(solution)/shard_map/ppermute | solution.py:427
  35.0 1.3 %collective-permute-start.10 = (bf16[32,1024]{1,0:T(8,128)(2,1)S(1)}, bf16[32,1024]{1,0:T(8,128)(2,1)S(1)}, u32[]{:S(2)}, u32[]{:S(2)}) collective-permute-start(bf16[32,1024]{1,0:T(8,128)(2,1)S(1)} %add_convert_fusion.2), channel_id=1, source_target_pairs={{0,16},{8,24},{16,0},{24,8},{1,17},{9,25},{17,1},{25,9},{2,18},{10... | collective-permute-start | bytes 196616 | tf_op jit(solution)/shard_map/ppermute | solution.py:427
  36.3 2.0 %pack.4.refs_0_ = bf16[8,32,1664]{2,1,0:T(8,128)(2,1)S(1)} custom-call(s32[8]{0:T(128)S(1)} %iota_xor_fusion.1.order_ref, s32[24,128]{1,0:T(8,128)S(1)} %get-tuple-element.52.start_ref, s32[40,128]{1,0:T(8,128)S(1)} %get-tuple-element.53.inner_ref, s32[40,128]{1,0:T(8,128)S(1)} %get-tuple-element.54.tile_ref, ...), custom_call_target="tpu_custom_call" | custom-call | flops 335544320 | bytes 327680 | tf_op jit(solution)/shard_map/pack/pallas_call | solution.py:443
  38.9 1.7 %pack.5.refs_0_ = bf16[8,32,1664]{2,1,0:T(8,128)(2,1)S(1)} custom-call(s32[8]{0:T(128)S(1)} %iota_xor_fusion.1.order_ref, s32[24,128]{1,0:T(8,128)S(1)} %get-tuple-element.52.start_ref, s32[40,128]{1,0:T(8,128)S(1)} %get-tuple-element.53.inner_ref, s32[40,128]{1,0:T(8,128)S(1)} %get-tuple-element.54.tile_ref, bf16[8,32,1664]{2,1,0:T(8,128)(2,1)S(1)} %pack.4.refs_0_, ...), custom_call_target="tpu_custom_call" | custom-call | flops 201326592 | bytes 196608 | tf_op jit(solution)/shard_map/pack/pallas_call | solution.py:443
  40.6 1.4 %pack.6 = (bf16[32,1280]{1,0:T(8,128)(2,1)S(1)}, bf16[32,1280]{1,0:T(8,128)(2,1)S(1)}, bf16[32,1280]{1,0:T(8,128)(2,1)S(1)}, bf16[32,1280]{1,0:T(8,128)(2,1)S(1)...) custom-call(s32[8]{0:T(128)S(1)} %iota_xor_fusion.1.order_ref, ...), custom_call_target="tpu_custom_call" | custom-call | flops 134217728 | bytes 131072 | tf_op jit(solution)/shard_map/pack/pallas_call | solution.py:443
  42.1 1.7 %collective-permute-start.11 = (bf16[32,5120]{1,0:T(8,128)(2,1)S(1)}, bf16[32,5120]{1,0:T(8,128)(2,1)S(1)}, u32[]{:S(2)}, u32[]{:S(2)}) collective-permute-start(bf16[32,5120]{1,0:T(8,128)(2,1)S(1)} %get-tuple-element.74), channel_id=1, source_target_pairs={{0,16},{8,24},{16,0},{24,8},{1,17},{9,25},{17,1},{25,9},{2,18},{10... | collective-permute-start | bytes 983048 | tf_op jit(solution)/shard_map/ppermute | solution.py:476
  43.8 4.6 %collective-permute-start.12 = (bf16[32,1280]{1,0:T(8,128)(2,1)S(1)}, bf16[32,1280]{1,0:T(8,128)(2,1)S(1)}, u32[]{:S(2)}, u32[]{:S(2)}) collective-permute-start(bf16[32,1280]{1,0:T(8,128)(2,1)S(1)} %get-tuple-element.83), channel_id=1, source_target_pairs={{0,7},{1,6},{2,5},{3,4},{4,3},{5,2},{6,1},{7,0},{8,15},{9,14},{10,... | collective-permute-start | bytes 245768 | tf_op jit(solution)/shard_map/ppermute | solution.py:464
  48.6 0.7 collective-permute-start.21
  49.3 2.1 %collective-permute-start.22 = (bf16[32,1280]{1,0:T(8,128)(2,1)S(1)}, bf16[32,1280]{1,0:T(8,128)(2,1)S(1)}, u32[]{:S(2)}, u32[]{:S(2)}) collective-permute-start(bf16[32,1280]{1,0:T(8,128)(2,1)S(1)} %get-tuple-element.94), channel_id=1, source_target_pairs={{0,4},{1,5},{2,6},{3,7},{4,0},{5,1},{6,2},{7,3},{8,12},{9,13},{10,... | collective-permute-start | bytes 245768 | tf_op jit(solution)/shard_map/ppermute | solution.py:464
  51.4 2.2 %collective-permute-start.23 = (bf16[32,1280]{1,0:T(8,128)(2,1)S(1)}, bf16[32,1280]{1,0:T(8,128)(2,1)S(1)}, u32[]{:S(2)}, u32[]{:S(2)}) collective-permute-start(bf16[32,1280]{1,0:T(8,128)(2,1)S(1)} %get-tuple-element.95), channel_id=1, source_target_pairs={{0,3},{1,2},{2,1},{3,0},{4,7},{5,6},{6,5},{7,4},{8,11},{9,10},{10,... | collective-permute-start | bytes 245768 | tf_op jit(solution)/shard_map/ppermute | solution.py:464
  53.6 2.9 %pack.7 = (bf16[32,1280]{1,0:T(8,128)(2,1)S(1)}, bf16[32,1280]{1,0:T(8,128)(2,1)S(1)}, bf16[32,1280]{1,0:T(8,128)(2,1)S(1)}, bf16[32,1280]{1,0:T(8,128)(2,1)S(1)...) custom-call(s32[8]{0:T(128)S(1)} %iota_xor_fusion.1.order_ref, ...), custom_call_target="tpu_custom_call" | custom-call | flops 671088640 | bytes 655360 | tf_op jit(solution)/shard_map/pack/pallas_call | solution.py:443
  56.6 0.8 %collective-permute-start.24 = (bf16[32,1280]{1,0:T(8,128)(2,1)S(1)}, bf16[32,1280]{1,0:T(8,128)(2,1)S(1)}, u32[]{:S(2)}, u32[]{:S(2)}) collective-permute-start(bf16[32,1280]{1,0:T(8,128)(2,1)S(1)} %get-tuple-element.96), channel_id=1, source_target_pairs={{0,2},{1,3},{2,0},{3,1},{4,6},{5,7},{6,4},{7,5},{8,10},{9,11},{10,... | collective-permute-start | bytes 245768 | tf_op jit(solution)/shard_map/ppermute | solution.py:464
  58.0 2.1 %collective-permute-done.21.refs_2_ = bf16[32,1280]{1,0:T(8,128)(2,1)S(1)} collective-permute-done((bf16[32,1280]{1,0:T(8,128)(2,1)S(1)}, bf16[32,1280]{1,0:T(8,128)(2,1)S(1)}, u32[]{:S(2)}, u32[]{:S(2)}) %collective-permute-start.21) | collective-permute-done | bytes 81952 | tf_op jit(solution)/shard_map/ppermute | solution.py:464
  60.1 4.2 %collective-permute-start.14 = (bf16[32,1280]{1,0:T(8,128)(2,1)S(1)}, bf16[32,1280]{1,0:T(8,128)(2,1)S(1)}, u32[]{:S(2)}, u32[]{:S(2)}) collective-permute-start(bf16[32,1280]{1,0:T(8,128)(2,1)S(1)} %get-tuple-element.85), channel_id=1, source_target_pairs={{0,7},{1,6},{2,5},{3,4},{4,3},{5,2},{6,1},{7,0},{8,15},{9,14},{10,... | collective-permute-start | bytes 245768 | tf_op jit(solution)/shard_map/ppermute | solution.py:464
  64.3 0.9 %collective-permute-start.15 = (bf16[32,1280]{1,0:T(8,128)(2,1)S(1)}, bf16[32,1280]{1,0:T(8,128)(2,1)S(1)}, u32[]{:S(2)}, u32[]{:S(2)}) collective-permute-start(bf16[32,1280]{1,0:T(8,128)(2,1)S(1)} %get-tuple-element.86), channel_id=1, source_target_pairs={{0,6},{1,7},{2,4},{3,5},{4,2},{5,3},{6,0},{7,1},{8,14},{9,15},{10,... | collective-permute-start | bytes 245768 | tf_op jit(solution)/shard_map/ppermute | solution.py:464
  65.2 2.8 %collective-permute-start.17 = (bf16[32,1280]{1,0:T(8,128)(2,1)S(1)}, bf16[32,1280]{1,0:T(8,128)(2,1)S(1)}, u32[]{:S(2)}, u32[]{:S(2)}) collective-permute-start(bf16[32,1280]{1,0:T(8,128)(2,1)S(1)} %get-tuple-element.88), channel_id=1, source_target_pairs={{0,4},{1,5},{2,6},{3,7},{4,0},{5,1},{6,2},{7,3},{8,12},{9,13},{10,... | collective-permute-start | bytes 245768 | tf_op jit(solution)/shard_map/ppermute | solution.py:464
  68.0 1.6 %collective-permute-start.18 = (bf16[32,1280]{1,0:T(8,128)(2,1)S(1)}, bf16[32,1280]{1,0:T(8,128)(2,1)S(1)}, u32[]{:S(2)}, u32[]{:S(2)}) collective-permute-start(bf16[32,1280]{1,0:T(8,128)(2,1)S(1)} %get-tuple-element.89), channel_id=1, source_target_pairs={{0,3},{1,2},{2,1},{3,0},{4,7},{5,6},{6,5},{7,4},{8,11},{9,10},{10,... | collective-permute-start | bytes 245768 | tf_op jit(solution)/shard_map/ppermute | solution.py:464
  69.6 1.4 %collective-permute-start.19 = (bf16[32,1280]{1,0:T(8,128)(2,1)S(1)}, bf16[32,1280]{1,0:T(8,128)(2,1)S(1)}, u32[]{:S(2)}, u32[]{:S(2)}) collective-permute-start(bf16[32,1280]{1,0:T(8,128)(2,1)S(1)} %get-tuple-element.90), channel_id=1, source_target_pairs={{0,2},{1,3},{2,0},{3,1},{4,6},{5,7},{6,4},{7,5},{8,10},{9,11},{10,... | collective-permute-start | bytes 245768 | tf_op jit(solution)/shard_map/ppermute | solution.py:464
  71.2 0.7 collective-permute-start.20
  71.9 1.4 %assemble.2.refs_8_ = bf16[8,64,1280]{2,1,0:T(8,128)(2,1)} custom-call(s32[8]{0:T(128)S(1)} %iota_xor_fusion.1.order_ref, bf16[32,1280]{1,0:T(8,128)(2,1)S(1)} %collective-permute-done.12.refs_8_.refs_0_, bf16[32,1280]{1,0:T(8,128)(2,1)S(1)} %collective-permute-done.13.refs_9_.refs_1_, bf16[32,1280]{1,0:T(8,128)(2,1)S(1)} %collective-permute-done.21.refs_2_, ...), custom_call_target="tpu_custom_call" | custom-call | tf_op jit(solution)/shard_map/assemble/pallas_call | solution.py:494
  73.3 1.8 %collective-permute-done.16.refs_2_ = bf16[32,1280]{1,0:T(8,128)(2,1)S(1)} collective-permute-done((bf16[32,1280]{1,0:T(8,128)(2,1)S(1)}, bf16[32,1280]{1,0:T(8,128)(2,1)S(1)}, u32[]{:S(2)}, u32[]{:S(2)}) %collective-permute-start.16) | collective-permute-done | bytes 81952 | tf_op jit(solution)/shard_map/ppermute | solution.py:464
  75.8 0.8 %collective-permute-done.19.refs_5_ = bf16[32,1280]{1,0:T(8,128)(2,1)S(1)} collective-permute-done((bf16[32,1280]{1,0:T(8,128)(2,1)S(1)}, bf16[32,1280]{1,0:T(8,128)(2,1)S(1)}, u32[]{:S(2)}, u32[]{:S(2)}) %collective-permute-start.19) | collective-permute-done | bytes 81952 | tf_op jit(solution)/shard_map/ppermute | solution.py:464
  76.7 1.4 %assemble.3 = bf16[8,64,1280]{2,1,0:T(8,128)(2,1)} custom-call(s32[8]{0:T(128)S(1)} %iota_xor_fusion.1.order_ref, bf16[32,1280]{1,0:T(8,128)(2,1)S(1)} %collective-permute-done.14.refs_0_, bf16[32,1280]{1,0:T(8,128)(2,1)S(1)} %collective-permute-done.15.refs_1_, ...), custom_call_target="tpu_custom_call", output_to_operand_aliasing={{}: (9, {})} | custom-call | tf_op jit(solution)/shard_map/assemble/pallas_call | solution.py:494
  (43 shorter events, 5.4 us)
Async XLA Ops:
  1.2 12.1 %collective-permute-start.2 = (bf16[64,1408]{1,0:T(8,128)(2,1)S(1)}, bf16[64,1408]{1,0:T(8,128)(2,1)S(1)}, u32[]{:S(2)}, u32[]{:S(2)}) collective-permute-start(bf16[64,1408]{1,0:T(8,128)(2,1)S(1)} %get-tuple-element.99), channel_id=1, source_target_pairs={{0,24},{8,16},{16,8},{24,0},{1,25},{9,17},{17,9},{25,1},{2,26},{10... | collective-permute-start | bytes 540680 | tf_op jit(solution)/shard_map/ppermute | solution.py:338
  3.7 1.7 %collective-permute-start = (bf16[64,1408]{1,0:T(8,128)(2,1)S(1)}, bf16[64,1408]{1,0:T(8,128)(2,1)S(1)}, u32[]{:S(2)}, u32[]{:S(2)}) collective-permute-start(bf16[64,1408]{1,0:T(8,128)(2,1)S(1)} %get-tuple-element.100), channel_id=1, source_target_pairs={{0,8},{8,0},{16,24},{24,16},{1,9},{9,1},{17,25},{25,17},{2,10},{10... | collective-permute-start | bytes 540680 | tf_op jit(solution)/shard_map/ppermute | solution.py:338
  4.4 9.0 %collective-permute-start.1 = (bf16[64,1408]{1,0:T(8,128)(2,1)S(1)}, bf16[64,1408]{1,0:T(8,128)(2,1)S(1)}, u32[]{:S(2)}, u32[]{:S(2)}) collective-permute-start(bf16[64,1408]{1,0:T(8,128)(2,1)S(1)} %get-tuple-element.102), channel_id=1, source_target_pairs={{0,16},{8,24},{16,0},{24,8},{1,17},{9,25},{17,1},{25,9},{2,18},{10... | collective-permute-start | bytes 540680 | tf_op jit(solution)/shard_map/ppermute | solution.py:338
  5.4 7.9 %copy-start = (f32[3,1408,16]{1,2,0:T(8,128)S(1)}, f32[3,1408,16]{1,2,0:T(8,128)}, u32[]{:S(2)}) copy-start(f32[3,1408,16]{1,2,0:T(8,128)} %param.6) | copy-start | bytes 811012
  20.2 4.3 %collective-permute-start.3 = (bf16[128,1024]{1,0:T(8,128)(2,1)S(1)}, bf16[128,1024]{1,0:T(8,128)(2,1)S(1)}, u32[]{:S(2)}, u32[]{:S(2)}) collective-permute-start(bf16[128,1024]{1,0:T(8,128)(2,1)S(1)} %get-tuple-element.59), channel_id=1, source_target_pairs={{0,8},{8,0},{16,24},{24,16},{1,9},{9,1},{17,25},{25,17},{2,10},{10... | collective-permute-start | bytes 786440 | tf_op jit(solution)/shard_map/ppermute | solution.py:427
  24.2 5.7 %collective-permute-start.5 = (bf16[128,1536]{1,0:T(8,128)(2,1)S(1)}, bf16[128,1536]{1,0:T(8,128)(2,1)S(1)}, u32[]{:S(2)}, u32[]{:S(2)}) collective-permute-start(bf16[128,1536]{1,0:T(8,128)(2,1)S(1)} %get-tuple-element.62), channel_id=1, source_target_pairs={{0,8},{8,0},{16,24},{24,16},{1,9},{9,1},{17,25},{25,17},{2,10},{10... | collective-permute-start | bytes 1179656 | tf_op jit(solution)/shard_map/ppermute | solution.py:427
  24.5 6.0 %collective-permute-start.4 = (bf16[32,1024]{1,0:T(8,128)(2,1)S(1)}, bf16[32,1024]{1,0:T(8,128)(2,1)S(1)}, u32[]{:S(2)}, u32[]{:S(2)}) collective-permute-start(bf16[32,1024]{1,0:T(8,128)(2,1)S(1)} %add_convert_fusion.3.refs_3_), channel_id=1, source_target_pairs={{0,16},{8,24},{16,0},{24,8},{1,17},{9,25},{17,1},{25,9},{2,18},{10... | collective-permute-start | bytes 196616 | tf_op jit(solution)/shard_map/ppermute | solution.py:427
  29.9 3.3 %collective-permute-start.7 = (bf16[128,1536]{1,0:T(8,128)(2,1)S(1)}, bf16[128,1536]{1,0:T(8,128)(2,1)S(1)}, u32[]{:S(2)}, u32[]{:S(2)}) collective-permute-start(bf16[128,1536]{1,0:T(8,128)(2,1)S(1)} %get-tuple-element.67), channel_id=1, source_target_pairs={{0,8},{8,0},{16,24},{24,16},{1,9},{9,1},{17,25},{25,17},{2,10},{10... | collective-permute-start | bytes 1179656 | tf_op jit(solution)/shard_map/ppermute | solution.py:427
  30.0 6.3 %collective-permute-start.6 = (bf16[32,1536]{1,0:T(8,128)(2,1)S(1)}, bf16[32,1536]{1,0:T(8,128)(2,1)S(1)}, u32[]{:S(2)}, u32[]{:S(2)}) collective-permute-start(bf16[32,1536]{1,0:T(8,128)(2,1)S(1)} %add_convert_fusion.1.refs_3_), channel_id=1, source_target_pairs={{0,16},{8,24},{16,0},{24,8},{1,17},{9,25},{17,1},{25,9},{2,18},{10... | collective-permute-start | bytes 294920 | tf_op jit(solution)/shard_map/ppermute | solution.py:427
  33.0 2.0 %collective-permute-start.9 = (bf16[128,1024]{1,0:T(8,128)(2,1)S(1)}, bf16[128,1024]{1,0:T(8,128)(2,1)S(1)}, u32[]{:S(2)}, u32[]{:S(2)}) collective-permute-start(bf16[128,1024]{1,0:T(8,128)(2,1)S(1)} %get-tuple-element.72), channel_id=1, source_target_pairs={{0,8},{8,0},{16,24},{24,16},{1,9},{9,1},{17,25},{25,17},{2,10},{10... | collective-permute-start | bytes 786440 | tf_op jit(solution)/shard_map/ppermute | solution.py:427
  33.2 5.7 %collective-permute-start.8 = (bf16[32,1536]{1,0:T(8,128)(2,1)S(1)}, bf16[32,1536]{1,0:T(8,128)(2,1)S(1)}, u32[]{:S(2)}, u32[]{:S(2)}) collective-permute-start(bf16[32,1536]{1,0:T(8,128)(2,1)S(1)} %add_convert_fusion), channel_id=1, source_target_pairs={{0,16},{8,24},{16,0},{24,8},{1,17},{9,25},{17,1},{25,9},{2,18},{10... | collective-permute-start | bytes 294920 | tf_op jit(solution)/shard_map/ppermute | solution.py:427
  35.0 5.7 %collective-permute-start.10 = (bf16[32,1024]{1,0:T(8,128)(2,1)S(1)}, bf16[32,1024]{1,0:T(8,128)(2,1)S(1)}, u32[]{:S(2)}, u32[]{:S(2)}) collective-permute-start(bf16[32,1024]{1,0:T(8,128)(2,1)S(1)} %add_convert_fusion.2), channel_id=1, source_target_pairs={{0,16},{8,24},{16,0},{24,8},{1,17},{9,25},{17,1},{25,9},{2,18},{10... | collective-permute-start | bytes 196616 | tf_op jit(solution)/shard_map/ppermute | solution.py:427
  42.1 9.4 %collective-permute-start.11 = (bf16[32,5120]{1,0:T(8,128)(2,1)S(1)}, bf16[32,5120]{1,0:T(8,128)(2,1)S(1)}, u32[]{:S(2)}, u32[]{:S(2)}) collective-permute-start(bf16[32,5120]{1,0:T(8,128)(2,1)S(1)} %get-tuple-element.74), channel_id=1, source_target_pairs={{0,16},{8,24},{16,0},{24,8},{1,17},{9,25},{17,1},{25,9},{2,18},{10... | collective-permute-start | bytes 983048 | tf_op jit(solution)/shard_map/ppermute | solution.py:476
  43.8 12.8 %collective-permute-start.12 = (bf16[32,1280]{1,0:T(8,128)(2,1)S(1)}, bf16[32,1280]{1,0:T(8,128)(2,1)S(1)}, u32[]{:S(2)}, u32[]{:S(2)}) collective-permute-start(bf16[32,1280]{1,0:T(8,128)(2,1)S(1)} %get-tuple-element.83), channel_id=1, source_target_pairs={{0,7},{1,6},{2,5},{3,4},{4,3},{5,2},{6,1},{7,0},{8,15},{9,14},{10,... | collective-permute-start | bytes 245768 | tf_op jit(solution)/shard_map/ppermute | solution.py:464
  48.3 9.1 %collective-permute-start.13 = (bf16[32,1280]{1,0:T(8,128)(2,1)S(1)}, bf16[32,1280]{1,0:T(8,128)(2,1)S(1)}, u32[]{:S(2)}, u32[]{:S(2)}) collective-permute-start(bf16[32,1280]{1,0:T(8,128)(2,1)S(1)} %get-tuple-element.84), channel_id=1, source_target_pairs={{0,6},{1,7},{2,4},{3,5},{4,2},{5,3},{6,0},{7,1},{8,14},{9,15},{10,... | collective-permute-start | bytes 245768 | tf_op jit(solution)/shard_map/ppermute | solution.py:464
  48.6 11.5 %collective-permute-start.21 = (bf16[32,1280]{1,0:T(8,128)(2,1)S(1)}, bf16[32,1280]{1,0:T(8,128)(2,1)S(1)}, u32[]{:S(2)}, u32[]{:S(2)}) collective-permute-start(bf16[32,1280]{1,0:T(8,128)(2,1)S(1)} %get-tuple-element.93), channel_id=1, source_target_pairs={{0,5},{1,4},{2,7},{3,6},{4,1},{5,0},{6,3},{7,2},{8,13},{9,12},{10,... | collective-permute-start | bytes 245768 | tf_op jit(solution)/shard_map/ppermute | solution.py:464
  49.3 15.0 %collective-permute-start.22 = (bf16[32,1280]{1,0:T(8,128)(2,1)S(1)}, bf16[32,1280]{1,0:T(8,128)(2,1)S(1)}, u32[]{:S(2)}, u32[]{:S(2)}) collective-permute-start(bf16[32,1280]{1,0:T(8,128)(2,1)S(1)} %get-tuple-element.94), channel_id=1, source_target_pairs={{0,4},{1,5},{2,6},{3,7},{4,0},{5,1},{6,2},{7,3},{8,12},{9,13},{10,... | collective-permute-start | bytes 245768 | tf_op jit(solution)/shard_map/ppermute | solution.py:464
  51.4 13.7 %collective-permute-start.23 = (bf16[32,1280]{1,0:T(8,128)(2,1)S(1)}, bf16[32,1280]{1,0:T(8,128)(2,1)S(1)}, u32[]{:S(2)}, u32[]{:S(2)}) collective-permute-start(bf16[32,1280]{1,0:T(8,128)(2,1)S(1)} %get-tuple-element.95), channel_id=1, source_target_pairs={{0,3},{1,2},{2,1},{3,0},{4,7},{5,6},{6,5},{7,4},{8,11},{9,10},{10,... | collective-permute-start | bytes 245768 | tf_op jit(solution)/shard_map/ppermute | solution.py:464
  56.6 8.6 %collective-permute-start.24 = (bf16[32,1280]{1,0:T(8,128)(2,1)S(1)}, bf16[32,1280]{1,0:T(8,128)(2,1)S(1)}, u32[]{:S(2)}, u32[]{:S(2)}) collective-permute-start(bf16[32,1280]{1,0:T(8,128)(2,1)S(1)} %get-tuple-element.96), channel_id=1, source_target_pairs={{0,2},{1,3},{2,0},{3,1},{4,6},{5,7},{6,4},{7,5},{8,10},{9,11},{10,... | collective-permute-start | bytes 245768 | tf_op jit(solution)/shard_map/ppermute | solution.py:464
  57.4 10.6 %collective-permute-start.25 = (bf16[32,1280]{1,0:T(8,128)(2,1)S(1)}, bf16[32,1280]{1,0:T(8,128)(2,1)S(1)}, u32[]{:S(2)}, u32[]{:S(2)}) collective-permute-start(bf16[32,1280]{1,0:T(8,128)(2,1)S(1)} %get-tuple-element.97), channel_id=1, source_target_pairs={{0,1},{1,0},{2,3},{3,2},{4,5},{5,4},{6,7},{7,6},{8,9},{9,8},{10,11... | collective-permute-start | bytes 245768 | tf_op jit(solution)/shard_map/ppermute | solution.py:464
  60.1 9.5 %collective-permute-start.14 = (bf16[32,1280]{1,0:T(8,128)(2,1)S(1)}, bf16[32,1280]{1,0:T(8,128)(2,1)S(1)}, u32[]{:S(2)}, u32[]{:S(2)}) collective-permute-start(bf16[32,1280]{1,0:T(8,128)(2,1)S(1)} %get-tuple-element.85), channel_id=1, source_target_pairs={{0,7},{1,6},{2,5},{3,4},{4,3},{5,2},{6,1},{7,0},{8,15},{9,14},{10,... | collective-permute-start | bytes 245768 | tf_op jit(solution)/shard_map/ppermute | solution.py:464
  64.3 6.9 %collective-permute-start.15 = (bf16[32,1280]{1,0:T(8,128)(2,1)S(1)}, bf16[32,1280]{1,0:T(8,128)(2,1)S(1)}, u32[]{:S(2)}, u32[]{:S(2)}) collective-permute-start(bf16[32,1280]{1,0:T(8,128)(2,1)S(1)} %get-tuple-element.86), channel_id=1, source_target_pairs={{0,6},{1,7},{2,4},{3,5},{4,2},{5,3},{6,0},{7,1},{8,14},{9,15},{10,... | collective-permute-start | bytes 245768 | tf_op jit(solution)/shard_map/ppermute | solution.py:464
  65.2 10.0 %collective-permute-start.16 = (bf16[32,1280]{1,0:T(8,128)(2,1)S(1)}, bf16[32,1280]{1,0:T(8,128)(2,1)S(1)}, u32[]{:S(2)}, u32[]{:S(2)}) collective-permute-start(bf16[32,1280]{1,0:T(8,128)(2,1)S(1)} %get-tuple-element.87), channel_id=1, source_target_pairs={{0,5},{1,4},{2,7},{3,6},{4,1},{5,0},{6,3},{7,2},{8,13},{9,12},{10,... | collective-permute-start | bytes 245768 | tf_op jit(solution)/shard_map/ppermute | solution.py:464
  65.2 10.6 %collective-permute-start.17 = (bf16[32,1280]{1,0:T(8,128)(2,1)S(1)}, bf16[32,1280]{1,0:T(8,128)(2,1)S(1)}, u32[]{:S(2)}, u32[]{:S(2)}) collective-permute-start(bf16[32,1280]{1,0:T(8,128)(2,1)S(1)} %get-tuple-element.88), channel_id=1, source_target_pairs={{0,4},{1,5},{2,6},{3,7},{4,0},{5,1},{6,2},{7,3},{8,12},{9,13},{10,... | collective-permute-start | bytes 245768 | tf_op jit(solution)/shard_map/ppermute | solution.py:464
  68.0 7.9 %collective-permute-start.18 = (bf16[32,1280]{1,0:T(8,128)(2,1)S(1)}, bf16[32,1280]{1,0:T(8,128)(2,1)S(1)}, u32[]{:S(2)}, u32[]{:S(2)}) collective-permute-start(bf16[32,1280]{1,0:T(8,128)(2,1)S(1)} %get-tuple-element.89), channel_id=1, source_target_pairs={{0,3},{1,2},{2,1},{3,0},{4,7},{5,6},{6,5},{7,4},{8,11},{9,10},{10,... | collective-permute-start | bytes 245768 | tf_op jit(solution)/shard_map/ppermute | solution.py:464
  69.6 7.1 %collective-permute-start.19 = (bf16[32,1280]{1,0:T(8,128)(2,1)S(1)}, bf16[32,1280]{1,0:T(8,128)(2,1)S(1)}, u32[]{:S(2)}, u32[]{:S(2)}) collective-permute-start(bf16[32,1280]{1,0:T(8,128)(2,1)S(1)} %get-tuple-element.90), channel_id=1, source_target_pairs={{0,2},{1,3},{2,0},{3,1},{4,6},{5,7},{6,4},{7,5},{8,10},{9,11},{10,... | collective-permute-start | bytes 245768 | tf_op jit(solution)/shard_map/ppermute | solution.py:464
  71.2 5.5 %collective-permute-start.20 = (bf16[32,1280]{1,0:T(8,128)(2,1)S(1)}, bf16[32,1280]{1,0:T(8,128)(2,1)S(1)}, u32[]{:S(2)}, u32[]{:S(2)}) collective-permute-start(bf16[32,1280]{1,0:T(8,128)(2,1)S(1)} %get-tuple-element.91), channel_id=1, source_target_pairs={{0,1},{1,0},{2,3},{3,2},{4,5},{5,4},{6,7},{7,6},{8,9},{9,8},{10,11... | collective-permute-start | bytes 245768 | tf_op jit(solution)/shard_map/ppermute | solution.py:464

commit v16 on v15

--- a/solution.py
+++ b/solution.py
@@ -18,7 +18,6 @@
 COPIES = (((0, 4), (1, 6)), ((2, 2), (2, 2)), (), ((2, 2), (3, 1)), ((3, 2), (3, 1)))
 PACKS = (0, 2, 3, 4)
 PACK_STEP = 4
-GATE = 2
 MIB = 1 << 20
 
 VMEM = functools.partial(pl.BlockSpec, memory_space=pltpu.VMEM)
@@ -230,36 +229,17 @@
     )(design, *taken, *after, *([weights] if ahead else []))
 
 
-def add_rows(terms, each, first, out_ref):
-    at, rows = 0, out_ref.shape[0]
-    for c in range(0, len(terms), each):
-        chunk, width = terms[c : c + each], terms[c].shape[1]
-        total = sum(term[first : first + rows, :].astype(jnp.float32) for term in chunk)
-        out_ref[:, at : at + width] = total.astype(jnp.bfloat16)
-        at += width
-
-
-def pack_kernel(spread, widths, places, first, later, outs, order_ref, start_ref, inner_ref, tile_ref, *refs):
+def pack_kernel(spread, widths, places, first, outs, order_ref, start_ref, inner_ref, tile_ref, *refs):
     *refs, summed, packed = refs
-    if later:
-        count, each = later
-        *refs, send_ref, keep_ref = refs
     terms, out_refs = refs[: len(refs) - outs], refs[len(refs) - outs :]
-    if later:
-        rows = packed.shape[1]
-        add_rows(terms[-count:], each, 3 * rows, send_ref)
-        add_rows(terms[-count:], each, rows, keep_ref)
-        terms = terms[:-count]
     owners, rows = packed.shape[:2]
     if first:
         packed[...] = terms.pop(0)[...]
     else:
         packed[...] = jnp.zeros_like(packed)
     at = 0
-    for width, spots in zip(widths, places):
-        total = 0.0
-        for row, column in spots:
-            total = total + terms.pop(0)[row : row + rows, column : column + width].astype(jnp.float32)
+    for width, count in zip(widths, places):
+        total = sum(terms.pop(0)[:rows, :].astype(jnp.float32) for _ in range(count))
         summed[:, at : at + width] = total.astype(jnp.bfloat16)
         at += width
     step = VOX_BLOCK // LANES
@@ -409,7 +389,6 @@
     )(order, place, early, filters, weights, *series)
     keep_pieces(1, pieces)
 
-    half = time_block // 2
     widths, sums, sent, got = [], [], [], []
     for c in range(CHUNKS):
         after = sent[max(c - 2, 0) : max(c - 1, 0)] + got[max(c - 3, 0) : max(c - 2, 0)]
@@ -421,7 +400,7 @@
         for bit in range(bits):
             if bit > 0:
                 rows = own[-1].shape[0] // 2
-                send = added(own, rows, half if bit == bits - 1 else rows)
+                send = added(own, rows, rows)
                 if bit == bits - 1:
                     sent.append(send)
             own.append(lax.ppermute(send, "chan", [(i, i ^ (1 << bit)) for i in range(parts)]))
@@ -430,31 +409,29 @@
     here = lax.axis_index("vox")
     targets = jnp.arange(owners, dtype=jnp.int32) ^ here
 
-    def pack(chunks, terms, spots, packed=(), later=()):
+    def pack(chunks, packed):
         sizes = [widths[c] for c in chunks]
-        spec = (len(later), bits) if later else None
+        terms = [term for c in chunks for term in sums[c]]
         if chunks[-1] == CHUNKS - 1:
-            outs = [pltpu.VMEM((half, send_cap), jnp.bfloat16)] * owners
+            outs = [pltpu.VMEM((time_block, send_cap), jnp.bfloat16)] * owners
         else:
-            outs = [jax.ShapeDtypeStruct((owners, half, spread * SLOT_TILE), jnp.bfloat16)]
-        more = []
-        if later:
-            more = [jax.ShapeDtypeStruct((half, voxels), jnp.bfloat16), pltpu.VMEM((half, voxels), jnp.bfloat16)]
+            outs = [jax.ShapeDtypeStruct((owners, time_block, spread * SLOT_TILE), jnp.bfloat16)]
+        counts = [len(sums[c]) for c in chunks]
         return pl.pallas_call(
             functools.partial(
-                pack_kernel, spread, sizes, spots, sum(widths[: chunks[0]]) // VOX_BLOCK, spec, len(outs)
+                pack_kernel, spread, sizes, counts, sum(widths[: chunks[0]]) // VOX_BLOCK, len(outs)
             ),
-            in_specs=[SMEM(), SMEM(), VMEM(), VMEM()] + [VMEM()] * (len(packed) + len(terms) + len(later)),
-            out_specs=[VMEM()] * (len(outs) + len(more)),
-            out_shape=outs + more,
+            in_specs=[SMEM(), SMEM(), VMEM(), VMEM()] + [VMEM()] * (len(packed) + len(terms)),
+            out_specs=[VMEM()] * len(outs),
+            out_shape=outs,
             scratch_shapes=[
-                pltpu.VMEM((half, sum(sizes)), jnp.bfloat16),
-                pltpu.VMEM((owners, half, spread * SLOT_TILE), jnp.bfloat16),
+                pltpu.VMEM((time_block, sum(sizes)), jnp.bfloat16),
+                pltpu.VMEM((owners, time_block, spread * SLOT_TILE), jnp.bfloat16),
             ],
             compiler_params=pltpu.CompilerParams(vmem_limit_bytes=8 * MIB),
-            cost_estimate=cost(2 * half * owners * VOX_BLOCK * sum(sizes), 4 * half * sum(sizes)),
+            cost_estimate=cost(2 * time_block * owners * VOX_BLOCK * sum(sizes), 4 * time_block * sum(sizes)),
             name="pack",
-        )(targets, starts, inner, tiles, *packed, *terms, *later)
+        )(targets, starts, inner, tiles, *packed, *terms)
 
     turns = range(owners - 1, 0, -1)
 
@@ -464,35 +441,16 @@
             got[d] = lax.ppermute(packed[d], "vox", [(i, i ^ d) for i in range(owners)])
         return got
 
-    def early_terms(chunks):
-        return [term for c in chunks for term in sums[c]], [[(0, 0)] * len(sums[c]) for c in chunks]
-
     packed = []
     for low, high in zip(PACKS, PACKS[1:]):
-        chunks = range(low, high)
-        later = [term for own in sums for term in own[:-1]] if high == CHUNKS else []
-        packed = pack(chunks, *early_terms(chunks), packed=packed, later=later)
-    *one, late_send, late_own = packed
-    late = lax.ppermute(late_send, "chan", [(i, i ^ (1 << (bits - 1))) for i in range(parts)])
-    one = deliver(one)
-    starting = [sum(widths[:c]) for c in range(CHUNKS)]
-    two = pack(range(CHUNKS), [late_own, late] * CHUNKS, [[(0, first)] * 2 for first in starting])
-    two = pl.pallas_call(
-        gate_kernel,
-        in_specs=[VMEM()] * (owners + GATE),
-        out_specs=[VMEM()] * owners,
-        out_shape=[pltpu.VMEM((half, send_cap), jnp.bfloat16)] * owners,
-        compiler_params=pltpu.CompilerParams(vmem_limit_bytes=4 * MIB),
-        name="gate",
-    )(*two, *(one[d] for d in turns[:GATE]))
-    two = deliver(two)
-    owned = None
-    everyone = [*turns, 0]
-    for first, got, which in ((0, one, everyone), (half, two, everyone)):
+        packed = pack(range(low, high), packed)
+    got = deliver(packed)
+    owned, middle = None, owners // 2
+    for which in ([0, *turns[: middle - 1]], turns[middle - 1 :]):
         given = [] if owned is None else [owned]
         count = len(which)
         owned = pl.pallas_call(
-            functools.partial(assemble_kernel, tuple(which), first),
+            functools.partial(assemble_kernel, tuple(which)),
             in_specs=[SMEM()] + [VMEM()] * count + [HBM()] * len(given),
             out_specs=HBM(),
             out_shape=jax.ShapeDtypeStruct((owners, time_block, send_cap), jnp.bfloat16),
@@ -504,18 +462,11 @@
     return jnp.transpose(owned, (0, 2, 1))
 
 
-def gate_kernel(*refs):
-    count = (len(refs) - GATE) // 2
-    for given, out in zip(refs[:count], refs[count + GATE :]):
-        out[...] = given[...]
-
-
-def assemble_kernel(which, first, order_ref, *refs):
+def assemble_kernel(which, order_ref, *refs):
     parts, (out_ref, sems) = refs[: len(which)], refs[-2:]
     copies = []
     for i, (d, ref) in enumerate(zip(which, parts)):
-        rows = pl.ds(first, ref.shape[0])
-        copies.append(pltpu.make_async_copy(ref, out_ref.at[order_ref[d], rows, :], sems.at[i]))
+        copies.append(pltpu.make_async_copy(ref, out_ref.at[order_ref[d]], sems.at[i]))
         copies[-1].start()
     wait_all(copies)
 

time: 78.5 us -> 83.5 us (1.064)
  waiting for transfers between devices: 6.54 us -> 11.1 us
  starting transfers between devices: 33.9 us -> 36.2 us
  Pallas kernels: 35.4 us -> 33.6 us
    ppermute x14 -> x7, starting transfers between devices: 22.9 us -> 26.9 us  [deliver(): got[d] = lax.ppermute(packed[d], 'vox', [(i, i ^ d) for i in range(owners)])]
    ppermute x8, waiting for transfers between devices: 0.62 us -> 3.28 us  [shards(): lax.ppermute(send, 'chan', [(i, i ^ 1 << bit) for i in range(parts)])]
    ppermute x14 -> x7, waiting for transfers between devices: 5.59 us -> 7.5 us  [deliver(): got[d] = lax.ppermute(packed[d], 'vox', [(i, i ^ d) for i in range(owners)])]
    pallas_call x7 -> x5, Pallas kernels: 11 us -> 9.17 us  [the longest x3 6.35 us: pack(): pl.pallas_call(functools.partial(pack_kernel, spread, sizes, counts, sum(...]
    ppermute x1 -> x0, starting transfers between devices: 1.73 us -> none  [shards(): lax.ppermute(late_send, 'chan', [(i, i ^ 1 << bits - 1) for i in range(pa...]
  transfers between devices with their start and end apart: 26 -> 18, of which waited for: 7 -> 5; matrix products, arithmetic and copies ran while one was open for 1% -> 1% of each run, Pallas kernels for 33% -> 29%
where the time goes in v16:
time: 83.5 us; the launch traced here: 83.4 us
  starting transfers between devices  36.2 us (43%)
  Pallas kernels  33.6 us (40%)
  waiting for transfers between devices  11.1 us (13%)
  local copies, waits for them, and re-layouts  1.94 us (2%)
    ppermute x7, starting transfers between devices, deliver(): got[d] = lax.ppermute(packed[d], 'vox', [(i, i ^ d) for i in range(owners)])  26.9 us
    pallas_call x4, Pallas kernels, product(): pl.pallas_call(functools.partial(product_kernel, len(taken), len(after),...  12.3 us
    pallas_call x1, Pallas kernels, shards(): pl.pallas_call(functools.partial(early_kernel, owners, spread), in_specs=...  7.9 us
    ppermute x7, waiting for transfers between devices, deliver(): got[d] = lax.ppermute(packed[d], 'vox', [(i, i ^ d) for i in range(owners)])  7.5 us
    pallas_call x3, Pallas kernels, pack(): pl.pallas_call(functools.partial(pack_kernel, spread, sizes, counts, sum(...  6.35 us
    ppermute x8, starting transfers between devices, shards(): lax.ppermute(send, 'chan', [(i, i ^ 1 << bit) for i in range(parts)])  6.15 us
    pallas_call x1, Pallas kernels, shards(): pl.pallas_call(functools.partial(design_kernel, parts, firsts[1]), in_spe...  4.26 us
    ppermute x8, waiting for transfers between devices, shards(): lax.ppermute(send, 'chan', [(i, i ^ 1 << bit) for i in range(parts)])  3.28 us
  transfers between devices with their start and end apart: 18, of which 5 were waited for; matrix products, arithmetic and copies ran while one was open for 1% of the time, Pallas kernels for 29%

profile of v16, /device:TPU:0, one launch (start us, length us, event | category | flops | bytes accessed | tf_op | source)
XLA Modules:
  0.0 83.4 jit_solution(7252537266507040712)
XLA Ops:
  0.0 1.2 %constant_dynamic-slice_fusion = (bf16[64,1408]{1,0:T(8,128)(2,1)S(1)}, bf16[64,1408]{1,0:T(8,128)(2,1)S(1)}, bf16[64,1408]{1,0:T(8,128)(2,1)S(1)}, bf16[64,1408]{1,0:T(8,128)(2,1)S(1)}) fusion(bf16[64,5632]{1,0:T(8,128)(2,1)} %param.5, s32[]{:T(128)S(6)} %select_n.15, s32[]{:T(128)S(6)} %select_n.13, s32[]{:T(128)S(6)} %select_n.12, s32[]{:T(128)S(6)} %select_n.14), kind=kLoop, calls=%fused_computation.5 | loop fusion | bytes 1441808 | tf_op jit(solution)/shard_map/dynamic_slice | solution.py:316
  1.2 2.4 %collective-permute-start.2 = (bf16[64,1408]{1,0:T(8,128)(2,1)S(1)}, bf16[64,1408]{1,0:T(8,128)(2,1)S(1)}, u32[]{:S(2)}, u32[]{:S(2)}) collective-permute-start(bf16[64,1408]{1,0:T(8,128)(2,1)S(1)} %get-tuple-element.63), channel_id=1, source_target_pairs={{0,24},{8,16},{16,8},{24,0},{1,25},{9,17},{17,9},{25,1},{2,26},{10... | collective-permute-start | bytes 540680 | tf_op jit(solution)/shard_map/ppermute | solution.py:318
  3.7 0.7 collective-permute-start
  4.4 0.7 pad_bitcast_fusion.table_ref
  5.1 0.3 collective-permute-done.pair_ref.refs_1_
  5.4 7.9 %early.1 = (s32[40,128]{1,0:T(8,128)S(1)}, s32[40,128]{1,0:T(8,128)S(1)}, s32[24,128]{1,0:T(8,128)S(1)}, bf16[96,4224]{1,0:T(8,128)(2,1)S(1)}, bf16[3,1408,1024]...) custom-call(s32[4]{0:T(128)S(1)} %get-tuple-element.68.order_ref, ...), custom_call_target="tpu_custom_call" | custom-call | bytes 21626880 | tf_op jit(solution)/shard_map/early/pallas_call | solution.py:349
  13.4 4.3 %design.1 = (bf16[256,4224]{1,0:T(8,128)(2,1)S(1)}, bf16[3,1408,512]{2,1,0:T(8,128)(2,1)S(1)}, bf16[3,1408,512]{2,1,0:T(8,128)(2,1)S(1)}) custom-call(s32[4]{0:T(128)S(1)} %get-tuple-element.68.order_ref, s32[4]{0:T(128)S(1)} %get-tuple-element.67.place_ref, bf16[96,4224]{1,0:T(8,128)(2,1)S(1)} %get-tuple-element.37.early_ref, f32[3,16,1408]{2,1,0:T(8,128)S(1)} %bitcast.6, ...), custom_call_target="tpu_custom_call" | custom-call | bytes 8650752 | tf_op jit(solution)/shard_map/design/pallas_call | solution.py:380
  17.6 2.5 %product.4 = (bf16[128,1024]{1,0:T(8,128)(2,1)S(1)}, bf16[128,1024]{1,0:T(8,128)(2,1)S(1)}) custom-call(bf16[256,4224]{1,0:T(8,128)(2,1)S(1)} %get-tuple-element.38.design_ref, bf16[3,1408,1024]{2,1,0:T(8,128)(2,1)S(1)} %get-tuple-element.39.refs_0_), custom_call_target="tpu_custom_call" | custom-call | flops 2214592512 | bytes 8650752 | tf_op jit(solution)/shard_map/product/pallas_call | solution.py:220
  20.2 0.4 collective-permute-start.3
  20.6 3.6 %product.5 = (bf16[128,1536]{1,0:T(8,128)(2,1)S(1)}, bf16[128,1536]{1,0:T(8,128)(2,1)S(1)}, bf16[3,1408,512]{2,1,0:T(8,128)(2,1)S(1)}, bf16[3,1408,256]{2,1,0:T(8,128)(2,1)S(1)}) custom-call(bf16[256,4224]{1,0:T(8,128)(2,1)S(1)} %get-tuple-element.38.design_ref, bf16[3,1408,1536]{2,1,0:T(8,128)(2,1)S(1)} %get-tuple-element.42.refs_0_, ...), custom_call_target="tpu_custom_call" | custom-call | flops 3321888768 | bytes 12976128 | tf_op jit(solution)/shard_map/product/pallas_call | solution.py:220
  24.5 1.7 %collective-permute-start.4 = (bf16[64,1024]{1,0:T(8,128)(2,1)S(1)}, bf16[64,1024]{1,0:T(8,128)(2,1)S(1)}, u32[]{:S(2)}, u32[]{:S(2)}) collective-permute-start(bf16[64,1024]{1,0:T(8,128)(2,1)S(1)} %add_convert_fusion.3.refs_3_), channel_id=1, source_target_pairs={{0,16},{8,24},{16,0},{24,8},{1,17},{9,25},{17,1},{25,9},{2,18},{10... | collective-permute-start | bytes 393224 | tf_op jit(solution)/shard_map/ppermute | solution.py:406
  26.2 3.7 %product.6 = (bf16[128,1536]{1,0:T(8,128)(2,1)S(1)}, bf16[128,1536]{1,0:T(8,128)(2,1)S(1)}, bf16[3,1408,512]{2,1,0:T(8,128)(2,1)S(1)}, bf16[3,1408,256]{2,1,0:T(8,128)(2,1)S(1)}) custom-call(bf16[256,4224]{1,0:T(8,128)(2,1)S(1)} %get-tuple-element.38.design_ref, bf16[3,1408,512]{2,1,0:T(8,128)(2,1)S(1)} %get-tuple-element.45.refs_0_, ...), custom_call_target="tpu_custom_call" | custom-call | flops 3321888768 | bytes 12976128 | tf_op jit(solution)/shard_map/product/pallas_call | solution.py:220
  30.1 0.5 collective-permute-start.6
  30.5 2.5 %product.7 = (bf16[128,1024]{1,0:T(8,128)(2,1)S(1)}, bf16[128,1024]{1,0:T(8,128)(2,1)S(1)}) custom-call(bf16[256,4224]{1,0:T(8,128)(2,1)S(1)} %get-tuple-element.38.design_ref, bf16[3,1408,256]{2,1,0:T(8,128)(2,1)S(1)} %get-tuple-element.50.refs_0_, bf16[3,1408,512]{2,1,0:T(8,128)(2,1)S(1)} %get-tuple-element.51.refs_1_, ...), custom_call_target="tpu_custom_call" | custom-call | flops 2214592512 | bytes 8650752 | tf_op jit(solution)/shard_map/product/pallas_call | solution.py:220
  33.3 1.7 %collective-permute-start.8 = (bf16[64,1536]{1,0:T(8,128)(2,1)S(1)}, bf16[64,1536]{1,0:T(8,128)(2,1)S(1)}, u32[]{:S(2)}, u32[]{:S(2)}) collective-permute-start(bf16[64,1536]{1,0:T(8,128)(2,1)S(1)} %add_convert_fusion), channel_id=1, source_target_pairs={{0,16},{8,24},{16,0},{24,8},{1,17},{9,25},{17,1},{25,9},{2,18},{10... | collective-permute-start | bytes 589832 | tf_op jit(solution)/shard_map/ppermute | solution.py:406
  35.0 1.3 %collective-permute-start.10 = (bf16[64,1024]{1,0:T(8,128)(2,1)S(1)}, bf16[64,1024]{1,0:T(8,128)(2,1)S(1)}, u32[]{:S(2)}, u32[]{:S(2)}) collective-permute-start(bf16[64,1024]{1,0:T(8,128)(2,1)S(1)} %add_convert_fusion.2), channel_id=1, source_target_pairs={{0,16},{8,24},{16,0},{24,8},{1,17},{9,25},{17,1},{25,9},{2,18},{10... | collective-permute-start | bytes 393224 | tf_op jit(solution)/shard_map/ppermute | solution.py:406
  36.3 1.5 %collective-permute-done.6.refs_5_ = bf16[64,1536]{1,0:T(8,128)(2,1)S(1)} collective-permute-done((bf16[64,1536]{1,0:T(8,128)(2,1)S(1)}, bf16[64,1536]{1,0:T(8,128)(2,1)S(1)}, u32[]{:S(2)}, u32[]{:S(2)}) %collective-permute-start.6) | collective-permute-done | bytes 196640 | tf_op jit(solution)/shard_map/ppermute | solution.py:406
  37.8 2.8 %pack.3.refs_0_ = bf16[8,64,1664]{2,1,0:T(8,128)(2,1)S(1)} custom-call(s32[8]{0:T(128)S(1)} %iota_xor_fusion.1.order_ref, s32[24,128]{1,0:T(8,128)S(1)} %get-tuple-element.34.start_ref, s32[40,128]{1,0:T(8,128)S(1)} %get-tuple-element.35.inner_ref, s32[40,128]{1,0:T(8,128)S(1)} %get-tuple-element.36.tile_ref, ...), custom_call_target="tpu_custom_call" | custom-call | flops 671088640 | bytes 655360 | tf_op jit(solution)/shard_map/pack/pallas_call | solution.py:420
  40.7 1.4 %collective-permute-done.8.refs_3_ = bf16[64,1536]{1,0:T(8,128)(2,1)S(1)} collective-permute-done((bf16[64,1536]{1,0:T(8,128)(2,1)S(1)}, bf16[64,1536]{1,0:T(8,128)(2,1)S(1)}, u32[]{:S(2)}, u32[]{:S(2)}) %collective-permute-start.8) | collective-permute-done | bytes 196640 | tf_op jit(solution)/shard_map/ppermute | solution.py:406
  42.0 2.0 %pack.4.refs_0_ = bf16[8,64,1664]{2,1,0:T(8,128)(2,1)S(1)} custom-call(s32[8]{0:T(128)S(1)} %iota_xor_fusion.1.order_ref, s32[24,128]{1,0:T(8,128)S(1)} %get-tuple-element.34.start_ref, s32[40,128]{1,0:T(8,128)S(1)} %get-tuple-element.35.inner_ref, s32[40,128]{1,0:T(8,128)S(1)} %get-tuple-element.36.tile_ref, bf16[8,64,1664]{2,1,0:T(8,128)(2,1)S(1)} %pack.3.refs_0_, ...), custom_call_target="tpu_custom_call" | custom-call | flops 402653184 | bytes 393216 | tf_op jit(solution)/shard_map/pack/pallas_call | solution.py:420
  44.0 0.4 collective-permute-done.10.refs_3_
  44.4 1.5 %pack.5 = (bf16[64,1280]{1,0:T(8,128)(2,1)S(1)}, bf16[64,1280]{1,0:T(8,128)(2,1)S(1)}, bf16[64,1280]{1,0:T(8,128)(2,1)S(1)}, bf16[64,1280]{1,0:T(8,128)(2,1)S(1)...) custom-call(s32[8]{0:T(128)S(1)} %iota_xor_fusion.1.order_ref, ...), custom_call_target="tpu_custom_call" | custom-call | flops 268435456 | bytes 262144 | tf_op jit(solution)/shard_map/pack/pallas_call | solution.py:420
  46.0 4.6 %collective-permute-start.15 = (bf16[64,1280]{1,0:T(8,128)(2,1)S(1)}, bf16[64,1280]{1,0:T(8,128)(2,1)S(1)}, u32[]{:S(2)}, u32[]{:S(2)}) collective-permute-start(bf16[64,1280]{1,0:T(8,128)(2,1)S(1)} %get-tuple-element.60), channel_id=1, source_target_pairs={{0,7},{1,6},{2,5},{3,4},{4,3},{5,2},{6,1},{7,0},{8,15},{9,14},{10,... | collective-permute-start | bytes 491528 | tf_op jit(solution)/shard_map/ppermute | solution.py:441
  50.6 0.2 collective-permute-start.16
  50.8 0.8 collective-permute-start.11
  51.6 3.3 %collective-permute-start.12 = (bf16[64,1280]{1,0:T(8,128)(2,1)S(1)}, bf16[64,1280]{1,0:T(8,128)(2,1)S(1)}, u32[]{:S(2)}, u32[]{:S(2)}) collective-permute-start(bf16[64,1280]{1,0:T(8,128)(2,1)S(1)} %get-tuple-element.56), channel_id=1, source_target_pairs={{0,3},{1,2},{2,1},{3,0},{4,7},{5,6},{6,5},{7,4},{8,11},{9,10},{10,... | collective-permute-start | bytes 491528 | tf_op jit(solution)/shard_map/ppermute | solution.py:441
  54.9 1.0 %collective-permute-start.17 = (bf16[64,1280]{1,0:T(8,128)(2,1)S(1)}, bf16[64,1280]{1,0:T(8,128)(2,1)S(1)}, u32[]{:S(2)}, u32[]{:S(2)}) collective-permute-start(bf16[64,1280]{1,0:T(8,128)(2,1)S(1)} %get-tuple-element.62), channel_id=1, source_target_pairs={{0,5},{1,4},{2,7},{3,6},{4,1},{5,0},{6,3},{7,2},{8,13},{9,12},{10,... | collective-permute-start | bytes 491528 | tf_op jit(solution)/shard_map/ppermute | solution.py:441
  55.9 15.4 %collective-permute-start.13 = (bf16[64,1280]{1,0:T(8,128)(2,1)S(1)}, bf16[64,1280]{1,0:T(8,128)(2,1)S(1)}, u32[]{:S(2)}, u32[]{:S(2)}) collective-permute-start(bf16[64,1280]{1,0:T(8,128)(2,1)S(1)} %get-tuple-element.57), channel_id=1, source_target_pairs={{0,2},{1,3},{2,0},{3,1},{4,6},{5,7},{6,4},{7,5},{8,10},{9,11},{10,... | collective-permute-start | bytes 491528 | tf_op jit(solution)/shard_map/ppermute | solution.py:441
  71.3 1.6 %collective-permute-start.14 = (bf16[64,1280]{1,0:T(8,128)(2,1)S(1)}, bf16[64,1280]{1,0:T(8,128)(2,1)S(1)}, u32[]{:S(2)}, u32[]{:S(2)}) collective-permute-start(bf16[64,1280]{1,0:T(8,128)(2,1)S(1)} %get-tuple-element.58), channel_id=1, source_target_pairs={{0,1},{1,0},{2,3},{3,2},{4,5},{5,4},{6,7},{7,6},{8,9},{9,8},{10,11... | collective-permute-start | bytes 491528 | tf_op jit(solution)/shard_map/ppermute | solution.py:441
  72.8 7.5 %collective-permute-done.17.refs_3_ = bf16[64,1280]{1,0:T(8,128)(2,1)S(1)} collective-permute-done((bf16[64,1280]{1,0:T(8,128)(2,1)S(1)}, bf16[64,1280]{1,0:T(8,128)(2,1)S(1)}, u32[]{:S(2)}, u32[]{:S(2)}) %collective-permute-start.17) | collective-permute-done | bytes 163872 | tf_op jit(solution)/shard_map/ppermute | solution.py:441
  80.3 1.4 %assemble.2.refs_4_ = bf16[8,64,1280]{2,1,0:T(8,128)(2,1)} custom-call(s32[8]{0:T(128)S(1)} %iota_xor_fusion.1.order_ref, bf16[64,1280]{1,0:T(8,128)(2,1)S(1)} %get-tuple-element.59.refs_0_, bf16[64,1280]{1,0:T(8,128)(2,1)S(1)} %collective-permute-done.15.refs_1_, bf16[64,1280]{1,0:T(8,128)(2,1)S(1)} %collective-permute-done.16.refs_2_, ...), custom_call_target="tpu_custom_call" | custom-call | tf_op jit(solution)/shard_map/assemble/pallas_call | solution.py:452
  81.8 1.4 %assemble.3 = bf16[8,64,1280]{2,1,0:T(8,128)(2,1)} custom-call(s32[8]{0:T(128)S(1)} %iota_xor_fusion.1.order_ref, bf16[64,1280]{1,0:T(8,128)(2,1)S(1)} %collective-permute-done.11.refs_0_, bf16[64,1280]{1,0:T(8,128)(2,1)S(1)} %collective-permute-done.12.refs_1_, ...), custom_call_target="tpu_custom_call", output_to_operand_aliasing={{}: (5, {})} | custom-call | tf_op jit(solution)/shard_map/assemble/pallas_call | solution.py:452
  (25 shorter events, 0.8 us)
Async XLA Ops:
  1.2 12.1 %collective-permute-start.2 = (bf16[64,1408]{1,0:T(8,128)(2,1)S(1)}, bf16[64,1408]{1,0:T(8,128)(2,1)S(1)}, u32[]{:S(2)}, u32[]{:S(2)}) collective-permute-start(bf16[64,1408]{1,0:T(8,128)(2,1)S(1)} %get-tuple-element.63), channel_id=1, source_target_pairs={{0,24},{8,16},{16,8},{24,0},{1,25},{9,17},{17,9},{25,1},{2,26},{10... | collective-permute-start | bytes 540680 | tf_op jit(solution)/shard_map/ppermute | solution.py:318
  3.7 1.7 %collective-permute-start = (bf16[64,1408]{1,0:T(8,128)(2,1)S(1)}, bf16[64,1408]{1,0:T(8,128)(2,1)S(1)}, u32[]{:S(2)}, u32[]{:S(2)}) collective-permute-start(bf16[64,1408]{1,0:T(8,128)(2,1)S(1)} %get-tuple-element.64), channel_id=1, source_target_pairs={{0,8},{8,0},{16,24},{24,16},{1,9},{9,1},{17,25},{25,17},{2,10},{10... | collective-permute-start | bytes 540680 | tf_op jit(solution)/shard_map/ppermute | solution.py:318
  4.4 9.0 %collective-permute-start.1 = (bf16[64,1408]{1,0:T(8,128)(2,1)S(1)}, bf16[64,1408]{1,0:T(8,128)(2,1)S(1)}, u32[]{:S(2)}, u32[]{:S(2)}) collective-permute-start(bf16[64,1408]{1,0:T(8,128)(2,1)S(1)} %get-tuple-element.66), channel_id=1, source_target_pairs={{0,16},{8,24},{16,0},{24,8},{1,17},{9,25},{17,1},{25,9},{2,18},{10... | collective-permute-start | bytes 540680 | tf_op jit(solution)/shard_map/ppermute | solution.py:318
  5.4 7.9 %copy-start = (f32[3,1408,16]{1,2,0:T(8,128)S(1)}, f32[3,1408,16]{1,2,0:T(8,128)}, u32[]{:S(2)}) copy-start(f32[3,1408,16]{1,2,0:T(8,128)} %param.6) | copy-start | bytes 811012
  20.2 4.3 %collective-permute-start.3 = (bf16[128,1024]{1,0:T(8,128)(2,1)S(1)}, bf16[128,1024]{1,0:T(8,128)(2,1)S(1)}, u32[]{:S(2)}, u32[]{:S(2)}) collective-permute-start(bf16[128,1024]{1,0:T(8,128)(2,1)S(1)} %get-tuple-element.41), channel_id=1, source_target_pairs={{0,8},{8,0},{16,24},{24,16},{1,9},{9,1},{17,25},{25,17},{2,10},{10... | collective-permute-start | bytes 786440 | tf_op jit(solution)/shard_map/ppermute | solution.py:406
  24.2 5.7 %collective-permute-start.5 = (bf16[128,1536]{1,0:T(8,128)(2,1)S(1)}, bf16[128,1536]{1,0:T(8,128)(2,1)S(1)}, u32[]{:S(2)}, u32[]{:S(2)}) collective-permute-start(bf16[128,1536]{1,0:T(8,128)(2,1)S(1)} %get-tuple-element.44), channel_id=1, source_target_pairs={{0,8},{8,0},{16,24},{24,16},{1,9},{9,1},{17,25},{25,17},{2,10},{10... | collective-permute-start | bytes 1179656 | tf_op jit(solution)/shard_map/ppermute | solution.py:406
  24.5 6.0 %collective-permute-start.4 = (bf16[64,1024]{1,0:T(8,128)(2,1)S(1)}, bf16[64,1024]{1,0:T(8,128)(2,1)S(1)}, u32[]{:S(2)}, u32[]{:S(2)}) collective-permute-start(bf16[64,1024]{1,0:T(8,128)(2,1)S(1)} %add_convert_fusion.3.refs_3_), channel_id=1, source_target_pairs={{0,16},{8,24},{16,0},{24,8},{1,17},{9,25},{17,1},{25,9},{2,18},{10... | collective-permute-start | bytes 393224 | tf_op jit(solution)/shard_map/ppermute | solution.py:406
  29.9 3.3 %collective-permute-start.7 = (bf16[128,1536]{1,0:T(8,128)(2,1)S(1)}, bf16[128,1536]{1,0:T(8,128)(2,1)S(1)}, u32[]{:S(2)}, u32[]{:S(2)}) collective-permute-start(bf16[128,1536]{1,0:T(8,128)(2,1)S(1)} %get-tuple-element.49), channel_id=1, source_target_pairs={{0,8},{8,0},{16,24},{24,16},{1,9},{9,1},{17,25},{25,17},{2,10},{10... | collective-permute-start | bytes 1179656 | tf_op jit(solution)/shard_map/ppermute | solution.py:406
  30.1 7.8 %collective-permute-start.6 = (bf16[64,1536]{1,0:T(8,128)(2,1)S(1)}, bf16[64,1536]{1,0:T(8,128)(2,1)S(1)}, u32[]{:S(2)}, u32[]{:S(2)}) collective-permute-start(bf16[64,1536]{1,0:T(8,128)(2,1)S(1)} %add_convert_fusion.1.refs_3_), channel_id=1, source_target_pairs={{0,16},{8,24},{16,0},{24,8},{1,17},{9,25},{17,1},{25,9},{2,18},{10... | collective-permute-start | bytes 589832 | tf_op jit(solution)/shard_map/ppermute | solution.py:406
  33.0 2.0 %collective-permute-start.9 = (bf16[128,1024]{1,0:T(8,128)(2,1)S(1)}, bf16[128,1024]{1,0:T(8,128)(2,1)S(1)}, u32[]{:S(2)}, u32[]{:S(2)}) collective-permute-start(bf16[128,1024]{1,0:T(8,128)(2,1)S(1)} %get-tuple-element.54), channel_id=1, source_target_pairs={{0,8},{8,0},{16,24},{24,16},{1,9},{9,1},{17,25},{25,17},{2,10},{10... | collective-permute-start | bytes 786440 | tf_op jit(solution)/shard_map/ppermute | solution.py:406
  33.3 8.8 %collective-permute-start.8 = (bf16[64,1536]{1,0:T(8,128)(2,1)S(1)}, bf16[64,1536]{1,0:T(8,128)(2,1)S(1)}, u32[]{:S(2)}, u32[]{:S(2)}) collective-permute-start(bf16[64,1536]{1,0:T(8,128)(2,1)S(1)} %add_convert_fusion), channel_id=1, source_target_pairs={{0,16},{8,24},{16,0},{24,8},{1,17},{9,25},{17,1},{25,9},{2,18},{10... | collective-permute-start | bytes 589832 | tf_op jit(solution)/shard_map/ppermute | solution.py:406
  35.0 9.4 %collective-permute-start.10 = (bf16[64,1024]{1,0:T(8,128)(2,1)S(1)}, bf16[64,1024]{1,0:T(8,128)(2,1)S(1)}, u32[]{:S(2)}, u32[]{:S(2)}) collective-permute-start(bf16[64,1024]{1,0:T(8,128)(2,1)S(1)} %add_convert_fusion.2), channel_id=1, source_target_pairs={{0,16},{8,24},{16,0},{24,8},{1,17},{9,25},{17,1},{25,9},{2,18},{10... | collective-permute-start | bytes 393224 | tf_op jit(solution)/shard_map/ppermute | solution.py:406
  46.0 9.9 %collective-permute-start.15 = (bf16[64,1280]{1,0:T(8,128)(2,1)S(1)}, bf16[64,1280]{1,0:T(8,128)(2,1)S(1)}, u32[]{:S(2)}, u32[]{:S(2)}) collective-permute-start(bf16[64,1280]{1,0:T(8,128)(2,1)S(1)} %get-tuple-element.60), channel_id=1, source_target_pairs={{0,7},{1,6},{2,5},{3,4},{4,3},{5,2},{6,1},{7,0},{8,15},{9,14},{10,... | collective-permute-start | bytes 491528 | tf_op jit(solution)/shard_map/ppermute | solution.py:441
  50.6 20.7 %collective-permute-start.16 = (bf16[64,1280]{1,0:T(8,128)(2,1)S(1)}, bf16[64,1280]{1,0:T(8,128)(2,1)S(1)}, u32[]{:S(2)}, u32[]{:S(2)}) collective-permute-start(bf16[64,1280]{1,0:T(8,128)(2,1)S(1)} %get-tuple-element.61), channel_id=1, source_target_pairs={{0,6},{1,7},{2,4},{3,5},{4,2},{5,3},{6,0},{7,1},{8,14},{9,15},{10,... | collective-permute-start | bytes 491528 | tf_op jit(solution)/shard_map/ppermute | solution.py:441
  50.8 30.9 %collective-permute-start.11 = (bf16[64,1280]{1,0:T(8,128)(2,1)S(1)}, bf16[64,1280]{1,0:T(8,128)(2,1)S(1)}, u32[]{:S(2)}, u32[]{:S(2)}) collective-permute-start(bf16[64,1280]{1,0:T(8,128)(2,1)S(1)} %get-tuple-element.55), channel_id=1, source_target_pairs={{0,4},{1,5},{2,6},{3,7},{4,0},{5,1},{6,2},{7,3},{8,12},{9,13},{10,... | collective-permute-start | bytes 491528 | tf_op jit(solution)/shard_map/ppermute | solution.py:441
  51.6 30.2 %collective-permute-start.12 = (bf16[64,1280]{1,0:T(8,128)(2,1)S(1)}, bf16[64,1280]{1,0:T(8,128)(2,1)S(1)}, u32[]{:S(2)}, u32[]{:S(2)}) collective-permute-start(bf16[64,1280]{1,0:T(8,128)(2,1)S(1)} %get-tuple-element.56), channel_id=1, source_target_pairs={{0,3},{1,2},{2,1},{3,0},{4,7},{5,6},{6,5},{7,4},{8,11},{9,10},{10,... | collective-permute-start | bytes 491528 | tf_op jit(solution)/shard_map/ppermute | solution.py:441
  54.9 25.4 %collective-permute-start.17 = (bf16[64,1280]{1,0:T(8,128)(2,1)S(1)}, bf16[64,1280]{1,0:T(8,128)(2,1)S(1)}, u32[]{:S(2)}, u32[]{:S(2)}) collective-permute-start(bf16[64,1280]{1,0:T(8,128)(2,1)S(1)} %get-tuple-element.62), channel_id=1, source_target_pairs={{0,5},{1,4},{2,7},{3,6},{4,1},{5,0},{6,3},{7,2},{8,13},{9,12},{10,... | collective-permute-start | bytes 491528 | tf_op jit(solution)/shard_map/ppermute | solution.py:441
  55.9 25.9 %collective-permute-start.13 = (bf16[64,1280]{1,0:T(8,128)(2,1)S(1)}, bf16[64,1280]{1,0:T(8,128)(2,1)S(1)}, u32[]{:S(2)}, u32[]{:S(2)}) collective-permute-start(bf16[64,1280]{1,0:T(8,128)(2,1)S(1)} %get-tuple-element.57), channel_id=1, source_target_pairs={{0,2},{1,3},{2,0},{3,1},{4,6},{5,7},{6,4},{7,5},{8,10},{9,11},{10,... | collective-permute-start | bytes 491528 | tf_op jit(solution)/shard_map/ppermute | solution.py:441
  71.3 10.5 %collective-permute-start.14 = (bf16[64,1280]{1,0:T(8,128)(2,1)S(1)}, bf16[64,1280]{1,0:T(8,128)(2,1)S(1)}, u32[]{:S(2)}, u32[]{:S(2)}) collective-permute-start(bf16[64,1280]{1,0:T(8,128)(2,1)S(1)} %get-tuple-element.58), channel_id=1, source_target_pairs={{0,1},{1,0},{2,3},{3,2},{4,5},{5,4},{6,7},{7,6},{8,9},{9,8},{10,11... | collective-permute-start | bytes 491528 | tf_op jit(solution)/shard_map/ppermute | solution.py:441

commit v17 on v15

--- a/solution.py
+++ b/solution.py
@@ -14,9 +14,9 @@
 VOX_BLOCK = 256
 COLUMNS = 512
 ROWS = 32
-CHUNKS = 4
-COPIES = (((0, 4), (1, 6)), ((2, 2), (2, 2)), (), ((2, 2), (3, 1)), ((3, 2), (3, 1)))
-PACKS = (0, 2, 3, 4)
+CHUNKS = 3
+COPIES = (((0, 6), (1, 4)), ((1, 2), (1, 2)), ((2, 2), (2, 1)), ((2, 2), (2, 1)))
+PACKS = (0, 1, 2, 3)
 PACK_STEP = 4
 GATE = 2
 MIB = 1 << 20

time: 78.5 us -> 78.4 us (level)
  waiting for transfers between devices: 6.54 us -> 11.3 us
  starting transfers between devices: 33.9 us -> 29.4 us
    ppermute x8 -> x6, waiting for transfers between devices: 0.62 us -> 3.77 us  [shards(): lax.ppermute(send, 'chan', [(i, i ^ 1 << bit) for i in range(parts)])]
    ppermute x8 -> x6, starting transfers between devices: 6.17 us -> 3.43 us  [shards(): lax.ppermute(send, 'chan', [(i, i ^ 1 << bit) for i in range(parts)])]
    ppermute x1, starting transfers between devices: 1.73 us -> 0.5 us  [shards(): lax.ppermute(late_send, 'chan', [(i, i ^ 1 << bits - 1) for i in range(pa...]
    ppermute x1, waiting for transfers between devices: 0.01 us -> 1.2 us  [shards(): lax.ppermute(late_send, 'chan', [(i, i ^ 1 << bits - 1) for i in range(pa...]
    pallas_call x4 -> x3, Pallas kernels: 12.3 us -> 12 us  [product(): pl.pallas_call(functools.partial(product_kernel, len(taken), len(after),...]
  transfers between devices with their start and end apart: 26 -> 24, of which waited for: 7 -> 9; matrix products, arithmetic and copies ran while one was open for 1% -> 1% of each run, Pallas kernels for 33% -> 31%
where the time goes in v17:
time: 78.4 us; the launch traced here: 78.2 us
  Pallas kernels  35.2 us (45%)
  starting transfers between devices  29.4 us (38%)
  waiting for transfers between devices  11.3 us (14%)
  local copies, waits for them, and re-layouts  1.94 us (2%)
    ppermute x14, starting transfers between devices, deliver(): got[d] = lax.ppermute(packed[d], 'vox', [(i, i ^ d) for i in range(owners)])  22.3 us
    pallas_call x3, Pallas kernels, product(): pl.pallas_call(functools.partial(product_kernel, len(taken), len(after),...  12 us
    pallas_call x4, Pallas kernels, pack(): pl.pallas_call(functools.partial(pack_kernel, spread, sizes, spots, sum(w...  8.11 us
    pallas_call x1, Pallas kernels, shards(): pl.pallas_call(functools.partial(early_kernel, owners, spread), in_specs=...  7.9 us
    ppermute x14, waiting for transfers between devices, deliver(): got[d] = lax.ppermute(packed[d], 'vox', [(i, i ^ d) for i in range(owners)])  5.97 us
    pallas_call x1, Pallas kernels, shards(): pl.pallas_call(functools.partial(design_kernel, parts, firsts[1]), in_spe...  4.26 us
    ppermute x6, waiting for transfers between devices, shards(): lax.ppermute(send, 'chan', [(i, i ^ 1 << bit) for i in range(parts)])  3.77 us
    ppermute x6, starting transfers between devices, shards(): lax.ppermute(send, 'chan', [(i, i ^ 1 << bit) for i in range(parts)])  3.43 us
  transfers between devices with their start and end apart: 24, of which 9 were waited for; matrix products, arithmetic and copies ran while one was open for 1% of the time, Pallas kernels for 31%

profile of v17, /device:TPU:0, one launch (start us, length us, event | category | flops | bytes accessed | tf_op | source)
XLA Modules:
  0.0 78.2 jit_solution(9206945418587217396)
XLA Ops:
  0.0 1.2 %constant_dynamic-slice_fusion = (bf16[64,1408]{1,0:T(8,128)(2,1)S(1)}, bf16[64,1408]{1,0:T(8,128)(2,1)S(1)}, bf16[64,1408]{1,0:T(8,128)(2,1)S(1)}, bf16[64,1408]{1,0:T(8,128)(2,1)S(1)}) fusion(bf16[64,5632]{1,0:T(8,128)(2,1)} %param.5, s32[]{:T(128)S(6)} %select_n.15, s32[]{:T(128)S(6)} %select_n.13, s32[]{:T(128)S(6)} %select_n.12, s32[]{:T(128)S(6)} %select_n.14), kind=kLoop, calls=%fused_computation.4 | loop fusion | bytes 1441808 | tf_op jit(solution)/shard_map/dynamic_slice | solution.py:336
  1.2 2.4 %collective-permute-start.2 = (bf16[64,1408]{1,0:T(8,128)(2,1)S(1)}, bf16[64,1408]{1,0:T(8,128)(2,1)S(1)}, u32[]{:S(2)}, u32[]{:S(2)}) collective-permute-start(bf16[64,1408]{1,0:T(8,128)(2,1)S(1)} %get-tuple-element.95), channel_id=1, source_target_pairs={{0,24},{8,16},{16,8},{24,0},{1,25},{9,17},{17,9},{25,1},{2,26},{10... | collective-permute-start | bytes 540680 | tf_op jit(solution)/shard_map/ppermute | solution.py:338
  3.7 0.7 collective-permute-start
  4.4 0.7 pad_bitcast_fusion.table_ref
  5.4 7.9 %early.1 = (s32[40,128]{1,0:T(8,128)S(1)}, s32[40,128]{1,0:T(8,128)S(1)}, s32[24,128]{1,0:T(8,128)S(1)}, bf16[96,4224]{1,0:T(8,128)(2,1)S(1)}, bf16[3,1408,1536]...) custom-call(s32[4]{0:T(128)S(1)} %get-tuple-element.100.order_ref, ...), custom_call_target="tpu_custom_call" | custom-call | bytes 21626880 | tf_op jit(solution)/shard_map/early/pallas_call | solution.py:369
  13.4 4.3 %design.1 = (bf16[256,4224]{1,0:T(8,128)(2,1)S(1)}, bf16[3,1408,512]{2,1,0:T(8,128)(2,1)S(1)}, bf16[3,1408,512]{2,1,0:T(8,128)(2,1)S(1)}) custom-call(s32[4]{0:T(128)S(1)} %get-tuple-element.100.order_ref, s32[4]{0:T(128)S(1)} %get-tuple-element.99.place_ref, bf16[96,4224]{1,0:T(8,128)(2,1)S(1)} %get-tuple-element.53.early_ref, f32[3,16,1408]{2,1,0:T(8,128)S(1)} %bitcast.6, ...), custom_call_target="tpu_custom_call" | custom-call | bytes 8650752 | tf_op jit(solution)/shard_map/design/pallas_call | solution.py:400
  17.6 3.6 %product.3 = (bf16[128,1536]{1,0:T(8,128)(2,1)S(1)}, bf16[128,1536]{1,0:T(8,128)(2,1)S(1)}, bf16[3,1408,512]{2,1,0:T(8,128)(2,1)S(1)}, bf16[3,1408,256]{2,1,0:T(8,128)(2,1)S(1)}) custom-call(bf16[256,4224]{1,0:T(8,128)(2,1)S(1)} %get-tuple-element.54.design_ref, bf16[3,1408,1536]{2,1,0:T(8,128)(2,1)S(1)} %get-tuple-element.55.refs_0_, ...), custom_call_target="tpu_custom_call" | custom-call | flops 3321888768 | bytes 12976128 | tf_op jit(solution)/shard_map/product/pallas_call | solution.py:221
  21.7 4.8 %product.4 = (bf16[128,2048]{1,0:T(8,128)(2,1)S(1)}, bf16[128,2048]{1,0:T(8,128)(2,1)S(1)}, bf16[3,1408,512]{2,1,0:T(8,128)(2,1)S(1)}, bf16[3,1408,256]{2,1,0:T(8,128)(2,1)S(1)}) custom-call(bf16[256,4224]{1,0:T(8,128)(2,1)S(1)} %get-tuple-element.54.design_ref, bf16[3,1408,1024]{2,1,0:T(8,128)(2,1)S(1)} %get-tuple-element.58.refs_0_, ...), custom_call_target="tpu_custom_call" | custom-call | flops 4429185024 | bytes 17301504 | tf_op jit(solution)/shard_map/product/pallas_call | solution.py:221
  26.7 1.7 %collective-permute-start.4 = (bf16[32,1536]{1,0:T(8,128)(2,1)S(1)}, bf16[32,1536]{1,0:T(8,128)(2,1)S(1)}, u32[]{:S(2)}, u32[]{:S(2)}) collective-permute-start(bf16[32,1536]{1,0:T(8,128)(2,1)S(1)} %add_convert_fusion.2.refs_4_), channel_id=1, source_target_pairs={{0,16},{8,24},{16,0},{24,8},{1,17},{9,25},{17,1},{25,9},{2,18},{10... | collective-permute-start | bytes 294920 | tf_op jit(solution)/shard_map/ppermute | solution.py:427
  28.5 3.6 %product.5 = (bf16[128,1536]{1,0:T(8,128)(2,1)S(1)}, bf16[128,1536]{1,0:T(8,128)(2,1)S(1)}) custom-call(bf16[256,4224]{1,0:T(8,128)(2,1)S(1)} %get-tuple-element.54.design_ref, bf16[3,1408,512]{2,1,0:T(8,128)(2,1)S(1)} %get-tuple-element.63.refs_0_, bf16[3,1408,256]{2,1,0:T(8,128)(2,1)S(1)} %get-tuple-element.64.refs_1_, ...), custom_call_target="tpu_custom_call" | custom-call | flops 3321888768 | bytes 12976128 | tf_op jit(solution)/shard_map/product/pallas_call | solution.py:221
  32.7 1.2 %collective-permute-done.7.refs_2_.refs_9_ = bf16[128,1536]{1,0:T(8,128)(2,1)S(1)} collective-permute-done((bf16[128,1536]{1,0:T(8,128)(2,1)S(1)}, bf16[128,1536]{1,0:T(8,128)(2,1)S(1)}, u32[]{:S(2)}, u32[]{:S(2)}) %collective-permute-start.7) | collective-permute-done | bytes 393248 | tf_op jit(solution)/shard_map/ppermute | solution.py:427
  34.4 1.6 %pack.4.refs_0_ = bf16[8,32,1664]{2,1,0:T(8,128)(2,1)S(1)} custom-call(s32[8]{0:T(128)S(1)} %iota_xor_fusion.1.order_ref, s32[24,128]{1,0:T(8,128)S(1)} %get-tuple-element.50.start_ref, s32[40,128]{1,0:T(8,128)S(1)} %get-tuple-element.51.inner_ref, s32[40,128]{1,0:T(8,128)S(1)} %get-tuple-element.52.tile_ref, ...), custom_call_target="tpu_custom_call" | custom-call | flops 201326592 | bytes 196608 | tf_op jit(solution)/shard_map/pack/pallas_call | solution.py:443
  36.0 2.6 %collective-permute-done.6.refs_3_ = bf16[32,2048]{1,0:T(8,128)(2,1)S(1)} collective-permute-done((bf16[32,2048]{1,0:T(8,128)(2,1)S(1)}, bf16[32,2048]{1,0:T(8,128)(2,1)S(1)}, u32[]{:S(2)}, u32[]{:S(2)}) %collective-permute-start.6) | collective-permute-done | bytes 131104 | tf_op jit(solution)/shard_map/ppermute | solution.py:427
  38.6 1.7 %pack.5.refs_0_ = bf16[8,32,1664]{2,1,0:T(8,128)(2,1)S(1)} custom-call(s32[8]{0:T(128)S(1)} %iota_xor_fusion.1.order_ref, s32[24,128]{1,0:T(8,128)S(1)} %get-tuple-element.50.start_ref, s32[40,128]{1,0:T(8,128)S(1)} %get-tuple-element.51.inner_ref, s32[40,128]{1,0:T(8,128)S(1)} %get-tuple-element.52.tile_ref, bf16[8,32,1664]{2,1,0:T(8,128)(2,1)S(1)} %pack.4.refs_0_, ...), custom_call_target="tpu_custom_call" | custom-call | flops 268435456 | bytes 262144 | tf_op jit(solution)/shard_map/pack/pallas_call | solution.py:443
  40.3 1.9 %pack.6 = (bf16[32,1280]{1,0:T(8,128)(2,1)S(1)}, bf16[32,1280]{1,0:T(8,128)(2,1)S(1)}, bf16[32,1280]{1,0:T(8,128)(2,1)S(1)}, bf16[32,1280]{1,0:T(8,128)(2,1)S(1)...) custom-call(s32[8]{0:T(128)S(1)} %iota_xor_fusion.1.order_ref, ...), custom_call_target="tpu_custom_call" | custom-call | flops 201326592 | bytes 196608 | tf_op jit(solution)/shard_map/pack/pallas_call | solution.py:443
  42.7 4.7 %collective-permute-start.10 = (bf16[32,1280]{1,0:T(8,128)(2,1)S(1)}, bf16[32,1280]{1,0:T(8,128)(2,1)S(1)}, u32[]{:S(2)}, u32[]{:S(2)}) collective-permute-start(bf16[32,1280]{1,0:T(8,128)(2,1)S(1)} %get-tuple-element.79), channel_id=1, source_target_pairs={{0,7},{1,6},{2,5},{3,4},{4,3},{5,2},{6,1},{7,0},{8,15},{9,14},{10,... | collective-permute-start | bytes 245768 | tf_op jit(solution)/shard_map/ppermute | solution.py:464
  47.6 0.7 collective-permute-start.19
  48.3 2.0 %collective-permute-start.20 = (bf16[32,1280]{1,0:T(8,128)(2,1)S(1)}, bf16[32,1280]{1,0:T(8,128)(2,1)S(1)}, u32[]{:S(2)}, u32[]{:S(2)}) collective-permute-start(bf16[32,1280]{1,0:T(8,128)(2,1)S(1)} %get-tuple-element.90), channel_id=1, source_target_pairs={{0,4},{1,5},{2,6},{3,7},{4,0},{5,1},{6,2},{7,3},{8,12},{9,13},{10,... | collective-permute-start | bytes 245768 | tf_op jit(solution)/shard_map/ppermute | solution.py:464
  50.4 1.2 %collective-permute-done.9.refs_1_.refs_3_.refs_5_ = bf16[32,5120]{1,0:T(8,128)(2,1)S(1)} collective-permute-done((bf16[32,5120]{1,0:T(8,128)(2,1)S(1)}, bf16[32,5120]{1,0:T(8,128)(2,1)S(1)}, u32[]{:S(2)}, u32[]{:S(2)}) %collective-permute-start.9) | collective-permute-done | bytes 327712 | tf_op jit(solution)/shard_map/ppermute | solution.py:476
  51.6 2.5 %collective-permute-start.21 = (bf16[32,1280]{1,0:T(8,128)(2,1)S(1)}, bf16[32,1280]{1,0:T(8,128)(2,1)S(1)}, u32[]{:S(2)}, u32[]{:S(2)}) collective-permute-start(bf16[32,1280]{1,0:T(8,128)(2,1)S(1)} %get-tuple-element.91), channel_id=1, source_target_pairs={{0,3},{1,2},{2,1},{3,0},{4,7},{5,6},{6,5},{7,4},{8,11},{9,10},{10,... | collective-permute-start | bytes 245768 | tf_op jit(solution)/shard_map/ppermute | solution.py:464
  54.1 2.9 %pack.7 = (bf16[32,1280]{1,0:T(8,128)(2,1)S(1)}, bf16[32,1280]{1,0:T(8,128)(2,1)S(1)}, bf16[32,1280]{1,0:T(8,128)(2,1)S(1)}, bf16[32,1280]{1,0:T(8,128)(2,1)S(1)...) custom-call(s32[8]{0:T(128)S(1)} %iota_xor_fusion.1.order_ref, ...), custom_call_target="tpu_custom_call" | custom-call | flops 671088640 | bytes 655360 | tf_op jit(solution)/shard_map/pack/pallas_call | solution.py:443
  58.1 2.0 %collective-permute-done.19.refs_2_ = bf16[32,1280]{1,0:T(8,128)(2,1)S(1)} collective-permute-done((bf16[32,1280]{1,0:T(8,128)(2,1)S(1)}, bf16[32,1280]{1,0:T(8,128)(2,1)S(1)}, u32[]{:S(2)}, u32[]{:S(2)}) %collective-permute-start.19) | collective-permute-done | bytes 81952 | tf_op jit(solution)/shard_map/ppermute | solution.py:464
  60.1 3.5 %collective-permute-start.12 = (bf16[32,1280]{1,0:T(8,128)(2,1)S(1)}, bf16[32,1280]{1,0:T(8,128)(2,1)S(1)}, u32[]{:S(2)}, u32[]{:S(2)}) collective-permute-start(bf16[32,1280]{1,0:T(8,128)(2,1)S(1)} %get-tuple-element.81), channel_id=1, source_target_pairs={{0,7},{1,6},{2,5},{3,4},{4,3},{5,2},{6,1},{7,0},{8,15},{9,14},{10,... | collective-permute-start | bytes 245768 | tf_op jit(solution)/shard_map/ppermute | solution.py:464
  63.5 1.2 %collective-permute-start.13 = (bf16[32,1280]{1,0:T(8,128)(2,1)S(1)}, bf16[32,1280]{1,0:T(8,128)(2,1)S(1)}, u32[]{:S(2)}, u32[]{:S(2)}) collective-permute-start(bf16[32,1280]{1,0:T(8,128)(2,1)S(1)} %get-tuple-element.82), channel_id=1, source_target_pairs={{0,6},{1,7},{2,4},{3,5},{4,2},{5,3},{6,0},{7,1},{8,14},{9,15},{10,... | collective-permute-start | bytes 245768 | tf_op jit(solution)/shard_map/ppermute | solution.py:464
  64.8 2.9 %collective-permute-start.15 = (bf16[32,1280]{1,0:T(8,128)(2,1)S(1)}, bf16[32,1280]{1,0:T(8,128)(2,1)S(1)}, u32[]{:S(2)}, u32[]{:S(2)}) collective-permute-start(bf16[32,1280]{1,0:T(8,128)(2,1)S(1)} %get-tuple-element.84), channel_id=1, source_target_pairs={{0,4},{1,5},{2,6},{3,7},{4,0},{5,1},{6,2},{7,3},{8,12},{9,13},{10,... | collective-permute-start | bytes 245768 | tf_op jit(solution)/shard_map/ppermute | solution.py:464
  67.7 1.2 %collective-permute-start.16 = (bf16[32,1280]{1,0:T(8,128)(2,1)S(1)}, bf16[32,1280]{1,0:T(8,128)(2,1)S(1)}, u32[]{:S(2)}, u32[]{:S(2)}) collective-permute-start(bf16[32,1280]{1,0:T(8,128)(2,1)S(1)} %get-tuple-element.85), channel_id=1, source_target_pairs={{0,3},{1,2},{2,1},{3,0},{4,7},{5,6},{6,5},{7,4},{8,11},{9,10},{10,... | collective-permute-start | bytes 245768 | tf_op jit(solution)/shard_map/ppermute | solution.py:464
  68.9 1.7 %collective-permute-start.17 = (bf16[32,1280]{1,0:T(8,128)(2,1)S(1)}, bf16[32,1280]{1,0:T(8,128)(2,1)S(1)}, u32[]{:S(2)}, u32[]{:S(2)}) collective-permute-start(bf16[32,1280]{1,0:T(8,128)(2,1)S(1)} %get-tuple-element.86), channel_id=1, source_target_pairs={{0,2},{1,3},{2,0},{3,1},{4,6},{5,7},{6,4},{7,5},{8,10},{9,11},{10,... | collective-permute-start | bytes 245768 | tf_op jit(solution)/shard_map/ppermute | solution.py:464
  71.2 1.4 %assemble.2.refs_8_ = bf16[8,64,1280]{2,1,0:T(8,128)(2,1)} custom-call(s32[8]{0:T(128)S(1)} %iota_xor_fusion.1.order_ref, bf16[32,1280]{1,0:T(8,128)(2,1)S(1)} %collective-permute-done.10.refs_8_.refs_0_, bf16[32,1280]{1,0:T(8,128)(2,1)S(1)} %collective-permute-done.11.refs_9_.refs_1_, bf16[32,1280]{1,0:T(8,128)(2,1)S(1)} %collective-permute-done.19.refs_2_, ...), custom_call_target="tpu_custom_call" | custom-call | tf_op jit(solution)/shard_map/assemble/pallas_call | solution.py:494
  72.7 2.4 %collective-permute-done.14.refs_2_ = bf16[32,1280]{1,0:T(8,128)(2,1)S(1)} collective-permute-done((bf16[32,1280]{1,0:T(8,128)(2,1)S(1)}, bf16[32,1280]{1,0:T(8,128)(2,1)S(1)}, u32[]{:S(2)}, u32[]{:S(2)}) %collective-permute-start.14) | collective-permute-done | bytes 81952 | tf_op jit(solution)/shard_map/ppermute | solution.py:464
  75.0 0.8 %collective-permute-done.15.refs_3_ = bf16[32,1280]{1,0:T(8,128)(2,1)S(1)} collective-permute-done((bf16[32,1280]{1,0:T(8,128)(2,1)S(1)}, bf16[32,1280]{1,0:T(8,128)(2,1)S(1)}, u32[]{:S(2)}, u32[]{:S(2)}) %collective-permute-start.15) | collective-permute-done | bytes 81952 | tf_op jit(solution)/shard_map/ppermute | solution.py:464
  75.9 0.7 collective-permute-done.17.refs_5_
  76.6 1.4 %assemble.3 = bf16[8,64,1280]{2,1,0:T(8,128)(2,1)} custom-call(s32[8]{0:T(128)S(1)} %iota_xor_fusion.1.order_ref, bf16[32,1280]{1,0:T(8,128)(2,1)S(1)} %collective-permute-done.12.refs_0_, bf16[32,1280]{1,0:T(8,128)(2,1)S(1)} %collective-permute-done.13.refs_1_, ...), custom_call_target="tpu_custom_call", output_to_operand_aliasing={{}: (9, {})} | custom-call | tf_op jit(solution)/shard_map/assemble/pallas_call | solution.py:494
  (37 shorter events, 4.6 us)
Async XLA Ops:
  1.2 12.1 %collective-permute-start.2 = (bf16[64,1408]{1,0:T(8,128)(2,1)S(1)}, bf16[64,1408]{1,0:T(8,128)(2,1)S(1)}, u32[]{:S(2)}, u32[]{:S(2)}) collective-permute-start(bf16[64,1408]{1,0:T(8,128)(2,1)S(1)} %get-tuple-element.95), channel_id=1, source_target_pairs={{0,24},{8,16},{16,8},{24,0},{1,25},{9,17},{17,9},{25,1},{2,26},{10... | collective-permute-start | bytes 540680 | tf_op jit(solution)/shard_map/ppermute | solution.py:338
  3.7 1.7 %collective-permute-start = (bf16[64,1408]{1,0:T(8,128)(2,1)S(1)}, bf16[64,1408]{1,0:T(8,128)(2,1)S(1)}, u32[]{:S(2)}, u32[]{:S(2)}) collective-permute-start(bf16[64,1408]{1,0:T(8,128)(2,1)S(1)} %get-tuple-element.96), channel_id=1, source_target_pairs={{0,8},{8,0},{16,24},{24,16},{1,9},{9,1},{17,25},{25,17},{2,10},{10... | collective-permute-start | bytes 540680 | tf_op jit(solution)/shard_map/ppermute | solution.py:338
  4.4 9.0 %collective-permute-start.1 = (bf16[64,1408]{1,0:T(8,128)(2,1)S(1)}, bf16[64,1408]{1,0:T(8,128)(2,1)S(1)}, u32[]{:S(2)}, u32[]{:S(2)}) collective-permute-start(bf16[64,1408]{1,0:T(8,128)(2,1)S(1)} %get-tuple-element.98), channel_id=1, source_target_pairs={{0,16},{8,24},{16,0},{24,8},{1,17},{9,25},{17,1},{25,9},{2,18},{10... | collective-permute-start | bytes 540680 | tf_op jit(solution)/shard_map/ppermute | solution.py:338
  5.4 7.9 %copy-start = (f32[3,1408,16]{1,2,0:T(8,128)S(1)}, f32[3,1408,16]{1,2,0:T(8,128)}, u32[]{:S(2)}) copy-start(f32[3,1408,16]{1,2,0:T(8,128)} %param.6) | copy-start | bytes 811012
  21.3 5.4 %collective-permute-start.3 = (bf16[128,1536]{1,0:T(8,128)(2,1)S(1)}, bf16[128,1536]{1,0:T(8,128)(2,1)S(1)}, u32[]{:S(2)}, u32[]{:S(2)}) collective-permute-start(bf16[128,1536]{1,0:T(8,128)(2,1)S(1)} %get-tuple-element.57), channel_id=1, source_target_pairs={{0,8},{8,0},{16,24},{24,16},{1,9},{9,1},{17,25},{25,17},{2,10},{10... | collective-permute-start | bytes 1179656 | tf_op jit(solution)/shard_map/ppermute | solution.py:427
  26.5 5.7 %collective-permute-start.5 = (bf16[128,2048]{1,0:T(8,128)(2,1)S(1)}, bf16[128,2048]{1,0:T(8,128)(2,1)S(1)}, u32[]{:S(2)}, u32[]{:S(2)}) collective-permute-start(bf16[128,2048]{1,0:T(8,128)(2,1)S(1)} %get-tuple-element.62), channel_id=1, source_target_pairs={{0,8},{8,0},{16,24},{24,16},{1,9},{9,1},{17,25},{25,17},{2,10},{10... | collective-permute-start | bytes 1572872 | tf_op jit(solution)/shard_map/ppermute | solution.py:427
  26.7 7.7 %collective-permute-start.4 = (bf16[32,1536]{1,0:T(8,128)(2,1)S(1)}, bf16[32,1536]{1,0:T(8,128)(2,1)S(1)}, u32[]{:S(2)}, u32[]{:S(2)}) collective-permute-start(bf16[32,1536]{1,0:T(8,128)(2,1)S(1)} %add_convert_fusion.2.refs_4_), channel_id=1, source_target_pairs={{0,16},{8,24},{16,0},{24,8},{1,17},{9,25},{17,1},{25,9},{2,18},{10... | collective-permute-start | bytes 294920 | tf_op jit(solution)/shard_map/ppermute | solution.py:427
  32.1 1.8 %collective-permute-start.7 = (bf16[128,1536]{1,0:T(8,128)(2,1)S(1)}, bf16[128,1536]{1,0:T(8,128)(2,1)S(1)}, u32[]{:S(2)}, u32[]{:S(2)}) collective-permute-start(bf16[128,1536]{1,0:T(8,128)(2,1)S(1)} %get-tuple-element.68), channel_id=1, source_target_pairs={{0,8},{8,0},{16,24},{24,16},{1,9},{9,1},{17,25},{25,17},{2,10},{10... | collective-permute-start | bytes 1179656 | tf_op jit(solution)/shard_map/ppermute | solution.py:427
  32.2 6.4 %collective-permute-start.6 = (bf16[32,2048]{1,0:T(8,128)(2,1)S(1)}, bf16[32,2048]{1,0:T(8,128)(2,1)S(1)}, u32[]{:S(2)}, u32[]{:S(2)}) collective-permute-start(bf16[32,2048]{1,0:T(8,128)(2,1)S(1)} %add_convert_fusion), channel_id=1, source_target_pairs={{0,16},{8,24},{16,0},{24,8},{1,17},{9,25},{17,1},{25,9},{2,18},{10... | collective-permute-start | bytes 393224 | tf_op jit(solution)/shard_map/ppermute | solution.py:427
  33.9 6.4 %collective-permute-start.8 = (bf16[32,1536]{1,0:T(8,128)(2,1)S(1)}, bf16[32,1536]{1,0:T(8,128)(2,1)S(1)}, u32[]{:S(2)}, u32[]{:S(2)}) collective-permute-start(bf16[32,1536]{1,0:T(8,128)(2,1)S(1)} %add_convert_fusion.1), channel_id=1, source_target_pairs={{0,16},{8,24},{16,0},{24,8},{1,17},{9,25},{17,1},{25,9},{2,18},{10... | collective-permute-start | bytes 294920 | tf_op jit(solution)/shard_map/ppermute | solution.py:427
  42.2 9.3 %collective-permute-start.9 = (bf16[32,5120]{1,0:T(8,128)(2,1)S(1)}, bf16[32,5120]{1,0:T(8,128)(2,1)S(1)}, u32[]{:S(2)}, u32[]{:S(2)}) collective-permute-start(bf16[32,5120]{1,0:T(8,128)(2,1)S(1)} %get-tuple-element.70), channel_id=1, source_target_pairs={{0,16},{8,24},{16,0},{24,8},{1,17},{9,25},{17,1},{25,9},{2,18},{10... | collective-permute-start | bytes 983048 | tf_op jit(solution)/shard_map/ppermute | solution.py:476
  42.7 14.3 %collective-permute-start.10 = (bf16[32,1280]{1,0:T(8,128)(2,1)S(1)}, bf16[32,1280]{1,0:T(8,128)(2,1)S(1)}, u32[]{:S(2)}, u32[]{:S(2)}) collective-permute-start(bf16[32,1280]{1,0:T(8,128)(2,1)S(1)} %get-tuple-element.79), channel_id=1, source_target_pairs={{0,7},{1,6},{2,5},{3,4},{4,3},{5,2},{6,1},{7,0},{8,15},{9,14},{10,... | collective-permute-start | bytes 245768 | tf_op jit(solution)/shard_map/ppermute | solution.py:464
  47.4 10.2 %collective-permute-start.11 = (bf16[32,1280]{1,0:T(8,128)(2,1)S(1)}, bf16[32,1280]{1,0:T(8,128)(2,1)S(1)}, u32[]{:S(2)}, u32[]{:S(2)}) collective-permute-start(bf16[32,1280]{1,0:T(8,128)(2,1)S(1)} %get-tuple-element.80), channel_id=1, source_target_pairs={{0,6},{1,7},{2,4},{3,5},{4,2},{5,3},{6,0},{7,1},{8,14},{9,15},{10,... | collective-permute-start | bytes 245768 | tf_op jit(solution)/shard_map/ppermute | solution.py:464
  47.6 12.5 %collective-permute-start.19 = (bf16[32,1280]{1,0:T(8,128)(2,1)S(1)}, bf16[32,1280]{1,0:T(8,128)(2,1)S(1)}, u32[]{:S(2)}, u32[]{:S(2)}) collective-permute-start(bf16[32,1280]{1,0:T(8,128)(2,1)S(1)} %get-tuple-element.89), channel_id=1, source_target_pairs={{0,5},{1,4},{2,7},{3,6},{4,1},{5,0},{6,3},{7,2},{8,13},{9,12},{10,... | collective-permute-start | bytes 245768 | tf_op jit(solution)/shard_map/ppermute | solution.py:464
  48.3 15.2 %collective-permute-start.20 = (bf16[32,1280]{1,0:T(8,128)(2,1)S(1)}, bf16[32,1280]{1,0:T(8,128)(2,1)S(1)}, u32[]{:S(2)}, u32[]{:S(2)}) collective-permute-start(bf16[32,1280]{1,0:T(8,128)(2,1)S(1)} %get-tuple-element.90), channel_id=1, source_target_pairs={{0,4},{1,5},{2,6},{3,7},{4,0},{5,1},{6,2},{7,3},{8,12},{9,13},{10,... | collective-permute-start | bytes 245768 | tf_op jit(solution)/shard_map/ppermute | solution.py:464
  51.6 13.2 %collective-permute-start.21 = (bf16[32,1280]{1,0:T(8,128)(2,1)S(1)}, bf16[32,1280]{1,0:T(8,128)(2,1)S(1)}, u32[]{:S(2)}, u32[]{:S(2)}) collective-permute-start(bf16[32,1280]{1,0:T(8,128)(2,1)S(1)} %get-tuple-element.91), channel_id=1, source_target_pairs={{0,3},{1,2},{2,1},{3,0},{4,7},{5,6},{6,5},{7,4},{8,11},{9,10},{10,... | collective-permute-start | bytes 245768 | tf_op jit(solution)/shard_map/ppermute | solution.py:464
  57.0 7.7 %collective-permute-start.22 = (bf16[32,1280]{1,0:T(8,128)(2,1)S(1)}, bf16[32,1280]{1,0:T(8,128)(2,1)S(1)}, u32[]{:S(2)}, u32[]{:S(2)}) collective-permute-start(bf16[32,1280]{1,0:T(8,128)(2,1)S(1)} %get-tuple-element.92), channel_id=1, source_target_pairs={{0,2},{1,3},{2,0},{3,1},{4,6},{5,7},{6,4},{7,5},{8,10},{9,11},{10,... | collective-permute-start | bytes 245768 | tf_op jit(solution)/shard_map/ppermute | solution.py:464
  57.5 10.2 %collective-permute-start.23 = (bf16[32,1280]{1,0:T(8,128)(2,1)S(1)}, bf16[32,1280]{1,0:T(8,128)(2,1)S(1)}, u32[]{:S(2)}, u32[]{:S(2)}) collective-permute-start(bf16[32,1280]{1,0:T(8,128)(2,1)S(1)} %get-tuple-element.93), channel_id=1, source_target_pairs={{0,1},{1,0},{2,3},{3,2},{4,5},{5,4},{6,7},{7,6},{8,9},{9,8},{10,11... | collective-permute-start | bytes 245768 | tf_op jit(solution)/shard_map/ppermute | solution.py:464
  60.1 8.8 %collective-permute-start.12 = (bf16[32,1280]{1,0:T(8,128)(2,1)S(1)}, bf16[32,1280]{1,0:T(8,128)(2,1)S(1)}, u32[]{:S(2)}, u32[]{:S(2)}) collective-permute-start(bf16[32,1280]{1,0:T(8,128)(2,1)S(1)} %get-tuple-element.81), channel_id=1, source_target_pairs={{0,7},{1,6},{2,5},{3,4},{4,3},{5,2},{6,1},{7,0},{8,15},{9,14},{10,... | collective-permute-start | bytes 245768 | tf_op jit(solution)/shard_map/ppermute | solution.py:464
  63.5 7.2 %collective-permute-start.13 = (bf16[32,1280]{1,0:T(8,128)(2,1)S(1)}, bf16[32,1280]{1,0:T(8,128)(2,1)S(1)}, u32[]{:S(2)}, u32[]{:S(2)}) collective-permute-start(bf16[32,1280]{1,0:T(8,128)(2,1)S(1)} %get-tuple-element.82), channel_id=1, source_target_pairs={{0,6},{1,7},{2,4},{3,5},{4,2},{5,3},{6,0},{7,1},{8,14},{9,15},{10,... | collective-permute-start | bytes 245768 | tf_op jit(solution)/shard_map/ppermute | solution.py:464
  64.8 10.3 %collective-permute-start.14 = (bf16[32,1280]{1,0:T(8,128)(2,1)S(1)}, bf16[32,1280]{1,0:T(8,128)(2,1)S(1)}, u32[]{:S(2)}, u32[]{:S(2)}) collective-permute-start(bf16[32,1280]{1,0:T(8,128)(2,1)S(1)} %get-tuple-element.83), channel_id=1, source_target_pairs={{0,5},{1,4},{2,7},{3,6},{4,1},{5,0},{6,3},{7,2},{8,13},{9,12},{10,... | collective-permute-start | bytes 245768 | tf_op jit(solution)/shard_map/ppermute | solution.py:464
  64.8 11.1 %collective-permute-start.15 = (bf16[32,1280]{1,0:T(8,128)(2,1)S(1)}, bf16[32,1280]{1,0:T(8,128)(2,1)S(1)}, u32[]{:S(2)}, u32[]{:S(2)}) collective-permute-start(bf16[32,1280]{1,0:T(8,128)(2,1)S(1)} %get-tuple-element.84), channel_id=1, source_target_pairs={{0,4},{1,5},{2,6},{3,7},{4,0},{5,1},{6,2},{7,3},{8,12},{9,13},{10,... | collective-permute-start | bytes 245768 | tf_op jit(solution)/shard_map/ppermute | solution.py:464
  67.7 8.1 %collective-permute-start.16 = (bf16[32,1280]{1,0:T(8,128)(2,1)S(1)}, bf16[32,1280]{1,0:T(8,128)(2,1)S(1)}, u32[]{:S(2)}, u32[]{:S(2)}) collective-permute-start(bf16[32,1280]{1,0:T(8,128)(2,1)S(1)} %get-tuple-element.85), channel_id=1, source_target_pairs={{0,3},{1,2},{2,1},{3,0},{4,7},{5,6},{6,5},{7,4},{8,11},{9,10},{10,... | collective-permute-start | bytes 245768 | tf_op jit(solution)/shard_map/ppermute | solution.py:464
  68.9 7.7 %collective-permute-start.17 = (bf16[32,1280]{1,0:T(8,128)(2,1)S(1)}, bf16[32,1280]{1,0:T(8,128)(2,1)S(1)}, u32[]{:S(2)}, u32[]{:S(2)}) collective-permute-start(bf16[32,1280]{1,0:T(8,128)(2,1)S(1)} %get-tuple-element.86), channel_id=1, source_target_pairs={{0,2},{1,3},{2,0},{3,1},{4,6},{5,7},{6,4},{7,5},{8,10},{9,11},{10,... | collective-permute-start | bytes 245768 | tf_op jit(solution)/shard_map/ppermute | solution.py:464
  70.7 5.9 %collective-permute-start.18 = (bf16[32,1280]{1,0:T(8,128)(2,1)S(1)}, bf16[32,1280]{1,0:T(8,128)(2,1)S(1)}, u32[]{:S(2)}, u32[]{:S(2)}) collective-permute-start(bf16[32,1280]{1,0:T(8,128)(2,1)S(1)} %get-tuple-element.87), channel_id=1, source_target_pairs={{0,1},{1,0},{2,3},{3,2},{4,5},{5,4},{6,7},{7,6},{8,9},{9,8},{10,11... | collective-permute-start | bytes 245768 | tf_op jit(solution)/shard_map/ppermute | solution.py:464

commit v18 on v15

--- a/solution.py
+++ b/solution.py
@@ -85,7 +85,7 @@
         bases = jnp.where(mine, dot(before, totals), bases)
         starts = jnp.where(mark_lane == o, dot(block_ahead, totals), starts)
     slots = slots.astype(jnp.int32)
-    start_ref[...] = starts.astype(jnp.int32)
+    start_ref[...] = starts.astype(jnp.int32)[:, :owners]
     tile_ref[...] = owner * spread + (slots >> 7)
     inner_ref[...] = (slots - (bases.astype(jnp.int32) & -SLOT_TILE)) & (2 * SLOT_TILE - 1)
 
@@ -250,6 +250,8 @@
         add_rows(terms[-count:], each, 3 * rows, send_ref)
         add_rows(terms[-count:], each, rows, keep_ref)
         terms = terms[:-count]
+    if outs == 1:
+        packed = out_refs[0]
     owners, rows = packed.shape[:2]
     if first:
         packed[...] = terms.pop(0)[...]
@@ -316,9 +318,7 @@
     lax.fori_loop(0, count // PACK_STEP, some, 0)
     if count % PACK_STEP:
         blocks(range(count - count % PACK_STEP, count))
-    if outs == 1:
-        out_refs[0][...] = packed[...]
-    else:
+    if outs > 1:
         for d, ref in enumerate(out_refs):
             ref[...] = packed[order_ref[d], :, : ref.shape[1]]
 
@@ -373,7 +373,7 @@
         out_shape=[
             jax.ShapeDtypeStruct((voxels // LANES, LANES), jnp.int32),
             jax.ShapeDtypeStruct((voxels // LANES, LANES), jnp.int32),
-            jax.ShapeDtypeStruct((marks, LANES), jnp.int32),
+            jax.ShapeDtypeStruct((marks, owners), jnp.int32),
             jax.ShapeDtypeStruct((early_rows, lanes), jnp.bfloat16),
         ]
         + room(0),

time: 78.5 us -> 78.3 us (level)
  no operation moved by 1% of the time
where the time goes in v18:
time: 78.3 us; the launch traced here: 78.2 us
  Pallas kernels  35.3 us (45%)
  starting transfers between devices  33.8 us (43%)
  waiting for transfers between devices  6.62 us (8%)
  local copies, waits for them, and re-layouts  1.94 us (2%)
    ppermute x14, starting transfers between devices, deliver(): got[d] = lax.ppermute(packed[d], 'vox', [(i, i ^ d) for i in range(owners)])  22.8 us
    pallas_call x4, Pallas kernels, product(): pl.pallas_call(functools.partial(product_kernel, len(taken), len(after),...  12.3 us
    pallas_call x4, Pallas kernels, pack(): pl.pallas_call(functools.partial(pack_kernel, spread, sizes, spots, sum(w...  7.94 us
    pallas_call x1, Pallas kernels, shards(): pl.pallas_call(functools.partial(early_kernel, owners, spread), in_specs=...  7.9 us
    ppermute x8, starting transfers between devices, shards(): lax.ppermute(send, 'chan', [(i, i ^ 1 << bit) for i in range(parts)])  6.17 us
    ppermute x14, waiting for transfers between devices, deliver(): got[d] = lax.ppermute(packed[d], 'vox', [(i, i ^ d) for i in range(owners)])  5.61 us
    pallas_call x1, Pallas kernels, shards(): pl.pallas_call(functools.partial(design_kernel, parts, firsts[1]), in_spe...  4.26 us
    ppermute x3, starting transfers between devices, shards(): lax.ppermute(series[d], 'chan', [(i, i ^ d) for i in range(parts)])  3.16 us
  transfers between devices with their start and end apart: 26, of which 7 were waited for; matrix products, arithmetic and copies ran while one was open for 1% of the time, Pallas kernels for 33%

profile of v18, /device:TPU:0, one launch (start us, length us, event | category | flops | bytes accessed | tf_op | source)
XLA Modules:
  0.0 78.2 jit_solution(9451523060129306729)
XLA Ops:
  0.0 1.2 %constant_dynamic-slice_fusion = (bf16[64,1408]{1,0:T(8,128)(2,1)S(1)}, bf16[64,1408]{1,0:T(8,128)(2,1)S(1)}, bf16[64,1408]{1,0:T(8,128)(2,1)S(1)}, bf16[64,1408]{1,0:T(8,128)(2,1)S(1)}) fusion(bf16[64,5632]{1,0:T(8,128)(2,1)} %param.5, s32[]{:T(128)S(6)} %select_n.15, s32[]{:T(128)S(6)} %select_n.13, s32[]{:T(128)S(6)} %select_n.12, s32[]{:T(128)S(6)} %select_n.14), kind=kLoop, calls=%fused_computation.5 | loop fusion | bytes 1441808 | tf_op jit(solution)/shard_map/dynamic_slice | solution.py:336
  1.2 2.4 %collective-permute-start.2 = (bf16[64,1408]{1,0:T(8,128)(2,1)S(1)}, bf16[64,1408]{1,0:T(8,128)(2,1)S(1)}, u32[]{:S(2)}, u32[]{:S(2)}) collective-permute-start(bf16[64,1408]{1,0:T(8,128)(2,1)S(1)} %get-tuple-element.99), channel_id=1, source_target_pairs={{0,24},{8,16},{16,8},{24,0},{1,25},{9,17},{17,9},{25,1},{2,26},{10... | collective-permute-start | bytes 540680 | tf_op jit(solution)/shard_map/ppermute | solution.py:338
  4.4 0.7 pad_bitcast_fusion.table_ref
  5.4 7.9 %early.1 = (s32[40,128]{1,0:T(8,128)S(1)}, s32[40,128]{1,0:T(8,128)S(1)}, s32[24,8]{1,0:T(8,128)S(1)}, bf16[96,4224]{1,0:T(8,128)(2,1)S(1)}, bf16[3,1408,1024]{2...) custom-call(s32[4]{0:T(128)S(1)} %get-tuple-element.104.order_ref, ...), custom_call_target="tpu_custom_call" | custom-call | bytes 21626880 | tf_op jit(solution)/shard_map/early/pallas_call | solution.py:369
  13.4 4.3 %design.1 = (bf16[256,4224]{1,0:T(8,128)(2,1)S(1)}, bf16[3,1408,512]{2,1,0:T(8,128)(2,1)S(1)}, bf16[3,1408,512]{2,1,0:T(8,128)(2,1)S(1)}) custom-call(s32[4]{0:T(128)S(1)} %get-tuple-element.104.order_ref, s32[4]{0:T(128)S(1)} %get-tuple-element.103.place_ref, bf16[96,4224]{1,0:T(8,128)(2,1)S(1)} %get-tuple-element.55.early_ref, f32[3,16,1408]{2,1,0:T(8,128)S(1)} %bitcast.6, ...), custom_call_target="tpu_custom_call" | custom-call | bytes 8650752 | tf_op jit(solution)/shard_map/design/pallas_call | solution.py:400
  17.6 2.5 %product.4 = (bf16[128,1024]{1,0:T(8,128)(2,1)S(1)}, bf16[128,1024]{1,0:T(8,128)(2,1)S(1)}) custom-call(bf16[256,4224]{1,0:T(8,128)(2,1)S(1)} %get-tuple-element.56.design_ref, bf16[3,1408,1024]{2,1,0:T(8,128)(2,1)S(1)} %get-tuple-element.57.refs_0_), custom_call_target="tpu_custom_call" | custom-call | flops 2214592512 | bytes 8650752 | tf_op jit(solution)/shard_map/product/pallas_call | solution.py:221
  20.6 3.6 %product.5 = (bf16[128,1536]{1,0:T(8,128)(2,1)S(1)}, bf16[128,1536]{1,0:T(8,128)(2,1)S(1)}, bf16[3,1408,512]{2,1,0:T(8,128)(2,1)S(1)}, bf16[3,1408,256]{2,1,0:T(8,128)(2,1)S(1)}) custom-call(bf16[256,4224]{1,0:T(8,128)(2,1)S(1)} %get-tuple-element.56.design_ref, bf16[3,1408,1536]{2,1,0:T(8,128)(2,1)S(1)} %get-tuple-element.60.refs_0_, ...), custom_call_target="tpu_custom_call" | custom-call | flops 3321888768 | bytes 12976128 | tf_op jit(solution)/shard_map/product/pallas_call | solution.py:221
  24.5 1.7 %collective-permute-start.4 = (bf16[32,1024]{1,0:T(8,128)(2,1)S(1)}, bf16[32,1024]{1,0:T(8,128)(2,1)S(1)}, u32[]{:S(2)}, u32[]{:S(2)}) collective-permute-start(bf16[32,1024]{1,0:T(8,128)(2,1)S(1)} %add_convert_fusion.3.refs_3_), channel_id=1, source_target_pairs={{0,16},{8,24},{16,0},{24,8},{1,17},{9,25},{17,1},{25,9},{2,18},{10... | collective-permute-start | bytes 196616 | tf_op jit(solution)/shard_map/ppermute | solution.py:427
  26.2 3.7 %product.6 = (bf16[128,1536]{1,0:T(8,128)(2,1)S(1)}, bf16[128,1536]{1,0:T(8,128)(2,1)S(1)}, bf16[3,1408,512]{2,1,0:T(8,128)(2,1)S(1)}, bf16[3,1408,256]{2,1,0:T(8,128)(2,1)S(1)}) custom-call(bf16[256,4224]{1,0:T(8,128)(2,1)S(1)} %get-tuple-element.56.design_ref, bf16[3,1408,512]{2,1,0:T(8,128)(2,1)S(1)} %get-tuple-element.63.refs_0_, ...), custom_call_target="tpu_custom_call" | custom-call | flops 3321888768 | bytes 12976128 | tf_op jit(solution)/shard_map/product/pallas_call | solution.py:221
  30.5 2.5 %product.7 = (bf16[128,1024]{1,0:T(8,128)(2,1)S(1)}, bf16[128,1024]{1,0:T(8,128)(2,1)S(1)}) custom-call(bf16[256,4224]{1,0:T(8,128)(2,1)S(1)} %get-tuple-element.56.design_ref, bf16[3,1408,256]{2,1,0:T(8,128)(2,1)S(1)} %get-tuple-element.68.refs_0_, bf16[3,1408,512]{2,1,0:T(8,128)(2,1)S(1)} %get-tuple-element.69.refs_1_, ...), custom_call_target="tpu_custom_call" | custom-call | flops 2214592512 | bytes 8650752 | tf_op jit(solution)/shard_map/product/pallas_call | solution.py:221
  33.2 1.7 %collective-permute-start.8 = (bf16[32,1536]{1,0:T(8,128)(2,1)S(1)}, bf16[32,1536]{1,0:T(8,128)(2,1)S(1)}, u32[]{:S(2)}, u32[]{:S(2)}) collective-permute-start(bf16[32,1536]{1,0:T(8,128)(2,1)S(1)} %add_convert_fusion), channel_id=1, source_target_pairs={{0,16},{8,24},{16,0},{24,8},{1,17},{9,25},{17,1},{25,9},{2,18},{10... | collective-permute-start | bytes 294920 | tf_op jit(solution)/shard_map/ppermute | solution.py:427
  35.0 1.3 %collective-permute-start.10 = (bf16[32,1024]{1,0:T(8,128)(2,1)S(1)}, bf16[32,1024]{1,0:T(8,128)(2,1)S(1)}, u32[]{:S(2)}, u32[]{:S(2)}) collective-permute-start(bf16[32,1024]{1,0:T(8,128)(2,1)S(1)} %add_convert_fusion.2), channel_id=1, source_target_pairs={{0,16},{8,24},{16,0},{24,8},{1,17},{9,25},{17,1},{25,9},{2,18},{10... | collective-permute-start | bytes 196616 | tf_op jit(solution)/shard_map/ppermute | solution.py:427
  36.3 1.9 %pack.4.refs_0_ = bf16[8,32,1664]{2,1,0:T(8,128)(2,1)S(1)} custom-call(s32[8]{0:T(128)S(1)} %iota_xor_fusion.1.order_ref, s32[24,8]{1,0:T(8,128)S(1)} %get-tuple-element.52.start_ref, s32[40,128]{1,0:T(8,128)S(1)} %get-tuple-element.53.inner_ref, s32[40,128]{1,0:T(8,128)S(1)} %get-tuple-element.54.tile_ref, ...), custom_call_target="tpu_custom_call" | custom-call | flops 335544320 | bytes 327680 | tf_op jit(solution)/shard_map/pack/pallas_call | solution.py:443
  38.9 1.7 %pack.5.refs_0_ = bf16[8,32,1664]{2,1,0:T(8,128)(2,1)S(1)} custom-call(s32[8]{0:T(128)S(1)} %iota_xor_fusion.1.order_ref, s32[24,8]{1,0:T(8,128)S(1)} %get-tuple-element.52.start_ref, s32[40,128]{1,0:T(8,128)S(1)} %get-tuple-element.53.inner_ref, s32[40,128]{1,0:T(8,128)S(1)} %get-tuple-element.54.tile_ref, bf16[8,32,1664]{2,1,0:T(8,128)(2,1)S(1)} %pack.4.refs_0_, ...), custom_call_target="tpu_custom_call" | custom-call | flops 201326592 | bytes 196608 | tf_op jit(solution)/shard_map/pack/pallas_call | solution.py:443
  40.6 1.4 %pack.6 = (bf16[32,1280]{1,0:T(8,128)(2,1)S(1)}, bf16[32,1280]{1,0:T(8,128)(2,1)S(1)}, bf16[32,1280]{1,0:T(8,128)(2,1)S(1)}, bf16[32,1280]{1,0:T(8,128)(2,1)S(1)...) custom-call(s32[8]{0:T(128)S(1)} %iota_xor_fusion.1.order_ref, ...), custom_call_target="tpu_custom_call" | custom-call | flops 134217728 | bytes 131072 | tf_op jit(solution)/shard_map/pack/pallas_call | solution.py:443
  42.0 1.7 %collective-permute-start.11 = (bf16[32,5120]{1,0:T(8,128)(2,1)S(1)}, bf16[32,5120]{1,0:T(8,128)(2,1)S(1)}, u32[]{:S(2)}, u32[]{:S(2)}) collective-permute-start(bf16[32,5120]{1,0:T(8,128)(2,1)S(1)} %get-tuple-element.74), channel_id=1, source_target_pairs={{0,16},{8,24},{16,0},{24,8},{1,17},{9,25},{17,1},{25,9},{2,18},{10... | collective-permute-start | bytes 983048 | tf_op jit(solution)/shard_map/ppermute | solution.py:476
  43.7 4.6 %collective-permute-start.12 = (bf16[32,1280]{1,0:T(8,128)(2,1)S(1)}, bf16[32,1280]{1,0:T(8,128)(2,1)S(1)}, u32[]{:S(2)}, u32[]{:S(2)}) collective-permute-start(bf16[32,1280]{1,0:T(8,128)(2,1)S(1)} %get-tuple-element.83), channel_id=1, source_target_pairs={{0,7},{1,6},{2,5},{3,4},{4,3},{5,2},{6,1},{7,0},{8,15},{9,14},{10,... | collective-permute-start | bytes 245768 | tf_op jit(solution)/shard_map/ppermute | solution.py:464
  48.5 0.7 collective-permute-start.21
  49.3 2.1 %collective-permute-start.22 = (bf16[32,1280]{1,0:T(8,128)(2,1)S(1)}, bf16[32,1280]{1,0:T(8,128)(2,1)S(1)}, u32[]{:S(2)}, u32[]{:S(2)}) collective-permute-start(bf16[32,1280]{1,0:T(8,128)(2,1)S(1)} %get-tuple-element.94), channel_id=1, source_target_pairs={{0,4},{1,5},{2,6},{3,7},{4,0},{5,1},{6,2},{7,3},{8,12},{9,13},{10,... | collective-permute-start | bytes 245768 | tf_op jit(solution)/shard_map/ppermute | solution.py:464
  51.4 2.2 %collective-permute-start.23 = (bf16[32,1280]{1,0:T(8,128)(2,1)S(1)}, bf16[32,1280]{1,0:T(8,128)(2,1)S(1)}, u32[]{:S(2)}, u32[]{:S(2)}) collective-permute-start(bf16[32,1280]{1,0:T(8,128)(2,1)S(1)} %get-tuple-element.95), channel_id=1, source_target_pairs={{0,3},{1,2},{2,1},{3,0},{4,7},{5,6},{6,5},{7,4},{8,11},{9,10},{10,... | collective-permute-start | bytes 245768 | tf_op jit(solution)/shard_map/ppermute | solution.py:464
  53.6 2.9 %pack.7 = (bf16[32,1280]{1,0:T(8,128)(2,1)S(1)}, bf16[32,1280]{1,0:T(8,128)(2,1)S(1)}, bf16[32,1280]{1,0:T(8,128)(2,1)S(1)}, bf16[32,1280]{1,0:T(8,128)(2,1)S(1)...) custom-call(s32[8]{0:T(128)S(1)} %iota_xor_fusion.1.order_ref, ...), custom_call_target="tpu_custom_call" | custom-call | flops 671088640 | bytes 655360 | tf_op jit(solution)/shard_map/pack/pallas_call | solution.py:443
  56.5 0.8 %collective-permute-start.24 = (bf16[32,1280]{1,0:T(8,128)(2,1)S(1)}, bf16[32,1280]{1,0:T(8,128)(2,1)S(1)}, u32[]{:S(2)}, u32[]{:S(2)}) collective-permute-start(bf16[32,1280]{1,0:T(8,128)(2,1)S(1)} %get-tuple-element.96), channel_id=1, source_target_pairs={{0,2},{1,3},{2,0},{3,1},{4,6},{5,7},{6,4},{7,5},{8,10},{9,11},{10,... | collective-permute-start | bytes 245768 | tf_op jit(solution)/shard_map/ppermute | solution.py:464
  57.9 2.1 %collective-permute-done.21.refs_2_ = bf16[32,1280]{1,0:T(8,128)(2,1)S(1)} collective-permute-done((bf16[32,1280]{1,0:T(8,128)(2,1)S(1)}, bf16[32,1280]{1,0:T(8,128)(2,1)S(1)}, u32[]{:S(2)}, u32[]{:S(2)}) %collective-permute-start.21) | collective-permute-done | bytes 81952 | tf_op jit(solution)/shard_map/ppermute | solution.py:464
  60.0 4.3 %collective-permute-start.14 = (bf16[32,1280]{1,0:T(8,128)(2,1)S(1)}, bf16[32,1280]{1,0:T(8,128)(2,1)S(1)}, u32[]{:S(2)}, u32[]{:S(2)}) collective-permute-start(bf16[32,1280]{1,0:T(8,128)(2,1)S(1)} %get-tuple-element.85), channel_id=1, source_target_pairs={{0,7},{1,6},{2,5},{3,4},{4,3},{5,2},{6,1},{7,0},{8,15},{9,14},{10,... | collective-permute-start | bytes 245768 | tf_op jit(solution)/shard_map/ppermute | solution.py:464
  64.3 0.9 %collective-permute-start.15 = (bf16[32,1280]{1,0:T(8,128)(2,1)S(1)}, bf16[32,1280]{1,0:T(8,128)(2,1)S(1)}, u32[]{:S(2)}, u32[]{:S(2)}) collective-permute-start(bf16[32,1280]{1,0:T(8,128)(2,1)S(1)} %get-tuple-element.86), channel_id=1, source_target_pairs={{0,6},{1,7},{2,4},{3,5},{4,2},{5,3},{6,0},{7,1},{8,14},{9,15},{10,... | collective-permute-start | bytes 245768 | tf_op jit(solution)/shard_map/ppermute | solution.py:464
  65.2 2.9 %collective-permute-start.17 = (bf16[32,1280]{1,0:T(8,128)(2,1)S(1)}, bf16[32,1280]{1,0:T(8,128)(2,1)S(1)}, u32[]{:S(2)}, u32[]{:S(2)}) collective-permute-start(bf16[32,1280]{1,0:T(8,128)(2,1)S(1)} %get-tuple-element.88), channel_id=1, source_target_pairs={{0,4},{1,5},{2,6},{3,7},{4,0},{5,1},{6,2},{7,3},{8,12},{9,13},{10,... | collective-permute-start | bytes 245768 | tf_op jit(solution)/shard_map/ppermute | solution.py:464
  68.0 1.6 %collective-permute-start.18 = (bf16[32,1280]{1,0:T(8,128)(2,1)S(1)}, bf16[32,1280]{1,0:T(8,128)(2,1)S(1)}, u32[]{:S(2)}, u32[]{:S(2)}) collective-permute-start(bf16[32,1280]{1,0:T(8,128)(2,1)S(1)} %get-tuple-element.89), channel_id=1, source_target_pairs={{0,3},{1,2},{2,1},{3,0},{4,7},{5,6},{6,5},{7,4},{8,11},{9,10},{10,... | collective-permute-start | bytes 245768 | tf_op jit(solution)/shard_map/ppermute | solution.py:464
  69.7 1.3 %collective-permute-start.19 = (bf16[32,1280]{1,0:T(8,128)(2,1)S(1)}, bf16[32,1280]{1,0:T(8,128)(2,1)S(1)}, u32[]{:S(2)}, u32[]{:S(2)}) collective-permute-start(bf16[32,1280]{1,0:T(8,128)(2,1)S(1)} %get-tuple-element.90), channel_id=1, source_target_pairs={{0,2},{1,3},{2,0},{3,1},{4,6},{5,7},{6,4},{7,5},{8,10},{9,11},{10,... | collective-permute-start | bytes 245768 | tf_op jit(solution)/shard_map/ppermute | solution.py:464
  72.0 1.4 %assemble.2.refs_8_ = bf16[8,64,1280]{2,1,0:T(8,128)(2,1)} custom-call(s32[8]{0:T(128)S(1)} %iota_xor_fusion.1.order_ref, bf16[32,1280]{1,0:T(8,128)(2,1)S(1)} %collective-permute-done.12.refs_8_.refs_0_, bf16[32,1280]{1,0:T(8,128)(2,1)S(1)} %collective-permute-done.13.refs_9_.refs_1_, bf16[32,1280]{1,0:T(8,128)(2,1)S(1)} %collective-permute-done.21.refs_2_, ...), custom_call_target="tpu_custom_call" | custom-call | tf_op jit(solution)/shard_map/assemble/pallas_call | solution.py:494
  73.4 1.7 %collective-permute-done.16.refs_2_ = bf16[32,1280]{1,0:T(8,128)(2,1)S(1)} collective-permute-done((bf16[32,1280]{1,0:T(8,128)(2,1)S(1)}, bf16[32,1280]{1,0:T(8,128)(2,1)S(1)}, u32[]{:S(2)}, u32[]{:S(2)}) %collective-permute-start.16) | collective-permute-done | bytes 81952 | tf_op jit(solution)/shard_map/ppermute | solution.py:464
  75.8 0.8 collective-permute-done.19.refs_5_
  76.6 1.4 %assemble.3 = bf16[8,64,1280]{2,1,0:T(8,128)(2,1)} custom-call(s32[8]{0:T(128)S(1)} %iota_xor_fusion.1.order_ref, bf16[32,1280]{1,0:T(8,128)(2,1)S(1)} %collective-permute-done.14.refs_0_, bf16[32,1280]{1,0:T(8,128)(2,1)S(1)} %collective-permute-done.15.refs_1_, ...), custom_call_target="tpu_custom_call", output_to_operand_aliasing={{}: (9, {})} | custom-call | tf_op jit(solution)/shard_map/assemble/pallas_call | solution.py:494
  (43 shorter events, 5.6 us)
Async XLA Ops:
  1.2 12.1 %collective-permute-start.2 = (bf16[64,1408]{1,0:T(8,128)(2,1)S(1)}, bf16[64,1408]{1,0:T(8,128)(2,1)S(1)}, u32[]{:S(2)}, u32[]{:S(2)}) collective-permute-start(bf16[64,1408]{1,0:T(8,128)(2,1)S(1)} %get-tuple-element.99), channel_id=1, source_target_pairs={{0,24},{8,16},{16,8},{24,0},{1,25},{9,17},{17,9},{25,1},{2,26},{10... | collective-permute-start | bytes 540680 | tf_op jit(solution)/shard_map/ppermute | solution.py:338
  3.7 1.7 %collective-permute-start = (bf16[64,1408]{1,0:T(8,128)(2,1)S(1)}, bf16[64,1408]{1,0:T(8,128)(2,1)S(1)}, u32[]{:S(2)}, u32[]{:S(2)}) collective-permute-start(bf16[64,1408]{1,0:T(8,128)(2,1)S(1)} %get-tuple-element.100), channel_id=1, source_target_pairs={{0,8},{8,0},{16,24},{24,16},{1,9},{9,1},{17,25},{25,17},{2,10},{10... | collective-permute-start | bytes 540680 | tf_op jit(solution)/shard_map/ppermute | solution.py:338
  4.4 9.0 %collective-permute-start.1 = (bf16[64,1408]{1,0:T(8,128)(2,1)S(1)}, bf16[64,1408]{1,0:T(8,128)(2,1)S(1)}, u32[]{:S(2)}, u32[]{:S(2)}) collective-permute-start(bf16[64,1408]{1,0:T(8,128)(2,1)S(1)} %get-tuple-element.102), channel_id=1, source_target_pairs={{0,16},{8,24},{16,0},{24,8},{1,17},{9,25},{17,1},{25,9},{2,18},{10... | collective-permute-start | bytes 540680 | tf_op jit(solution)/shard_map/ppermute | solution.py:338
  5.4 7.9 %copy-start = (f32[3,1408,16]{1,2,0:T(8,128)S(1)}, f32[3,1408,16]{1,2,0:T(8,128)}, u32[]{:S(2)}) copy-start(f32[3,1408,16]{1,2,0:T(8,128)} %param.6) | copy-start | bytes 811012
  20.2 4.3 %collective-permute-start.3 = (bf16[128,1024]{1,0:T(8,128)(2,1)S(1)}, bf16[128,1024]{1,0:T(8,128)(2,1)S(1)}, u32[]{:S(2)}, u32[]{:S(2)}) collective-permute-start(bf16[128,1024]{1,0:T(8,128)(2,1)S(1)} %get-tuple-element.59), channel_id=1, source_target_pairs={{0,8},{8,0},{16,24},{24,16},{1,9},{9,1},{17,25},{25,17},{2,10},{10... | collective-permute-start | bytes 786440 | tf_op jit(solution)/shard_map/ppermute | solution.py:427
  24.2 5.7 %collective-permute-start.5 = (bf16[128,1536]{1,0:T(8,128)(2,1)S(1)}, bf16[128,1536]{1,0:T(8,128)(2,1)S(1)}, u32[]{:S(2)}, u32[]{:S(2)}) collective-permute-start(bf16[128,1536]{1,0:T(8,128)(2,1)S(1)} %get-tuple-element.62), channel_id=1, source_target_pairs={{0,8},{8,0},{16,24},{24,16},{1,9},{9,1},{17,25},{25,17},{2,10},{10... | collective-permute-start | bytes 1179656 | tf_op jit(solution)/shard_map/ppermute | solution.py:427
  24.5 6.0 %collective-permute-start.4 = (bf16[32,1024]{1,0:T(8,128)(2,1)S(1)}, bf16[32,1024]{1,0:T(8,128)(2,1)S(1)}, u32[]{:S(2)}, u32[]{:S(2)}) collective-permute-start(bf16[32,1024]{1,0:T(8,128)(2,1)S(1)} %add_convert_fusion.3.refs_3_), channel_id=1, source_target_pairs={{0,16},{8,24},{16,0},{24,8},{1,17},{9,25},{17,1},{25,9},{2,18},{10... | collective-permute-start | bytes 196616 | tf_op jit(solution)/shard_map/ppermute | solution.py:427
  29.9 3.3 %collective-permute-start.7 = (bf16[128,1536]{1,0:T(8,128)(2,1)S(1)}, bf16[128,1536]{1,0:T(8,128)(2,1)S(1)}, u32[]{:S(2)}, u32[]{:S(2)}) collective-permute-start(bf16[128,1536]{1,0:T(8,128)(2,1)S(1)} %get-tuple-element.67), channel_id=1, source_target_pairs={{0,8},{8,0},{16,24},{24,16},{1,9},{9,1},{17,25},{25,17},{2,10},{10... | collective-permute-start | bytes 1179656 | tf_op jit(solution)/shard_map/ppermute | solution.py:427
  30.0 6.3 %collective-permute-start.6 = (bf16[32,1536]{1,0:T(8,128)(2,1)S(1)}, bf16[32,1536]{1,0:T(8,128)(2,1)S(1)}, u32[]{:S(2)}, u32[]{:S(2)}) collective-permute-start(bf16[32,1536]{1,0:T(8,128)(2,1)S(1)} %add_convert_fusion.1.refs_3_), channel_id=1, source_target_pairs={{0,16},{8,24},{16,0},{24,8},{1,17},{9,25},{17,1},{25,9},{2,18},{10... | collective-permute-start | bytes 294920 | tf_op jit(solution)/shard_map/ppermute | solution.py:427
  33.0 2.0 %collective-permute-start.9 = (bf16[128,1024]{1,0:T(8,128)(2,1)S(1)}, bf16[128,1024]{1,0:T(8,128)(2,1)S(1)}, u32[]{:S(2)}, u32[]{:S(2)}) collective-permute-start(bf16[128,1024]{1,0:T(8,128)(2,1)S(1)} %get-tuple-element.72), channel_id=1, source_target_pairs={{0,8},{8,0},{16,24},{24,16},{1,9},{9,1},{17,25},{25,17},{2,10},{10... | collective-permute-start | bytes 786440 | tf_op jit(solution)/shard_map/ppermute | solution.py:427
  33.2 5.7 %collective-permute-start.8 = (bf16[32,1536]{1,0:T(8,128)(2,1)S(1)}, bf16[32,1536]{1,0:T(8,128)(2,1)S(1)}, u32[]{:S(2)}, u32[]{:S(2)}) collective-permute-start(bf16[32,1536]{1,0:T(8,128)(2,1)S(1)} %add_convert_fusion), channel_id=1, source_target_pairs={{0,16},{8,24},{16,0},{24,8},{1,17},{9,25},{17,1},{25,9},{2,18},{10... | collective-permute-start | bytes 294920 | tf_op jit(solution)/shard_map/ppermute | solution.py:427
  35.0 5.6 %collective-permute-start.10 = (bf16[32,1024]{1,0:T(8,128)(2,1)S(1)}, bf16[32,1024]{1,0:T(8,128)(2,1)S(1)}, u32[]{:S(2)}, u32[]{:S(2)}) collective-permute-start(bf16[32,1024]{1,0:T(8,128)(2,1)S(1)} %add_convert_fusion.2), channel_id=1, source_target_pairs={{0,16},{8,24},{16,0},{24,8},{1,17},{9,25},{17,1},{25,9},{2,18},{10... | collective-permute-start | bytes 196616 | tf_op jit(solution)/shard_map/ppermute | solution.py:427
  42.0 9.4 %collective-permute-start.11 = (bf16[32,5120]{1,0:T(8,128)(2,1)S(1)}, bf16[32,5120]{1,0:T(8,128)(2,1)S(1)}, u32[]{:S(2)}, u32[]{:S(2)}) collective-permute-start(bf16[32,5120]{1,0:T(8,128)(2,1)S(1)} %get-tuple-element.74), channel_id=1, source_target_pairs={{0,16},{8,24},{16,0},{24,8},{1,17},{9,25},{17,1},{25,9},{2,18},{10... | collective-permute-start | bytes 983048 | tf_op jit(solution)/shard_map/ppermute | solution.py:476
  43.7 12.8 %collective-permute-start.12 = (bf16[32,1280]{1,0:T(8,128)(2,1)S(1)}, bf16[32,1280]{1,0:T(8,128)(2,1)S(1)}, u32[]{:S(2)}, u32[]{:S(2)}) collective-permute-start(bf16[32,1280]{1,0:T(8,128)(2,1)S(1)} %get-tuple-element.83), channel_id=1, source_target_pairs={{0,7},{1,6},{2,5},{3,4},{4,3},{5,2},{6,1},{7,0},{8,15},{9,14},{10,... | collective-permute-start | bytes 245768 | tf_op jit(solution)/shard_map/ppermute | solution.py:464
  48.3 9.1 %collective-permute-start.13 = (bf16[32,1280]{1,0:T(8,128)(2,1)S(1)}, bf16[32,1280]{1,0:T(8,128)(2,1)S(1)}, u32[]{:S(2)}, u32[]{:S(2)}) collective-permute-start(bf16[32,1280]{1,0:T(8,128)(2,1)S(1)} %get-tuple-element.84), channel_id=1, source_target_pairs={{0,6},{1,7},{2,4},{3,5},{4,2},{5,3},{6,0},{7,1},{8,14},{9,15},{10,... | collective-permute-start | bytes 245768 | tf_op jit(solution)/shard_map/ppermute | solution.py:464
  48.5 11.5 %collective-permute-start.21 = (bf16[32,1280]{1,0:T(8,128)(2,1)S(1)}, bf16[32,1280]{1,0:T(8,128)(2,1)S(1)}, u32[]{:S(2)}, u32[]{:S(2)}) collective-permute-start(bf16[32,1280]{1,0:T(8,128)(2,1)S(1)} %get-tuple-element.93), channel_id=1, source_target_pairs={{0,5},{1,4},{2,7},{3,6},{4,1},{5,0},{6,3},{7,2},{8,13},{9,12},{10,... | collective-permute-start | bytes 245768 | tf_op jit(solution)/shard_map/ppermute | solution.py:464
  49.3 15.0 %collective-permute-start.22 = (bf16[32,1280]{1,0:T(8,128)(2,1)S(1)}, bf16[32,1280]{1,0:T(8,128)(2,1)S(1)}, u32[]{:S(2)}, u32[]{:S(2)}) collective-permute-start(bf16[32,1280]{1,0:T(8,128)(2,1)S(1)} %get-tuple-element.94), channel_id=1, source_target_pairs={{0,4},{1,5},{2,6},{3,7},{4,0},{5,1},{6,2},{7,3},{8,12},{9,13},{10,... | collective-permute-start | bytes 245768 | tf_op jit(solution)/shard_map/ppermute | solution.py:464
  51.4 13.8 %collective-permute-start.23 = (bf16[32,1280]{1,0:T(8,128)(2,1)S(1)}, bf16[32,1280]{1,0:T(8,128)(2,1)S(1)}, u32[]{:S(2)}, u32[]{:S(2)}) collective-permute-start(bf16[32,1280]{1,0:T(8,128)(2,1)S(1)} %get-tuple-element.95), channel_id=1, source_target_pairs={{0,3},{1,2},{2,1},{3,0},{4,7},{5,6},{6,5},{7,4},{8,11},{9,10},{10,... | collective-permute-start | bytes 245768 | tf_op jit(solution)/shard_map/ppermute | solution.py:464
  56.5 8.6 %collective-permute-start.24 = (bf16[32,1280]{1,0:T(8,128)(2,1)S(1)}, bf16[32,1280]{1,0:T(8,128)(2,1)S(1)}, u32[]{:S(2)}, u32[]{:S(2)}) collective-permute-start(bf16[32,1280]{1,0:T(8,128)(2,1)S(1)} %get-tuple-element.96), channel_id=1, source_target_pairs={{0,2},{1,3},{2,0},{3,1},{4,6},{5,7},{6,4},{7,5},{8,10},{9,11},{10,... | collective-permute-start | bytes 245768 | tf_op jit(solution)/shard_map/ppermute | solution.py:464
  57.4 10.7 %collective-permute-start.25 = (bf16[32,1280]{1,0:T(8,128)(2,1)S(1)}, bf16[32,1280]{1,0:T(8,128)(2,1)S(1)}, u32[]{:S(2)}, u32[]{:S(2)}) collective-permute-start(bf16[32,1280]{1,0:T(8,128)(2,1)S(1)} %get-tuple-element.97), channel_id=1, source_target_pairs={{0,1},{1,0},{2,3},{3,2},{4,5},{5,4},{6,7},{7,6},{8,9},{9,8},{10,11... | collective-permute-start | bytes 245768 | tf_op jit(solution)/shard_map/ppermute | solution.py:464
  60.0 9.6 %collective-permute-start.14 = (bf16[32,1280]{1,0:T(8,128)(2,1)S(1)}, bf16[32,1280]{1,0:T(8,128)(2,1)S(1)}, u32[]{:S(2)}, u32[]{:S(2)}) collective-permute-start(bf16[32,1280]{1,0:T(8,128)(2,1)S(1)} %get-tuple-element.85), channel_id=1, source_target_pairs={{0,7},{1,6},{2,5},{3,4},{4,3},{5,2},{6,1},{7,0},{8,15},{9,14},{10,... | collective-permute-start | bytes 245768 | tf_op jit(solution)/shard_map/ppermute | solution.py:464
  64.3 7.0 %collective-permute-start.15 = (bf16[32,1280]{1,0:T(8,128)(2,1)S(1)}, bf16[32,1280]{1,0:T(8,128)(2,1)S(1)}, u32[]{:S(2)}, u32[]{:S(2)}) collective-permute-start(bf16[32,1280]{1,0:T(8,128)(2,1)S(1)} %get-tuple-element.86), channel_id=1, source_target_pairs={{0,6},{1,7},{2,4},{3,5},{4,2},{5,3},{6,0},{7,1},{8,14},{9,15},{10,... | collective-permute-start | bytes 245768 | tf_op jit(solution)/shard_map/ppermute | solution.py:464
  65.2 10.0 %collective-permute-start.16 = (bf16[32,1280]{1,0:T(8,128)(2,1)S(1)}, bf16[32,1280]{1,0:T(8,128)(2,1)S(1)}, u32[]{:S(2)}, u32[]{:S(2)}) collective-permute-start(bf16[32,1280]{1,0:T(8,128)(2,1)S(1)} %get-tuple-element.87), channel_id=1, source_target_pairs={{0,5},{1,4},{2,7},{3,6},{4,1},{5,0},{6,3},{7,2},{8,13},{9,12},{10,... | collective-permute-start | bytes 245768 | tf_op jit(solution)/shard_map/ppermute | solution.py:464
  65.2 10.6 %collective-permute-start.17 = (bf16[32,1280]{1,0:T(8,128)(2,1)S(1)}, bf16[32,1280]{1,0:T(8,128)(2,1)S(1)}, u32[]{:S(2)}, u32[]{:S(2)}) collective-permute-start(bf16[32,1280]{1,0:T(8,128)(2,1)S(1)} %get-tuple-element.88), channel_id=1, source_target_pairs={{0,4},{1,5},{2,6},{3,7},{4,0},{5,1},{6,2},{7,3},{8,12},{9,13},{10,... | collective-permute-start | bytes 245768 | tf_op jit(solution)/shard_map/ppermute | solution.py:464
  68.0 7.7 %collective-permute-start.18 = (bf16[32,1280]{1,0:T(8,128)(2,1)S(1)}, bf16[32,1280]{1,0:T(8,128)(2,1)S(1)}, u32[]{:S(2)}, u32[]{:S(2)}) collective-permute-start(bf16[32,1280]{1,0:T(8,128)(2,1)S(1)} %get-tuple-element.89), channel_id=1, source_target_pairs={{0,3},{1,2},{2,1},{3,0},{4,7},{5,6},{6,5},{7,4},{8,11},{9,10},{10,... | collective-permute-start | bytes 245768 | tf_op jit(solution)/shard_map/ppermute | solution.py:464
  69.7 6.9 %collective-permute-start.19 = (bf16[32,1280]{1,0:T(8,128)(2,1)S(1)}, bf16[32,1280]{1,0:T(8,128)(2,1)S(1)}, u32[]{:S(2)}, u32[]{:S(2)}) collective-permute-start(bf16[32,1280]{1,0:T(8,128)(2,1)S(1)} %get-tuple-element.90), channel_id=1, source_target_pairs={{0,2},{1,3},{2,0},{3,1},{4,6},{5,7},{6,4},{7,5},{8,10},{9,11},{10,... | collective-permute-start | bytes 245768 | tf_op jit(solution)/shard_map/ppermute | solution.py:464
  71.3 5.2 %collective-permute-start.20 = (bf16[32,1280]{1,0:T(8,128)(2,1)S(1)}, bf16[32,1280]{1,0:T(8,128)(2,1)S(1)}, u32[]{:S(2)}, u32[]{:S(2)}) collective-permute-start(bf16[32,1280]{1,0:T(8,128)(2,1)S(1)} %get-tuple-element.91), channel_id=1, source_target_pairs={{0,1},{1,0},{2,3},{3,2},{4,5},{5,4},{6,7},{7,6},{8,9},{9,8},{10,11... | collective-permute-start | bytes 245768 | tf_op jit(solution)/shard_map/ppermute | solution.py:464
